TPU v7x, 32 devices: a whole 2x2x4 slice. The times are simulated.
32 devices in a mesh: ep: 2 (over x), row: 4 (over y, core), col: 4 (over z).
Axes of the slice: x: 2, y: 2, z: 4, core: 2. Of those that a mesh axis runs over, the one named last changes fastest.
Arguments:
- design: bfloat16 [512, 16384], P(('ep', 'col'), 'row'), may hold values from -0.125 to 0.125
- taps: float32 [64], replicated, may hold values from -1 to 1
- tap_count: int32 [512], P(('ep', 'col')), may hold values from 32 to 64
- order: int32 [16384], P('row'), may hold values from 0 to 16383, as said below
- regular: float32 [16384], replicated, may hold values from 0.5 to 2
Outputs:
- factored: float32 [16384, 16384], P('row', ('ep', 'col'))
Inputs may be any that keep to these rules, and one draw needn't show every extreme that they name: `order`: a permutation of 0 to 16383 that maps every index into its own aligned group of 128.
All inputs are finite; a program needn't handle non-finite values.
Results may differ from a plain program's by a relative error of at most 0.0037.
Values may be sent and summed in bfloat16 or wider, within the bound.
No kernel may reach another device: no remote copies, remote signals or barrier semaphores. Data moves between devices by JAX's collectives and lax.ppermute only.
A program may use at most 128 MiB of HBM per device.

v0:
```python
import jax
import jax.numpy as jnp
from jax import lax
from jax.sharding import PartitionSpec as P

P_SIZE = 16384
PANEL = 256
PB = 128


def from_behind(block, axis, distance):
    devices = range(lax.axis_size(axis))
    route = [(i - distance, i) for i in devices if i - distance in devices]
    return lax.ppermute(block, axis, route)


def broadcast(block, axis, source):
    block = jnp.where(lax.axis_index(axis) == source, block, jnp.zeros_like(block))
    return lax.psum(block, axis)


def contract_epochs(left_rows, right_cols):
    return lax.dot_general(
        left_rows, right_cols, (((0,), (0,)), ((), ())), preferred_element_type=jnp.float32
    )


def solve_right(factor, matrix):
    return jax.scipy.linalg.solve_triangular(factor, matrix.T, lower=True).T


def on_device(design, taps, tap_count, order, regular):
    local_epochs, rows_dev = design.shape
    tap_total = taps.shape[0]
    lag_rows = tap_total - 1
    earlier = from_behind(design[local_epochs - lag_rows :], ("ep", "col"), 1)
    extended = jnp.concatenate([earlier, design], axis=0)
    row_index = jnp.arange(local_epochs, dtype=jnp.int32)[:, None]
    col_index = jnp.arange(local_epochs + lag_rows, dtype=jnp.int32)[None, :]
    offset = row_index + lag_rows - col_index
    tap_ids = jnp.arange(tap_total, dtype=jnp.int32)[None, None, :]
    matches = (offset[:, :, None] == tap_ids) & (tap_ids < tap_count[:, None, None])
    toeplitz = jnp.sum(jnp.where(matches, taps[None, None, :], 0.0), axis=2).astype(jnp.bfloat16)
    filtered = jnp.dot(toeplitz, extended, preferred_element_type=jnp.float32).astype(jnp.bfloat16)
    group_count = rows_dev // PB
    local_index = (order % PB).reshape(group_count, PB)
    one_hot = (local_index[:, :, None] == jnp.arange(PB, dtype=jnp.int32)[None, None, :]).astype(
        jnp.bfloat16
    )
    permuted = jnp.einsum(
        "tbk,bjk->tbj",
        filtered.reshape(local_epochs, group_count, PB),
        one_hot,
        preferred_element_type=jnp.float32,
    )
    permuted = permuted.astype(jnp.bfloat16).reshape(local_epochs, rows_dev)
    column_groups = lax.axis_size(("ep", "col"))
    cols_dev = P_SIZE // column_groups
    column_group = lax.axis_index(("ep", "col"))
    grid_row = lax.axis_index("row")
    left_rows = lax.all_gather(permuted, ("ep", "col"), axis=0, tiled=True)
    wide_rows = lax.all_gather(permuted, "row", axis=1, tiled=True)
    right_cols = lax.all_to_all(wide_rows, ("ep", "col"), split_axis=1, concat_axis=0, tiled=True)
    normal_tile = contract_epochs(left_rows, right_cols)
    global_rows = grid_row * rows_dev + jnp.arange(rows_dev, dtype=jnp.int32)
    global_cols = column_group * cols_dev + jnp.arange(cols_dev, dtype=jnp.int32)
    reg_rows = lax.dynamic_slice_in_dim(regular, grid_row * rows_dev, rows_dev, 0)
    reg_cols = lax.dynamic_slice_in_dim(regular, column_group * cols_dev, cols_dev, 0)
    on_diagonal = global_rows[:, None] == global_cols[None, :]
    normal_tile = normal_tile + jnp.where(on_diagonal, reg_rows[:, None], 0.0)
    rebuilt_history = []
    for section in range(2):
        start_col = section * PANEL
        end_col = start_col + PANEL
        col_owner, col_offset = divmod(start_col, cols_dev)
        panel_epochs = broadcast(
            right_cols[:, col_offset : col_offset + PANEL], ("ep", "col"), col_owner
        )
        panel_ids = start_col + jnp.arange(PANEL, dtype=jnp.int32)
        rows_term = contract_epochs(left_rows, panel_epochs)
        rows_term = rows_term + jnp.where(
            global_rows[:, None] == panel_ids[None, :], reg_rows[:, None], 0.0
        )
        cols_term = contract_epochs(right_cols, panel_epochs)
        cols_term = cols_term + jnp.where(
            global_cols[:, None] == panel_ids[None, :], reg_cols[:, None], 0.0
        )
        diag_block = contract_epochs(panel_epochs, panel_epochs) + jnp.diag(
            regular[start_col:end_col]
        )
        for old_epochs, old_factor, old_rows, old_cols in rebuilt_history:
            cross = contract_epochs(panel_epochs, old_epochs)
            old_diag = solve_right(old_factor, cross)
            rows_term = rows_term - jnp.dot(old_rows, old_diag.T, precision=lax.Precision.HIGHEST)
            cols_term = cols_term - jnp.dot(old_cols, old_diag.T, precision=lax.Precision.HIGHEST)
            diag_block = diag_block - jnp.dot(old_diag, old_diag.T, precision=lax.Precision.HIGHEST)
        factor = jnp.linalg.cholesky(diag_block)
        panel_rows = jnp.where(
            (global_rows >= start_col)[:, None], solve_right(factor, rows_term), 0.0
        )
        panel_cols = jnp.where(
            (global_cols >= start_col)[:, None], solve_right(factor, cols_term), 0.0
        )
        rebuilt_history.append((panel_epochs, factor, panel_rows, panel_cols))
        in_panel = (global_cols >= start_col) & (global_cols < end_col)
        beyond_panel = global_cols >= end_col
        below_panel = global_rows >= end_col
        update = normal_tile - jnp.dot(panel_rows, panel_cols.T, precision=lax.Precision.HIGHEST)
        keep_update = below_panel[:, None] & beyond_panel[None, :]
        normal_tile = jnp.where(
            keep_update, update, jnp.where(beyond_panel[None, :], 0.0, normal_tile)
        )
        normal_tile = lax.dynamic_update_slice(
            normal_tile,
            jnp.where(
                in_panel[None, col_offset : col_offset + PANEL],
                panel_rows,
                normal_tile[:, col_offset : col_offset + PANEL],
            ),
            (0, col_offset),
        )
    return normal_tile


def solution(mesh):
    in_specs = (P(("ep", "col"), "row"), P(), P(("ep", "col")), P("row"), P())
    out_specs = P("row", ("ep", "col"))
    return jax.shard_map(
        on_device, mesh=mesh, in_specs=in_specs, out_specs=out_specs, check_vma=False
    )
```

profile of v0, /device:TPU:0, one launch (start us, length us, event | category | flops | bytes accessed | tf_op | source)
XLA Modules:
  0.0 516.8 jit_solution(55118658324207868)
XLA Ops:
  6.5 1.2 slice.85
  7.7 5.0 collective-permute-start
  13.5 1.5 select_reduce_fusion
  15.7 8.1 %collective-permute-done = bf16[63,4096]{1,0:T(8,128)(2,1)S(1)} collective-permute-done((bf16[63,4096]{1,0:T(8,128)(2,1)S(1)}, bf16[63,4096]{1,0:T(8,128)(2,1)S(1)}, u32[]{:S(2)}, u32[]{:S(2)}) %collective-permute-start) | collective-permute-done | bytes 516128 | tf_op jit(solution)/shard_map/ppermute | solution.py:14
  23.8 1.4 fusion.18
  28.0 24.1 %all-gather.5.cloned.1.call-done = bf16[64,16384]{1,0:T(8,128)(2,1)} async-done(((bf16[64,4096]{1,0:T(8,128)(2,1)}), bf16[64,16384]{1,0:T(8,128)(2,1)}) %all-gather.5.cloned.1.call-update) | async-done | bytes 2097168 | tf_op jit(solution)/shard_map/all_gather | solution.py:62
  52.1 3.2 copy.89
  55.3 5.5 %all-to-all-start = ((bf16[64,8,2048]{2,0,1:T(8,128)(2,1)}), bf16[64,8,2048]{2,0,1:T(8,128)(2,1)S(1)}, u32[]{:S(2)}, u32[]{:S(2)}) async-start(bf16[64,8,2048]{2,0,1:T(8,128)(2,1)} %bitcast.132), calls=%async_computation | async-start | bytes 4194304 | tf_op jit(solution)/shard_map/all_to_all | solution.py:63
  63.7 77.0 %all-to-all-done = bf16[64,8,2048]{2,0,1:T(8,128)(2,1)S(1)} async-done(((bf16[64,8,2048]{2,0,1:T(8,128)(2,1)}), bf16[64,8,2048]{2,0,1:T(8,128)(2,1)S(1)}, u32[]{:S(2)}, u32[]{:S(2)}) %all-to-all-start) | async-done | bytes 2097184 | tf_op jit(solution)/shard_map/all_to_all | solution.py:63
  141.6 19.7 %all-gather.3.cloned.1.call-done = bf16[512,4096]{1,0:T(8,128)(2,1)} async-done(((bf16[64,4096]{1,0:T(8,128)(2,1)}), bf16[512,4096]{1,0:T(8,128)(2,1)}) %all-gather.3.cloned.1.call-update) | async-done | bytes 4194320 | tf_op jit(solution)/shard_map/all_gather | solution.py:61
  161.3 19.0 %fusion.77 = f32[4096,2048]{1,0:T(8,128)} fusion(bf16[512,4096]{1,0:T(8,128)(2,1)} %all-gather.3.cloned.1.call-done, bf16[512,2048]{1,0:T(8,128)(2,1)S(1)} %bitcast.129), kind=kOutput, calls=%fused_computation.155 | convolution fusion | flops 8589934592 | bytes 39845888 | tf_op jit(solution)/shard_map/dot_general | solution.py:23
  180.2 56.1 %all-reduce.4.cloned.1.call-done = (bf16[512,256]{1,0:T(8,128)(2,1)}, bf16[512,256]{1,0:T(8,128)(2,1)}) async-done(((bf16[512,256]{1,0:T(8,128)(2,1)}, bf16[512,256]{1,0:T(8,128)(2,1)}), (bf16[512,256]{1,0:T(8,128)(2,1)}, bf16[512,256]{1,0:T(8,128)(2,1)})) %all-reduce.4.cloned.1.call-update) | async-done | bytes 524304 | tf_op jit(solution)/shard_map/psum | solution.py:19
  236.3 1.3 convolution_add_fusion.5
  237.8 11.7 %cholesky.130 = f32[128,128]{1,0:T(8,128)S(1)} custom-call(f32[128,128]{1,0:T(8,128)S(1)} %cholesky.194), custom_call_target="Cholesky" | custom-call | tf_op jit(solution)/shard_map/jit(cholesky)/cholesky | solution.py:97
  249.6 9.8 %custom-call.22 = f32[1,128,128]{1,2,0:T(8,128)S(1)} custom-call(f32[1,128,128]{2,1,0:T(8,128)S(1)} %get-tuple-element.115), custom_call_target="InvertDiagBlocksLowerTriangular" | custom-call | tf_op jit(solution)/shard_map/jit(cholesky)/cholesky | solution.py:97
  259.9 11.7 %cholesky.147 = f32[128,128]{1,0:T(8,128)S(1)} custom-call(f32[128,128]{1,0:T(8,128)S(1)} %convolution_subtract_fusion.9), custom_call_target="Cholesky" | custom-call | tf_op jit(solution)/shard_map/jit(cholesky)/cholesky | solution.py:97
  274.0 4.0 while.9
  274.6 1.3 dynamic-slice.21
  276.7 1.3 dynamic-slice.21
  278.1 19.9 %custom-call.23 = f32[2,128,128]{1,2,0:T(8,128)S(1)} custom-call(f32[2,128,128]{2,1,0:T(8,128)S(1)} %get-tuple-element.44), custom_call_target="InvertDiagBlocksLowerTriangular" | custom-call | tf_op jit(solution)/shard_map/jit(_solve_triangular)/triangular_solve | solution.py:29
  298.0 4.6 convolution_add_fusion.1
  302.6 2.0 fusion.4
  304.6 1.4 copy-done
  305.9 4.9 convolution_subtract_fusion.2
  310.9 3.3 copy.57
  315.4 2.2 convolution_add_fusion.3
  317.6 2.1 convolution_add_fusion.2
  323.2 11.7 %cholesky.164 = f32[128,128]{1,0:T(8,128)S(1)} custom-call(f32[128,128]{1,0:T(8,128)S(1)} %cholesky.197), custom_call_target="Cholesky" | custom-call | tf_op jit(solution)/shard_map/jit(cholesky)/cholesky | solution.py:97
  335.0 9.8 %custom-call.25 = f32[1,128,128]{1,2,0:T(8,128)S(1)} custom-call(f32[1,128,128]{2,1,0:T(8,128)S(1)} %get-tuple-element.111), custom_call_target="InvertDiagBlocksLowerTriangular" | custom-call | tf_op jit(solution)/shard_map/jit(cholesky)/cholesky | solution.py:97
  346.9 11.9 %cholesky.181 = f32[128,128]{1,0:T(8,128)S(1)} custom-call(f32[128,128]{1,0:T(8,128)S(1)} %convolution_subtract_fusion.8), custom_call_target="Cholesky" | custom-call | tf_op jit(solution)/shard_map/jit(cholesky)/cholesky | solution.py:97
  362.4 3.9 while.10
  363.0 1.3 bitcast_dynamic-update-slice_fusion.5
  365.0 1.3 bitcast_dynamic-update-slice_fusion.5
  366.9 20.5 %custom-call.26 = f32[2,128,128]{1,2,0:T(8,128)S(1)} custom-call(f32[2,128,128]{2,1,0:T(8,128)} %copy-done.17), custom_call_target="InvertDiagBlocksLowerTriangular" | custom-call | tf_op jit(solution)/shard_map/jit(_solve_triangular)/triangular_solve | solution.py:29
  387.5 1.8 fusion.51
  389.7 2.3 convolution_add_fusion
  392.1 3.5 convolution_subtract_fusion
  395.6 1.9 fusion.2
  397.5 5.2 %convolution_subtract_fusion.1 = f32[128,4096]{0,1:T(8,128)} fusion(f32[128,4096]{1,0:T(8,128)S(1)} %fusion.2, f32[256,4096]{0,1:T(8,128)S(1)} %convolution_subtract_fusion, f32[256,256]{1,0:T(8,128)S(1)} %get-tuple-element.232), kind=kOutput, calls=%fused_computation.9 | convolution fusion | flops 805830656 | bytes 6356992 | tf_op jit(solution)/shard_map/jit(_solve_triangular)/triangular_solve | solution.py:29
  402.7 1.8 copy.67
  404.5 2.4 fusion.21
  409.1 2.0 convolution_subtract_fusion.3
  412.2 2.0 convolution_subtract_fusion.4
  415.3 1.8 fusion.46
  417.5 41.4 %select_select_fusion.1 = f32[4096,2048]{1,0:T(8,128)} fusion(f32[4096,2048]{1,0:T(8,128)} %fusion.77, f32[4096]{0:T(1024)S(1)} %copy-done.19, s32[2048]{0:T(1024)S(1)} %iota_add_fusion.1, s32[4096]{0:T(1024)S(1)} %copy-done.21, pred[2048]{0:T(1024)(128)(4,1)S(1)} %get-tuple-element.123, pred[4096]{0:T(1024)(128)(4,1)S(1)} %get-tuple-element.120, ...), kind=kOutput, calls=%fused_computation.5 | convolution fusion | flops 25831669760 | bytes 73453568 | tf_op jit(solution)/shard_map/dot_general | solution.py:108
  458.9 6.3 %fusion.1 = f32[4096,2048]{1,0:T(8,128)} fusion(f32[4096,2048]{1,0:T(8,128)} %select_select_fusion.1, f32[128,4096]{0,1:T(8,128)S(1)} %copy-done.5, f32[128,4096]{0,1:T(8,128)S(1)} %copy-done.3, pred[4096]{0:T(1024)(128)(4,1)S(1)} %fusion.58, pred[256]{0:T(512)(128)(4,1)S(1)} %copy-done.23), kind=kLoop, calls=%fused_computation.15 | loop fusion | flops 3145728 | bytes 12587264 | tf_op jit(solution)/shard_map/dynamic_update_slice | solution.py:113
  465.2 38.6 %select_select_fusion = f32[4096,2048]{1,0:T(8,128)} fusion(f32[4096,2048]{1,0:T(8,128)} %fusion.1, pred[2048]{0:T(1024)(128)(4,1)S(1)} %fusion.63, pred[4096]{0:T(1024)(128)(4,1)S(1)} %get-tuple-element.121, f32[128,4096]{0,1:T(8,128)S(1)} %fusion.46, f32[128,4096]{0,1:T(8,128)S(1)} %copy-done.1, f32[128,2048]{1,0:T(8,128)S(1)} %fusion.45, ...), kind=kOutput, calls=%fused_computation.4 | convolution fusion | flops 25806503936 | bytes 73412608 | tf_op jit(solution)/shard_map/dot_general | solution.py:108
  503.8 6.2 %fusion = f32[4096,2048]{1,0:T(8,128)} fusion(f32[4096,2048]{1,0:T(8,128)} %select_select_fusion, f32[128,4096]{0,1:T(8,128)S(1)} %fusion.46, f32[128,4096]{0,1:T(8,128)S(1)} %copy-done.1, pred[4096]{0:T(1024)(128)(4,1)S(1)} %get-tuple-element.120, pred[256]{0:T(512)(128)(4,1)S(1)} %copy-done.22), kind=kLoop, calls=%fused_computation.13 | loop fusion | flops 3145728 | bytes 12587264 | tf_op jit(solution)/shard_map/dynamic_update_slice | solution.py:113
  (129 shorter events, 27.4 us)
Async XLA Ops:
  6.5 45.6 %all-gather.5.cloned.1.call-start = ((), (), s32[]{:S(2)}) async-start(), calls=%async_computation.2 | async-start | bytes 2621440 | tf_op jit(solution)/shard_map/all_gather | solution.py:62
  7.7 16.1 %collective-permute-start = (bf16[63,4096]{1,0:T(8,128)(2,1)S(1)}, bf16[63,4096]{1,0:T(8,128)(2,1)S(1)}, u32[]{:S(2)}, u32[]{:S(2)}) collective-permute-start(bf16[63,4096]{1,0:T(8,128)(2,1)S(1)} %slice.85), channel_id=1, source_target_pairs={{0,1},{1,2},{2,3},{3,16},{16,17},{17,18},{18,19},{4,5},{5,6},{6,7}... | collective-permute-start | bytes 1548296 | tf_op jit(solution)/shard_map/ppermute | solution.py:14
  27.2 134.1 %all-gather.3.cloned.1.call-start = ((), (), s32[]{:S(2)}) async-start(), calls=%async_computation.1 | async-start | bytes 4718592 | tf_op jit(solution)/shard_map/all_gather | solution.py:61
  55.3 85.4 %all-to-all-start = ((bf16[64,8,2048]{2,0,1:T(8,128)(2,1)}), bf16[64,8,2048]{2,0,1:T(8,128)(2,1)S(1)}, u32[]{:S(2)}, u32[]{:S(2)}) async-start(bf16[64,8,2048]{2,0,1:T(8,128)(2,1)} %bitcast.132), calls=%async_computation | async-start | bytes 4194304 | tf_op jit(solution)/shard_map/all_to_all | solution.py:63
  60.8 175.6 %all-reduce.4.cloned.1.call-start = ((), (), s32[]{:S(2)}) async-start(), calls=%async_computation.3 | async-start | bytes 1048576 | tf_op jit(solution)/shard_map/psum | solution.py:19
  62.3 327.0 %copy-start.18 = (f32[4096]{0:T(1024)}, f32[4096]{0:T(1024)S(1)}, u32[]{:S(2)}) copy-start(f32[4096]{0:T(1024)S(1)} %dynamic_slice.6) | copy-start | bytes 49156
  62.4 326.9 %copy-start.20 = (s32[4096]{0:T(1024)}, s32[4096]{0:T(1024)S(1)}, u32[]{:S(2)}) copy-start(s32[4096]{0:T(1024)S(1)} %iota_add_fusion) | copy-start | bytes 49156
  259.6 38.3 %copy-start.11 = (bf16[512,256]{1,0:T(8,128)(2,1)S(1)}, bf16[512,256]{1,0:T(8,128)(2,1)}, u32[]{:S(2)}) copy-start(bf16[512,256]{1,0:T(8,128)(2,1)} %get-tuple-element.100) | copy-start | bytes 786436
  278.1 24.5 %copy-start.25 = (s32[2,2]{1,0:T(2,128)}, s32[2,2]{1,0:T(2,128)S(1)}, u32[]{:S(2)}) copy-start(s32[2,2]{1,0:T(2,128)S(1)} %get-tuple-element.239) | copy-start | bytes 52
  304.6 1.4 copy-start
  310.9 3.3 copy-start.10
  320.0 42.4 %copy-start.26 = (s32[2,2]{1,0:T(2,128)S(1)}, s32[2,2]{1,0:T(2,128)}, u32[]{:S(2)}) copy-start(s32[2,2]{1,0:T(2,128)} %copy-done.25) | copy-start | bytes 52
  320.6 66.8 %copy-start.6 = (f32[128,4096]{0,1:T(8,128)S(1)}, f32[128,4096]{0,1:T(8,128)}, u32[]{:S(2)}) copy-start(f32[128,4096]{0,1:T(8,128)} %convolution_subtract_fusion.2) | copy-start | bytes 6291460
  322.5 0.7 copy-start.14
  358.8 2.5 copy-start.13
  366.3 0.7 copy-start.17
  366.9 30.6 %copy-start.12 = (f32[256,256]{1,0:T(8,128)}, f32[256,256]{1,0:T(8,128)S(1)}, u32[]{:S(2)}) copy-start(f32[256,256]{1,0:T(8,128)S(1)} %get-tuple-element.232) | copy-start | bytes 786436
  387.5 8.1 %copy-start.15 = (f32[2,128,128]{1,2,0:T(8,128)}, f32[2,128,128]{1,2,0:T(8,128)S(1)}, u32[]{:S(2)}) copy-start(f32[2,128,128]{1,2,0:T(8,128)S(1)} %custom-call.26) | copy-start | bytes 393220
  387.5 2.2 copy-start.24
  389.7 2.3 copy-start.4
  389.7 2.3 copy-start.2
  404.5 2.4 copy-start.9
  406.9 2.1 copy-start.8
  409.1 2.0 copy-start.16
  412.2 3.1 copy-start.7
  415.3 1.8 copy-start.3
  415.3 2.2 copy-start.5
  415.3 2.2 copy-start.19
  415.3 2.2 copy-start.21
  417.5 41.4 %copy-start.23 = (pred[256]{0:T(512)(128)(4,1)S(1)}, pred[256]{0:T(512)(128)(4,1)}, u32[]{:S(2)}) copy-start(pred[256]{0:T(512)(128)(4,1)} %get-tuple-element.117) | copy-start | bytes 772
  458.9 6.3 %copy-start.1 = (f32[128,4096]{0,1:T(8,128)S(1)}, f32[128,4096]{0,1:T(8,128)}, u32[]{:S(2)}) copy-start(f32[128,4096]{0,1:T(8,128)} %copy.67) | copy-start | bytes 6291460
  465.2 38.6 %copy-start.22 = (pred[256]{0:T(512)(128)(4,1)S(1)}, pred[256]{0:T(512)(128)(4,1)}, u32[]{:S(2)}) copy-start(pred[256]{0:T(512)(128)(4,1)} %get-tuple-element.116) | copy-start | bytes 772
Sparse Core Ops, SparseCore 0:
  27.3 24.7 all-gather.4
  54.2 106.9 all-gather.2
  164.7 71.5 all-reduce.3
where the time goes:
time: 523 us; the launch traced here: 517 us
  waiting for transfers between devices  186 us (36%)
  matrix products  150 us (29%)
  other arithmetic  128 us (24%)
  local copies, waits for them, and re-layouts  25.5 us (5%)
  between operations  16.5 us (3%)
  starting transfers between devices  10.6 us (2%)
    dot_general x2, matrix products, on_device(): jnp.dot(panel_rows, panel_cols.T, precision=lax.Precision.HIGHEST)  80 us
    all_to_all x1, waiting for transfers between devices, on_device(): lax.all_to_all(wide_rows, ('ep', 'col'), split_axis=1, concat_axis=0, til...  77 us
    another operation x13, other arithmetic, on_device(): factor = jnp.linalg.cholesky(diag_block)  68.8 us
    psum x1, waiting for transfers between devices, broadcast(): return lax.psum(block, axis)  56.1 us
    another operation x5, other arithmetic, solve_right(): return jax.scipy.linalg.solve_triangular(factor, matrix.T, lower=True).T  41.4 us
    dot_general x8, matrix products, contract_epochs(): lax.dot_general(left_rows, right_cols, (((0,), (0,)), ((), ())), preferre...  32 us
    another operation x15, matrix products, solve_right(): return jax.scipy.linalg.solve_triangular(factor, matrix.T, lower=True).T  27.1 us
    all_gather x1, waiting for transfers between devices, on_device(): wide_rows = lax.all_gather(permuted, 'row', axis=1, tiled=True)  24.1 us
  transfers between devices with their start and end apart: 5, of which 5 were waited for; matrix products, arithmetic and copies ran while one was open for 6% of the time, Pallas kernels for 0%

commit v1 on v0

v1 whole, which is shorter than its diff:
```python
import functools

import jax
import jax.numpy as jnp
from jax import lax
from jax.experimental import pallas as pl
from jax.experimental.pallas import tpu as pltpu
from jax.sharding import PartitionSpec as P

PANEL = 256
SECTIONS = 2
HEAD = PANEL * SECTIONS
PB = 128
BLOCK = 128
SUB = 8
EXACT = lax.Precision.HIGHEST
F32 = jnp.float32
BF16 = jnp.bfloat16


def iota(shape, axis):
    return lax.broadcasted_iota(jnp.int32, shape, axis)


def dot(left, right, contract=((1,), (0,)), precision=None):
    return lax.dot_general(
        left, right, (contract, ((), ())), preferred_element_type=F32, precision=precision
    )


def apply_band(band, columns, store):
    for b in range(columns.shape[0] // BLOCK):
        here = slice(b * BLOCK, (b + 1) * BLOCK)
        if b == 0:
            got = dot(band[here, BLOCK:], columns[here, :])
        else:
            got = dot(band[here, :], columns[(b - 1) * BLOCK : (b + 1) * BLOCK, :])
        store(here, got.astype(BF16))


def permute_kernel(order_ref, counts_ref, design_ref, out_ref, head_ref):
    epochs, rows = design_ref.shape
    for g in range(rows // PB):
        cols = slice(g * PB, (g + 1) * PB)
        local = order_ref[:, cols] - (order_ref[:, cols] // PB) * PB
        one_hot = jnp.where(iota((PB, PB), 0) == local, 1.0, 0.0).astype(BF16)
        out_ref[:, cols] = dot(design_ref[:, cols], one_hot).astype(BF16)
    head_ref[:, :HEAD] = out_ref[:, :HEAD]
    head_ref[:, HEAD:] = jnp.broadcast_to(counts_ref[...], (epochs, PB)).astype(F32).astype(BF16)


def permute_local(design, order, tap_count):
    epochs, rows = design.shape
    return pl.pallas_call(
        permute_kernel,
        out_shape=(
            jax.ShapeDtypeStruct((epochs, rows), BF16),
            jax.ShapeDtypeStruct((epochs, HEAD + PB), BF16),
        ),
        name="permute_local",
    )(order.reshape(1, rows), tap_count.reshape(epochs, 1), design)


def spread(tile, lane):
    return jnp.broadcast_to(tile[:, lane : lane + 1], (SUB, tile.shape[1]))


def row_of(tile, k):
    return jnp.broadcast_to(tile[k : k + 1, :], (SUB, tile.shape[1]))


def factor_block(work):
    halves = work.shape[1] // BLOCK
    groups = BLOCK // SUB
    for g in range(groups):
        rows = slice(g * SUB, (g + 1) * SUB)
        own = [work[rows, h * BLOCK : (h + 1) * BLOCK] for h in range(halves)]
        cols = [spread(own[0], g * SUB + j) for j in range(SUB)]
        a = {(i, j): row_of(cols[j], i) for j in range(SUB) for i in range(j, SUB)}
        u = [[row_of(own[h], k) for k in range(SUB)] for h in range(halves)]
        inv = []
        low = {}
        for k in range(SUB):
            r = lax.rsqrt(a[k, k])
            inv.append(r)
            for i in range(k + 1, SUB):
                low[i, k] = a[i, k] * r
            for j in range(k + 1, SUB):
                for i in range(j, SUB):
                    a[i, j] = a[i, j] - low[i, k] * low[j, k]
            for h in range(halves):
                u[h][k] = u[h][k] * r
                for j in range(k + 1, SUB):
                    u[h][j] = u[h][j] - low[j, k] * u[h][k]
        for h in range(halves):
            merged = u[h][0]
            for k in range(1, SUB):
                merged = jnp.where(iota((SUB, BLOCK), 0) == k, u[h][k], merged)
            work[rows, h * BLOCK : (h + 1) * BLOCK] = merged
        for t in range(g + 1, groups):
            below = slice(t * SUB, (t + 1) * SUB)
            tile = [work[below, h * BLOCK : (h + 1) * BLOCK] for h in range(halves)]
            left = [spread(tile[0], g * SUB + j) for j in range(SUB)]
            for k in range(SUB):
                left[k] = left[k] * inv[k]
                for j in range(k + 1, SUB):
                    left[j] = left[j] - low[j, k] * left[k]
                for h in range(halves):
                    tile[h] = tile[h] - left[k] * u[h][k]
            for h in range(halves):
                work[below, h * BLOCK : (h + 1) * BLOCK] = tile[h]


def panel_kernel(
    taps_ref, head_ref, reg_ref, band_ref, factor_ref, w_ref, high_ref, low_ref, aug, a1, work
):
    epochs = head_ref.shape[0]
    lag = iota((BLOCK, 2 * BLOCK), 0) + BLOCK - iota((BLOCK, 2 * BLOCK), 1)
    base = lax.fori_loop(
        0,
        taps_ref.shape[0],
        lambda k, kept: jnp.where(lag == k, taps_ref[k], kept),
        jnp.zeros((BLOCK, 2 * BLOCK), F32),
    )
    lag = lag.astype(F32)
    for b in range(epochs // BLOCK):
        here = slice(b * BLOCK, (b + 1) * BLOCK)
        counts = head_ref[here, HEAD:].astype(F32)
        for side in (slice(0, BLOCK), slice(BLOCK, 2 * BLOCK)):
            kept = jnp.where(lag[:, side] < counts, base[:, side], 0.0)
            band_ref[here, side] = kept.astype(BF16)

    def store(here, got):
        a1[here, :] = got

    apply_band(band_ref, head_ref.at[:, :HEAD], store)
    columns = a1[...]
    square = (HEAD, HEAD)
    on_diagonal = iota(square, 0) == iota(square, 1)
    aug[:, :HEAD] = dot(columns, columns, ((0,), (0,))) + jnp.where(on_diagonal, reg_ref[...], 0.0)
    aug[:, HEAD:] = columns.astype(F32).T

    eye = jnp.where(iota((BLOCK, BLOCK), 0) == iota((BLOCK, BLOCK), 1), 1.0, 0.0)

    def eliminate(kb, carry):
        start = pl.multiple_of(kb * BLOCK, BLOCK)
        work[:, :BLOCK] = aug[pl.ds(start, BLOCK), pl.ds(start, BLOCK)]
        work[:, BLOCK:] = eye
        factor_block(work)
        u = dot(work[:, BLOCK:], aug[pl.ds(start, BLOCK), :], precision=EXACT)
        aug[pl.ds(start, BLOCK), :] = u

        def below(rb, inner):
            at = pl.multiple_of(rb * BLOCK, BLOCK)
            side = aug[pl.ds(start, BLOCK), pl.ds(at, BLOCK)]
            aug[pl.ds(at, BLOCK), :] -= dot(
                side, aug[pl.ds(start, BLOCK), :], ((0,), (0,)), precision=EXACT
            )
            return inner

        lax.fori_loop(kb + 1, HEAD // BLOCK, below, 0)
        return carry

    lax.fori_loop(0, HEAD // BLOCK, eliminate, 0)
    factor_ref[...] = jnp.where(iota(square, 0) >= iota(square, 1), aug[:, :HEAD].T, 0.0)
    wt = aug[:, HEAD:]
    w_ref[...] = wt.T.astype(BF16)
    for b in range(epochs // BLOCK):
        here = slice(b * BLOCK, (b + 1) * BLOCK)
        shape = (BLOCK, epochs)
        unit = jnp.where(iota(shape, 0) + b * BLOCK == iota(shape, 1), 1.0, 0.0)
        middle = unit - dot(wt[:, here], wt, ((0,), (0,)), precision=EXACT)
        high = middle.astype(BF16)
        high_ref[here, :] = high
        low_ref[here, :] = (middle - high.astype(F32)).astype(BF16)


def factor_panel(head, taps, regular):
    epochs = head.shape[0]
    vmem = pl.BlockSpec(memory_space=pltpu.VMEM)
    return pl.pallas_call(
        panel_kernel,
        out_shape=(
            jax.ShapeDtypeStruct((epochs, 2 * BLOCK), BF16),
            jax.ShapeDtypeStruct((HEAD, HEAD), F32),
            jax.ShapeDtypeStruct((epochs, HEAD), BF16),
            jax.ShapeDtypeStruct((epochs, epochs), BF16),
            jax.ShapeDtypeStruct((epochs, epochs), BF16),
        ),
        in_specs=[pl.BlockSpec(memory_space=pltpu.SMEM), vmem, vmem],
        scratch_shapes=[
            pltpu.VMEM((HEAD, HEAD + epochs), F32),
            pltpu.VMEM((epochs, HEAD), BF16),
            pltpu.VMEM((BLOCK, 2 * BLOCK), F32),
        ],
        compiler_params=pltpu.CompilerParams(vmem_limit_bytes=48 << 20),
        name="factor_panel",
    )(taps, head, regular[:HEAD].reshape(1, HEAD))


def columns_kernel(place_ref, right_ref, band_ref, w_ref, high_ref, low_ref, out_ref, filtered):
    def store(here, got):
        filtered[here, :] = got

    apply_band(band_ref, right_ref, store)
    out_ref[...] = (dot(high_ref[...], filtered[...]) + dot(low_ref[...], filtered[...])).astype(BF16)

    @pl.when((place_ref[1] == 0) & (pl.program_id(0) == 0))
    def _():
        out_ref[...] = w_ref[...]


def project_columns(place, right, band, w, high, low):
    epochs, cols = right.shape
    whole = lambda i, place: (0, 0)
    return pl.pallas_call(
        columns_kernel,
        out_shape=jax.ShapeDtypeStruct((epochs, cols), BF16),
        grid_spec=pltpu.PrefetchScalarGridSpec(
            num_scalar_prefetch=1,
            grid=(cols // HEAD,),
            in_specs=[
                pl.BlockSpec((epochs, HEAD), lambda i, place: (0, i)),
                pl.BlockSpec(band.shape, whole),
                pl.BlockSpec(w.shape, whole),
                pl.BlockSpec(high.shape, whole),
                pl.BlockSpec(low.shape, whole),
            ],
            out_specs=pl.BlockSpec((epochs, HEAD), lambda i, place: (0, i)),
            scratch_shapes=[pltpu.VMEM((epochs, HEAD), BF16)],
        ),
        compiler_params=pltpu.CompilerParams(vmem_limit_bytes=48 << 20),
        name="project_columns",
    )(place, right, band, w, high, low)


def tile_kernel(place_ref, left_ref, band_ref, right_ref, reg_ref, factor_ref, out_ref, filtered):
    def store(here, got):
        filtered[here, :] = got

    rows, cols = out_ref.shape
    dev_rows = pl.num_programs(0) * rows
    first_row = place_ref[0] * dev_rows + pl.program_id(0) * rows
    first_col = place_ref[1] * cols

    @pl.when(first_row >= HEAD)
    def _():
        apply_band(band_ref, left_ref, store)
        out_ref[...] = dot(filtered[...], right_ref[...], ((0,), (0,)))

        @pl.when((first_row >= first_col) & (first_row < first_col + cols))
        def _():
            at = pl.multiple_of(first_row - first_col, rows)
            on_diagonal = iota((rows, rows), 0) == iota((rows, rows), 1)
            out_ref[:, pl.ds(at, rows)] += jnp.where(on_diagonal, reg_ref[...], 0.0)

    @pl.when(first_row < HEAD)
    def _():
        out_ref[...] = jnp.zeros_like(out_ref)

        @pl.when(first_col == 0)
        def _():
            at = pl.multiple_of(first_row, rows)
            out_ref[:, :HEAD] = factor_ref[pl.ds(at, rows), :]


def multiply_tile(place, left, band, right, regular, factor, rows=256):
    epochs, dev_rows = left.shape
    cols = right.shape[1]
    steps = dev_rows // rows
    whole = lambda i, place: (0, 0)
    return pl.pallas_call(
        tile_kernel,
        out_shape=jax.ShapeDtypeStruct((dev_rows, cols), F32),
        grid_spec=pltpu.PrefetchScalarGridSpec(
            num_scalar_prefetch=1,
            grid=(steps,),
            in_specs=[
                pl.BlockSpec((epochs, rows), lambda i, place: (0, i)),
                pl.BlockSpec(band.shape, whole),
                pl.BlockSpec(right.shape, whole),
                pl.BlockSpec((1, rows), lambda i, place: (0, place[0] * steps + i)),
                pl.BlockSpec(factor.shape, whole),
            ],
            out_specs=pl.BlockSpec((rows, cols), lambda i, place: (i, 0)),
            scratch_shapes=[pltpu.VMEM((epochs, rows), BF16)],
        ),
        compiler_params=pltpu.CompilerParams(vmem_limit_bytes=48 << 20),
        name="multiply_tile",
    )(place, left, band, right, regular.reshape(1, -1), factor)


AXES = ("ep", "row", "col")


def spread_rows(block, owner_of):
    rows = lax.axis_size("row")
    groups = lax.axis_size(("ep", "col"))
    width = lax.axis_size("col")
    row = lax.axis_index("row")
    owner = jnp.asarray([owner_of(g) for g in range(groups)], jnp.int32)[lax.axis_index(("ep", "col"))]
    distance = rows // 2
    while distance >= 1:
        route = []
        for g in range(groups):
            for other in range(0, rows, 2 * distance):
                source = owner_of(g) ^ other
                place = lambda at: ((g // width) * rows + at) * width + g % width
                route.append((place(source), place(source ^ distance)))
        came = lax.ppermute(block, AXES, route)
        takes = ((row ^ owner) & (2 * distance - 1)) == distance
        block = jnp.where(takes, came, block)
        distance //= 2
    return block


def on_device(design, taps, tap_count, order, regular):
    epochs_dev, rows_dev = design.shape
    groups = lax.axis_size(("ep", "col"))
    cols_dev = regular.shape[0] // groups
    row = lax.axis_index("row")
    group = lax.axis_index(("ep", "col"))
    place = jnp.stack([row, group]).astype(jnp.int32)
    permuted, head = permute_local(design, order, tap_count)
    head = spread_rows(head, lambda g: 0)
    head = lax.all_gather(head, ("ep", "col"), axis=0, tiled=True)
    left = lax.all_gather(permuted, ("ep", "col"), axis=0, tiled=True)
    at = (group * cols_dev) % rows_dev
    right = lax.dynamic_slice_in_dim(left, at, cols_dev, 1)
    right = spread_rows(right, lambda g: g * cols_dev // rows_dev)
    band, factor, w, high, low = factor_panel(head, taps, regular)
    right = project_columns(place, right, band, w, high, low)
    return multiply_tile(place, left, band, right, regular, factor)


def solution(mesh):
    in_specs = (P(("ep", "col"), "row"), P(), P(("ep", "col")), P("row"), P())
    out_specs = P("row", ("ep", "col"))
    return jax.shard_map(
        on_device, mesh=mesh, in_specs=in_specs, out_specs=out_specs, check_vma=False
    )
```

time: 523 us -> 225 us (0.43)
  matrix products: 150 us -> 0 us
  other arithmetic: 128 us -> 2.77 us
  waiting for transfers between devices: 186 us -> 100 us
  Pallas kernels: 0 us -> 56.5 us
  blocking collectives: 0 us -> 33 us
  local copies, waits for them, and re-layouts: 25.5 us -> 3.71 us
    dot_general x15 -> x0, matrix products: 120 us -> none  [the longest x2 80 us: on_device(): jnp.dot(panel_rows, panel_cols.T, precision=lax.Precision.HIGHEST)]
    another operation x18 -> x1, other arithmetic: 110 us -> 0.08 us  [on_device(): place = jnp.stack([row, group]).astype(jnp.int32)]
    all_to_all x1 -> x0, waiting for transfers between devices: 77 us -> none  [on_device(): lax.all_to_all(wide_rows, ('ep', 'col'), split_axis=1, concat_axis=0, til...]
    pallas_call x0 -> x4, Pallas kernels: none -> 56.5 us  [the longest x1 29.7 us: factor_panel(): pl.pallas_call(panel_kernel, out_shape=(jax.ShapeDtypeStruct((epochs, 2 *...]
    psum x1 -> x0, waiting for transfers between devices: 56.1 us -> none  [broadcast(): return lax.psum(block, axis)]
    all_gather x0 -> x1, blocking collectives: none -> 33 us  [on_device(): head = lax.all_gather(head, ('ep', 'col'), axis=0, tiled=True)]
    all_gather x2 -> x1, waiting for transfers between devices: 43.9 us -> 76.2 us  [on_device(): left = lax.all_gather(permuted, ('ep', 'col'), axis=0, tiled=True)]
    another operation x19 -> x0, matrix products: 29.7 us -> none  [the longest x15 27.1 us: solve_right(): return jax.scipy.linalg.solve_triangular(factor, matrix.T, lower=True).T]
  transfers between devices with their start and end apart: 5 -> 5, of which waited for: 5 -> 4; matrix products, arithmetic and copies ran while one was open for 6% -> 0% of each run, Pallas kernels for 0% -> 13%
where the time goes in v1:
time: 225 us; the launch traced here: 224 us
  waiting for transfers between devices  100 us (44%)
  Pallas kernels  56.5 us (25%)
  blocking collectives  33 us (15%)
  between operations  14.2 us (6%)
  starting transfers between devices  13.7 us (6%)
  local copies, waits for them, and re-layouts  3.71 us (2%)
  other arithmetic  2.77 us (1%)
    all_gather x1, waiting for transfers between devices, on_device(): left = lax.all_gather(permuted, ('ep', 'col'), axis=0, tiled=True)  76.2 us
    all_gather x1, blocking collectives, on_device(): head = lax.all_gather(head, ('ep', 'col'), axis=0, tiled=True)  33 us
    pallas_call x1, Pallas kernels, factor_panel(): pl.pallas_call(panel_kernel, out_shape=(jax.ShapeDtypeStruct((epochs, 2 *...  29.7 us
    ppermute x4, waiting for transfers between devices, spread_rows(): came = lax.ppermute(block, AXES, route)  23.8 us
    pallas_call x1, Pallas kernels, multiply_tile(): pl.pallas_call(tile_kernel, out_shape=jax.ShapeDtypeStruct((dev_rows, col...  19.9 us
    ppermute x4, starting transfers between devices, spread_rows(): came = lax.ppermute(block, AXES, route)  13.7 us
    pallas_call x1, Pallas kernels, project_columns(): pl.pallas_call(columns_kernel, out_shape=jax.ShapeDtypeStruct((epochs, co...  4.57 us
  transfers between devices with their start and end apart: 5, of which 4 were waited for; matrix products, arithmetic and copies ran while one was open for 0% of the time, Pallas kernels for 13%

profile of v1, /device:TPU:0, one launch (start us, length us, event | category | flops | bytes accessed | tf_op | source)
XLA Modules:
  0.0 223.9 jit_solution(12332502020785192263)
XLA Ops:
  6.5 0.0 all-gather.2.cloned.1.call-start
  6.5 1.4 copy.8.counts_ref
  7.9 2.3 %permute_local.1 = (bf16[64,4096]{1,0:T(8,128)(2,1)}, bf16[64,640]{1,0:T(8,128)(2,1)}) custom-call(s32[1,4096]{1,0:T(1,128)} %bitcast.9, s32[64,1]{1,0:T(8,128)} %copy.8.counts_ref, bf16[64,4096]{1,0:T(8,128)(2,1)} %design_ref.1), custom_call_target="tpu_custom_call" | custom-call | tf_op jit(solution)/shard_map/permute_local/pallas_call | solution.py:54
  10.2 0.0 all-gather.2.cloned.1.call-update
  10.2 0.0 copy-start.3
  10.3 76.2 %all-gather.2.cloned.1.call-done.left_ref = bf16[512,4096]{1,0:T(8,128)(2,1)} async-done(((bf16[64,4096]{1,0:T(8,128)(2,1)}), bf16[512,4096]{1,0:T(8,128)(2,1)}) %all-gather.2.cloned.1.call-update) | async-done | bytes 4194320 | tf_op jit(solution)/shard_map/all_gather | solution.py:327
  86.5 1.7 constant_dynamic-slice_fusion
  88.2 4.7 %collective-permute-start.2 = (bf16[512,2048]{1,0:T(8,128)(2,1)S(1)}, bf16[512,2048]{1,0:T(8,128)(2,1)}, u32[]{:S(2)}, u32[]{:S(2)}) collective-permute-start(bf16[512,2048]{1,0:T(8,128)(2,1)S(1)} %constant_dynamic-slice_fusion), channel_id=1, source_target_pairs={{0,8},{1,9},{6,14},{7,15},{24,16},{25,17},{30,22},{31,23}} | collective-permute-start | bytes 6291464 | tf_op jit(solution)/shard_map/ppermute | solution.py:310
  92.9 0.0 copy-done.3
  92.9 0.6 dynamic_slice.10
  94.2 0.0 copy-start.2
  94.2 0.0 copy-start
  94.2 0.0 copy-start.1
  94.2 20.9 %collective-permute-done.2 = bf16[512,2048]{1,0:T(8,128)(2,1)} collective-permute-done((bf16[512,2048]{1,0:T(8,128)(2,1)S(1)}, bf16[512,2048]{1,0:T(8,128)(2,1)}, u32[]{:S(2)}, u32[]{:S(2)}) %collective-permute-start.2) | collective-permute-done | bytes 2097184 | tf_op jit(solution)/shard_map/ppermute | solution.py:310
  115.1 2.4 %broadcast_select_fusion = bf16[512,2048]{1,0:T(8,128)(2,1)S(1)} fusion(bf16[512,2048]{1,0:T(8,128)(2,1)} %collective-permute-done.2, pred[]{:T(512)S(6)} %eq.17, bf16[512,4096]{1,0:T(8,128)(2,1)} %all-gather.2.cloned.1.call-done.left_ref, s32[]{:T(128)S(6)} %select_n.50), kind=kLoop, calls=%fused_computation | loop fusion | flops 1048576 | bytes 6291461 | tf_op jit(solution)/shard_map/jit(_where)/select_n | solution.py:312
  117.5 2.6 %collective-permute-start.3 = (bf16[512,2048]{1,0:T(8,128)(2,1)S(1)}, bf16[512,2048]{1,0:T(8,128)(2,1)}, u32[]{:S(2)}, u32[]{:S(2)}) collective-permute-start(bf16[512,2048]{1,0:T(8,128)(2,1)S(1)} %broadcast_select_fusion), channel_id=1, source_target_pairs={{0,4},{8,12},{1,5},{9,13},{6,2},{14,10},{7,3},{15,11},{24,28},{16,... | collective-permute-start | bytes 6291464 | tf_op jit(solution)/shard_map/ppermute | solution.py:310
  120.1 0.0 copy-done.2
  120.1 5.1 %collective-permute-start = (bf16[64,640]{1,0:T(8,128)(2,1)S(1)}, bf16[64,640]{1,0:T(8,128)(2,1)S(1)}, u32[]{:S(2)}, u32[]{:S(2)}) collective-permute-start(bf16[64,640]{1,0:T(8,128)(2,1)S(1)} %copy-done.2), channel_id=1, source_target_pairs={{0,8},{1,9},{2,10},{3,11},{16,24},{17,25},{18,26},{19,27}} | collective-permute-start | bytes 245768 | tf_op jit(solution)/shard_map/ppermute | solution.py:310
  125.3 0.0 copy-done
  125.3 2.0 collective-permute-done
  127.3 1.3 collective-permute-start.1
  128.6 0.1 pad_add_fusion.place_ref
  128.7 0.8 collective-permute-done.1
  129.5 33.0 %all_gather.7.head_ref = bf16[512,640]{1,0:T(8,128)(2,1)S(1)} all-gather(bf16[64,640]{1,0:T(8,128)(2,1)S(1)} %broadcast_select_fusion.3), channel_id=1, replica_groups=mesh['ep'=2,'row'=4,'col'=4] {'ep','col'}, dimensions={0}, use_global_device_ids=true | all-gather | bytes 737280 | tf_op jit(solution)/shard_map/all_gather | solution.py:326
  162.5 0.0 copy-done.1
  162.5 29.7 %factor_panel.1 = (bf16[512,256]{1,0:T(8,128)(2,1)S(1)}, f32[512,512]{1,0:T(8,128)S(1)}, bf16[512,512]{1,0:T(8,128)(2,1)S(1)}, bf16[512,512]{1,0:T(8,128)(2,1)S(1)}, bf16[512,512]{1,0:T(8,128)(2,1)S(1)}) custom-call(f32[64]{0:T(128)S(1)} %copy-done.1, bf16[512,640]{1,0:T(8,128)(2,1)S(1)} %all_gather.7.head_ref, f32[1,512]{1,0:T(1,128)S(1)} %bitcast.8), custom_call_target="tpu_custom_call" | custom-call | tf_op jit(solution)/shard_map/factor_panel/pallas_call | solution.py:181
  192.2 0.0 collective-permute-done.3
  192.2 0.3 broadcast_select_fusion.1.right_ref
  192.5 4.6 %project_columns.1.right_ref = bf16[512,2048]{1,0:T(8,128)(2,1)S(1)} custom-call(s32[2]{0:T(128)S(1)} %pad_add_fusion.place_ref, bf16[512,2048]{1,0:T(8,128)(2,1)S(1)} %broadcast_select_fusion.1.right_ref, bf16[512,256]{1,0:T(8,128)(2,1)S(1)} %get-tuple-element.14.band_ref, bf16[512,512]{1,0:T(8,128)(2,1)S(1)} %get-tuple-element.15.w_ref, ...), custom_call_target="tpu_custom_call" | custom-call | tf_op jit(solution)/shard_map/project_columns/pallas_call | solution.py:216
  197.1 19.9 %multiply_tile.1 = f32[4096,2048]{1,0:T(8,128)} custom-call(s32[2]{0:T(128)S(1)} %pad_add_fusion.place_ref, bf16[512,4096]{1,0:T(8,128)(2,1)} %all-gather.2.cloned.1.call-done.left_ref, bf16[512,256]{1,0:T(8,128)(2,1)S(1)} %get-tuple-element.14.band_ref, bf16[512,2048]{1,0:T(8,128)(2,1)S(1)} %project_columns.1.right_ref, f32[1,16384]{1,0:T(1,128)S(1)} %bitcast.7, ...), custom_call_target="tpu_custom_call" | custom-call | tf_op jit(solution)/shard_map/multiply_tile/pallas_call | solution.py:272
  (3 shorter events, 0.0 us)
Async XLA Ops:
  6.5 79.9 %all-gather.2.cloned.1.call-start = ((), (), s32[]{:S(2)}) async-start(), calls=%async_computation | async-start | bytes 4718592 | tf_op jit(solution)/shard_map/all_gather | solution.py:327
  10.2 82.7 %copy-start.3 = (s32[8]{0:T(128)S(1)}, s32[8]{0:T(128)}, u32[]{:S(2)}) copy-start(s32[8]{0:T(128)} %constant.44.clone) | copy-start | bytes 100
  88.2 26.9 %collective-permute-start.2 = (bf16[512,2048]{1,0:T(8,128)(2,1)S(1)}, bf16[512,2048]{1,0:T(8,128)(2,1)}, u32[]{:S(2)}, u32[]{:S(2)}) collective-permute-start(bf16[512,2048]{1,0:T(8,128)(2,1)S(1)} %constant_dynamic-slice_fusion), channel_id=1, source_target_pairs={{0,8},{1,9},{6,14},{7,15},{24,16},{25,17},{30,22},{31,23}} | collective-permute-start | bytes 6291464 | tf_op jit(solution)/shard_map/ppermute | solution.py:310
  94.2 26.0 %copy-start.2 = (bf16[64,640]{1,0:T(8,128)(2,1)S(1)}, bf16[64,640]{1,0:T(8,128)(2,1)}, u32[]{:S(2)}) copy-start(bf16[64,640]{1,0:T(8,128)(2,1)} %get-tuple-element.13) | copy-start | bytes 245764
  94.2 31.1 %copy-start = (f32[16384]{0:T(1024)S(1)}, f32[16384]{0:T(1024)}, u32[]{:S(2)}) copy-start(f32[16384]{0:T(1024)} %param.11) | copy-start | bytes 196612
  94.2 68.3 %copy-start.1 = (f32[64]{0:T(128)S(1)}, f32[64]{0:T(128)}, u32[]{:S(2)}) copy-start(f32[64]{0:T(128)} %taps_ref.1) | copy-start | bytes 772
  117.5 74.7 %collective-permute-start.3 = (bf16[512,2048]{1,0:T(8,128)(2,1)S(1)}, bf16[512,2048]{1,0:T(8,128)(2,1)}, u32[]{:S(2)}, u32[]{:S(2)}) collective-permute-start(bf16[512,2048]{1,0:T(8,128)(2,1)S(1)} %broadcast_select_fusion), channel_id=1, source_target_pairs={{0,4},{8,12},{1,5},{9,13},{6,2},{14,10},{7,3},{15,11},{24,28},{16,... | collective-permute-start | bytes 6291464 | tf_op jit(solution)/shard_map/ppermute | solution.py:310
  120.1 7.2 %collective-permute-start = (bf16[64,640]{1,0:T(8,128)(2,1)S(1)}, bf16[64,640]{1,0:T(8,128)(2,1)S(1)}, u32[]{:S(2)}, u32[]{:S(2)}) collective-permute-start(bf16[64,640]{1,0:T(8,128)(2,1)S(1)} %copy-done.2), channel_id=1, source_target_pairs={{0,8},{1,9},{2,10},{3,11},{16,24},{17,25},{18,26},{19,27}} | collective-permute-start | bytes 245768 | tf_op jit(solution)/shard_map/ppermute | solution.py:310
  127.3 2.2 collective-permute-start.1
Sparse Core Ops, SparseCore 0:
  10.3 76.0 all-gather.1

commit v2 on v1

v2 whole, which is shorter than its diff:
```python
import functools

import jax
import jax.numpy as jnp
from jax import lax
from jax.experimental import pallas as pl
from jax.experimental.pallas import tpu as pltpu
from jax.sharding import PartitionSpec as P

PANEL = 256
SECTIONS = 2
HEAD = PANEL * SECTIONS
PB = 128
LANES = 128
BLOCK = 128
HALF = 256
SUB = 8
NOTE = 16
EXACT = lax.Precision.HIGHEST
F32 = jnp.float32
BF16 = jnp.bfloat16


def iota(shape, axis):
    return lax.broadcasted_iota(jnp.int32, shape, axis)


def dot(left, right, contract=((1,), (0,)), precision=None):
    return lax.dot_general(
        left, right, (contract, ((), ())), preferred_element_type=F32, precision=precision
    )


NT = ((1,), (1,))
TN = ((0,), (0,))
VMEM = pl.BlockSpec(memory_space=pltpu.VMEM)
SMEM = pl.BlockSpec(memory_space=pltpu.SMEM)
LIMIT = pltpu.CompilerParams(vmem_limit_bytes=48 << 20)


def permute_kernel(order_ref, counts_ref, design_ref, *out_refs):
    *chunk_refs, note_ref = out_refs
    epochs, rows = design_ref.shape
    halves = chunk_refs[0].shape[0]
    per_half = len(chunk_refs)
    local = order_ref[...] & (PB - 1)
    local = local.astype(F32).T
    lane = iota((PB, PB), 1).astype(F32)
    none = jnp.zeros((epochs, PB), BF16)
    for block in range(rows // (2 * HALF)):
        h, i = divmod(block, per_half)
        for part in range(HALF // PB):
            first = block * (2 * HALF // PB) + part
            second = first + HALF // PB
            pick = [jnp.where(local[:, g : g + 1] == lane, 1.0, 0.0) for g in (first, second)]
            pick = jnp.concatenate(pick, axis=1).astype(BF16)
            top = jnp.concatenate([design_ref[:, first * PB : (first + 1) * PB], none], axis=1)
            low = jnp.concatenate([none, design_ref[:, second * PB : (second + 1) * PB]], axis=1)
            packed = dot(pick, jnp.concatenate([top, low], axis=0), NT)
            chunk_refs[i][h, part * PB : (part + 1) * PB, :] = packed.astype(BF16)
    note_ref[:HALF, :] = chunk_refs[0][0]
    note_ref[HALF:, :] = jnp.broadcast_to(counts_ref[...].astype(F32), (NOTE, LANES)).astype(BF16)


def permute_local(design, order, tap_count, cols_dev):
    epochs, rows = design.shape
    halves, per_half = rows // cols_dev, cols_dev // (2 * HALF)
    chunk = jax.ShapeDtypeStruct((halves, HALF, LANES), BF16)
    note = jax.ShapeDtypeStruct((HALF + NOTE, LANES), BF16)
    counts = jnp.tile(tap_count, LANES // epochs).reshape(1, LANES)
    return pl.pallas_call(
        permute_kernel,
        out_shape=(chunk,) * per_half + (note,),
        in_specs=[VMEM] * 3,
        compiler_params=LIMIT,
        name="permute_local",
    )(order.reshape(rows // PB, PB), counts, design)


def filter_rows(blocks, band_ref, store):
    per = HALF // (LANES // 2)
    for b in range(band_ref.shape[0]):
        first = max(b * per - 1, 0)
        skip = 0 if b else LANES
        packed = jnp.concatenate([blocks(e) for e in range(first, (b + 1) * per)], axis=1)
        for half in range(2):
            got = dot(packed, band_ref[b, half, skip:, :]).astype(BF16)
            store(slice(half * HALF, (half + 1) * HALF), slice(b * HALF, (b + 1) * HALF), got)


def spread(tile, lane):
    return jnp.broadcast_to(tile[:, lane : lane + 1], (SUB, tile.shape[1]))


def row_of(tile, k):
    return jnp.broadcast_to(tile[k : k + 1, :], (SUB, tile.shape[1]))


def factor_block(work):
    halves = work.shape[1] // BLOCK
    groups = BLOCK // SUB
    for g in range(groups):
        rows = slice(g * SUB, (g + 1) * SUB)
        own = [work[rows, h * BLOCK : (h + 1) * BLOCK] for h in range(halves)]
        cols = [spread(own[0], g * SUB + j) for j in range(SUB)]
        a = {(i, j): row_of(cols[j], i) for j in range(SUB) for i in range(j, SUB)}
        u = [[row_of(own[h], k) for k in range(SUB)] for h in range(halves)]
        inv = []
        low = {}
        for k in range(SUB):
            r = lax.rsqrt(a[k, k])
            inv.append(r)
            for i in range(k + 1, SUB):
                low[i, k] = a[i, k] * r
            for j in range(k + 1, SUB):
                for i in range(j, SUB):
                    a[i, j] = a[i, j] - low[i, k] * low[j, k]
            for h in range(halves):
                u[h][k] = u[h][k] * r
                for j in range(k + 1, SUB):
                    u[h][j] = u[h][j] - low[j, k] * u[h][k]
        for h in range(halves):
            merged = u[h][0]
            for k in range(1, SUB):
                merged = jnp.where(iota((SUB, BLOCK), 0) == k, u[h][k], merged)
            work[rows, h * BLOCK : (h + 1) * BLOCK] = merged
        for t in range(g + 1, groups):
            below = slice(t * SUB, (t + 1) * SUB)
            tile = [work[below, h * BLOCK : (h + 1) * BLOCK] for h in range(halves)]
            left = [spread(tile[0], g * SUB + j) for j in range(SUB)]
            for k in range(SUB):
                left[k] = left[k] * inv[k]
                for j in range(k + 1, SUB):
                    left[j] = left[j] - low[j, k] * left[k]
                for h in range(halves):
                    tile[h] = tile[h] - left[k] * u[h][k]
            for h in range(halves):
                work[below, h * BLOCK : (h + 1) * BLOCK] = tile[h]


def start_kernel(
    sources, place_ref, taps_ref, own_ref, came_ref, reg_ref, band_ref, aug_ref, notes, a1, work
):
    chain, steps = sources
    epochs = aug_ref.shape[1] - HEAD
    half = LANES // 2

    @pl.when(place_ref[0] % 2 == 0)
    def _():
        for rel, at in enumerate(steps):
            notes[place_ref[chain + rel]] = own_ref[rel]

    @pl.when(place_ref[0] % 2 == 1)
    def _():
        for rel, at in enumerate(steps):
            notes[place_ref[chain + rel]] = came_ref[rel]

    shape = (half, LANES)
    lag = iota(shape, 1) - iota(shape, 0)
    base = lax.fori_loop(
        0,
        taps_ref.shape[0],
        lambda k, kept: jnp.where(lag == k, taps_ref[k], kept),
        jnp.zeros(shape, F32),
    )
    lane = iota(shape, 1)
    swapped = jnp.concatenate([base[:, half:], base[:, :half]], axis=1)
    early = jnp.where(lane < half, swapped, 0.0)
    late = jnp.where(lane >= half, swapped, 0.0)
    none = jnp.zeros(shape, F32)
    patterns = [(early, none), (base, none), (late, early), (none, base), (none, late)]
    row = iota((1, LANES), 1)
    band_ref[...] = jnp.zeros_like(band_ref)
    for b in range(epochs // HALF):
        for side in range(HALF // LANES):
            e = (b * HALF + side * LANES) // half
            counts = [notes[e + n, HALF : HALF + NOTE, :].astype(F32)[:1] for n in range(2)]
            counts = jnp.where(row < half, counts[0], counts[1])
            for j, pattern in enumerate(patterns):
                at = (lag + side * LANES + half - half * j).astype(F32)
                kept = jnp.where(at < counts, pattern[side], 0.0).astype(BF16)
                for h in range(2):
                    rows = slice(j * LANES + h * half, j * LANES + (h + 1) * half)
                    band_ref[b, h, rows, side * LANES : (side + 1) * LANES] = kept

    def store(rows, cols, got):
        a1[rows, cols] = got

    filter_rows(lambda e: notes[e, :HALF, :], band_ref, store)
    columns = a1[...]
    square = (HEAD, HEAD)
    on_diagonal = iota(square, 0) == iota(square, 1)
    aug_ref[:, :HEAD] = dot(columns, columns, NT) + jnp.where(on_diagonal, reg_ref[...], 0.0)
    aug_ref[:, HEAD:] = columns.astype(F32)
    eliminate(aug_ref, 0, work)


def eliminate(aug, kb, work):
    here = slice(kb * BLOCK, (kb + 1) * BLOCK)
    work[:, :BLOCK] = aug[here, here]
    work[:, BLOCK:] = jnp.where(iota((BLOCK, BLOCK), 0) == iota((BLOCK, BLOCK), 1), 1.0, 0.0)
    factor_block(work)
    rest = slice(kb * BLOCK, aug.shape[1])
    aug[here, rest] = dot(work[:, BLOCK:], aug[here, rest], precision=EXACT)
    for rb in range(kb + 1, HEAD // BLOCK):
        below = slice(rb * BLOCK, (rb + 1) * BLOCK)
        rest = slice(rb * BLOCK, aug.shape[1])
        aug[below, rest] -= dot(aug[here, below], aug[here, rest], TN, precision=EXACT)


def next_kernel(kb, aug_in, aug_ref, work):
    done = slice(0, kb * BLOCK)
    aug_ref[...] = aug_in[...]
    eliminate(aug_ref, kb, work)


def last_kernel(kb, aug_in, factor_ref, w_ref, high_ref, low_ref, aug, work):
    aug[...] = aug_in[...]
    eliminate(aug, kb, work)
    square = (HEAD, HEAD)
    epochs = aug.shape[1] - HEAD
    factor_ref[...] = jnp.where(iota(square, 0) >= iota(square, 1), aug[:, :HEAD].T, 0.0)
    wt = aug[:, HEAD:]
    w_ref[...] = wt.T.astype(BF16)
    for b in range(epochs // BLOCK):
        here = slice(b * BLOCK, (b + 1) * BLOCK)
        shape = (BLOCK, epochs)
        unit = jnp.where(iota(shape, 0) + b * BLOCK == iota(shape, 1), 1.0, 0.0)
        middle = unit - dot(wt[:, here], wt, TN, precision=EXACT)
        high = middle.astype(BF16)
        high_ref[here, :] = high
        low_ref[here, :] = (middle - high.astype(F32)).astype(BF16)


def start_panel(place, chain, taps, own, came, regular):
    sources, epochs = own.shape[0], own.shape[0] * (LANES // 2)
    per = HALF // (LANES // 2)
    return pl.pallas_call(
        functools.partial(start_kernel, (chain, range(sources))),
        out_shape=(
            jax.ShapeDtypeStruct((epochs // HALF, 2, (per + 1) * LANES, HALF), BF16),
            jax.ShapeDtypeStruct((HEAD, HEAD + epochs), F32),
        ),
        in_specs=[SMEM, SMEM, VMEM, VMEM, VMEM],
        out_specs=(VMEM, VMEM),
        scratch_shapes=[
            pltpu.VMEM(own.shape, BF16),
            pltpu.VMEM((HEAD, epochs), BF16),
            pltpu.VMEM((BLOCK, 2 * BLOCK), F32),
        ],
        compiler_params=LIMIT,
        cost_estimate=pl.CostEstimate(flops=1 << 30, bytes_accessed=24 << 20, transcendentals=0),
        name="start_panel",
    )(place, taps, own, came, regular[:HEAD].reshape(1, HEAD))


def next_panel(kb, aug):
    return pl.pallas_call(
        functools.partial(next_kernel, kb),
        out_shape=jax.ShapeDtypeStruct(aug.shape, F32),
        in_specs=[VMEM],
        out_specs=VMEM,
        scratch_shapes=[pltpu.VMEM((BLOCK, 2 * BLOCK), F32)],
        compiler_params=LIMIT,
        cost_estimate=pl.CostEstimate(flops=1 << 30, bytes_accessed=20 << 20, transcendentals=0),
        name="next_panel",
    )(aug)


def last_panel(kb, aug):
    epochs = aug.shape[1] - HEAD
    return pl.pallas_call(
        functools.partial(last_kernel, kb),
        out_shape=(
            jax.ShapeDtypeStruct((HEAD, HEAD), F32),
            jax.ShapeDtypeStruct((epochs, HEAD), BF16),
            jax.ShapeDtypeStruct((epochs, epochs), BF16),
            jax.ShapeDtypeStruct((epochs, epochs), BF16),
        ),
        in_specs=[VMEM],
        out_specs=(VMEM,) * 4,
        scratch_shapes=[pltpu.VMEM(aug.shape, F32), pltpu.VMEM((BLOCK, 2 * BLOCK), F32)],
        compiler_params=LIMIT,
        cost_estimate=pl.CostEstimate(flops=1 << 30, bytes_accessed=24 << 20, transcendentals=0),
        name="last_panel",
    )(aug)


def tile_kernel(chunks, halves, place_ref, *refs):
    own_refs, other_refs = refs[:chunks], refs[chunks : 2 * chunks]
    right_refs, came_refs = refs[2 * chunks : 3 * chunks], refs[3 * chunks : 4 * chunks]
    band_ref, w_ref, high_ref, low_ref, factor_ref, reg_ref, out_ref = refs[4 * chunks : -3]
    blocks, filtered, right = refs[-3:]
    rows, cols = out_ref.shape
    width = own_refs[0].shape[0]
    step = pl.program_id(0)
    row, group, side, takes = (place_ref[n] for n in range(4))
    first_row = (row * chunks * halves + (step % halves) * chunks + step // halves) * rows
    first_col = group * cols

    def store(at_rows, at_cols, got):
        filtered[at_rows, at_cols] = got

    @pl.when(step == 0)
    def _():
        for i in range(chunks):

            @pl.when(takes == 0)
            def _():
                blocks[...] = right_refs[i][...]

            @pl.when(takes != 0)
            def _():
                blocks[...] = came_refs[i][...]

            filter_rows(lambda e: blocks[e], band_ref, store)
            columns = filtered[...]
            projected = dot(high_ref[...], columns, NT) + dot(low_ref[...], columns, NT)
            right[:, i * rows : (i + 1) * rows] = projected.astype(BF16)

        @pl.when(group == 0)
        def _():
            right[:, :HEAD] = w_ref[...]

    @pl.when(first_row >= HEAD)
    def _():
        for i in range(chunks):
            for h in range(halves):

                @pl.when(step == i * halves + h)
                def _():
                    blocks[pl.ds(side * width, width)] = own_refs[i][:, h]
                    blocks[pl.ds((1 - side) * width, width)] = other_refs[i][:, h]

        filter_rows(lambda e: blocks[e], band_ref, store)
        out_ref[...] = dot(filtered[...], right[...])

        @pl.when((first_row >= first_col) & (first_row < first_col + cols))
        def _():
            at = pl.multiple_of(first_row - first_col, rows)
            on_diagonal = iota((rows, rows), 0) == iota((rows, rows), 1)
            out_ref[:, pl.ds(at, rows)] += jnp.where(on_diagonal, reg_ref[...], 0.0)

    @pl.when(first_row < HEAD)
    def _():
        out_ref[...] = jnp.zeros_like(out_ref)

        @pl.when(first_col == 0)
        def _():
            out_ref[:, :HEAD] = factor_ref[...]


def multiply_tile(place, own, other, right, came, band, w, high, low, factor, regular, cols):
    chunks, (width, halves) = len(own), own[0].shape[:2]
    rows = 2 * HALF
    steps = chunks * halves
    epochs = high.shape[0]
    block = lambda i: (i % halves) * chunks + i // halves
    fixed = lambda array: pl.BlockSpec(
        array.shape, lambda i, place: (0,) * array.ndim, pipeline_mode=pl.Buffered(1)
    )
    operands = (*own, *other, *right, *came, band, w, high, low, factor)
    return pl.pallas_call(
        functools.partial(tile_kernel, chunks, halves),
        out_shape=jax.ShapeDtypeStruct((steps * rows, cols), F32),
        grid_spec=pltpu.PrefetchScalarGridSpec(
            num_scalar_prefetch=1,
            grid=(steps,),
            in_specs=[fixed(array) for array in operands]
            + [pl.BlockSpec((1, rows), lambda i, place: (0, place[0] * steps + block(i)))],
            out_specs=pl.BlockSpec((rows, cols), lambda i, place: (block(i), 0)),
            scratch_shapes=[
                pltpu.VMEM((epochs // (LANES // 2), HALF, LANES), BF16),
                pltpu.VMEM((rows, epochs), BF16),
                pltpu.VMEM((epochs, cols), BF16),
            ],
        ),
        compiler_params=pltpu.CompilerParams(vmem_limit_bytes=56 << 20),
        name="multiply_tile",
    )(place, *operands, regular.reshape(1, -1))


AXES = ("ep", "row", "col")


def flat(ep, row, col):
    return (ep * lax.axis_size("row") + row) * lax.axis_size("col") + col


def spread_rows(block, owner_of, distances):
    row = lax.axis_index("row")
    eps, cols, rows = (lax.axis_size(axis) for axis in ("ep", "col", "row"))
    owners = jnp.asarray([owner_of(e, c) for e in range(eps) for c in range(cols)], jnp.int32)
    owner = owners[lax.axis_index(("ep", "col"))]
    for n, distance in enumerate(distances):
        route = []
        for e in range(eps):
            for c in range(cols):
                for other in range(0, rows, 2 * distance):
                    source = owner_of(e, c) ^ other
                    route.append((flat(e, source, c), flat(e, source ^ distance, c)))
        came = lax.ppermute(block, AXES, route)
        takes = ((row ^ owner) & (2 * distance - 1)) == distance
        if n == len(distances) - 1:
            return block, came, takes
        block = jnp.where(takes, came, block)


def doubling(count, least):
    distances = []
    distance = count // 2
    while distance >= least:
        distances.append(distance)
        distance //= 2
    return distances


def gather_panel(note):
    eps, cols, rows = (lax.axis_size(axis) for axis in ("ep", "col", "row"))
    distances = doubling(rows, 2)
    if distances:
        block, came, takes = spread_rows(note, lambda e, c: 0, distances)
        note = jnp.where(takes, came, block)
    notes = [note]
    steps = [(0, 0)]
    for de in range(eps):
        for dc in range(cols):
            if de or dc:
                route = [
                    (flat(e, r, c), flat((e + de) % eps, r, (c + dc) % cols))
                    for e in range(eps)
                    for r in range(0, rows, 2)
                    for c in range(cols)
                ]
                notes.append(lax.ppermute(note, AXES, route))
                steps.append((de, dc))
    notes = jnp.stack(notes)
    came = lax.ppermute(notes, "row", [(r, r + 1) for r in range(0, rows, 2)])
    ep, col = lax.axis_index("ep"), lax.axis_index("col")
    order = [((ep - de) % eps) * cols + (col - dc) % cols for de, dc in steps]
    return notes, came, order


def on_device(design, taps, tap_count, order, regular):
    epochs_dev, rows_dev = design.shape
    eps, cols, rows = (lax.axis_size(axis) for axis in ("ep", "col", "row"))
    groups = eps * cols
    cols_dev = regular.shape[0] // groups
    row, ep = lax.axis_index("row"), lax.axis_index("ep")
    group = lax.axis_index(("ep", "col"))
    *chunks, note = permute_local(design, order, tap_count, cols_dev)
    notes, came, sources = gather_panel(note)
    column = [lax.all_gather(chunk, "col", axis=0) for chunk in chunks]
    other = [lax.ppermute(chunk, "ep", [(0, 1), (1, 0)]) for chunk in column]
    owner = lambda e, c: (e * cols + c) * cols_dev // rows_dev
    half = (group * cols_dev % rows_dev) // cols_dev
    right, right_came = [], []
    for mine, theirs in zip(column, other):
        mine = lax.dynamic_index_in_dim(mine, half, 1, keepdims=False)
        theirs = lax.dynamic_index_in_dim(theirs, half, 1, keepdims=False)
        low = jnp.where(ep == 0, mine, theirs)
        high = jnp.where(ep == 0, theirs, mine)
        block, got, takes = spread_rows(jnp.concatenate([low, high]), owner, doubling(rows, 1))
        right.append(block)
        right_came.append(got)
    place = jnp.stack([row, group, ep, takes.astype(jnp.int32), *sources]).astype(jnp.int32)
    band, aug = start_panel(place, 4, taps, notes, came, regular)
    panels = HEAD // BLOCK
    for kb in range(1, panels - 1):
        aug = next_panel(kb, aug)
    factor, w, high, low = last_panel(panels - 1, aug)
    return multiply_tile(
        place, column, other, right, right_came, band, w, high, low, factor, regular, cols_dev
    )


def solution(mesh):
    in_specs = (P(("ep", "col"), "row"), P(), P(("ep", "col")), P("row"), P())
    out_specs = P("row", ("ep", "col"))
    return jax.shard_map(
        on_device, mesh=mesh, in_specs=in_specs, out_specs=out_specs, check_vma=False
    )
```

time: 225 us -> 226 us (level)
  waiting for transfers between devices: 100 us -> 35.4 us
  starting transfers between devices: 13.7 us -> 47.2 us
  blocking collectives: 33 us -> 62.2 us
  local copies, waits for them, and re-layouts: 3.71 us -> 20.5 us
  between operations: 14.2 us -> 1.22 us
  Pallas kernels: 56.5 us -> 54 us
    all_gather x1 -> x0, waiting for transfers between devices: 76.2 us -> none  [on_device(): left = lax.all_gather(permuted, ('ep', 'col'), axis=0, tiled=True)]
    all_gather x1 -> x4, blocking collectives: 33 us -> 62.2 us  [on_device(): column = [lax.all_gather(chunk, 'col', axis=0) for chunk in chunks]]
    ppermute x0 -> x12, starting transfers between devices: none -> 28.1 us  [the longest x7 22.3 us: gather_panel(): notes.append(lax.ppermute(note, AXES, route))]
    ppermute x0 -> x12, waiting for transfers between devices: none -> 24.8 us  [the longest x7 24.8 us: gather_panel(): notes.append(lax.ppermute(note, AXES, route))]
    ppermute x4 -> x9, waiting for transfers between devices: 23.8 us -> 10.6 us  [spread_rows(): came = lax.ppermute(block, AXES, route)]
    ppermute x0 -> x4, local copies, waits for them, and re-layouts: none -> 7.59 us  [on_device(): other = [lax.ppermute(chunk, 'ep', [(0, 1), (1, 0)]) for chunk in column]]
    unnamed x8 -> x42, local copies, waits for them, and re-layouts: 0.02 us -> 7.14 us
    ppermute x4 -> x9, starting transfers between devices: 13.7 us -> 19.1 us  [spread_rows(): came = lax.ppermute(block, AXES, route)]
  transfers between devices with their start and end apart: 5 -> 21, of which waited for: 4 -> 10; matrix products, arithmetic and copies ran while one was open for 0% -> 7% of each run, Pallas kernels for 13% -> 12%
where the time goes in v2:
time: 226 us; the launch traced here: 224 us
  blocking collectives  62.2 us (28%)
  Pallas kernels  54 us (24%)
  starting transfers between devices  47.2 us (21%)
  waiting for transfers between devices  35.4 us (16%)
  local copies, waits for them, and re-layouts  20.5 us (9%)
  other arithmetic  3.93 us (2%)
    all_gather x4, blocking collectives, on_device(): column = [lax.all_gather(chunk, 'col', axis=0) for chunk in chunks]  62.2 us
    pallas_call x1, Pallas kernels, multiply_tile(): pl.pallas_call(functools.partial(tile_kernel, chunks, halves), out_shape=...  25.1 us
    ppermute x7, waiting for transfers between devices, gather_panel(): notes.append(lax.ppermute(note, AXES, route))  24.8 us
    ppermute x7, starting transfers between devices, gather_panel(): notes.append(lax.ppermute(note, AXES, route))  22.3 us
    ppermute x9, starting transfers between devices, spread_rows(): came = lax.ppermute(block, AXES, route)  19.1 us
    pallas_call x2, Pallas kernels, next_panel(): pl.pallas_call(functools.partial(next_kernel, kb), out_shape=jax.ShapeDty...  12.1 us
    ppermute x9, waiting for transfers between devices, spread_rows(): came = lax.ppermute(block, AXES, route)  10.6 us
    pallas_call x1, Pallas kernels, start_panel(): pl.pallas_call(functools.partial(start_kernel, (chain, range(sources))),...  8.62 us
  transfers between devices with their start and end apart: 21, of which 10 were waited for; matrix products, arithmetic and copies ran while one was open for 7% of the time, Pallas kernels for 12%

profile of v2, /device:TPU:0, one launch (start us, length us, event | category | flops | bytes accessed | tf_op | source)
XLA Modules:
  0.0 224.4 jit_solution(7640763318905358048)
XLA Ops:
  0.7 1.0 copy-done.5
  2.5 0.9 permute_local.1
  3.5 4.9 %collective-permute-start.12 = (bf16[272,128]{1,0:T(8,128)(2,1)S(1)}, bf16[272,128]{1,0:T(8,128)(2,1)S(1)}, u32[]{:S(2)}, u32[]{:S(2)}) collective-permute-start(bf16[272,128]{1,0:T(8,128)(2,1)S(1)} %get-tuple-element.20), channel_id=1, source_target_pairs={{0,8},{1,9},{2,10},{3,11},{16,24},{17,25},{18,26},{19,27}} | collective-permute-start | bytes 208904 | tf_op jit(solution)/shard_map/ppermute | solution.py:402
  8.3 16.2 %all-gather.3 = bf16[8,256,128]{2,1,0:T(8,128)(2,1)S(1)} all-gather(bf16[2,256,128]{2,1,0:T(8,128)(2,1)S(1)} %get-tuple-element.19), channel_id=5, replica_groups=mesh['ep'=2,'row'=4,'col'=4] {'col'}, dimensions={0}, use_global_device_ids=true | all-gather | bytes 655360 | tf_op jit(solution)/shard_map/all_gather | solution.py:453
  25.4 1.5 collective-permute-start.3
  26.9 16.1 %all-gather.2 = bf16[8,256,128]{2,1,0:T(8,128)(2,1)S(1)} all-gather(bf16[2,256,128]{2,1,0:T(8,128)(2,1)S(1)} %get-tuple-element.18), channel_id=4, replica_groups=mesh['ep'=2,'row'=4,'col'=4] {'col'}, dimensions={0}, use_global_device_ids=true | all-gather | bytes 655360 | tf_op jit(solution)/shard_map/all_gather | solution.py:453
  44.5 14.9 %all-gather.1 = bf16[8,256,128]{2,1,0:T(8,128)(2,1)S(1)} all-gather(bf16[2,256,128]{2,1,0:T(8,128)(2,1)S(1)} %get-tuple-element.17), channel_id=3, replica_groups=mesh['ep'=2,'row'=4,'col'=4] {'col'}, dimensions={0}, use_global_device_ids=true | all-gather | bytes 655360 | tf_op jit(solution)/shard_map/all_gather | solution.py:453
  60.2 1.5 collective-permute-start.1
  61.8 3.6 %collective-permute-start.13 = (bf16[272,128]{1,0:T(8,128)(2,1)S(1)}, bf16[272,128]{1,0:T(8,128)(2,1)S(1)}, u32[]{:S(2)}, u32[]{:S(2)}) collective-permute-start(bf16[272,128]{1,0:T(8,128)(2,1)S(1)} %get-tuple-element.28), channel_id=1, source_target_pairs={{0,1},{1,2},{2,3},{3,0},{8,9},{9,10},{10,11},{11,8},{16,17},{17,18... | collective-permute-start | bytes 208904 | tf_op jit(solution)/shard_map/ppermute | solution.py:435
  65.3 15.0 %all-gather = bf16[8,256,128]{2,1,0:T(8,128)(2,1)S(1)} all-gather(bf16[2,256,128]{2,1,0:T(8,128)(2,1)S(1)} %get-tuple-element.16), channel_id=2, replica_groups=mesh['ep'=2,'row'=4,'col'=4] {'col'}, dimensions={0}, use_global_device_ids=true | all-gather | bytes 655360 | tf_op jit(solution)/shard_map/all_gather | solution.py:453
  83.5 2.6 %collective-permute-start.14 = (bf16[272,128]{1,0:T(8,128)(2,1)S(1)}, bf16[272,128]{1,0:T(8,128)(2,1)S(1)}, u32[]{:S(2)}, u32[]{:S(2)}) collective-permute-start(bf16[272,128]{1,0:T(8,128)(2,1)S(1)} %get-tuple-element.28), channel_id=1, source_target_pairs={{0,2},{1,3},{2,0},{3,1},{8,10},{9,11},{10,8},{11,9},{16,18},{17,19... | collective-permute-start | bytes 208904 | tf_op jit(solution)/shard_map/ppermute | solution.py:435
  86.1 4.7 %collective-permute-done.14 = bf16[272,128]{1,0:T(8,128)(2,1)S(1)} collective-permute-done((bf16[272,128]{1,0:T(8,128)(2,1)S(1)}, bf16[272,128]{1,0:T(8,128)(2,1)S(1)}, u32[]{:S(2)}, u32[]{:S(2)}) %collective-permute-start.14) | collective-permute-done | bytes 69664 | tf_op jit(solution)/shard_map/ppermute | solution.py:435
  90.9 4.0 %collective-permute-start.15 = (bf16[272,128]{1,0:T(8,128)(2,1)S(1)}, bf16[272,128]{1,0:T(8,128)(2,1)S(1)}, u32[]{:S(2)}, u32[]{:S(2)}) collective-permute-start(bf16[272,128]{1,0:T(8,128)(2,1)S(1)} %get-tuple-element.28), channel_id=1, source_target_pairs={{0,3},{1,0},{2,1},{3,2},{8,11},{9,8},{10,9},{11,10},{16,19},{17,16... | collective-permute-start | bytes 208904 | tf_op jit(solution)/shard_map/ppermute | solution.py:435
  94.9 2.2 collective-permute-done.15
  97.1 3.1 %collective-permute-start.16 = (bf16[272,128]{1,0:T(8,128)(2,1)S(1)}, bf16[272,128]{1,0:T(8,128)(2,1)S(1)}, u32[]{:S(2)}, u32[]{:S(2)}) collective-permute-start(bf16[272,128]{1,0:T(8,128)(2,1)S(1)} %get-tuple-element.28), channel_id=1, source_target_pairs={{0,16},{1,17},{2,18},{3,19},{8,24},{9,25},{10,26},{11,27},{16,0},{... | collective-permute-start | bytes 208904 | tf_op jit(solution)/shard_map/ppermute | solution.py:435
  100.2 3.1 %collective-permute-done.16 = bf16[272,128]{1,0:T(8,128)(2,1)S(1)} collective-permute-done((bf16[272,128]{1,0:T(8,128)(2,1)S(1)}, bf16[272,128]{1,0:T(8,128)(2,1)S(1)}, u32[]{:S(2)}, u32[]{:S(2)}) %collective-permute-start.16) | collective-permute-done | bytes 69664 | tf_op jit(solution)/shard_map/ppermute | solution.py:435
  103.3 2.3 %collective-permute-start.17 = (bf16[272,128]{1,0:T(8,128)(2,1)S(1)}, bf16[272,128]{1,0:T(8,128)(2,1)S(1)}, u32[]{:S(2)}, u32[]{:S(2)}) collective-permute-start(bf16[272,128]{1,0:T(8,128)(2,1)S(1)} %get-tuple-element.28), channel_id=1, source_target_pairs={{0,17},{1,18},{2,19},{3,16},{8,25},{9,26},{10,27},{11,24},{16,1},{... | collective-permute-start | bytes 208904 | tf_op jit(solution)/shard_map/ppermute | solution.py:435
  105.6 6.5 %collective-permute-done.17 = bf16[272,128]{1,0:T(8,128)(2,1)S(1)} collective-permute-done((bf16[272,128]{1,0:T(8,128)(2,1)S(1)}, bf16[272,128]{1,0:T(8,128)(2,1)S(1)}, u32[]{:S(2)}, u32[]{:S(2)}) %collective-permute-start.17) | collective-permute-done | bytes 69664 | tf_op jit(solution)/shard_map/ppermute | solution.py:435
  112.1 2.2 collective-permute-start.18
  114.3 5.8 %collective-permute-done.18 = bf16[272,128]{1,0:T(8,128)(2,1)S(1)} collective-permute-done((bf16[272,128]{1,0:T(8,128)(2,1)S(1)}, bf16[272,128]{1,0:T(8,128)(2,1)S(1)}, u32[]{:S(2)}, u32[]{:S(2)}) %collective-permute-start.18) | collective-permute-done | bytes 69664 | tf_op jit(solution)/shard_map/ppermute | solution.py:435
  120.1 4.6 %collective-permute-start.19 = (bf16[272,128]{1,0:T(8,128)(2,1)S(1)}, bf16[272,128]{1,0:T(8,128)(2,1)S(1)}, u32[]{:S(2)}, u32[]{:S(2)}) collective-permute-start(bf16[272,128]{1,0:T(8,128)(2,1)S(1)} %get-tuple-element.28), channel_id=1, source_target_pairs={{0,19},{1,16},{2,17},{3,18},{8,27},{9,24},{10,25},{11,26},{16,3},{... | collective-permute-start | bytes 208904 | tf_op jit(solution)/shard_map/ppermute | solution.py:435
  124.7 2.5 %collective-permute-done.19 = bf16[272,128]{1,0:T(8,128)(2,1)S(1)} collective-permute-done((bf16[272,128]{1,0:T(8,128)(2,1)S(1)}, bf16[272,128]{1,0:T(8,128)(2,1)S(1)}, u32[]{:S(2)}, u32[]{:S(2)}) %collective-permute-start.19) | collective-permute-done | bytes 69664 | tf_op jit(solution)/shard_map/ppermute | solution.py:435
  127.2 1.3 collective-permute-start.20
  128.6 1.3 select_bitcast_fusion.1
  130.0 2.6 %collective-permute-start.6 = (bf16[8,256,128]{2,1,0:T(8,128)(2,1)S(1)}, bf16[8,256,128]{2,1,0:T(8,128)(2,1)S(1)}, u32[]{:S(2)}, u32[]{:S(2)}) collective-permute-start(bf16[8,256,128]{2,1,0:T(8,128)(2,1)S(1)} %pad_maximum_fusion.2), channel_id=1, source_target_pairs={{0,8},{1,9},{6,14},{7,15},{24,16},{25,17},{30,22},{31,23}} | collective-permute-start | bytes 1572872 | tf_op jit(solution)/shard_map/ppermute | solution.py:402
  132.7 1.3 collective-permute-start.7
  134.0 1.3 select_bitcast_fusion.5
  135.4 1.3 collective-permute-start.4
  136.8 1.3 collective-permute-start.5
  138.1 1.1 collective-permute-done.6
  139.3 2.1 collective-permute-start.10
  141.5 3.4 %collective-permute-done.7 = bf16[8,256,128]{2,1,0:T(8,128)(2,1)S(1)} collective-permute-done((bf16[8,256,128]{2,1,0:T(8,128)(2,1)S(1)}, bf16[8,256,128]{2,1,0:T(8,128)(2,1)S(1)}, u32[]{:S(2)}, u32[]{:S(2)}) %collective-permute-start.7) | collective-permute-done | bytes 524320 | tf_op jit(solution)/shard_map/ppermute | solution.py:402
  145.0 2.2 collective-permute-start.11
  147.1 3.4 %collective-permute-done.4 = bf16[8,256,128]{2,1,0:T(8,128)(2,1)S(1)} collective-permute-done((bf16[8,256,128]{2,1,0:T(8,128)(2,1)S(1)}, bf16[8,256,128]{2,1,0:T(8,128)(2,1)S(1)}, u32[]{:S(2)}, u32[]{:S(2)}) %collective-permute-start.4) | collective-permute-done | bytes 524320 | tf_op jit(solution)/shard_map/ppermute | solution.py:402
  151.4 2.1 collective-permute-start.8
  153.4 2.7 %collective-permute-done.5 = bf16[8,256,128]{2,1,0:T(8,128)(2,1)S(1)} collective-permute-done((bf16[8,256,128]{2,1,0:T(8,128)(2,1)S(1)}, bf16[8,256,128]{2,1,0:T(8,128)(2,1)S(1)}, u32[]{:S(2)}, u32[]{:S(2)}) %collective-permute-start.5) | collective-permute-done | bytes 524320 | tf_op jit(solution)/shard_map/ppermute | solution.py:402
  156.2 1.3 collective-permute-start.9
  158.4 2.0 copy.42.refs_7_
  160.4 1.9 copy.41.refs_6_
  162.3 1.9 copy.40.refs_5_
  164.1 1.9 copy.39.refs_4_
  166.0 8.6 %start_panel.1 = (bf16[2,2,640,256]{3,2,1,0:T(8,128)(2,1)S(1)}, f32[512,1024]{1,0:T(8,128)S(1)}) custom-call(s32[12]{0:T(128)S(1)} %stack.82.place_ref, f32[64]{0:T(128)S(1)} %copy-done.8, bf16[8,272,128]{2,1,0:T(8,128)(2,1)S(1)} %bitcast_dynamic-update-slice_fusion.own_ref, bf16[8,272,128]{2,1,0:T(8,128)(2,1)S(1)} %collective-permute-done.20.came_ref, ...), custom_call_target="tpu_custom_call" | custom-call | flops 1073741824 | bytes 25165824 | tf_op jit(solution)/shard_map/start_panel/pallas_call | solution.py:238
  174.7 1.1 copy-done
  175.8 6.1 %next_panel.2.aug_in = f32[512,1024]{1,0:T(8,128)S(1)} custom-call(f32[512,1024]{1,0:T(8,128)S(1)} %get-tuple-element.22.aug_in), custom_call_target="tpu_custom_call" | custom-call | flops 1073741824 | bytes 20971520 | tf_op jit(solution)/shard_map/next_panel/pallas_call | solution.py:258
  181.9 6.0 %next_panel.3.aug_in = f32[512,1024]{1,0:T(8,128)S(1)} custom-call(f32[512,1024]{1,0:T(8,128)S(1)} %next_panel.2.aug_in), custom_call_target="tpu_custom_call" | custom-call | flops 1073741824 | bytes 20971520 | tf_op jit(solution)/shard_map/next_panel/pallas_call | solution.py:258
  187.9 7.2 %last_panel.1 = (f32[512,512]{1,0:T(8,128)S(1)}, bf16[512,512]{1,0:T(8,128)(2,1)S(1)}, bf16[512,512]{1,0:T(8,128)(2,1)S(1)}, bf16[512,512]{1,0:T(8,128)(2,1)S(1)}) custom-call(f32[512,1024]{1,0:T(8,128)S(1)} %next_panel.3.aug_in), custom_call_target="tpu_custom_call" | custom-call | flops 1073741824 | bytes 25165824 | tf_op jit(solution)/shard_map/last_panel/pallas_call | solution.py:272
  195.1 1.0 copy-done.1
  199.3 25.1 %multiply_tile.1 = f32[4096,2048]{1,0:T(8,128)} custom-call(s32[12]{0:T(128)} %copy-done.7, bf16[4,2,256,128]{3,2,1,0:T(8,128)(2,1)} %bitcast.65, bf16[4,2,256,128]{3,2,1,0:T(8,128)(2,1)} %bitcast.62, bf16[4,2,256,128]{3,2,1,0:T(8,128)(2,1)} %bitcast.59, bf16[4,2,256,128]{3,2,1,0:T(8,128)(2,1)} %bitcast.56, bf16[4,2,256,128]{3,2,1,0:T(8,128)(2,1)} %copy.39.refs_4_, ...), custom_call_target="tpu_custom_call" | custom-call | tf_op jit(solution)/shard_map/multiply_tile/pallas_call | solution.py:363
  (71 shorter events, 12.6 us)
Async XLA Ops:
  0.7 1.0 copy-start.5
  1.8 0.7 copy-start.6
  3.5 58.3 %collective-permute-start.12 = (bf16[272,128]{1,0:T(8,128)(2,1)S(1)}, bf16[272,128]{1,0:T(8,128)(2,1)S(1)}, u32[]{:S(2)}, u32[]{:S(2)}) collective-permute-start(bf16[272,128]{1,0:T(8,128)(2,1)S(1)} %get-tuple-element.20), channel_id=1, source_target_pairs={{0,8},{1,9},{2,10},{3,11},{16,24},{17,25},{18,26},{19,27}} | collective-permute-start | bytes 208904 | tf_op jit(solution)/shard_map/ppermute | solution.py:402
  24.5 104.1 %copy-start.9 = (bf16[8,256,128]{2,1,0:T(8,128)(2,1)}, bf16[8,256,128]{2,1,0:T(8,128)(2,1)S(1)}, u32[]{:S(2)}) copy-start(bf16[8,256,128]{2,1,0:T(8,128)(2,1)S(1)} %all-gather.3) | copy-start | bytes 1572868
  25.4 103.2 %collective-permute-start.3 = (bf16[4,2,256,128]{3,2,0,1:T(8,128)(2,1)}, bf16[4,2,256,128]{3,2,0,1:T(8,128)(2,1)}, u32[]{:S(2)}, u32[]{:S(2)}) collective-permute-start(bf16[4,2,256,128]{3,2,0,1:T(8,128)(2,1)} %copy.34), channel_id=1, source_target_pairs={{0,16},{16,0},{1,17},{17,1},{2,18},{18,2},{3,19},{19,3},{4,20},{20... | collective-permute-start | bytes 1572872 | tf_op jit(solution)/shard_map/ppermute | solution.py:454
  43.0 85.6 %copy-start.10 = (bf16[8,256,128]{2,1,0:T(8,128)(2,1)}, bf16[8,256,128]{2,1,0:T(8,128)(2,1)S(1)}, u32[]{:S(2)}) copy-start(bf16[8,256,128]{2,1,0:T(8,128)(2,1)S(1)} %all-gather.2) | copy-start | bytes 1572868
  43.9 38.2 %copy-start.17 = (s32[8]{0:T(128)S(1)}, s32[8]{0:T(128)}, u32[]{:S(2)}) copy-start(s32[8]{0:T(128)} %constant.131.clone) | copy-start | bytes 100
  43.9 84.7 %collective-permute-start.2 = (bf16[4,2,256,128]{3,2,0,1:T(8,128)(2,1)}, bf16[4,2,256,128]{3,2,0,1:T(8,128)(2,1)}, u32[]{:S(2)}, u32[]{:S(2)}) collective-permute-start(bf16[4,2,256,128]{3,2,0,1:T(8,128)(2,1)} %copy.33), channel_id=1, source_target_pairs={{0,16},{16,0},{1,17},{17,1},{2,18},{18,2},{3,19},{19,3},{4,20},{20... | collective-permute-start | bytes 1572872 | tf_op jit(solution)/shard_map/ppermute | solution.py:454
  59.3 74.7 %copy-start.11 = (bf16[8,256,128]{2,1,0:T(8,128)(2,1)}, bf16[8,256,128]{2,1,0:T(8,128)(2,1)S(1)}, u32[]{:S(2)}) copy-start(bf16[8,256,128]{2,1,0:T(8,128)(2,1)S(1)} %all-gather.1) | copy-start | bytes 1572868
  60.2 73.8 %collective-permute-start.1 = (bf16[4,2,256,128]{3,2,0,1:T(8,128)(2,1)}, bf16[4,2,256,128]{3,2,0,1:T(8,128)(2,1)}, u32[]{:S(2)}, u32[]{:S(2)}) collective-permute-start(bf16[4,2,256,128]{3,2,0,1:T(8,128)(2,1)} %copy.32), channel_id=1, source_target_pairs={{0,16},{16,0},{1,17},{17,1},{2,18},{18,2},{3,19},{19,3},{4,20},{20... | collective-permute-start | bytes 1572872 | tf_op jit(solution)/shard_map/ppermute | solution.py:454
  61.8 21.7 %collective-permute-start.13 = (bf16[272,128]{1,0:T(8,128)(2,1)S(1)}, bf16[272,128]{1,0:T(8,128)(2,1)S(1)}, u32[]{:S(2)}, u32[]{:S(2)}) collective-permute-start(bf16[272,128]{1,0:T(8,128)(2,1)S(1)} %get-tuple-element.28), channel_id=1, source_target_pairs={{0,1},{1,2},{2,3},{3,0},{8,9},{9,10},{10,11},{11,8},{16,17},{17,18... | collective-permute-start | bytes 208904 | tf_op jit(solution)/shard_map/ppermute | solution.py:435
  80.3 53.7 %copy-start.12 = (bf16[8,256,128]{2,1,0:T(8,128)(2,1)}, bf16[8,256,128]{2,1,0:T(8,128)(2,1)S(1)}, u32[]{:S(2)}) copy-start(bf16[8,256,128]{2,1,0:T(8,128)(2,1)S(1)} %all-gather) | copy-start | bytes 1572868
  81.2 52.8 %collective-permute-start = (bf16[4,2,256,128]{3,2,0,1:T(8,128)(2,1)}, bf16[4,2,256,128]{3,2,0,1:T(8,128)(2,1)}, u32[]{:S(2)}, u32[]{:S(2)}) collective-permute-start(bf16[4,2,256,128]{3,2,0,1:T(8,128)(2,1)} %copy.31), channel_id=1, source_target_pairs={{0,16},{16,0},{1,17},{17,1},{2,18},{18,2},{3,19},{19,3},{4,20},{20... | collective-permute-start | bytes 1572872 | tf_op jit(solution)/shard_map/ppermute | solution.py:454
  83.5 7.4 %collective-permute-start.14 = (bf16[272,128]{1,0:T(8,128)(2,1)S(1)}, bf16[272,128]{1,0:T(8,128)(2,1)S(1)}, u32[]{:S(2)}, u32[]{:S(2)}) collective-permute-start(bf16[272,128]{1,0:T(8,128)(2,1)S(1)} %get-tuple-element.28), channel_id=1, source_target_pairs={{0,2},{1,3},{2,0},{3,1},{8,10},{9,11},{10,8},{11,9},{16,18},{17,19... | collective-permute-start | bytes 208904 | tf_op jit(solution)/shard_map/ppermute | solution.py:435
  90.9 6.2 %collective-permute-start.15 = (bf16[272,128]{1,0:T(8,128)(2,1)S(1)}, bf16[272,128]{1,0:T(8,128)(2,1)S(1)}, u32[]{:S(2)}, u32[]{:S(2)}) collective-permute-start(bf16[272,128]{1,0:T(8,128)(2,1)S(1)} %get-tuple-element.28), channel_id=1, source_target_pairs={{0,3},{1,0},{2,1},{3,2},{8,11},{9,8},{10,9},{11,10},{16,19},{17,16... | collective-permute-start | bytes 208904 | tf_op jit(solution)/shard_map/ppermute | solution.py:435
  97.1 6.2 %collective-permute-start.16 = (bf16[272,128]{1,0:T(8,128)(2,1)S(1)}, bf16[272,128]{1,0:T(8,128)(2,1)S(1)}, u32[]{:S(2)}, u32[]{:S(2)}) collective-permute-start(bf16[272,128]{1,0:T(8,128)(2,1)S(1)} %get-tuple-element.28), channel_id=1, source_target_pairs={{0,16},{1,17},{2,18},{3,19},{8,24},{9,25},{10,26},{11,27},{16,0},{... | collective-permute-start | bytes 208904 | tf_op jit(solution)/shard_map/ppermute | solution.py:435
  103.3 8.9 %collective-permute-start.17 = (bf16[272,128]{1,0:T(8,128)(2,1)S(1)}, bf16[272,128]{1,0:T(8,128)(2,1)S(1)}, u32[]{:S(2)}, u32[]{:S(2)}) collective-permute-start(bf16[272,128]{1,0:T(8,128)(2,1)S(1)} %get-tuple-element.28), channel_id=1, source_target_pairs={{0,17},{1,18},{2,19},{3,16},{8,25},{9,26},{10,27},{11,24},{16,1},{... | collective-permute-start | bytes 208904 | tf_op jit(solution)/shard_map/ppermute | solution.py:435
  112.1 8.0 %collective-permute-start.18 = (bf16[272,128]{1,0:T(8,128)(2,1)S(1)}, bf16[272,128]{1,0:T(8,128)(2,1)S(1)}, u32[]{:S(2)}, u32[]{:S(2)}) collective-permute-start(bf16[272,128]{1,0:T(8,128)(2,1)S(1)} %get-tuple-element.28), channel_id=1, source_target_pairs={{0,18},{1,19},{2,16},{3,17},{8,26},{9,27},{10,24},{11,25},{16,2},{... | collective-permute-start | bytes 208904 | tf_op jit(solution)/shard_map/ppermute | solution.py:435
  120.1 7.1 %collective-permute-start.19 = (bf16[272,128]{1,0:T(8,128)(2,1)S(1)}, bf16[272,128]{1,0:T(8,128)(2,1)S(1)}, u32[]{:S(2)}, u32[]{:S(2)}) collective-permute-start(bf16[272,128]{1,0:T(8,128)(2,1)S(1)} %get-tuple-element.28), channel_id=1, source_target_pairs={{0,19},{1,16},{2,17},{3,18},{8,27},{9,24},{10,25},{11,26},{16,3},{... | collective-permute-start | bytes 208904 | tf_op jit(solution)/shard_map/ppermute | solution.py:435
  127.2 38.8 %collective-permute-start.20 = (bf16[8,272,128]{2,1,0:T(8,128)(2,1)S(1)}, bf16[8,272,128]{2,1,0:T(8,128)(2,1)S(1)}, u32[]{:S(2)}, u32[]{:S(2)}) collective-permute-start(bf16[8,272,128]{2,1,0:T(8,128)(2,1)S(1)} %bitcast_dynamic-update-slice_fusion.own_ref), channel_id=1, source_target_pairs={{0,4},{8,12},{1,5},{9,13},{2,6},{10,14},{3,7},{11,15},{16,20},{24,... | collective-permute-start | bytes 1671176 | tf_op jit(solution)/shard_map/ppermute | solution.py:438
  130.0 9.3 %collective-permute-start.6 = (bf16[8,256,128]{2,1,0:T(8,128)(2,1)S(1)}, bf16[8,256,128]{2,1,0:T(8,128)(2,1)S(1)}, u32[]{:S(2)}, u32[]{:S(2)}) collective-permute-start(bf16[8,256,128]{2,1,0:T(8,128)(2,1)S(1)} %pad_maximum_fusion.2), channel_id=1, source_target_pairs={{0,8},{1,9},{6,14},{7,15},{24,16},{25,17},{30,22},{31,23}} | collective-permute-start | bytes 1572872 | tf_op jit(solution)/shard_map/ppermute | solution.py:402
  132.7 12.2 %collective-permute-start.7 = (bf16[8,256,128]{2,1,0:T(8,128)(2,1)S(1)}, bf16[8,256,128]{2,1,0:T(8,128)(2,1)S(1)}, u32[]{:S(2)}, u32[]{:S(2)}) collective-permute-start(bf16[8,256,128]{2,1,0:T(8,128)(2,1)S(1)} %pad_maximum_fusion.3), channel_id=1, source_target_pairs={{0,8},{1,9},{6,14},{7,15},{24,16},{25,17},{30,22},{31,23}} | collective-permute-start | bytes 1572872 | tf_op jit(solution)/shard_map/ppermute | solution.py:402
  135.4 15.1 %collective-permute-start.4 = (bf16[8,256,128]{2,1,0:T(8,128)(2,1)S(1)}, bf16[8,256,128]{2,1,0:T(8,128)(2,1)S(1)}, u32[]{:S(2)}, u32[]{:S(2)}) collective-permute-start(bf16[8,256,128]{2,1,0:T(8,128)(2,1)S(1)} %pad_maximum_fusion), channel_id=1, source_target_pairs={{0,8},{1,9},{6,14},{7,15},{24,16},{25,17},{30,22},{31,23}} | collective-permute-start | bytes 1572872 | tf_op jit(solution)/shard_map/ppermute | solution.py:402
  136.8 19.3 %collective-permute-start.5 = (bf16[8,256,128]{2,1,0:T(8,128)(2,1)S(1)}, bf16[8,256,128]{2,1,0:T(8,128)(2,1)S(1)}, u32[]{:S(2)}, u32[]{:S(2)}) collective-permute-start(bf16[8,256,128]{2,1,0:T(8,128)(2,1)S(1)} %pad_maximum_fusion.1), channel_id=1, source_target_pairs={{0,8},{1,9},{6,14},{7,15},{24,16},{25,17},{30,22},{31,23}} | collective-permute-start | bytes 1572872 | tf_op jit(solution)/shard_map/ppermute | solution.py:402
  139.3 16.9 %copy-start.13 = (bf16[8,256,128]{2,1,0:T(8,128)(2,1)}, bf16[8,256,128]{2,1,0:T(8,128)(2,1)S(1)}, u32[]{:S(2)}) copy-start(bf16[8,256,128]{2,1,0:T(8,128)(2,1)S(1)} %broadcast_select_fusion.1.refs_10_) | copy-start | bytes 1572868
  139.3 59.1 %collective-permute-start.10 = (bf16[8,256,128]{2,1,0:T(8,128)(2,1)S(1)}, bf16[8,256,128]{2,1,0:T(8,128)(2,1)}, u32[]{:S(2)}, u32[]{:S(2)}) collective-permute-start(bf16[8,256,128]{2,1,0:T(8,128)(2,1)S(1)} %broadcast_select_fusion.1.refs_10_), channel_id=1, source_target_pairs={{0,4},{8,12},{1,5},{9,13},{6,2},{14,10},{7,3},{15,11},{24,28},{16,... | collective-permute-start | bytes 1572872 | tf_op jit(solution)/shard_map/ppermute | solution.py:402
  144.9 15.4 %copy-start.14 = (bf16[8,256,128]{2,1,0:T(8,128)(2,1)}, bf16[8,256,128]{2,1,0:T(8,128)(2,1)S(1)}, u32[]{:S(2)}) copy-start(bf16[8,256,128]{2,1,0:T(8,128)(2,1)S(1)} %broadcast_select_fusion.refs_11_) | copy-start | bytes 1572868
  145.0 53.5 %collective-permute-start.11 = (bf16[8,256,128]{2,1,0:T(8,128)(2,1)S(1)}, bf16[8,256,128]{2,1,0:T(8,128)(2,1)}, u32[]{:S(2)}, u32[]{:S(2)}) collective-permute-start(bf16[8,256,128]{2,1,0:T(8,128)(2,1)S(1)} %broadcast_select_fusion.refs_11_), channel_id=1, source_target_pairs={{0,4},{8,12},{1,5},{9,13},{6,2},{14,10},{7,3},{15,11},{24,28},{16,... | collective-permute-start | bytes 1572872 | tf_op jit(solution)/shard_map/ppermute | solution.py:402
  151.4 47.1 %collective-permute-start.8 = (bf16[8,256,128]{2,1,0:T(8,128)(2,1)}, bf16[8,256,128]{2,1,0:T(8,128)(2,1)}, u32[]{:S(2)}, u32[]{:S(2)}) collective-permute-start(bf16[8,256,128]{2,1,0:T(8,128)(2,1)} %broadcast_select_fusion.3.refs_8_), channel_id=1, source_target_pairs={{0,4},{8,12},{1,5},{9,13},{6,2},{14,10},{7,3},{15,11},{24,28},{16,... | collective-permute-start | bytes 1572872 | tf_op jit(solution)/shard_map/ppermute | solution.py:402
  156.2 9.8 %copy-start.15 = (bf16[8,256,128]{2,1,0:T(8,128)(2,1)}, bf16[8,256,128]{2,1,0:T(8,128)(2,1)S(1)}, u32[]{:S(2)}) copy-start(bf16[8,256,128]{2,1,0:T(8,128)(2,1)S(1)} %broadcast_select_fusion.2.refs_9_) | copy-start | bytes 1572868
  156.2 42.2 %collective-permute-start.9 = (bf16[8,256,128]{2,1,0:T(8,128)(2,1)S(1)}, bf16[8,256,128]{2,1,0:T(8,128)(2,1)S(1)}, u32[]{:S(2)}, u32[]{:S(2)}) collective-permute-start(bf16[8,256,128]{2,1,0:T(8,128)(2,1)S(1)} %broadcast_select_fusion.2.refs_9_), channel_id=1, source_target_pairs={{0,4},{8,12},{1,5},{9,13},{6,2},{14,10},{7,3},{15,11},{24,28},{16,... | collective-permute-start | bytes 1572872 | tf_op jit(solution)/shard_map/ppermute | solution.py:402
  158.4 7.6 %copy-start.7 = (s32[12]{0:T(128)}, s32[12]{0:T(128)S(1)}, u32[]{:S(2)}) copy-start(s32[12]{0:T(128)S(1)} %stack.82.place_ref) | copy-start | bytes 148
  158.4 7.6 %copy-start.8 = (f32[64]{0:T(128)S(1)}, f32[64]{0:T(128)}, u32[]{:S(2)}) copy-start(f32[64]{0:T(128)} %taps_ref.1) | copy-start | bytes 772
  174.7 1.1 copy-start
  195.0 1.0 copy-start.1
  196.0 0.8 copy-start.2
  196.8 0.8 copy-start.3
  197.6 0.8 copy-start.4
  198.4 0.8 copy-start.16

commit v3 on v2

v3 whole, which is shorter than its diff:
```python
import functools

import jax
import jax.numpy as jnp
from jax import lax
from jax.experimental import pallas as pl
from jax.experimental.pallas import tpu as pltpu
from jax.sharding import PartitionSpec as P

PANEL = 256
SECTIONS = 2
HEAD = PANEL * SECTIONS
PB = 128
LANES = 128
BLOCK = 128
HALF = 256
SUB = 8
NOTE = 16
EXACT = lax.Precision.HIGHEST
F32 = jnp.float32
BF16 = jnp.bfloat16


def iota(shape, axis):
    return lax.broadcasted_iota(jnp.int32, shape, axis)


def dot(left, right, contract=((1,), (0,)), precision=None):
    return lax.dot_general(
        left, right, (contract, ((), ())), preferred_element_type=F32, precision=precision
    )


NT = ((1,), (1,))
TN = ((0,), (0,))
VMEM = pl.BlockSpec(memory_space=pltpu.VMEM)
SMEM = pl.BlockSpec(memory_space=pltpu.SMEM)
ANY = pl.BlockSpec(memory_space=pl.ANY)
LIMIT = pltpu.CompilerParams(vmem_limit_bytes=48 << 20)


def permute_kernel(place_ref, order_ref, counts_ref, design_ref, *out_refs):
    *part_refs, note_ref = out_refs
    epochs = design_ref.shape[0]
    parts, per_part = len(part_refs), part_refs[0].shape[0]
    lane = iota((PB, PB), 1).astype(F32)
    none = jnp.zeros((epochs, PB), BF16)
    groups = 2 * HALF // PB

    def packed(local, columns, block, part):
        first = block * groups + part
        second = first + HALF // PB
        pick = [jnp.where(local[:, g : g + 1] == lane, 1.0, 0.0) for g in (first, second)]
        pick = jnp.concatenate(pick, axis=1).astype(BF16)
        top = jnp.concatenate([columns(first), none], axis=1)
        low = jnp.concatenate([none, columns(second)], axis=1)
        return dot(pick, jnp.concatenate([top, low], axis=0), NT).astype(BF16)

    def order_of(rows):
        return (order_ref[rows, :] & (PB - 1)).astype(F32).T

    local = order_of(slice(0, per_part * groups))
    for part in range(HALF // PB):
        columns = lambda g: design_ref[:, g * PB : (g + 1) * PB]
        note_ref[0, part * PB : (part + 1) * PB, :] = packed(local, columns, 0, part)
    counts = counts_ref[...].astype(F32)
    counts = jnp.concatenate([counts] * (LANES // epochs), axis=1)
    note_ref[0, HALF:, :] = jnp.broadcast_to(counts, (NOTE, LANES)).astype(BF16)
    for j in range(parts):
        piece = lax.rem(place_ref[PLACE_COL] + j, parts)
        at = pl.multiple_of(piece * per_part * groups, per_part * groups)
        local = order_of(pl.ds(at, per_part * groups))
        columns = lambda g: design_ref[:, pl.ds(pl.multiple_of((at + g) * PB, PB), PB)]
        for block in range(per_part):
            for part in range(HALF // PB):
                part_refs[j][block, part * PB : (part + 1) * PB, :] = packed(
                    local, columns, block, part
                )


def permute_local(place, design, order, tap_count, cols_dev):
    epochs, rows = design.shape
    parts, per_part = rows // cols_dev, cols_dev // (2 * HALF)
    piece = jax.ShapeDtypeStruct((per_part, HALF, LANES), BF16)
    note = jax.ShapeDtypeStruct((1, HALF + NOTE, LANES), BF16)
    return pl.pallas_call(
        permute_kernel,
        out_shape=(piece,) * parts + (note,),
        in_specs=[SMEM] + [VMEM] * 3,
        out_specs=(VMEM,) * (parts + 1),
        compiler_params=LIMIT,
        name="permute_local",
    )(place, order.reshape(rows // PB, PB), tap_count.reshape(1, epochs), design)


PLACE_ROW, PLACE_GROUP, PLACE_EP, PLACE_COL, PLACE_TAKES, PLACE_INSIDE, PLACE_OWNS, PLACE_BACK = range(8)


def assemble_kernel(flag, count, place_ref, *refs):
    first, second = refs[:count], refs[count : 2 * count]
    out_ref, sem = refs[-2:]

    def copy(sources):
        copies = [
            pltpu.make_async_copy(source, out_ref.at[n], sem.at[n]) for n, source in enumerate(sources)
        ]
        for c in copies:
            c.start()
        for c in copies:
            c.wait()

    if flag is None:
        copy(first)
        return

    @pl.when(place_ref[flag] != 0)
    def _():
        copy(first)

    @pl.when(place_ref[flag] == 0)
    def _():
        copy(second)


def assemble(place, first, second, flag, gated=(), after=()):
    count = len(first)
    shards = [*first, *(second if flag is not None else first)]

    def kernel(place_ref, *refs):
        inputs, rest = refs[: 2 * count], refs[2 * count + len(gated) + len(after) :]
        assemble_kernel(flag, count, place_ref, *inputs, rest[0], rest[-1])

    out = pl.pallas_call(
        kernel,
        out_shape=(
            jax.ShapeDtypeStruct((count,) + first[0].shape, BF16),
            *(jax.ShapeDtypeStruct(g.shape, g.dtype) for g in gated),
        ),
        in_specs=[SMEM] + [ANY] * (2 * count + len(gated) + len(after)),
        out_specs=(ANY,) * (1 + len(gated)),
        input_output_aliases={1 + 2 * count + n: 1 + n for n in range(len(gated))},
        scratch_shapes=[pltpu.SemaphoreType.DMA((count,))],
        compiler_params=LIMIT,
        name="assemble",
    )(place, *shards, *gated, *after)
    return out[0], list(out[1:])


def filter_rows(blocks, band_ref, store):
    per = HALF // (LANES // 2)
    for b in range(band_ref.shape[0]):
        first = max(b * per - 1, 0)
        skip = 0 if b else LANES
        packed = jnp.concatenate([blocks(e) for e in range(first, (b + 1) * per)], axis=1)
        for half in range(2):
            got = dot(packed, band_ref[b, half, skip:, :]).astype(BF16)
            store(slice(half * HALF, (half + 1) * HALF), slice(b * HALF, (b + 1) * HALF), got)


def spread(tile, lane):
    return jnp.broadcast_to(tile[:, lane : lane + 1], (SUB, tile.shape[1]))


def row_of(tile, k):
    return jnp.broadcast_to(tile[k : k + 1, :], (SUB, tile.shape[1]))


def factor_block(work):
    halves = work.shape[1] // BLOCK
    groups = BLOCK // SUB
    for g in range(groups):
        rows = slice(g * SUB, (g + 1) * SUB)
        own = [work[rows, h * BLOCK : (h + 1) * BLOCK] for h in range(halves)]
        cols = [spread(own[0], g * SUB + j) for j in range(SUB)]
        a = {(i, j): row_of(cols[j], i) for j in range(SUB) for i in range(j, SUB)}
        u = [[row_of(own[h], k) for k in range(SUB)] for h in range(halves)]
        inv = []
        low = {}
        for k in range(SUB):
            r = lax.rsqrt(a[k, k])
            inv.append(r)
            for i in range(k + 1, SUB):
                low[i, k] = a[i, k] * r
            for j in range(k + 1, SUB):
                for i in range(j, SUB):
                    a[i, j] = a[i, j] - low[i, k] * low[j, k]
            for h in range(halves):
                u[h][k] = u[h][k] * r
                for j in range(k + 1, SUB):
                    u[h][j] = u[h][j] - low[j, k] * u[h][k]
        for h in range(halves):
            merged = u[h][0]
            for k in range(1, SUB):
                merged = jnp.where(iota((SUB, BLOCK), 0) == k, u[h][k], merged)
            work[rows, h * BLOCK : (h + 1) * BLOCK] = merged
        for t in range(g + 1, groups):
            below = slice(t * SUB, (t + 1) * SUB)
            tile = [work[below, h * BLOCK : (h + 1) * BLOCK] for h in range(halves)]
            left = [spread(tile[0], g * SUB + j) for j in range(SUB)]
            for k in range(SUB):
                left[k] = left[k] * inv[k]
                for j in range(k + 1, SUB):
                    left[j] = left[j] - low[j, k] * left[k]
                for h in range(halves):
                    tile[h] = tile[h] - left[k] * u[h][k]
            for h in range(halves):
                work[below, h * BLOCK : (h + 1) * BLOCK] = tile[h]


def start_kernel(
    chain, place_ref, taps_ref, own_ref, came_ref, reg_ref, after, band_ref, aug_ref, notes, a1, work
):
    del after
    epochs = aug_ref.shape[1] - HEAD
    half = LANES // 2

    @pl.when(place_ref[0] % 2 == 0)
    def _():
        for rel in range(own_ref.shape[0]):
            notes[place_ref[chain + rel]] = own_ref[rel]

    @pl.when(place_ref[0] % 2 == 1)
    def _():
        for rel in range(own_ref.shape[0]):
            notes[place_ref[chain + rel]] = came_ref[rel]

    shape = (half, LANES)
    lag = iota(shape, 1) - iota(shape, 0)
    base = lax.fori_loop(
        0,
        taps_ref.shape[0],
        lambda k, kept: jnp.where(lag == k, taps_ref[k], kept),
        jnp.zeros(shape, F32),
    )
    lane = iota(shape, 1)
    swapped = jnp.concatenate([base[:, half:], base[:, :half]], axis=1)
    early = jnp.where(lane < half, swapped, 0.0)
    late = jnp.where(lane >= half, swapped, 0.0)
    none = jnp.zeros(shape, F32)
    patterns = [(early, none), (base, none), (late, early), (none, base), (none, late)]
    row = iota((1, LANES), 1)
    band_ref[...] = jnp.zeros_like(band_ref)
    for b in range(epochs // HALF):
        for side in range(HALF // LANES):
            e = (b * HALF + side * LANES) // half
            counts = [notes[e + n, HALF : HALF + NOTE, :].astype(F32)[:1] for n in range(2)]
            counts = jnp.where(row < half, counts[0], counts[1])
            for j, pattern in enumerate(patterns):
                at = (lag + side * LANES + half - half * j).astype(F32)
                kept = jnp.where(at < counts, pattern[side], 0.0).astype(BF16)
                for h in range(2):
                    rows = slice(j * LANES + h * half, j * LANES + (h + 1) * half)
                    band_ref[b, h, rows, side * LANES : (side + 1) * LANES] = kept

    def store(rows, cols, got):
        a1[rows, cols] = got

    filter_rows(lambda e: notes[e, :HALF, :], band_ref, store)
    columns = a1[...]
    square = (HEAD, HEAD)
    on_diagonal = iota(square, 0) == iota(square, 1)
    aug_ref[:, :HEAD] = dot(columns, columns, NT) + jnp.where(on_diagonal, reg_ref[...], 0.0)
    aug_ref[:, HEAD:] = columns.astype(F32)
    eliminate(aug_ref, 0, work)


def eliminate(aug, kb, work):
    here = slice(kb * BLOCK, (kb + 1) * BLOCK)
    work[:, :BLOCK] = aug[here, here]
    work[:, BLOCK:] = jnp.where(iota((BLOCK, BLOCK), 0) == iota((BLOCK, BLOCK), 1), 1.0, 0.0)
    factor_block(work)
    rest = slice(kb * BLOCK, aug.shape[1])
    aug[here, rest] = dot(work[:, BLOCK:], aug[here, rest], precision=EXACT)
    for rb in range(kb + 1, HEAD // BLOCK):
        below = slice(rb * BLOCK, (rb + 1) * BLOCK)
        rest = slice(rb * BLOCK, aug.shape[1])
        aug[below, rest] -= dot(aug[here, below], aug[here, rest], TN, precision=EXACT)


def next_kernel(kb, aug_in, after, aug_ref, work):
    del after
    aug_ref[...] = aug_in[...]
    eliminate(aug_ref, kb, work)


def last_kernel(kb, aug_in, after, factor_ref, w_ref, high_ref, low_ref, aug, work):
    del after
    aug[...] = aug_in[...]
    eliminate(aug, kb, work)
    square = (HEAD, HEAD)
    epochs = aug.shape[1] - HEAD
    factor_ref[...] = jnp.where(iota(square, 0) >= iota(square, 1), aug[:, :HEAD].T, 0.0)
    wt = aug[:, HEAD:]
    w_ref[...] = wt.T.astype(BF16)
    for b in range(epochs // BLOCK):
        here = slice(b * BLOCK, (b + 1) * BLOCK)
        shape = (BLOCK, epochs)
        unit = jnp.where(iota(shape, 0) + b * BLOCK == iota(shape, 1), 1.0, 0.0)
        middle = unit - dot(wt[:, here], wt, TN, precision=EXACT)
        high = middle.astype(BF16)
        high_ref[here, :] = high
        low_ref[here, :] = (middle - high.astype(F32)).astype(BF16)


def start_panel(place, chain, taps, own, came, regular, after):
    epochs = own.shape[0] * (LANES // 2)
    per = HALF // (LANES // 2)
    return pl.pallas_call(
        functools.partial(start_kernel, chain),
        out_shape=(
            jax.ShapeDtypeStruct((epochs // HALF, 2, (per + 1) * LANES, HALF), BF16),
            jax.ShapeDtypeStruct((HEAD, HEAD + epochs), F32),
        ),
        in_specs=[SMEM, SMEM, VMEM, VMEM, VMEM, ANY],
        out_specs=(VMEM, VMEM),
        scratch_shapes=[
            pltpu.VMEM(own.shape, BF16),
            pltpu.VMEM((HEAD, epochs), BF16),
            pltpu.VMEM((BLOCK, 2 * BLOCK), F32),
        ],
        compiler_params=LIMIT,
        cost_estimate=pl.CostEstimate(flops=7 << 30, bytes_accessed=24 << 20, transcendentals=0),
        name="start_panel",
    )(place, taps, own, came, regular[:HEAD].reshape(1, HEAD), after)


def next_panel(kb, aug, after):
    return pl.pallas_call(
        functools.partial(next_kernel, kb),
        out_shape=jax.ShapeDtypeStruct(aug.shape, F32),
        in_specs=[VMEM, ANY],
        out_specs=VMEM,
        scratch_shapes=[pltpu.VMEM((BLOCK, 2 * BLOCK), F32)],
        compiler_params=LIMIT,
        cost_estimate=pl.CostEstimate(flops=7 << 30, bytes_accessed=20 << 20, transcendentals=0),
        name="next_panel",
    )(aug, after)


def last_panel(kb, aug, after):
    epochs = aug.shape[1] - HEAD
    return pl.pallas_call(
        functools.partial(last_kernel, kb),
        out_shape=(
            jax.ShapeDtypeStruct((HEAD, HEAD), F32),
            jax.ShapeDtypeStruct((epochs, HEAD), BF16),
            jax.ShapeDtypeStruct((epochs, epochs), BF16),
            jax.ShapeDtypeStruct((epochs, epochs), BF16),
        ),
        in_specs=[VMEM, ANY],
        out_specs=(VMEM,) * 4,
        scratch_shapes=[pltpu.VMEM(aug.shape, F32), pltpu.VMEM((BLOCK, 2 * BLOCK), F32)],
        compiler_params=LIMIT,
        cost_estimate=pl.CostEstimate(flops=7 << 30, bytes_accessed=24 << 20, transcendentals=0),
        name="last_panel",
    )(aug, after)


def unpack(place_ref, own, other, blocks):
    width = own.shape[0]
    here = place_ref[PLACE_EP] * width
    there = width - here
    for n in range(width):
        back = place_ref[PLACE_BACK + n]
        blocks[here + back] = own[n, 0]
        blocks[there + back] = other[n, 0]


def choose(condition, yes, no):
    pl.when(condition)(yes)
    pl.when(jnp.logical_not(condition))(no)


def project_kernel(
    place_ref, own_ref, own_came, other_ref, other_came, band_ref, w_ref, high_ref, low_ref, after,
    out_ref, blocks, filtered,
):
    del after

    def store(rows, cols, got):
        filtered[rows, cols] = got

    choose(
        place_ref[PLACE_TAKES] != 0,
        lambda: unpack(place_ref, own_came, other_came, blocks),
        lambda: unpack(place_ref, own_ref, other_ref, blocks),
    )
    filter_rows(lambda e: blocks[e], band_ref, store)
    columns = filtered[...]
    projected = dot(high_ref[...], columns, NT) + dot(low_ref[...], columns, NT)
    out_ref[...] = projected.astype(BF16)

    @pl.when((place_ref[PLACE_GROUP] == 0) & (pl.program_id(0) == 0))
    def _():
        out_ref[...] = w_ref[...]


def fixed(array):
    return pl.BlockSpec(
        array.shape, lambda i, place: (0,) * array.ndim, pipeline_mode=pl.Buffered(1)
    )


def shards_spec(array):
    return pl.BlockSpec((array.shape[0], 1, HALF, LANES), lambda i, place: (0, i, 0, 0))


def project(place, shards, band, w, high, low, after):
    width, count = shards[0].shape[:2]
    epochs = high.shape[0]
    return pl.pallas_call(
        project_kernel,
        out_shape=jax.ShapeDtypeStruct((epochs, count * 2 * HALF), BF16),
        grid_spec=pltpu.PrefetchScalarGridSpec(
            num_scalar_prefetch=1,
            grid=(count,),
            in_specs=[shards_spec(array) for array in shards]
            + [fixed(array) for array in (band, w, high, low)]
            + [ANY],
            out_specs=pl.BlockSpec((epochs, 2 * HALF), lambda i, place: (0, i)),
            scratch_shapes=[
                pltpu.VMEM((epochs // (LANES // 2), HALF, LANES), BF16),
                pltpu.VMEM((2 * HALF, epochs), BF16),
            ],
        ),
        compiler_params=LIMIT,
        name="project",
    )(place, *shards, band, w, high, low, after)


def tile_kernel(
    part, parts, aliased, place_ref, own_ref, other_ref, theirs_ref, band_ref, right_ref, factor_ref,
    reg_ref, *refs,
):
    out_ref, blocks, filtered, made, sems = refs[aliased:]
    step, steps = pl.program_id(0), pl.num_programs(0)
    epochs, cols = right_ref.shape
    rows = 2 * HALF
    piece = lax.rem(place_ref[PLACE_COL] + part, parts)
    block = piece * steps + step
    first_row = (place_ref[PLACE_ROW] * parts * steps + block) * rows
    first_col = place_ref[PLACE_GROUP] * cols
    wide = rows
    count = cols // wide
    slot = lax.rem(step, 2)

    def copies(at_step, n):
        at_slot = lax.rem(at_step, 2)
        start = pl.multiple_of((piece * steps + at_step) * rows, rows)
        across = slice(n * wide, (n + 1) * wide)
        return pltpu.make_async_copy(
            made.at[at_slot, n], out_ref.at[pl.ds(start, rows), across], sems.at[at_slot, n]
        )

    def store(at_rows, at_cols, got):
        filtered[at_rows, at_cols] = got

    choose(
        (place_ref[PLACE_OWNS] != 0) & (part == 0),
        lambda: unpack(place_ref, own_ref, theirs_ref, blocks),
        lambda: unpack(place_ref, own_ref, other_ref, blocks),
    )
    filter_rows(lambda e: blocks[e], band_ref, store)
    for n in range(count):

        @pl.when(step >= 2)
        def _():
            copies(step - 2, n).wait()

        @pl.when(first_row >= HEAD)
        def _():
            made[slot, n] = dot(filtered[...], right_ref[:, n * wide : (n + 1) * wide])

            @pl.when(first_row == first_col + n * wide)
            def _():
                on_diagonal = iota((rows, rows), 0) == iota((rows, rows), 1)
                made[slot, n] += jnp.where(on_diagonal, reg_ref[...], 0.0)

        @pl.when(first_row < HEAD)
        def _():
            made[slot, n] = jnp.zeros((rows, wide), F32)
            if n == 0:

                @pl.when(first_col == 0)
                def _():
                    made[slot, n] = factor_ref[...]

        copies(step, n).start()

    @pl.when(step == steps - 1)
    def _():
        for n in range(count):

            @pl.when(steps > 1)
            def _():
                copies(step - 1, n).wait()

            copies(step, n).wait()


def multiply_part(part, parts, place, own, other, theirs, band, right, factor, regular, out):
    width, steps = own.shape[:2]
    rows = 2 * HALF
    epochs, cols = right.shape

    def reg_block(i, place):
        piece = lax.rem(place[PLACE_COL] + part, parts)
        return 0, (place[PLACE_ROW] * parts + piece) * steps + i

    aliased = 0 if out is None else 1
    return pl.pallas_call(
        functools.partial(tile_kernel, part, parts, aliased),
        out_shape=jax.ShapeDtypeStruct((parts * steps * rows, cols), F32),
        grid_spec=pltpu.PrefetchScalarGridSpec(
            num_scalar_prefetch=1,
            grid=(steps,),
            in_specs=[shards_spec(array) for array in (own, other, theirs)]
            + [fixed(array) for array in (band, right, factor)]
            + [pl.BlockSpec((1, rows), reg_block)]
            + [ANY] * aliased,
            out_specs=ANY,
            scratch_shapes=[
                pltpu.VMEM((epochs // (LANES // 2), HALF, LANES), BF16),
                pltpu.VMEM((rows, epochs), BF16),
                pltpu.VMEM((2, cols // rows, rows, rows), F32),
                pltpu.SemaphoreType.DMA((2, cols // rows)),
            ],
        ),
        input_output_aliases={8: 0} if aliased else {},
        compiler_params=pltpu.CompilerParams(vmem_limit_bytes=56 << 20),
        cost_estimate=pl.CostEstimate(
            flops=10 << 30, bytes_accessed=steps * rows * cols * 4, transcendentals=0
        ),
        name="multiply_part",
    )(
        place, own, other, theirs, band, right, factor, regular.reshape(1, -1),
        *([out] if aliased else []),
    )


AXES = ("ep", "row", "col")


def sizes():
    return tuple(lax.axis_size(axis) for axis in AXES)


def flat(ep, row, col):
    _, rows, cols = sizes()
    return (ep * rows + row) * cols + col


def doubling(count, least):
    distances = []
    distance = count // 2
    while distance >= least:
        distances.append(distance)
        distance //= 2
    return distances


def spread_step(block, owner_of, distance):
    eps, rows, cols = sizes()
    route = []
    for e in range(eps):
        for c in range(cols):
            for other in range(0, rows, 2 * distance):
                source = owner_of(e, c) ^ other
                route.append((flat(e, source, c), flat(e, source ^ distance, c)))
    return lax.ppermute(block, AXES, route)


def gather_panel(note):
    eps, rows, cols = sizes()
    row = lax.axis_index("row")
    for distance in doubling(rows, 2):
        came = spread_step(note, lambda e, c: 0, distance)
        note = jnp.where((row & (2 * distance - 1)) == distance, came, note)
    steps = [(0, 0)]
    hops = [(d, 0) for d in doubling(eps, 1)] + [(0, d) for d in reversed(doubling(cols, 1))]
    for de, dc in hops:
        route = [
            (flat(e, r, c), flat(e ^ de, r, c ^ dc))
            for e in range(eps)
            for r in range(0, rows, 2)
            for c in range(cols)
        ]
        note = jnp.concatenate([note, lax.ppermute(note, AXES, route)])
        steps += [(e ^ de, c ^ dc) for e, c in steps]
    came = lax.ppermute(note, "row", [(r, r + 1) for r in range(0, rows, 2)])
    ep, col = lax.axis_index("ep"), lax.axis_index("col")
    return note, came, [(ep ^ de) * cols + (col ^ dc) for de, dc in steps]


def on_device(design, taps, tap_count, order, regular):
    rows_dev = design.shape[1]
    eps, rows, cols = sizes()
    cols_dev = regular.shape[0] // (eps * cols)
    parts = rows_dev // cols_dev
    row, ep, col = (lax.axis_index(axis) for axis in ("row", "ep", "col"))
    group = lax.axis_index(("ep", "col"))
    everywhere = [(e, r, c) for e in range(eps) for r in range(rows) for c in range(cols)]
    owner = lambda e, c: (e * cols + c) * cols_dev // rows_dev
    home = lambda r: r * parts // cols
    inside = lambda r, c: c // parts == (r * parts % cols) // parts
    first_owner = group * cols_dev // rows_dev
    takes = ((row ^ first_owner) & 1) == 1
    is_inside = inside(row, col)
    owns = is_inside & (home(row) == ep)
    back = [(col - n) % cols for n in range(cols)]
    place = [row, group, ep, col, takes, is_inside, owns, *back]
    chain = len(place)
    steps = [(0, 0)]
    for de, dc in [(d, 0) for d in doubling(eps, 1)] + [(0, d) for d in reversed(doubling(cols, 1))]:
        steps += [(e ^ de, c ^ dc) for e, c in steps]
    place += [(ep ^ de) * cols + (col ^ dc) for de, dc in steps]
    place = jnp.stack([jnp.asarray(p, jnp.int32) for p in place])

    *local, note = permute_local(place, design, order, tap_count, cols_dev)
    notes, came, _ = gather_panel(note)

    def shift(block, n, wanted):
        route = [
            (flat(e, r, (c - n) % cols), flat(e, r, c)) for e, r, c in everywhere if wanted(r, c)
        ]
        return lax.ppermute(block, AXES, route)

    def across(block, wanted):
        route = [(flat(1 - e, r, c), flat(e, r, c)) for e, r, c in everywhere if wanted(e, r, c)]
        return lax.ppermute(block, AXES, route)

    def spread(block):
        distances = doubling(rows, 1)
        for distance in distances[:-1]:
            got = spread_step(block, owner, distance)
            hit = ((row ^ first_owner) & (2 * distance - 1)) == distance
            block = jnp.where(hit, got, block)
        return block, spread_step(block, owner, distances[-1])

    early = [shift(local[n % parts], n, inside) for n in range(1, cols)]
    mine_right, local = assemble(place, [local[0], *early], None, None, local)
    theirs_right = across(mine_right, lambda e, r, c: inside(r, c) and home(r) == e)
    own_block, own_came = spread(mine_right)
    other_block, other_came = spread(theirs_right)
    late = [shift(local[n % parts], n, lambda r, c: not inside(r, c)) for n in range(1, cols)]

    band, aug = start_panel(place, chain, taps, notes, came, regular, mine_right)
    first, local = assemble(
        place, [local[0], *early], [local[0], *late], PLACE_INSIDE, local, [aug]
    )
    mine = [first]
    others = [across(first, lambda e, r, c: not (inside(r, c) and home(r) == e))]
    late = [
        [shift(local[(n + j) % parts], n, lambda r, c: True) for n in range(1, cols)]
        for j in range(1, parts)
    ]
    panels = HEAD // BLOCK
    for kb in range(1, panels - 1):
        aug = next_panel(kb, aug, first if kb == 1 else other_block)
    factor, w, high, low = last_panel(panels - 1, aug, other_block)
    for j in range(1, parts):
        got, _ = assemble(place, [local[j], *late[j - 1]], None, None, (), [factor])
        mine.append(got)
        others.append(across(got, lambda e, r, c: True))
    shards = (own_block, own_came, other_block, other_came)
    right = project(place, shards, band, w, high, low, mine[-1])
    out = None
    for j in range(parts):
        out = multiply_part(
            j, parts, place, mine[j], others[j], theirs_right, band, right, factor, regular, out
        )
    return out


def solution(mesh):
    in_specs = (P(("ep", "col"), "row"), P(), P(("ep", "col")), P("row"), P())
    out_specs = P("row", ("ep", "col"))
    return jax.shard_map(
        on_device, mesh=mesh, in_specs=in_specs, out_specs=out_specs, check_vma=False
    )
```

time: 226 us -> 145 us (0.64)
  blocking collectives: 62.2 us -> 0 us
  waiting for transfers between devices: 35.4 us -> 23.5 us
  Pallas kernels: 54 us -> 65.3 us
  local copies, waits for them, and re-layouts: 20.5 us -> 9.45 us
  starting transfers between devices: 47.2 us -> 44.2 us
  other arithmetic: 3.93 us -> 1.57 us
    all_gather x4 -> x0, blocking collectives: 62.2 us -> none  [on_device(): column = [lax.all_gather(chunk, 'col', axis=0) for chunk in chunks]]
    ppermute x21, waiting for transfers between devices: 35.4 us -> 23.5 us  [the longest x3 13.1 us: gather_panel(): note = jnp.concatenate([note, lax.ppermute(note, AXES, route)])]
    pallas_call x3 -> x8, Pallas kernels: 34.7 us -> 46.2 us  [the longest x2 26.1 us: multiply_part(): pl.pallas_call(functools.partial(tile_kernel, part, parts, aliased), out_...]
    ppermute x4 -> x0, local copies, waits for them, and re-layouts: 7.59 us -> none  [on_device(): other = [lax.ppermute(chunk, 'ep', [(0, 1), (1, 0)]) for chunk in column]]
    all_gather x4 -> x0, local copies, waits for them, and re-layouts: 3.6 us -> none  [on_device(): column = [lax.all_gather(chunk, 'col', axis=0) for chunk in chunks]]
    ppermute x21, starting transfers between devices: 47.2 us -> 44.2 us  [the longest x5 14.4 us: spread_step(): return lax.ppermute(block, AXES, route)]
    unnamed x42 -> x28, local copies, waits for them, and re-layouts: 7.14 us -> 8.67 us
  transfers between devices with their start and end apart: 21 -> 21, of which waited for: 10 -> 5; matrix products, arithmetic and copies ran while one was open for 7% -> 2% of each run, Pallas kernels for 12% -> 35%
where the time goes in v3:
time: 145 us
  Pallas kernels  65.3 us (45%)
  starting transfers between devices  44.2 us (30%)
  waiting for transfers between devices  23.5 us (16%)
  local copies, waits for them, and re-layouts  9.45 us (7%)
  other arithmetic  1.57 us (1%)
    pallas_call x2, Pallas kernels, multiply_part(): pl.pallas_call(functools.partial(tile_kernel, part, parts, aliased), out_...  26.1 us
    ppermute x5, starting transfers between devices, spread_step(): return lax.ppermute(block, AXES, route)  14.4 us
    ppermute x9, starting transfers between devices, shift(): return lax.ppermute(block, AXES, route)  14.2 us
    ppermute x3, waiting for transfers between devices, gather_panel(): note = jnp.concatenate([note, lax.ppermute(note, AXES, route)])  13.1 us
    pallas_call x2, Pallas kernels, next_panel(): pl.pallas_call(functools.partial(next_kernel, kb), out_shape=jax.ShapeDty...  11.9 us
    ppermute x3, starting transfers between devices, gather_panel(): note = jnp.concatenate([note, lax.ppermute(note, AXES, route)])  9.85 us
    pallas_call x1, Pallas kernels, start_panel(): pl.pallas_call(functools.partial(start_kernel, chain), out_shape=(jax.Sha...  8.99 us
    unnamed x28, local copies, waits for them, and re-layouts  8.67 us
  transfers between devices with their start and end apart: 21, of which 5 were waited for; matrix products, arithmetic and copies ran while one was open for 2% of the time, Pallas kernels for 35%

profile of v3, /device:TPU:0, one launch (start us, length us, event | category | flops | bytes accessed | tf_op | source)
XLA Modules:
  0.0 144.6 jit_solution(2150671798543075692)
XLA Ops:
  0.0 0.1 stack.88.place_ref
  0.1 1.0 copy-done.4
  1.2 0.7 copy-done.6
  1.9 0.7 copy-done.7
  2.5 1.6 %permute_local.1 = (bf16[4,256,128]{2,1,0:T(8,128)(2,1)S(1)}, bf16[4,256,128]{2,1,0:T(8,128)(2,1)S(1)}, bf16[1,272,128]{2,1,0:T(8,128)(2,1)S(1)}) custom-call(s32[19]{0:T(128)S(1)} %stack.88.place_ref, s32[32,128]{1,0:T(8,128)S(1)} %bitcast.22, s32[1,64]{1,0:T(1,128)S(1)} %bitcast.24, bf16[64,4096]{1,0:T(8,128)(2,1)S(1)} %copy-done.4), custom_call_target="tpu_custom_call" | custom-call | tf_op jit(solution)/shard_map/permute_local/pallas_call | solution.py:86
  4.1 4.9 %collective-permute-start.6 = (bf16[1,272,128]{2,1,0:T(8,128)(2,1)S(1)}, bf16[1,272,128]{2,1,0:T(8,128)(2,1)S(1)}, u32[]{:S(2)}, u32[]{:S(2)}) collective-permute-start(bf16[1,272,128]{2,1,0:T(8,128)(2,1)S(1)} %get-tuple-element.24), channel_id=1, source_target_pairs={{0,8},{1,9},{2,10},{3,11},{16,24},{17,25},{18,26},{19,27}} | collective-permute-start | bytes 208904 | tf_op jit(solution)/shard_map/ppermute | solution.py:570
  9.0 1.9 %collective-permute-done.6 = bf16[1,272,128]{2,1,0:T(8,128)(2,1)S(1)} collective-permute-done((bf16[1,272,128]{2,1,0:T(8,128)(2,1)S(1)}, bf16[1,272,128]{2,1,0:T(8,128)(2,1)S(1)}, u32[]{:S(2)}, u32[]{:S(2)}) %collective-permute-start.6) | collective-permute-done | bytes 69664 | tf_op jit(solution)/shard_map/ppermute | solution.py:570
  10.9 3.4 %collective-permute-start.7 = (bf16[1,272,128]{2,1,0:T(8,128)(2,1)S(1)}, bf16[1,272,128]{2,1,0:T(8,128)(2,1)S(1)}, u32[]{:S(2)}, u32[]{:S(2)}) collective-permute-start(bf16[1,272,128]{2,1,0:T(8,128)(2,1)S(1)} %broadcast_select_fusion.2), channel_id=1, source_target_pairs={{0,16},{1,17},{2,18},{3,19},{8,24},{9,25},{10,26},{11,27},{16,0},{... | collective-permute-start | bytes 208904 | tf_op jit(solution)/shard_map/ppermute | solution.py:588
  14.4 1.3 collective-permute-start.1
  15.7 1.3 collective-permute-start.2
  17.0 4.6 %collective-permute-start = (bf16[4,256,128]{2,1,0:T(8,128)(2,1)S(1)}, bf16[4,256,128]{2,1,0:T(8,128)(2,1)S(1)}, u32[]{:S(2)}, u32[]{:S(2)}) collective-permute-start(bf16[4,256,128]{2,1,0:T(8,128)(2,1)S(1)} %get-tuple-element.21.refs_9_), channel_id=1, source_target_pairs={{3,0},{0,1},{5,6},{6,7},{11,8},{8,9},{13,14},{14,15},{19,16},{16,1... | collective-permute-start | bytes 786440 | tf_op jit(solution)/shard_map/ppermute | solution.py:626
  21.5 1.9 %collective-permute-start.8 = (bf16[2,272,128]{2,1,0:T(8,128)(2,1)S(1)}, bf16[2,272,128]{2,1,0:T(8,128)(2,1)S(1)}, u32[]{:S(2)}, u32[]{:S(2)}) collective-permute-start(bf16[2,272,128]{2,1,0:T(8,128)(2,1)S(1)} %pad_maximum_fusion.2), channel_id=1, source_target_pairs={{0,1},{1,0},{2,3},{3,2},{8,9},{9,8},{10,11},{11,10},{16,17},{17,16... | collective-permute-start | bytes 417800 | tf_op jit(solution)/shard_map/ppermute | solution.py:588
  23.5 5.7 %collective-permute-done.1.refs_2_.refs_6_ = bf16[4,256,128]{2,1,0:T(8,128)(2,1)S(1)} collective-permute-done((bf16[4,256,128]{2,1,0:T(8,128)(2,1)S(1)}, bf16[4,256,128]{2,1,0:T(8,128)(2,1)S(1)}, u32[]{:S(2)}, u32[]{:S(2)}) %collective-permute-start.1) | collective-permute-done | bytes 262176 | tf_op jit(solution)/shard_map/ppermute | solution.py:626
  29.2 0.7 assemble.3
  29.9 1.3 collective-permute-start.14
  31.3 4.5 %collective-permute-start.9 = (bf16[4,272,128]{2,1,0:T(8,128)(2,1)S(1)}, bf16[4,272,128]{2,1,0:T(8,128)(2,1)S(1)}, u32[]{:S(2)}, u32[]{:S(2)}) collective-permute-start(bf16[4,272,128]{2,1,0:T(8,128)(2,1)S(1)} %pad_maximum_fusion.1), channel_id=1, source_target_pairs={{0,2},{1,3},{2,0},{3,1},{8,10},{9,11},{10,8},{11,9},{16,18},{17,19... | collective-permute-start | bytes 835592 | tf_op jit(solution)/shard_map/ppermute | solution.py:588
  35.8 13.1 %collective-permute-done.9 = bf16[4,272,128]{2,1,0:T(8,128)(2,1)S(1)} collective-permute-done((bf16[4,272,128]{2,1,0:T(8,128)(2,1)S(1)}, bf16[4,272,128]{2,1,0:T(8,128)(2,1)S(1)}, u32[]{:S(2)}, u32[]{:S(2)}) %collective-permute-start.9) | collective-permute-done | bytes 278560 | tf_op jit(solution)/shard_map/ppermute | solution.py:588
  49.0 2.1 %collective-permute-start.10 = (bf16[8,272,128]{2,1,0:T(8,128)(2,1)S(1)}, bf16[8,272,128]{2,1,0:T(8,128)(2,1)}, u32[]{:S(2)}, u32[]{:S(2)}) collective-permute-start(bf16[8,272,128]{2,1,0:T(8,128)(2,1)S(1)} %pad_maximum_fusion.own_ref), channel_id=1, source_target_pairs={{0,4},{8,12},{1,5},{9,13},{2,6},{10,14},{3,7},{11,15},{16,20},{24,... | collective-permute-start | bytes 1671176 | tf_op jit(solution)/shard_map/ppermute | solution.py:590
  51.1 0.7 slice.3
  51.8 1.5 %collective-permute-start.4 = (bf16[4,256,128]{2,1,0:T(8,128)(2,1)S(1)}, bf16[4,256,128]{2,1,0:T(8,128)(2,1)S(1)}, u32[]{:S(2)}, u32[]{:S(2)}) collective-permute-start(bf16[4,256,128]{2,1,0:T(8,128)(2,1)S(1)} %get-tuple-element.22.refs_0_.refs_4_), channel_id=1, source_target_pairs={{0,2},{1,3},{6,4},{7,5},{8,10},{9,11},{14,12},{15,13},{16,18},{17,... | collective-permute-start | bytes 786440 | tf_op jit(solution)/shard_map/ppermute | solution.py:626
  53.3 1.3 collective-permute-start.5
  54.6 0.7 collective-permute-start.3
  55.3 5.4 %collective-permute-start.17 = (bf16[4,4,256,128]{3,2,1,0:T(8,128)(2,1)S(1)}, bf16[4,4,256,128]{3,2,1,0:T(8,128)(2,1)S(1)}, u32[]{:S(2)}, u32[]{:S(2)}) collective-permute-start(bf16[4,4,256,128]{3,2,1,0:T(8,128)(2,1)S(1)} %get-tuple-element.25.after), channel_id=1, source_target_pairs={{0,8},{1,9},{6,14},{7,15},{24,16},{25,17},{30,22},{31,23}} | collective-permute-start | bytes 3145736 | tf_op jit(solution)/shard_map/ppermute | solution.py:570
  60.7 1.4 collective-permute-start.15
  62.1 9.0 %start_panel.1 = (bf16[2,2,640,256]{3,2,1,0:T(8,128)(2,1)S(1)}, f32[512,1024]{1,0:T(8,128)S(1)}) custom-call(s32[19]{0:T(128)S(1)} %stack.88.place_ref, f32[64]{0:T(128)S(1)} %copy-done.8, bf16[8,272,128]{2,1,0:T(8,128)(2,1)S(1)} %pad_maximum_fusion.own_ref, bf16[8,272,128]{2,1,0:T(8,128)(2,1)} %collective-permute-done.10.came_ref, f32[1,512]{1,0:T(1,128)S(1)} %bitcast.23, ...), custom_call_target="tpu_custom_call" | custom-call | flops 7516192768 | bytes 25165824 | tf_op jit(solution)/shard_map/start_panel/pallas_call | solution.py:308
  71.1 1.0 copy-done
  72.2 0.7 assemble.4
  72.9 3.5 %collective-permute-start.13 = (bf16[4,256,128]{2,1,0:T(8,128)(2,1)S(1)}, bf16[4,256,128]{2,1,0:T(8,128)(2,1)S(1)}, u32[]{:S(2)}, u32[]{:S(2)}) collective-permute-start(bf16[4,256,128]{2,1,0:T(8,128)(2,1)S(1)} %get-tuple-element.28), channel_id=1, source_target_pairs={{1,0},{2,1},{3,2},{0,3},{5,4},{6,5},{7,6},{4,7},{9,8},{10,9},{11,1... | collective-permute-start | bytes 786440 | tf_op jit(solution)/shard_map/ppermute | solution.py:626
  76.4 1.5 %collective-permute-start.20 = (bf16[4,4,256,128]{3,2,1,0:T(8,128)(2,1)S(1)}, bf16[4,4,256,128]{3,2,1,0:T(8,128)(2,1)S(1)}, u32[]{:S(2)}, u32[]{:S(2)}) collective-permute-start(bf16[4,4,256,128]{3,2,1,0:T(8,128)(2,1)S(1)} %get-tuple-element.29.after.own_ref), channel_id=1, source_target_pairs={{18,2},{19,3},{20,4},{21,5},{24,8},{25,9},{26,10},{27,11},{28,12},... | collective-permute-start | bytes 3145736 | tf_op jit(solution)/shard_map/ppermute | solution.py:630
  78.0 6.1 %next_panel.2.aug_in = f32[512,1024]{1,0:T(8,128)S(1)} custom-call(f32[512,1024]{1,0:T(8,128)S(1)} %get-tuple-element.26.refs_10_.aug_in, bf16[4,4,256,128]{3,2,1,0:T(8,128)(2,1)S(1)} %get-tuple-element.29.after.own_ref), custom_call_target="tpu_custom_call" | custom-call | flops 7516192768 | bytes 20971520 | tf_op jit(solution)/shard_map/next_panel/pallas_call | solution.py:328
  84.1 0.1 broadcast_select_fusion.own_ref
  84.2 1.4 collective-permute-start.18
  85.6 1.3 broadcast_select_fusion.1.after.other_ref
  87.0 1.4 collective-permute-start.19
  88.3 5.7 %next_panel.3.aug_in = f32[512,1024]{1,0:T(8,128)S(1)} custom-call(f32[512,1024]{1,0:T(8,128)S(1)} %next_panel.2.aug_in, bf16[4,4,256,128]{3,2,1,0:T(8,128)(2,1)S(1)} %broadcast_select_fusion.1.after.other_ref), custom_call_target="tpu_custom_call" | custom-call | flops 7516192768 | bytes 20971520 | tf_op jit(solution)/shard_map/next_panel/pallas_call | solution.py:328
  94.1 1.3 copy-done.9
  95.4 1.6 %copy-done.10 = f32[512,1024]{1,0:T(8,128)S(1)} copy-done((f32[512,1024]{1,0:T(8,128)S(1)}, f32[512,1024]{1,0:T(8,128)}, u32[]{:S(2)}) %copy-start.10) | copy-done | bytes 2097176
  97.0 7.3 %last_panel.1 = (f32[512,512]{1,0:T(8,128)S(1)}, bf16[512,512]{1,0:T(8,128)(2,1)S(1)}, bf16[512,512]{1,0:T(8,128)(2,1)S(1)}, bf16[512,512]{1,0:T(8,128)(2,1)S(1)}) custom-call(f32[512,1024]{1,0:T(8,128)S(1)} %copy-done.10, bf16[4,4,256,128]{3,2,1,0:T(8,128)(2,1)S(1)} %broadcast_select_fusion.1.after.other_ref), custom_call_target="tpu_custom_call" | custom-call | flops 7516192768 | bytes 25165824 | tf_op jit(solution)/shard_map/last_panel/pallas_call | solution.py:342
  104.3 0.1 collective-permute-done.11.refs_1_.refs_5_
  104.4 0.7 assemble.5.after.own_ref
  105.1 0.2 copy-done.1
  105.3 0.9 collective-permute-start.16
  106.3 7.5 %project.1.right_ref = bf16[512,2048]{1,0:T(8,128)(2,1)} custom-call(s32[19]{0:T(128)S(1)} %stack.88.place_ref, bf16[4,4,256,128]{3,2,1,0:T(8,128)(2,1)S(1)} %broadcast_select_fusion.own_ref, bf16[4,4,256,128]{3,2,1,0:T(8,128)(2,1)S(1)} %collective-permute-done.18.own_came, bf16[4,4,256,128]{3,2,1,0:T(8,128)(2,1)S(1)} %broadcast_select_fusion.1.after.other_ref, ...), custom_call_target="tpu_custom_call" | custom-call | tf_op jit(solution)/shard_map/project/pallas_call | solution.py:411
  113.7 1.0 copy-done.12
  114.8 12.5 %multiply_part.2.refs_0_ = f32[4096,2048]{1,0:T(8,128)} custom-call(s32[19]{0:T(128)} %copy-done.5, bf16[4,4,256,128]{3,2,1,0:T(8,128)(2,1)} %copy-done.3, bf16[4,4,256,128]{3,2,1,0:T(8,128)(2,1)} %copy-done.12, bf16[4,4,256,128]{3,2,1,0:T(8,128)(2,1)} %collective-permute-done.14.theirs_ref, bf16[2,2,640,256]{3,2,1,0:T(8,128)(2,1)} %copy-done, ...), custom_call_target="tpu_custom_call" | custom-call | flops 10737418240 | bytes 16777216 | tf_op jit(solution)/shard_map/multiply_part/pallas_call | solution.py:511
  127.3 2.5 %collective-permute-done.16.other_ref = bf16[4,4,256,128]{3,2,1,0:T(8,128)(2,1)S(1)} collective-permute-done((bf16[4,4,256,128]{3,2,1,0:T(8,128)(2,1)S(1)}, bf16[4,4,256,128]{3,2,1,0:T(8,128)(2,1)S(1)}, u32[]{:S(2)}, u32[]{:S(2)}) %collective-permute-start.16) | collective-permute-done | bytes 1048608 | tf_op jit(solution)/shard_map/ppermute | solution.py:630
  129.8 1.0 copy-done.11
  130.7 13.6 %multiply_part.3 = f32[4096,2048]{1,0:T(8,128)} custom-call(s32[19]{0:T(128)} %copy-done.5, bf16[4,4,256,128]{3,2,1,0:T(8,128)(2,1)} %copy-done.2, bf16[4,4,256,128]{3,2,1,0:T(8,128)(2,1)} %copy-done.11, bf16[4,4,256,128]{3,2,1,0:T(8,128)(2,1)} %collective-permute-done.14.theirs_ref, ...), custom_call_target="tpu_custom_call", output_to_operand_aliasing={{}: (8, {})} | custom-call | flops 10737418240 | bytes 16777216 | tf_op jit(solution)/shard_map/multiply_part/pallas_call | solution.py:511
  (41 shorter events, 0.4 us)
Async XLA Ops:
  0.1 106.1 %copy-start.5 = (s32[19]{0:T(128)}, s32[19]{0:T(128)S(1)}, u32[]{:S(2)}) copy-start(s32[19]{0:T(128)S(1)} %stack.88.place_ref) | copy-start | bytes 232
  0.1 1.0 copy-start.4
  1.2 0.7 copy-start.6
  1.9 0.7 copy-start.7
  4.1 6.8 %collective-permute-start.6 = (bf16[1,272,128]{2,1,0:T(8,128)(2,1)S(1)}, bf16[1,272,128]{2,1,0:T(8,128)(2,1)S(1)}, u32[]{:S(2)}, u32[]{:S(2)}) collective-permute-start(bf16[1,272,128]{2,1,0:T(8,128)(2,1)S(1)} %get-tuple-element.24), channel_id=1, source_target_pairs={{0,8},{1,9},{2,10},{3,11},{16,24},{17,25},{18,26},{19,27}} | collective-permute-start | bytes 208904 | tf_op jit(solution)/shard_map/ppermute | solution.py:570
  10.9 10.6 %collective-permute-start.7 = (bf16[1,272,128]{2,1,0:T(8,128)(2,1)S(1)}, bf16[1,272,128]{2,1,0:T(8,128)(2,1)S(1)}, u32[]{:S(2)}, u32[]{:S(2)}) collective-permute-start(bf16[1,272,128]{2,1,0:T(8,128)(2,1)S(1)} %broadcast_select_fusion.2), channel_id=1, source_target_pairs={{0,16},{1,17},{2,18},{3,19},{8,24},{9,25},{10,26},{11,27},{16,0},{... | collective-permute-start | bytes 208904 | tf_op jit(solution)/shard_map/ppermute | solution.py:588
  14.4 14.9 %collective-permute-start.1 = (bf16[4,256,128]{2,1,0:T(8,128)(2,1)S(1)}, bf16[4,256,128]{2,1,0:T(8,128)(2,1)S(1)}, u32[]{:S(2)}, u32[]{:S(2)}) collective-permute-start(bf16[4,256,128]{2,1,0:T(8,128)(2,1)S(1)} %get-tuple-element.20.refs_0_.refs_4_), channel_id=1, source_target_pairs={{2,0},{3,1},{4,6},{5,7},{10,8},{11,9},{12,14},{13,15},{18,16},{19,... | collective-permute-start | bytes 786440 | tf_op jit(solution)/shard_map/ppermute | solution.py:626
  15.7 13.6 %collective-permute-start.2 = (bf16[4,256,128]{2,1,0:T(8,128)(2,1)S(1)}, bf16[4,256,128]{2,1,0:T(8,128)(2,1)S(1)}, u32[]{:S(2)}, u32[]{:S(2)}) collective-permute-start(bf16[4,256,128]{2,1,0:T(8,128)(2,1)S(1)} %get-tuple-element.21.refs_9_), channel_id=1, source_target_pairs={{1,0},{2,1},{7,6},{4,7},{9,8},{10,9},{15,14},{12,15},{17,16},{18,1... | collective-permute-start | bytes 786440 | tf_op jit(solution)/shard_map/ppermute | solution.py:626
  17.0 12.3 %collective-permute-start = (bf16[4,256,128]{2,1,0:T(8,128)(2,1)S(1)}, bf16[4,256,128]{2,1,0:T(8,128)(2,1)S(1)}, u32[]{:S(2)}, u32[]{:S(2)}) collective-permute-start(bf16[4,256,128]{2,1,0:T(8,128)(2,1)S(1)} %get-tuple-element.21.refs_9_), channel_id=1, source_target_pairs={{3,0},{0,1},{5,6},{6,7},{11,8},{8,9},{13,14},{14,15},{19,16},{16,1... | collective-permute-start | bytes 786440 | tf_op jit(solution)/shard_map/ppermute | solution.py:626
  21.5 9.7 %collective-permute-start.8 = (bf16[2,272,128]{2,1,0:T(8,128)(2,1)S(1)}, bf16[2,272,128]{2,1,0:T(8,128)(2,1)S(1)}, u32[]{:S(2)}, u32[]{:S(2)}) collective-permute-start(bf16[2,272,128]{2,1,0:T(8,128)(2,1)S(1)} %pad_maximum_fusion.2), channel_id=1, source_target_pairs={{0,1},{1,0},{2,3},{3,2},{8,9},{9,8},{10,11},{11,10},{16,17},{17,16... | collective-permute-start | bytes 417800 | tf_op jit(solution)/shard_map/ppermute | solution.py:588
  23.5 38.6 %copy-start.8 = (f32[64]{0:T(128)S(1)}, f32[64]{0:T(128)}, u32[]{:S(2)}) copy-start(f32[64]{0:T(128)} %taps_ref.1) | copy-start | bytes 772
  29.9 30.8 %collective-permute-start.14 = (bf16[4,4,256,128]{3,2,1,0:T(8,128)(2,1)S(1)}, bf16[4,4,256,128]{3,2,1,0:T(8,128)(2,1)}, u32[]{:S(2)}, u32[]{:S(2)}) collective-permute-start(bf16[4,4,256,128]{3,2,1,0:T(8,128)(2,1)S(1)} %get-tuple-element.25.after), channel_id=1, source_target_pairs={{16,0},{17,1},{22,6},{23,7},{8,24},{9,25},{14,30},{15,31}} | collective-permute-start | bytes 3145736 | tf_op jit(solution)/shard_map/ppermute | solution.py:630
  31.3 17.7 %collective-permute-start.9 = (bf16[4,272,128]{2,1,0:T(8,128)(2,1)S(1)}, bf16[4,272,128]{2,1,0:T(8,128)(2,1)S(1)}, u32[]{:S(2)}, u32[]{:S(2)}) collective-permute-start(bf16[4,272,128]{2,1,0:T(8,128)(2,1)S(1)} %pad_maximum_fusion.1), channel_id=1, source_target_pairs={{0,2},{1,3},{2,0},{3,1},{8,10},{9,11},{10,8},{11,9},{16,18},{17,19... | collective-permute-start | bytes 835592 | tf_op jit(solution)/shard_map/ppermute | solution.py:588
  49.0 6.3 %collective-permute-start.10 = (bf16[8,272,128]{2,1,0:T(8,128)(2,1)S(1)}, bf16[8,272,128]{2,1,0:T(8,128)(2,1)}, u32[]{:S(2)}, u32[]{:S(2)}) collective-permute-start(bf16[8,272,128]{2,1,0:T(8,128)(2,1)S(1)} %pad_maximum_fusion.own_ref), channel_id=1, source_target_pairs={{0,4},{8,12},{1,5},{9,13},{2,6},{10,14},{3,7},{11,15},{16,20},{24,... | collective-permute-start | bytes 1671176 | tf_op jit(solution)/shard_map/ppermute | solution.py:590
  51.8 20.4 %collective-permute-start.4 = (bf16[4,256,128]{2,1,0:T(8,128)(2,1)S(1)}, bf16[4,256,128]{2,1,0:T(8,128)(2,1)S(1)}, u32[]{:S(2)}, u32[]{:S(2)}) collective-permute-start(bf16[4,256,128]{2,1,0:T(8,128)(2,1)S(1)} %get-tuple-element.22.refs_0_.refs_4_), channel_id=1, source_target_pairs={{0,2},{1,3},{6,4},{7,5},{8,10},{9,11},{14,12},{15,13},{16,18},{17,... | collective-permute-start | bytes 786440 | tf_op jit(solution)/shard_map/ppermute | solution.py:626
  53.3 18.9 %collective-permute-start.5 = (bf16[4,256,128]{2,1,0:T(8,128)(2,1)S(1)}, bf16[4,256,128]{2,1,0:T(8,128)(2,1)S(1)}, u32[]{:S(2)}, u32[]{:S(2)}) collective-permute-start(bf16[4,256,128]{2,1,0:T(8,128)(2,1)S(1)} %get-tuple-element.23.refs_9_), channel_id=1, source_target_pairs={{3,2},{0,3},{5,4},{6,5},{11,10},{8,11},{13,12},{14,13},{19,18},{16... | collective-permute-start | bytes 786440 | tf_op jit(solution)/shard_map/ppermute | solution.py:626
  54.6 17.6 %collective-permute-start.3 = (bf16[4,256,128]{2,1,0:T(8,128)(2,1)S(1)}, bf16[4,256,128]{2,1,0:T(8,128)(2,1)S(1)}, u32[]{:S(2)}, u32[]{:S(2)}) collective-permute-start(bf16[4,256,128]{2,1,0:T(8,128)(2,1)S(1)} %get-tuple-element.23.refs_9_), channel_id=1, source_target_pairs={{1,2},{2,3},{7,4},{4,5},{9,10},{10,11},{15,12},{12,13},{17,18},{18... | collective-permute-start | bytes 786440 | tf_op jit(solution)/shard_map/ppermute | solution.py:626
  55.3 28.8 %collective-permute-start.17 = (bf16[4,4,256,128]{3,2,1,0:T(8,128)(2,1)S(1)}, bf16[4,4,256,128]{3,2,1,0:T(8,128)(2,1)S(1)}, u32[]{:S(2)}, u32[]{:S(2)}) collective-permute-start(bf16[4,4,256,128]{3,2,1,0:T(8,128)(2,1)S(1)} %get-tuple-element.25.after), channel_id=1, source_target_pairs={{0,8},{1,9},{6,14},{7,15},{24,16},{25,17},{30,22},{31,23}} | collective-permute-start | bytes 3145736 | tf_op jit(solution)/shard_map/ppermute | solution.py:570
  60.7 24.9 %collective-permute-start.15 = (bf16[4,4,256,128]{3,2,1,0:T(8,128)(2,1)}, bf16[4,4,256,128]{3,2,1,0:T(8,128)(2,1)S(1)}, u32[]{:S(2)}, u32[]{:S(2)}) collective-permute-start(bf16[4,4,256,128]{3,2,1,0:T(8,128)(2,1)} %collective-permute-done.14.theirs_ref), channel_id=1, source_target_pairs={{0,8},{1,9},{6,14},{7,15},{24,16},{25,17},{30,22},{31,23}} | collective-permute-start | bytes 3145736 | tf_op jit(solution)/shard_map/ppermute | solution.py:570
  71.1 1.1 copy-start
  72.8 11.3 %copy-start.3 = (bf16[4,4,256,128]{3,2,1,0:T(8,128)(2,1)}, bf16[4,4,256,128]{3,2,1,0:T(8,128)(2,1)S(1)}, u32[]{:S(2)}) copy-start(bf16[4,4,256,128]{3,2,1,0:T(8,128)(2,1)S(1)} %get-tuple-element.29.after.own_ref) | copy-start | bytes 3145732
  72.9 22.6 %collective-permute-start.12 = (bf16[4,256,128]{2,1,0:T(8,128)(2,1)S(1)}, bf16[4,256,128]{2,1,0:T(8,128)(2,1)S(1)}, u32[]{:S(2)}, u32[]{:S(2)}) collective-permute-start(bf16[4,256,128]{2,1,0:T(8,128)(2,1)S(1)} %get-tuple-element.27.refs_0_.refs_4_), channel_id=1, source_target_pairs={{2,0},{3,1},{0,2},{1,3},{6,4},{7,5},{4,6},{5,7},{10,8},{11,9},{8,1... | collective-permute-start | bytes 786440 | tf_op jit(solution)/shard_map/ppermute | solution.py:626
  72.9 31.4 %collective-permute-start.13 = (bf16[4,256,128]{2,1,0:T(8,128)(2,1)S(1)}, bf16[4,256,128]{2,1,0:T(8,128)(2,1)S(1)}, u32[]{:S(2)}, u32[]{:S(2)}) collective-permute-start(bf16[4,256,128]{2,1,0:T(8,128)(2,1)S(1)} %get-tuple-element.28), channel_id=1, source_target_pairs={{1,0},{2,1},{3,2},{0,3},{5,4},{6,5},{7,6},{4,7},{9,8},{10,9},{11,1... | collective-permute-start | bytes 786440 | tf_op jit(solution)/shard_map/ppermute | solution.py:626
  76.4 37.3 %collective-permute-start.20 = (bf16[4,4,256,128]{3,2,1,0:T(8,128)(2,1)S(1)}, bf16[4,4,256,128]{3,2,1,0:T(8,128)(2,1)S(1)}, u32[]{:S(2)}, u32[]{:S(2)}) collective-permute-start(bf16[4,4,256,128]{3,2,1,0:T(8,128)(2,1)S(1)} %get-tuple-element.29.after.own_ref), channel_id=1, source_target_pairs={{18,2},{19,3},{20,4},{21,5},{24,8},{25,9},{26,10},{27,11},{28,12},... | collective-permute-start | bytes 3145736 | tf_op jit(solution)/shard_map/ppermute | solution.py:630
  84.2 22.0 %collective-permute-start.18 = (bf16[4,4,256,128]{3,2,1,0:T(8,128)(2,1)S(1)}, bf16[4,4,256,128]{3,2,1,0:T(8,128)(2,1)S(1)}, u32[]{:S(2)}, u32[]{:S(2)}) collective-permute-start(bf16[4,4,256,128]{3,2,1,0:T(8,128)(2,1)S(1)} %broadcast_select_fusion.own_ref), channel_id=1, source_target_pairs={{0,4},{8,12},{1,5},{9,13},{6,2},{14,10},{7,3},{15,11},{24,28},{16,... | collective-permute-start | bytes 3145736 | tf_op jit(solution)/shard_map/ppermute | solution.py:570
  87.0 19.2 %collective-permute-start.19 = (bf16[4,4,256,128]{3,2,1,0:T(8,128)(2,1)S(1)}, bf16[4,4,256,128]{3,2,1,0:T(8,128)(2,1)S(1)}, u32[]{:S(2)}, u32[]{:S(2)}) collective-permute-start(bf16[4,4,256,128]{3,2,1,0:T(8,128)(2,1)S(1)} %broadcast_select_fusion.1.after.other_ref), channel_id=1, source_target_pairs={{0,4},{8,12},{1,5},{9,13},{6,2},{14,10},{7,3},{15,11},{24,28},{16,... | collective-permute-start | bytes 3145736 | tf_op jit(solution)/shard_map/ppermute | solution.py:570
  94.1 1.3 copy-start.9
  95.4 9.0 %collective-permute-start.11 = (bf16[4,256,128]{2,1,0:T(8,128)(2,1)S(1)}, bf16[4,256,128]{2,1,0:T(8,128)(2,1)S(1)}, u32[]{:S(2)}, u32[]{:S(2)}) collective-permute-start(bf16[4,256,128]{2,1,0:T(8,128)(2,1)S(1)} %get-tuple-element.28), channel_id=1, source_target_pairs={{3,0},{0,1},{1,2},{2,3},{7,4},{4,5},{5,6},{6,7},{11,8},{8,9},{9,10... | collective-permute-start | bytes 786440 | tf_op jit(solution)/shard_map/ppermute | solution.py:626
  95.4 1.6 %copy-start.10 = (f32[512,1024]{1,0:T(8,128)S(1)}, f32[512,1024]{1,0:T(8,128)}, u32[]{:S(2)}) copy-start(f32[512,1024]{1,0:T(8,128)} %copy-done.9) | copy-start | bytes 6291460
  104.3 1.0 copy-start.1
  105.3 1.0 copy-start.2
  105.3 24.5 %collective-permute-start.16 = (bf16[4,4,256,128]{3,2,1,0:T(8,128)(2,1)S(1)}, bf16[4,4,256,128]{3,2,1,0:T(8,128)(2,1)S(1)}, u32[]{:S(2)}, u32[]{:S(2)}) collective-permute-start(bf16[4,4,256,128]{3,2,1,0:T(8,128)(2,1)S(1)} %assemble.5.after.own_ref), channel_id=1, source_target_pairs={{16,0},{17,1},{18,2},{19,3},{20,4},{21,5},{22,6},{23,7},{24,8},{25... | collective-permute-start | bytes 3145736 | tf_op jit(solution)/shard_map/ppermute | solution.py:630
  113.7 1.0 copy-start.12
  129.8 1.0 copy-start.11

commit v4 on v3

v4 whole, which is shorter than its diff:
```python
import functools

import jax
import jax.numpy as jnp
from jax import lax
from jax.experimental import pallas as pl
from jax.experimental.pallas import tpu as pltpu
from jax.sharding import PartitionSpec as P

PANEL = 256
SECTIONS = 2
HEAD = PANEL * SECTIONS
PB = 128
LANES = 128
BLOCK = 128
HALF = 256
SUB = 8
NOTE = 16
EXACT = lax.Precision.HIGHEST
F32 = jnp.float32
BF16 = jnp.bfloat16


def iota(shape, axis):
    return lax.broadcasted_iota(jnp.int32, shape, axis)


def dot(left, right, contract=((1,), (0,)), precision=None):
    return lax.dot_general(
        left, right, (contract, ((), ())), preferred_element_type=F32, precision=precision
    )


NT = ((1,), (1,))
TN = ((0,), (0,))
VMEM = pl.BlockSpec(memory_space=pltpu.VMEM)
SMEM = pl.BlockSpec(memory_space=pltpu.SMEM)
ANY = pl.BlockSpec(memory_space=pl.ANY)
FREE = pl.CostEstimate(flops=0, bytes_accessed=0, transcendentals=0)
LIMIT = pltpu.CompilerParams(vmem_limit_bytes=48 << 20)


def permute_kernel(place_ref, order_ref, counts_ref, design_ref, *out_refs):
    *part_refs, both_ref, note_ref = out_refs
    epochs = design_ref.shape[0]
    parts, per_part = len(part_refs), part_refs[0].shape[0]
    lane = iota((PB, PB), 1).astype(F32)
    none = jnp.zeros((epochs, PB), BF16)
    groups = 2 * HALF // PB

    def packed(local, columns, block, part):
        first = block * groups + part
        second = first + HALF // PB
        pick = [jnp.where(local[:, g : g + 1] == lane, 1.0, 0.0) for g in (first, second)]
        pick = jnp.concatenate(pick, axis=1).astype(BF16)
        top = jnp.concatenate([columns(first), none], axis=1)
        low = jnp.concatenate([none, columns(second)], axis=1)
        return dot(pick, jnp.concatenate([top, low], axis=0), NT).astype(BF16)

    def order_of(rows):
        return (order_ref[rows, :] & (PB - 1)).astype(F32).T

    local = order_of(slice(0, per_part * groups))
    for part in range(HALF // PB):
        columns = lambda g: design_ref[:, g * PB : (g + 1) * PB]
        note_ref[0, part * PB : (part + 1) * PB, :] = packed(local, columns, 0, part)
    counts = counts_ref[...].astype(F32)
    counts = jnp.concatenate([counts] * (LANES // epochs), axis=1)
    note_ref[0, HALF:, :] = jnp.broadcast_to(counts, (NOTE, LANES)).astype(BF16)
    for j in range(parts):
        piece = lax.rem(place_ref[PLACE_COL] + j, parts)
        at = pl.multiple_of(piece * per_part * groups, per_part * groups)
        local = order_of(pl.ds(at, per_part * groups))
        columns = lambda g: design_ref[:, pl.ds(pl.multiple_of((at + g) * PB, PB), PB)]
        for block in range(per_part):
            for part in range(HALF // PB):
                rows = slice(part * PB, (part + 1) * PB)
                part_refs[j][block, rows, :] = packed(local, columns, block, part)
        both_ref[j] = part_refs[j][...]


def permute_local(place, design, order, tap_count, cols_dev):
    epochs, rows = design.shape
    parts, per_part = rows // cols_dev, cols_dev // (2 * HALF)
    piece = jax.ShapeDtypeStruct((per_part, HALF, LANES), BF16)
    both = jax.ShapeDtypeStruct((parts,) + piece.shape, BF16)
    note = jax.ShapeDtypeStruct((1, HALF + NOTE, LANES), BF16)
    return pl.pallas_call(
        permute_kernel,
        out_shape=(piece,) * parts + (both, note),
        in_specs=[SMEM] + [VMEM] * 3,
        out_specs=(VMEM,) * (parts + 2),
        compiler_params=LIMIT,
        name="permute_local",
    )(place, order.reshape(rows // PB, PB), tap_count.reshape(1, epochs), design)


PLACE_ROW, PLACE_GROUP, PLACE_EP, PLACE_COL, PLACE_TAKES, PLACE_OWNS, PLACE_BACK = range(7)


def assemble_kernel(count, gated, after, whole, place_ref, *refs):
    shards, kept = refs[:count], refs[count : count + gated]
    out_refs, sem = refs[count + gated + after : -1], refs[-1]
    copies = [(shard, out_refs[0].at[n]) for n, shard in enumerate(shards)]
    if whole:
        copies += [(shard, out_refs[-1].at[n]) for n, shard in enumerate([kept[0], *shards])]
    copies = [pltpu.make_async_copy(a, b, sem.at[n]) for n, (a, b) in enumerate(copies)]
    for copy in copies:
        copy.start()
    for copy in copies:
        copy.wait()


def assemble(place, shards, gated, after, whole):
    count = len(shards)
    out_shape = [jax.ShapeDtypeStruct((count,) + shards[0].shape, BF16)]
    out_shape += [jax.ShapeDtypeStruct(g.shape, g.dtype) for g in gated]
    if whole:
        out_shape.append(jax.ShapeDtypeStruct((count + 1,) + shards[0].shape, BF16))
    return pl.pallas_call(
        functools.partial(assemble_kernel, count, len(gated), len(after), whole),
        out_shape=out_shape,
        in_specs=[SMEM] + [ANY] * (count + len(gated) + len(after)),
        out_specs=[ANY] * len(out_shape),
        input_output_aliases={1 + count + n: 1 + n for n in range(len(gated))},
        scratch_shapes=[pltpu.SemaphoreType.DMA((2 * count + 1,))],
        compiler_params=LIMIT,
        cost_estimate=FREE,
        name="assemble",
    )(place, *shards, *gated, *after)


def gate(arrays, after):
    count = len(arrays)
    return pl.pallas_call(
        lambda *refs: None,
        out_shape=tuple(jax.ShapeDtypeStruct(x.shape, x.dtype) for x in arrays),
        in_specs=[ANY] * (count + 1),
        out_specs=(ANY,) * count,
        input_output_aliases={n: n for n in range(count)},
        compiler_params=LIMIT,
        cost_estimate=FREE,
        name="gate",
    )(*arrays, after)


def filter_rows(blocks, band_ref, store):
    per = HALF // (LANES // 2)
    for b in range(band_ref.shape[0]):
        first = max(b * per - 1, 0)
        skip = 0 if b else LANES
        packed = jnp.concatenate([blocks(e) for e in range(first, (b + 1) * per)], axis=1)
        for half in range(2):
            got = dot(packed, band_ref[b, half, skip:, :]).astype(BF16)
            store(slice(half * HALF, (half + 1) * HALF), slice(b * HALF, (b + 1) * HALF), got)


def spread(tile, lane):
    return jnp.broadcast_to(tile[:, lane : lane + 1], (SUB, tile.shape[1]))


def row_of(tile, k):
    return jnp.broadcast_to(tile[k : k + 1, :], (SUB, tile.shape[1]))


def factor_block(work):
    groups = BLOCK // SUB
    sub, lane = iota((SUB, BLOCK), 0), iota((SUB, BLOCK), 1)
    tiles = [work[g * SUB : (g + 1) * SUB, :] for g in range(groups)]
    for g in range(groups):
        inside = (lane >= g * SUB) & (lane < (g + 1) * SUB)
        cols = [spread(tiles[g], g * SUB + j) for j in range(SUB)]
        a = {(i, j): row_of(cols[j], i) for j in range(SUB) for i in range(j, SUB)}
        own = jnp.where(inside, jnp.where(lane - g * SUB == sub, 1.0, 0.0), tiles[g])
        u = [row_of(own, k) for k in range(SUB)]
        inv = []
        low = {}
        for k in range(SUB):
            r = lax.rsqrt(a[k, k])
            inv.append(r)
            for i in range(k + 1, SUB):
                low[i, k] = a[i, k] * r
            for j in range(k + 1, SUB):
                for i in range(j, SUB):
                    a[i, j] = a[i, j] - low[i, k] * low[j, k]
            u[k] = u[k] * r
            for j in range(k + 1, SUB):
                u[j] = u[j] - low[j, k] * u[k]
        for t in range(g + 1, groups):
            left = [spread(tiles[t], g * SUB + j) for j in range(SUB)]
            tile = jnp.where(inside, 0.0, tiles[t])
            for k in range(SUB):
                left[k] = left[k] * inv[k]
                for j in range(k + 1, SUB):
                    left[j] = left[j] - low[j, k] * left[k]
                tile = tile - left[k] * u[k]
            tiles[t] = tile
        merged = u[0]
        for k in range(1, SUB):
            merged = jnp.where(sub == k, u[k], merged)
        work[g * SUB : (g + 1) * SUB, :] = jnp.where(lane < (g + 1) * SUB, merged, 0.0)


def start_kernel(
    chain, place_ref, taps_ref, own_ref, came_ref, reg_ref, after, band_ref, aug_ref, notes, a1, work
):
    del after
    epochs = aug_ref.shape[1] - HEAD
    half = LANES // 2

    @pl.when(place_ref[0] % 2 == 0)
    def _():
        for rel in range(own_ref.shape[0]):
            notes[place_ref[chain + rel]] = own_ref[rel]

    @pl.when(place_ref[0] % 2 == 1)
    def _():
        for rel in range(own_ref.shape[0]):
            notes[place_ref[chain + rel]] = came_ref[rel]

    shape = (half, LANES)
    lag = iota(shape, 1) - iota(shape, 0)
    base = lax.fori_loop(
        0,
        taps_ref.shape[0],
        lambda k, kept: jnp.where(lag == k, taps_ref[k], kept),
        jnp.zeros(shape, F32),
    )
    lane = iota(shape, 1)
    swapped = jnp.concatenate([base[:, half:], base[:, :half]], axis=1)
    early = jnp.where(lane < half, swapped, 0.0)
    late = jnp.where(lane >= half, swapped, 0.0)
    none = jnp.zeros(shape, F32)
    patterns = [(early, none), (base, none), (late, early), (none, base), (none, late)]
    row = iota((1, LANES), 1)
    band_ref[...] = jnp.zeros_like(band_ref)
    for b in range(epochs // HALF):
        for side in range(HALF // LANES):
            e = (b * HALF + side * LANES) // half
            counts = [notes[e + n, HALF : HALF + NOTE, :].astype(F32)[:1] for n in range(2)]
            counts = jnp.where(row < half, counts[0], counts[1])
            for j, pattern in enumerate(patterns):
                at = (lag + side * LANES + half - half * j).astype(F32)
                kept = jnp.where(at < counts, pattern[side], 0.0).astype(BF16)
                for h in range(2):
                    rows = slice(j * LANES + h * half, j * LANES + (h + 1) * half)
                    band_ref[b, h, rows, side * LANES : (side + 1) * LANES] = kept

    def store(rows, cols, got):
        a1[rows, cols] = got

    filter_rows(lambda e: notes[e, :HALF, :], band_ref, store)
    columns = a1[...]
    square = (HEAD, HEAD)
    on_diagonal = iota(square, 0) == iota(square, 1)
    aug_ref[:, :HEAD] = dot(columns, columns, NT) + jnp.where(on_diagonal, reg_ref[:, :HEAD], 0.0)
    aug_ref[:, HEAD:] = columns.astype(F32)
    eliminate(aug_ref, 0, work)


def eliminate(aug, kb, work):
    here = slice(kb * BLOCK, (kb + 1) * BLOCK)
    work[...] = aug[here, here]
    factor_block(work)
    rest = slice(kb * BLOCK, aug.shape[1])
    aug[here, rest] = dot(work[...], aug[here, rest], precision=EXACT)
    for rb in range(kb + 1, HEAD // BLOCK):
        below = slice(rb * BLOCK, (rb + 1) * BLOCK)
        rest = slice(rb * BLOCK, aug.shape[1])
        aug[below, rest] -= dot(aug[here, below], aug[here, rest], TN, precision=EXACT)


def next_kernel(kb, aug_in, after, aug_ref, work):
    del after
    aug_ref[...] = aug_in[...]
    eliminate(aug_ref, kb, work)


def last_kernel(kb, aug_in, after, factor_ref, w_ref, high_ref, low_ref, aug, work):
    del after
    aug[...] = aug_in[...]
    eliminate(aug, kb, work)
    square = (HEAD, HEAD)
    epochs = aug.shape[1] - HEAD
    factor_ref[...] = jnp.where(iota(square, 0) >= iota(square, 1), aug[:, :HEAD].T, 0.0)
    wt = aug[:, HEAD:]
    w_ref[...] = wt.T.astype(BF16)
    for b in range(epochs // BLOCK):
        here = slice(b * BLOCK, (b + 1) * BLOCK)
        shape = (BLOCK, epochs)
        unit = jnp.where(iota(shape, 0) + b * BLOCK == iota(shape, 1), 1.0, 0.0)
        middle = unit - dot(wt[:, here], wt, TN, precision=EXACT)
        high = middle.astype(BF16)
        high_ref[here, :] = high
        low_ref[here, :] = (middle - high.astype(F32)).astype(BF16)


def start_panel(place, chain, taps, own, came, regular, after):
    epochs = own.shape[0] * (LANES // 2)
    per = HALF // (LANES // 2)
    return pl.pallas_call(
        functools.partial(start_kernel, chain),
        out_shape=(
            jax.ShapeDtypeStruct((epochs // HALF, 2, (per + 1) * LANES, HALF), BF16),
            jax.ShapeDtypeStruct((HEAD, HEAD + epochs), F32),
        ),
        in_specs=[SMEM, SMEM, VMEM, VMEM, VMEM, ANY],
        out_specs=(VMEM, VMEM),
        scratch_shapes=[
            pltpu.VMEM(own.shape, BF16),
            pltpu.VMEM((HEAD, epochs), BF16),
            pltpu.VMEM((BLOCK, BLOCK), F32),
        ],
        compiler_params=LIMIT,
        cost_estimate=FREE,
        name="start_panel",
    )(place, taps, own, came, regular.reshape(1, -1), after)


def next_panel(kb, aug, after):
    return pl.pallas_call(
        functools.partial(next_kernel, kb),
        out_shape=jax.ShapeDtypeStruct(aug.shape, F32),
        in_specs=[VMEM, ANY],
        out_specs=VMEM,
        scratch_shapes=[pltpu.VMEM((BLOCK, BLOCK), F32)],
        compiler_params=LIMIT,
        cost_estimate=FREE,
        name="next_panel",
    )(aug, after)


def last_panel(kb, aug, after):
    epochs = aug.shape[1] - HEAD
    return pl.pallas_call(
        functools.partial(last_kernel, kb),
        out_shape=(
            jax.ShapeDtypeStruct((HEAD, HEAD), F32),
            jax.ShapeDtypeStruct((epochs, HEAD), BF16),
            jax.ShapeDtypeStruct((epochs, epochs), BF16),
            jax.ShapeDtypeStruct((epochs, epochs), BF16),
        ),
        in_specs=[VMEM, ANY],
        out_specs=(VMEM,) * 4,
        scratch_shapes=[pltpu.VMEM(aug.shape, F32), pltpu.VMEM((BLOCK, BLOCK), F32)],
        compiler_params=LIMIT,
        cost_estimate=FREE,
        name="last_panel",
    )(aug, after)


def whole_shards(ref):
    return [ref.at[n, 0] for n in range(ref.shape[0])]


def split_shards(first, rest):
    return [first, *whole_shards(rest)]


def unpack(place_ref, own, other, blocks):
    width = len(own)
    here = place_ref[PLACE_EP] * width
    there = width - here
    for n in range(width):
        back = place_ref[PLACE_BACK + n]
        blocks[here + back] = own[n][...]
        blocks[there + back] = other[n][...]


def choose(condition, yes, no):
    pl.when(condition)(yes)
    pl.when(jnp.logical_not(condition))(no)


def fixed(array):
    return pl.BlockSpec(
        array.shape, lambda n, i, place: (0,) * array.ndim, pipeline_mode=pl.Buffered(1)
    )


def tile_kernel(
    part, parts, place_ref, own_first, own_rest, other_first, other_rest, band_ref, factor_ref, reg_ref,
    *refs,
):
    if part == 0:
        theirs_ref, *right_refs, w_ref, high_ref, low_ref = refs[:8]
        out_ref, right_ref, blocks, filtered, columns = refs[8:]
    else:
        right_ref, _, out_ref, blocks, filtered = refs
    n, i = pl.program_id(0), pl.program_id(1)
    rows, wide = out_ref.shape
    steps = pl.num_programs(1)
    block = lax.rem(place_ref[PLACE_COL] + part, parts) * steps + i
    first_row = (place_ref[PLACE_ROW] * parts * steps + block) * rows
    first_col = (place_ref[PLACE_GROUP] * pl.num_programs(0) + n) * wide
    at = pl.multiple_of(i * rows, rows)

    if part == 0:

        @pl.when(i == 0)
        def _():
            def store(rows, cols, got):
                columns[rows, cols] = got

            own, own_came, other, other_came = right_refs
            choose(
                place_ref[PLACE_TAKES] != 0,
                lambda: unpack(place_ref, whole_shards(own_came), whole_shards(other_came), blocks),
                lambda: unpack(place_ref, whole_shards(own), whole_shards(other), blocks),
            )
            filter_rows(lambda e: blocks[e], band_ref, store)
            wanted = columns[...]
            projected = dot(high_ref[...], wanted, NT) + dot(low_ref[...], wanted, NT)
            right_ref[...] = projected.astype(BF16)

            @pl.when(first_col == 0)
            def _():
                right_ref[...] = w_ref[...]

    @pl.when(n == 0)
    def _():
        def store(rows, cols, got):
            filtered[pl.ds(at + rows.start, HALF), cols] = got

        own = split_shards(own_first.at[0], own_rest)
        other = split_shards(other_first.at[0, 0], other_rest)
        if part == 0:
            choose(
                place_ref[PLACE_OWNS] != 0,
                lambda: unpack(place_ref, own, whole_shards(theirs_ref), blocks),
                lambda: unpack(place_ref, own, other, blocks),
            )
        else:
            unpack(place_ref, own, other, blocks)
        filter_rows(lambda e: blocks[e], band_ref, store)

    @pl.when(first_row >= HEAD)
    def _():
        out_ref[...] = dot(filtered[pl.ds(at, rows), :], right_ref[...])

        @pl.when(first_row == first_col)
        def _():
            on_diagonal = iota((rows, wide), 0) == iota((rows, wide), 1)
            out_ref[...] += jnp.where(on_diagonal, reg_ref[...], 0.0)

    @pl.when(first_row < HEAD)
    def _():
        out_ref[...] = jnp.zeros_like(out_ref)

        @pl.when(first_col == 0)
        def _():
            out_ref[...] = factor_ref[...]


def multiply_part(part, parts, place, own, other, band, factor, regular, extra, out, right):
    steps = own[0].shape[0]
    rows = wide = 2 * HALF
    epochs = band.shape[0] * HALF
    cols = steps * wide

    def row_block(i, place):
        return lax.rem(place[PLACE_COL] + part, parts) * steps + i

    def reg_block(n, i, place):
        return 0, place[PLACE_ROW] * parts * steps + row_block(i, place)

    def left_block(n, i, place):
        return 0, jnp.where(n == 0, i, steps - 1), 0, 0

    def own_block(n, i, place):
        return left_block(n, i, place)[1:]

    def other_block(n, i, place):
        return part, *left_block(n, i, place)[1:]

    def right_block(took):
        return lambda n, i, place: (0, jnp.where(place[PLACE_TAKES] == took, n, 0), 0, 0)

    def shards_spec(array, index):
        return pl.BlockSpec((array.shape[0], 1, HALF, LANES), index)

    out_shape = [jax.ShapeDtypeStruct((parts * steps * rows, cols), F32)]
    out_specs = [pl.BlockSpec((rows, wide), lambda n, i, place: (row_block(i, place), n))]
    right_spec = pl.BlockSpec((epochs, wide), lambda n, i, place: (0, n))
    scratch = [
        pltpu.VMEM((epochs // (LANES // 2), HALF, LANES), BF16),
        pltpu.VMEM((steps * rows, epochs), BF16),
    ]
    operands = [*own, *other, band, factor, regular.reshape(1, -1)]
    in_specs = [pl.BlockSpec((1, HALF, LANES), own_block), shards_spec(own[1], left_block)]
    in_specs += [pl.BlockSpec((1, 1, HALF, LANES), other_block), shards_spec(other[1], left_block)]
    in_specs += [fixed(band), fixed(factor)]
    in_specs += [pl.BlockSpec((1, rows), reg_block)]
    if part == 0:
        operands += extra
        in_specs += [shards_spec(extra[0], left_block)]
        in_specs += [shards_spec(extra[0], right_block(took)) for took in (0, 1, 0, 1)]
        in_specs += [fixed(array) for array in extra[5:]]
        out_shape.append(jax.ShapeDtypeStruct((epochs, cols), BF16))
        out_specs.append(right_spec)
        scratch.append(pltpu.VMEM((wide, epochs), BF16))
    else:
        operands += [right, out]
        in_specs += [right_spec, ANY]
    return pl.pallas_call(
        functools.partial(tile_kernel, part, parts),
        out_shape=out_shape,
        grid_spec=pltpu.PrefetchScalarGridSpec(
            num_scalar_prefetch=1,
            grid=(cols // wide, steps),
            in_specs=in_specs,
            out_specs=out_specs,
            scratch_shapes=scratch,
        ),
        input_output_aliases={len(operands): 0} if part else {},
        compiler_params=pltpu.CompilerParams(vmem_limit_bytes=48 << 20),
        cost_estimate=FREE,
        name="multiply_part",
    )(place, *operands)


AXES = ("ep", "row", "col")


def sizes():
    return tuple(lax.axis_size(axis) for axis in AXES)


def flat(ep, row, col):
    _, rows, cols = sizes()
    return (ep * rows + row) * cols + col


def doubling(count, least):
    distances = []
    distance = count // 2
    while distance >= least:
        distances.append(distance)
        distance //= 2
    return distances


def spread_step(block, owner_of, distance):
    eps, rows, cols = sizes()
    route = []
    for e in range(eps):
        for c in range(cols):
            for other in range(0, rows, 2 * distance):
                source = owner_of(e, c) ^ other
                route.append((flat(e, source, c), flat(e, source ^ distance, c)))
    return lax.ppermute(block, AXES, route)


def panel_hops():
    eps, _, cols = sizes()
    return [(d, 0) for d in doubling(eps, 1)] + [(0, d) for d in reversed(doubling(cols, 1))]


def gather_panel(note):
    eps, rows, cols = sizes()
    row = lax.axis_index("row")
    for distance in doubling(rows, 2):
        came = spread_step(note, lambda e, c: 0, distance)
        note = jnp.where((row & (2 * distance - 1)) == distance, came, note)
    for de, dc in panel_hops():
        route = [
            (flat(e, r, c), flat(e ^ de, r, c ^ dc))
            for e in range(eps)
            for r in range(0, rows, 2)
            for c in range(cols)
        ]
        note = jnp.concatenate([note, lax.ppermute(note, AXES, route)])
    came = lax.ppermute(note, "row", [(r, r + 1) for r in range(0, rows, 2)])
    return note, came


def on_device(design, taps, tap_count, order, regular):
    rows_dev = design.shape[1]
    eps, rows, cols = sizes()
    cols_dev = regular.shape[0] // (eps * cols)
    parts = rows_dev // cols_dev
    row, ep, col = (lax.axis_index(axis) for axis in ("row", "ep", "col"))
    group = lax.axis_index(("ep", "col"))
    everywhere = [(e, r, c) for e in range(eps) for r in range(rows) for c in range(cols)]
    owner = lambda e, c: (e * cols + c) * cols_dev // rows_dev
    owns = lambda e, r, c: (c // parts == (r * parts % cols) // parts) & (r * parts // cols == e)
    first_owner = group * cols_dev // rows_dev
    takes = ((row ^ first_owner) & 1) == 1
    back = [(col - n) % cols for n in range(cols)]
    place = [row, group, ep, col, takes, owns(ep, row, col), *back]
    chain = len(place)
    steps = [(0, 0)]
    for de, dc in panel_hops():
        steps += [(e ^ de, c ^ dc) for e, c in steps]
    place += [(ep ^ de) * cols + (col ^ dc) for de, dc in steps]
    place = jnp.stack([jnp.asarray(p, jnp.int32) for p in place])

    *local, both, note = permute_local(place, design, order, tap_count, cols_dev)

    def shift(block, n):
        route = [(flat(e, r, (c - n) % cols), flat(e, r, c)) for e, r, c in everywhere]
        return lax.ppermute(block, AXES, route)

    def across(block, wanted):
        route = [(flat(1 - e, r, c), flat(e, r, c)) for e, r, c in everywhere if wanted(e, r, c)]
        return lax.ppermute(block, AXES, route)

    distances = doubling(rows, 1)

    def spread_rest(block, got):
        for n, distance in enumerate(distances[1:]):
            hit = ((row ^ first_owner) & (4 * distance - 1)) == 2 * distance
            block = jnp.where(hit, got, block)
            got = spread_step(block, owner, distance)
        return block, got

    anyone = lambda e, r, c: True
    early = [shift(local[n % parts], n) for n in range(1, cols)]
    swapped = across(both, anyone)
    notes, came = lax.cond(
        tap_count[0] > 0,
        gather_panel,
        lambda note: (jnp.zeros((eps * cols,) + note.shape[1:], BF16),) * 2,
        note,
    )
    rest, *local, first = assemble(place, early, local, [notes, swapped], True)
    theirs = across(first, owns)
    own_got = spread_step(first, owner, distances[0])
    others = [across(rest, lambda e, r, c: not owns(e, r, c))]
    mine = [rest]
    late = [
        [shift(local[(n + j) % parts], n) for n in range(1, cols)] for j in range(1, parts)
    ]
    band, aug = start_panel(place, chain, taps, notes, came, regular, first)
    theirs, own_got, *begun = gate([theirs, own_got, *(shards[0] for shards in late)], aug)
    other_got = spread_step(theirs, owner, distances[0])
    own_block, own_came = spread_rest(first, own_got)
    aug = next_panel(1, aug, theirs)
    aug = next_panel(2, aug, theirs)
    flat_late = [shard for shards in late for shard in shards[1:]]
    other_got, others[0], *flat_late = gate([other_got, others[0], *flat_late], aug)
    for j in range(1, parts):
        shards = [begun[j - 1], *flat_late[(j - 1) * (cols - 2) : j * (cols - 2)]]
        (got,) = assemble(place, shards, [], [aug], False)
        mine.append(got)
        others.append(across(got, anyone))
    factor, w, high, low = last_panel(3, aug, mine[-1])
    other_block, other_came = spread_rest(theirs, other_got)
    extra = [theirs, own_block, own_came, other_block, other_came, w, high, low]
    mine = [(local[j], mine[j]) for j in range(parts)]
    others = [(swapped, others[j]) for j in range(parts)]
    out, right = multiply_part(
        0, parts, place, mine[0], others[0], band, factor, regular, extra, None, None
    )
    for j in range(1, parts):
        (out,) = multiply_part(
            j, parts, place, mine[j], others[j], band, factor, regular, None, out, right
        )
    return out


def solution(mesh):
    in_specs = (P(("ep", "col"), "row"), P(), P(("ep", "col")), P("row"), P())
    out_specs = P("row", ("ep", "col"))
    return jax.shard_map(
        on_device, mesh=mesh, in_specs=in_specs, out_specs=out_specs, check_vma=False
    )
```

time: 145 us -> 145 us (level)
  the two profiles are of different devices: /device:TPU:0 before, /device:TPU:29 now
where the time goes in v4:
time: 145 us; the launch traced here: 144 us
  Pallas kernels  69.9 us (48%)
  waiting for transfers between devices  39.1 us (27%)
  starting transfers between devices  26.4 us (18%)
  local copies, waits for them, and re-layouts  5.51 us (4%)
  other arithmetic  2.42 us (2%)
    pallas_call x2, Pallas kernels, multiply_part(): pl.pallas_call(functools.partial(tile_kernel, part, parts), out_shape=out...  38.2 us
    ppermute x1, waiting for transfers between devices, gather_panel(): came = lax.ppermute(note, 'row', [(r, r + 1) for r in range(0, rows, 2)])  31.9 us
    pallas_call x2, Pallas kernels, next_panel(): pl.pallas_call(functools.partial(next_kernel, kb), out_shape=jax.ShapeDty...  11.3 us
    ppermute x5, starting transfers between devices, spread_step(): return lax.ppermute(block, AXES, route)  9.77 us
    ppermute x4, starting transfers between devices, across(): return lax.ppermute(block, AXES, route)  9.63 us
    pallas_call x1, Pallas kernels, start_panel(): pl.pallas_call(functools.partial(start_kernel, chain), out_shape=(jax.Sha...  8.9 us
    pallas_call x1, Pallas kernels, last_panel(): pl.pallas_call(functools.partial(last_kernel, kb), out_shape=(jax.ShapeDt...  6.93 us
    unnamed x38, local copies, waits for them, and re-layouts  5.42 us
  transfers between devices with their start and end apart: 19, of which 4 were waited for; matrix products, arithmetic and copies ran while one was open for 2% of the time, Pallas kernels for 35%

profile of v4, /device:TPU:29, one launch (start us, length us, event | category | flops | bytes accessed | tf_op | source)
XLA Modules:
  0.0 143.8 jit_solution(7628334764905380929)
XLA Ops:
  0.0 0.1 stack.80.place_ref
  0.1 0.0 copy-start.11
  0.1 1.0 copy-done.11
  1.1 0.7 copy-done.12
  1.9 0.7 copy-done.13
  2.5 2.1 %permute_local.1 = (bf16[4,256,128]{2,1,0:T(8,128)(2,1)}, bf16[4,256,128]{2,1,0:T(8,128)(2,1)S(1)}, bf16[2,4,256,128]{3,2,1,0:T(8,128)(2,1)S(1)}, bf16[1,272,128]{2,1,0:T(8,128)(2,1)S(1)}) custom-call(s32[18]{0:T(128)S(1)} %stack.80.place_ref, s32[32,128]{1,0:T(8,128)S(1)} %bitcast.25, s32[1,64]{1,0:T(1,128)S(1)} %bitcast.26, bf16[64,4096]{1,0:T(8,128)(2,1)S(1)} %copy-done.11), custom_call_target="tpu_custom_call" | custom-call | tf_op jit(solution)/shard_map/permute_local/pallas_call | solution.py:88
  4.7 1.2 collective-permute-start.8
  5.9 0.1 collective-permute-start.6
  5.9 0.2 collective-permute-start.7
  6.1 3.1 %collective-permute-start.5 = (bf16[4,256,128]{2,1,0:T(8,128)(2,1)S(1)}, bf16[4,256,128]{2,1,0:T(8,128)(2,1)S(1)}, u32[]{:S(2)}, u32[]{:S(2)}) collective-permute-start(bf16[4,256,128]{2,1,0:T(8,128)(2,1)S(1)} %get-tuple-element.31.refs_4_), channel_id=1, source_target_pairs={{3,0},{0,1},{1,2},{2,3},{7,4},{4,5},{5,6},{6,7},{11,8},{8,9},{9,10... | collective-permute-start | bytes 786440 | tf_op jit(solution)/shard_map/ppermute | solution.py:602
  9.2 0.0 copy-start.10
  9.2 0.0 copy-start.14
  9.3 36.9 %conditional.1 = (bf16[8,272,128]{2,1,0:T(8,128)(2,1)}, bf16[8,272,128]{2,1,0:T(8,128)(2,1)}) conditional(s32[]{:T(128)} %bitcast.19, () %tuple.13, bf16[1,272,128]{2,1,0:T(8,128)(2,1)S(1)} %get-tuple-element.33), branch_computations={%region_0.1_spmd, %region_1.2_spmd} | conditional | flops 1218565 | bytes 6615310 | solution.py:620
  9.3 0.7 collective-permute-start
  10.0 0.7 collective-permute-start.1
  10.7 0.7 collective-permute-start.2
  11.4 0.7 collective-permute-start.3
  12.1 0.9 pad_maximum_fusion
  13.0 1.3 collective-permute-start.4
  14.3 31.9 %collective-permute-done.4 = bf16[8,272,128]{2,1,0:T(8,128)(2,1)} collective-permute-done((bf16[8,272,128]{2,1,0:T(8,128)(2,1)}, bf16[8,272,128]{2,1,0:T(8,128)(2,1)}, u32[]{:S(2)}, u32[]{:S(2)}) %collective-permute-start.4) | collective-permute-done | bytes 557088 | tf_op jit(solution)/shard_map/cond/branch_1_fun/ppermute | solution.py:573
  46.2 1.7 %assemble.2 = (bf16[3,4,256,128]{3,2,1,0:T(8,128)(2,1)}, bf16[4,256,128]{2,1,0:T(8,128)(2,1)}, bf16[4,256,128]{2,1,0:T(8,128)(2,1)S(1)}, bf16[4,4,256,128]{3,2,1,0:T(8,128)(2,1)S(1)}) custom-call(s32[18]{0:T(128)S(1)} %stack.80.place_ref, bf16[4,256,128]{2,1,0:T(8,128)(2,1)S(1)} %collective-permute-done.5.refs_0_, ...), custom_call_target="tpu_custom_call", output_to_operand_aliasing={{1}: (4, {}), {2}: (5, {})} | custom-call | tf_op jit(solution)/shard_map/assemble/pallas_call | solution.py:120
  48.0 1.3 collective-permute-start.10
  49.3 2.3 %collective-permute-start.9 = (bf16[4,4,256,128]{3,2,1,0:T(8,128)(2,1)S(1)}, bf16[4,4,256,128]{3,2,1,0:T(8,128)(2,1)S(1)}, u32[]{:S(2)}, u32[]{:S(2)}) collective-permute-start(bf16[4,4,256,128]{3,2,1,0:T(8,128)(2,1)S(1)} %get-tuple-element.37.after), channel_id=1, source_target_pairs={{16,0},{17,1},{22,6},{23,7},{8,24},{9,25},{14,30},{15,31}} | collective-permute-start | bytes 3145736 | tf_op jit(solution)/shard_map/ppermute | solution.py:606
  51.6 0.1 collective-permute-start.11
  51.7 8.9 %start_panel.1 = (bf16[2,2,640,256]{3,2,1,0:T(8,128)(2,1)S(1)}, f32[512,1024]{1,0:T(8,128)S(1)}) custom-call(s32[18]{0:T(128)S(1)} %stack.80.place_ref, f32[64]{0:T(128)S(1)} %copy-done.14, bf16[8,272,128]{2,1,0:T(8,128)(2,1)} %get-tuple-element.34.refs_5_.own_ref, bf16[8,272,128]{2,1,0:T(8,128)(2,1)} %get-tuple-element.39.came_ref, ...), custom_call_target="tpu_custom_call" | custom-call | tf_op jit(solution)/shard_map/start_panel/pallas_call | solution.py:301
  60.6 2.9 %collective-permute-done.10.refs_1_ = bf16[4,4,256,128]{3,2,1,0:T(8,128)(2,1)S(1)} collective-permute-done((bf16[4,4,256,128]{3,2,1,0:T(8,128)(2,1)S(1)}, bf16[4,4,256,128]{3,2,1,0:T(8,128)(2,1)S(1)}, u32[]{:S(2)}, u32[]{:S(2)}) %collective-permute-start.10) | collective-permute-done | bytes 1048608 | tf_op jit(solution)/shard_map/ppermute | solution.py:551
  63.5 0.0 copy-start.4
  63.6 1.0 copy-done.4
  64.5 0.7 copy-done.8
  65.2 1.3 collective-permute-start.12
  66.5 1.3 collective-permute-start.13
  67.8 0.2 collective-permute-start.15
  68.1 0.1 collective-permute-start.14
  68.1 5.8 %next_panel.2.aug_in = f32[512,1024]{1,0:T(8,128)S(1)} custom-call(f32[512,1024]{1,0:T(8,128)S(1)} %get-tuple-element.40.refs_3_.aug_in, bf16[4,4,256,128]{3,2,1,0:T(8,128)(2,1)S(1)} %get-tuple-element.42.after.refs_0_), custom_call_target="tpu_custom_call" | custom-call | tf_op jit(solution)/shard_map/next_panel/pallas_call | solution.py:321
  74.0 5.5 %next_panel.3.refs_4_.refs_3_.aug_in = f32[512,1024]{1,0:T(8,128)S(1)} custom-call(f32[512,1024]{1,0:T(8,128)S(1)} %next_panel.2.aug_in, bf16[4,4,256,128]{3,2,1,0:T(8,128)(2,1)S(1)} %get-tuple-element.42.after.refs_0_), custom_call_target="tpu_custom_call" | custom-call | tf_op jit(solution)/shard_map/next_panel/pallas_call | solution.py:321
  79.5 0.1 broadcast_select_fusion.2.refs_1_
  79.6 5.0 %collective-permute-start.17 = (bf16[4,4,256,128]{3,2,1,0:T(8,128)(2,1)S(1)}, bf16[4,4,256,128]{3,2,1,0:T(8,128)(2,1)S(1)}, u32[]{:S(2)}, u32[]{:S(2)}) collective-permute-start(bf16[4,4,256,128]{3,2,1,0:T(8,128)(2,1)S(1)} %broadcast_select_fusion.2.refs_1_), channel_id=1, source_target_pairs={{0,4},{8,12},{1,5},{9,13},{6,2},{14,10},{7,3},{15,11},{24,28},{16,... | collective-permute-start | bytes 3145736 | tf_op jit(solution)/shard_map/ppermute | solution.py:551
  84.6 2.8 %collective-permute-done.14.refs_2_ = bf16[4,256,128]{2,1,0:T(8,128)(2,1)S(1)} collective-permute-done((bf16[4,256,128]{2,1,0:T(8,128)(2,1)S(1)}, bf16[4,256,128]{2,1,0:T(8,128)(2,1)S(1)}, u32[]{:S(2)}, u32[]{:S(2)}) %collective-permute-start.14) | collective-permute-done | bytes 262176 | tf_op jit(solution)/shard_map/ppermute | solution.py:602
  87.4 1.4 collective-permute-done.13.refs_1_
  88.8 1.4 broadcast_select_fusion.1.refs_3_
  90.2 1.6 %collective-permute-start.18 = (bf16[4,4,256,128]{3,2,1,0:T(8,128)(2,1)S(1)}, bf16[4,4,256,128]{3,2,1,0:T(8,128)(2,1)S(1)}, u32[]{:S(2)}, u32[]{:S(2)}) collective-permute-start(bf16[4,4,256,128]{3,2,1,0:T(8,128)(2,1)S(1)} %broadcast_select_fusion.1.refs_3_), channel_id=1, source_target_pairs={{0,4},{8,12},{1,5},{9,13},{6,2},{14,10},{7,3},{15,11},{24,28},{16,... | collective-permute-start | bytes 3145736 | tf_op jit(solution)/shard_map/ppermute | solution.py:551
  91.8 0.7 assemble.3.after.own_rest
  92.5 4.8 %collective-permute-start.16 = (bf16[3,4,256,128]{3,2,1,0:T(8,128)(2,1)S(1)}, bf16[3,4,256,128]{3,2,1,0:T(8,128)(2,1)S(1)}, u32[]{:S(2)}, u32[]{:S(2)}) collective-permute-start(bf16[3,4,256,128]{3,2,1,0:T(8,128)(2,1)S(1)} %assemble.3.after.own_rest), channel_id=1, source_target_pairs={{16,0},{17,1},{18,2},{19,3},{20,4},{21,5},{22,6},{23,7},{24,8},{25... | collective-permute-start | bytes 2359304 | tf_op jit(solution)/shard_map/ppermute | solution.py:606
  97.3 6.9 %last_panel.1 = (f32[512,512]{1,0:T(8,128)S(1)}, bf16[512,512]{1,0:T(8,128)(2,1)S(1)}, bf16[512,512]{1,0:T(8,128)(2,1)S(1)}, bf16[512,512]{1,0:T(8,128)(2,1)S(1)}) custom-call(f32[512,1024]{1,0:T(8,128)S(1)} %next_panel.3.refs_4_.refs_3_.aug_in, bf16[3,4,256,128]{3,2,1,0:T(8,128)(2,1)S(1)} %assemble.3.after.own_rest), custom_call_target="tpu_custom_call" | custom-call | tf_op jit(solution)/shard_map/last_panel/pallas_call | solution.py:335
  104.3 1.0 copy-done.18
  105.3 0.3 copy-done.17
  105.6 22.0 %multiply_part.2 = (f32[4096,2048]{1,0:T(8,128)}, bf16[512,2048]{1,0:T(8,128)(2,1)}) custom-call(s32[18]{0:T(128)S(1)} %stack.80.place_ref, bf16[4,256,128]{2,1,0:T(8,128)(2,1)} %get-tuple-element.38.own_first, bf16[3,4,256,128]{3,2,1,0:T(8,128)(2,1)} %get-tuple-element.43.own_rest, bf16[2,4,256,128]{3,2,1,0:T(8,128)(2,1)S(1)} %copy-done.3, ...), custom_call_target="tpu_custom_call" | custom-call | tf_op jit(solution)/shard_map/multiply_part/pallas_call | solution.py:505
  127.6 16.2 %multiply_part.3 = f32[4096,2048]{1,0:T(8,128)} custom-call(s32[18]{0:T(128)S(1)} %stack.80.place_ref, bf16[4,256,128]{2,1,0:T(8,128)(2,1)S(1)} %get-tuple-element.36.own_first, bf16[3,4,256,128]{3,2,1,0:T(8,128)(2,1)S(1)} %assemble.3.after.own_rest, bf16[2,4,256,128]{3,2,1,0:T(8,128)(2,1)S(1)} %copy-done.3, ...), custom_call_target="tpu_custom_call", output_to_operand_aliasing={{}: (9, {})} | custom-call | tf_op jit(solution)/shard_map/multiply_part/pallas_call | solution.py:505
  (47 shorter events, 0.2 us)
Async XLA Ops:
  0.1 1.0 copy-start.11
  1.1 0.7 copy-start.12
  1.9 0.7 copy-start.13
  4.7 41.5 %collective-permute-start.8 = (bf16[2,4,256,128]{3,2,1,0:T(8,128)(2,1)S(1)}, bf16[2,4,256,128]{3,2,1,0:T(8,128)(2,1)S(1)}, u32[]{:S(2)}, u32[]{:S(2)}) collective-permute-start(bf16[2,4,256,128]{3,2,1,0:T(8,128)(2,1)S(1)} %get-tuple-element.35), channel_id=1, source_target_pairs={{16,0},{17,1},{18,2},{19,3},{20,4},{21,5},{22,6},{23,7},{24,8},{25... | collective-permute-start | bytes 1572872 | tf_op jit(solution)/shard_map/ppermute | solution.py:606
  5.9 40.3 %collective-permute-start.6 = (bf16[4,256,128]{2,1,0:T(8,128)(2,1)}, bf16[4,256,128]{2,1,0:T(8,128)(2,1)S(1)}, u32[]{:S(2)}, u32[]{:S(2)}) collective-permute-start(bf16[4,256,128]{2,1,0:T(8,128)(2,1)} %get-tuple-element.32.refs_3_), channel_id=1, source_target_pairs={{2,0},{3,1},{0,2},{1,3},{6,4},{7,5},{4,6},{5,7},{10,8},{11,9},{8,1... | collective-permute-start | bytes 786440 | tf_op jit(solution)/shard_map/ppermute | solution.py:602
  5.9 40.3 %collective-permute-start.7 = (bf16[4,256,128]{2,1,0:T(8,128)(2,1)S(1)}, bf16[4,256,128]{2,1,0:T(8,128)(2,1)S(1)}, u32[]{:S(2)}, u32[]{:S(2)}) collective-permute-start(bf16[4,256,128]{2,1,0:T(8,128)(2,1)S(1)} %get-tuple-element.31.refs_4_), channel_id=1, source_target_pairs={{1,0},{2,1},{3,2},{0,3},{5,4},{6,5},{7,6},{4,7},{9,8},{10,9},{11,1... | collective-permute-start | bytes 786440 | tf_op jit(solution)/shard_map/ppermute | solution.py:602
  6.1 40.1 %collective-permute-start.5 = (bf16[4,256,128]{2,1,0:T(8,128)(2,1)S(1)}, bf16[4,256,128]{2,1,0:T(8,128)(2,1)S(1)}, u32[]{:S(2)}, u32[]{:S(2)}) collective-permute-start(bf16[4,256,128]{2,1,0:T(8,128)(2,1)S(1)} %get-tuple-element.31.refs_4_), channel_id=1, source_target_pairs={{3,0},{0,1},{1,2},{2,3},{7,4},{4,5},{5,6},{6,7},{11,8},{8,9},{9,10... | collective-permute-start | bytes 786440 | tf_op jit(solution)/shard_map/ppermute | solution.py:602
  9.2 42.4 %copy-start.10 = (f32[16384]{0:T(1024)S(1)}, f32[16384]{0:T(1024)}, u32[]{:S(2)}) copy-start(f32[16384]{0:T(1024)} %param.11) | copy-start | bytes 196612
  9.2 42.4 %copy-start.14 = (f32[64]{0:T(128)S(1)}, f32[64]{0:T(128)}, u32[]{:S(2)}) copy-start(f32[64]{0:T(128)} %taps_ref.1) | copy-start | bytes 772
  9.3 0.7 collective-permute-start
  10.0 0.7 collective-permute-start.1
  10.7 0.7 collective-permute-start.2
  11.4 0.7 collective-permute-start.3
  13.0 33.2 %collective-permute-start.4 = (bf16[8,272,128]{2,1,0:T(8,128)(2,1)}, bf16[8,272,128]{2,1,0:T(8,128)(2,1)}, u32[]{:S(2)}, u32[]{:S(2)}) collective-permute-start(bf16[8,272,128]{2,1,0:T(8,128)(2,1)} %pad_maximum_fusion), channel_id=1, source_target_pairs={{0,4},{8,12},{1,5},{9,13},{2,6},{10,14},{3,7},{11,15},{16,20},{24,... | collective-permute-start | bytes 1671176 | tf_op jit(solution)/shard_map/cond/branch_1_fun/ppermute | solution.py:573
  46.2 1.8 %copy-start.2 = (bf16[2,4,256,128]{3,2,1,0:T(8,128)(2,1)}, bf16[2,4,256,128]{3,2,1,0:T(8,128)(2,1)S(1)}, u32[]{:S(2)}) copy-start(bf16[2,4,256,128]{3,2,1,0:T(8,128)(2,1)S(1)} %collective-permute-done.8.refs_6_.other_first) | copy-start | bytes 1572868
  48.0 15.6 %copy-start.6 = (bf16[4,4,256,128]{3,2,1,0:T(8,128)(2,1)}, bf16[4,4,256,128]{3,2,1,0:T(8,128)(2,1)S(1)}, u32[]{:S(2)}) copy-start(bf16[4,4,256,128]{3,2,1,0:T(8,128)(2,1)S(1)} %get-tuple-element.37.after) | copy-start | bytes 3145732
  48.0 15.5 %collective-permute-start.10 = (bf16[4,4,256,128]{3,2,1,0:T(8,128)(2,1)S(1)}, bf16[4,4,256,128]{3,2,1,0:T(8,128)(2,1)S(1)}, u32[]{:S(2)}, u32[]{:S(2)}) collective-permute-start(bf16[4,4,256,128]{3,2,1,0:T(8,128)(2,1)S(1)} %get-tuple-element.37.after), channel_id=1, source_target_pairs={{0,8},{1,9},{6,14},{7,15},{24,16},{25,17},{30,22},{31,23}} | collective-permute-start | bytes 3145736 | tf_op jit(solution)/shard_map/ppermute | solution.py:551
  49.3 14.2 %collective-permute-start.9 = (bf16[4,4,256,128]{3,2,1,0:T(8,128)(2,1)S(1)}, bf16[4,4,256,128]{3,2,1,0:T(8,128)(2,1)S(1)}, u32[]{:S(2)}, u32[]{:S(2)}) collective-permute-start(bf16[4,4,256,128]{3,2,1,0:T(8,128)(2,1)S(1)} %get-tuple-element.37.after), channel_id=1, source_target_pairs={{16,0},{17,1},{22,6},{23,7},{8,24},{9,25},{14,30},{15,31}} | collective-permute-start | bytes 3145736 | tf_op jit(solution)/shard_map/ppermute | solution.py:606
  51.6 9.0 %collective-permute-start.11 = (bf16[4,256,128]{2,1,0:T(8,128)(2,1)}, bf16[4,256,128]{2,1,0:T(8,128)(2,1)S(1)}, u32[]{:S(2)}, u32[]{:S(2)}) collective-permute-start(bf16[4,256,128]{2,1,0:T(8,128)(2,1)} %get-tuple-element.38.own_first), channel_id=1, source_target_pairs={{3,0},{0,1},{1,2},{2,3},{7,4},{4,5},{5,6},{6,7},{11,8},{8,9},{9,10... | collective-permute-start | bytes 786440 | tf_op jit(solution)/shard_map/ppermute | solution.py:602
  60.6 3.0 %copy-start = (bf16[2,2,640,256]{3,2,1,0:T(8,128)(2,1)}, bf16[2,2,640,256]{3,2,1,0:T(8,128)(2,1)S(1)}, u32[]{:S(2)}) copy-start(bf16[2,2,640,256]{3,2,1,0:T(8,128)(2,1)S(1)} %get-tuple-element.46.band_ref) | copy-start | bytes 3932164
  63.5 1.0 copy-start.4
  64.5 0.7 copy-start.8
  65.2 23.6 %collective-permute-start.12 = (bf16[4,4,256,128]{3,2,1,0:T(8,128)(2,1)S(1)}, bf16[4,4,256,128]{3,2,1,0:T(8,128)(2,1)}, u32[]{:S(2)}, u32[]{:S(2)}) collective-permute-start(bf16[4,4,256,128]{3,2,1,0:T(8,128)(2,1)S(1)} %get-tuple-element.42.after.refs_0_), channel_id=1, source_target_pairs={{0,8},{1,9},{6,14},{7,15},{24,16},{25,17},{30,22},{31,23}} | collective-permute-start | bytes 3145736 | tf_op jit(solution)/shard_map/ppermute | solution.py:551
  66.5 22.3 %collective-permute-start.13 = (bf16[3,4,256,128]{3,2,1,0:T(8,128)(2,1)}, bf16[3,4,256,128]{3,2,1,0:T(8,128)(2,1)}, u32[]{:S(2)}, u32[]{:S(2)}) collective-permute-start(bf16[3,4,256,128]{3,2,1,0:T(8,128)(2,1)} %get-tuple-element.43.own_rest), channel_id=1, source_target_pairs={{18,2},{19,3},{20,4},{21,5},{24,8},{25,9},{26,10},{27,11},{28,12},... | collective-permute-start | bytes 2359304 | tf_op jit(solution)/shard_map/ppermute | solution.py:606
  67.8 19.6 %collective-permute-start.15 = (bf16[4,256,128]{2,1,0:T(8,128)(2,1)}, bf16[4,256,128]{2,1,0:T(8,128)(2,1)S(1)}, u32[]{:S(2)}, u32[]{:S(2)}) collective-permute-start(bf16[4,256,128]{2,1,0:T(8,128)(2,1)} %get-tuple-element.38.own_first), channel_id=1, source_target_pairs={{1,0},{2,1},{3,2},{0,3},{5,4},{6,5},{7,6},{4,7},{9,8},{10,9},{11,1... | collective-permute-start | bytes 786440 | tf_op jit(solution)/shard_map/ppermute | solution.py:602
  68.1 19.3 %collective-permute-start.14 = (bf16[4,256,128]{2,1,0:T(8,128)(2,1)S(1)}, bf16[4,256,128]{2,1,0:T(8,128)(2,1)S(1)}, u32[]{:S(2)}, u32[]{:S(2)}) collective-permute-start(bf16[4,256,128]{2,1,0:T(8,128)(2,1)S(1)} %get-tuple-element.36.own_first), channel_id=1, source_target_pairs={{2,0},{3,1},{0,2},{1,3},{6,4},{7,5},{4,6},{5,7},{10,8},{11,9},{8,1... | collective-permute-start | bytes 786440 | tf_op jit(solution)/shard_map/ppermute | solution.py:602
  74.0 5.5 %copy-start.5 = (bf16[4,4,256,128]{3,2,1,0:T(8,128)(2,1)S(1)}, bf16[4,4,256,128]{3,2,1,0:T(8,128)(2,1)}, u32[]{:S(2)}) copy-start(bf16[4,4,256,128]{3,2,1,0:T(8,128)(2,1)} %copy-done.4) | copy-start | bytes 3145732
  74.0 5.5 %copy-start.7 = (bf16[4,4,256,128]{3,2,1,0:T(8,128)(2,1)S(1)}, bf16[4,4,256,128]{3,2,1,0:T(8,128)(2,1)}, u32[]{:S(2)}) copy-start(bf16[4,4,256,128]{3,2,1,0:T(8,128)(2,1)} %copy-done.6) | copy-start | bytes 3145732
  79.6 9.2 %copy-start.15 = (bf16[4,4,256,128]{3,2,1,0:T(8,128)(2,1)}, bf16[4,4,256,128]{3,2,1,0:T(8,128)(2,1)S(1)}, u32[]{:S(2)}) copy-start(bf16[4,4,256,128]{3,2,1,0:T(8,128)(2,1)S(1)} %broadcast_select_fusion.2.refs_1_) | copy-start | bytes 3145732
  79.6 24.6 %collective-permute-start.17 = (bf16[4,4,256,128]{3,2,1,0:T(8,128)(2,1)S(1)}, bf16[4,4,256,128]{3,2,1,0:T(8,128)(2,1)S(1)}, u32[]{:S(2)}, u32[]{:S(2)}) collective-permute-start(bf16[4,4,256,128]{3,2,1,0:T(8,128)(2,1)S(1)} %broadcast_select_fusion.2.refs_1_), channel_id=1, source_target_pairs={{0,4},{8,12},{1,5},{9,13},{6,2},{14,10},{7,3},{15,11},{24,28},{16,... | collective-permute-start | bytes 3145736 | tf_op jit(solution)/shard_map/ppermute | solution.py:551
  88.8 3.0 %copy-start.9 = (bf16[4,256,128]{2,1,0:T(8,128)(2,1)S(1)}, bf16[4,256,128]{2,1,0:T(8,128)(2,1)}, u32[]{:S(2)}) copy-start(bf16[4,256,128]{2,1,0:T(8,128)(2,1)} %copy-done.8) | copy-start | bytes 786436
  90.2 14.1 %copy-start.16 = (bf16[4,4,256,128]{3,2,1,0:T(8,128)(2,1)}, bf16[4,4,256,128]{3,2,1,0:T(8,128)(2,1)S(1)}, u32[]{:S(2)}) copy-start(bf16[4,4,256,128]{3,2,1,0:T(8,128)(2,1)S(1)} %broadcast_select_fusion.1.refs_3_) | copy-start | bytes 3145732
  90.2 14.1 %collective-permute-start.18 = (bf16[4,4,256,128]{3,2,1,0:T(8,128)(2,1)S(1)}, bf16[4,4,256,128]{3,2,1,0:T(8,128)(2,1)S(1)}, u32[]{:S(2)}, u32[]{:S(2)}) collective-permute-start(bf16[4,4,256,128]{3,2,1,0:T(8,128)(2,1)S(1)} %broadcast_select_fusion.1.refs_3_), channel_id=1, source_target_pairs={{0,4},{8,12},{1,5},{9,13},{6,2},{14,10},{7,3},{15,11},{24,28},{16,... | collective-permute-start | bytes 3145736 | tf_op jit(solution)/shard_map/ppermute | solution.py:551
  92.5 13.1 %copy-start.3 = (bf16[2,4,256,128]{3,2,1,0:T(8,128)(2,1)S(1)}, bf16[2,4,256,128]{3,2,1,0:T(8,128)(2,1)}, u32[]{:S(2)}) copy-start(bf16[2,4,256,128]{3,2,1,0:T(8,128)(2,1)} %copy-done.2) | copy-start | bytes 1572868
  92.5 35.1 %collective-permute-start.16 = (bf16[3,4,256,128]{3,2,1,0:T(8,128)(2,1)S(1)}, bf16[3,4,256,128]{3,2,1,0:T(8,128)(2,1)S(1)}, u32[]{:S(2)}, u32[]{:S(2)}) collective-permute-start(bf16[3,4,256,128]{3,2,1,0:T(8,128)(2,1)S(1)} %assemble.3.after.own_rest), channel_id=1, source_target_pairs={{16,0},{17,1},{18,2},{19,3},{20,4},{21,5},{22,6},{23,7},{24,8},{25... | collective-permute-start | bytes 2359304 | tf_op jit(solution)/shard_map/ppermute | solution.py:606
  104.3 1.3 copy-start.17
  104.3 1.0 copy-start.18
  105.6 22.0 %copy-start.1 = (bf16[2,2,640,256]{3,2,1,0:T(8,128)(2,1)S(1)}, bf16[2,2,640,256]{3,2,1,0:T(8,128)(2,1)}, u32[]{:S(2)}) copy-start(bf16[2,2,640,256]{3,2,1,0:T(8,128)(2,1)} %copy-done) | copy-start | bytes 3932164

commit v5 on v4

v5 whole, which is shorter than its diff:
```python
import functools

import jax
import jax.numpy as jnp
from jax import lax
from jax.experimental import pallas as pl
from jax.experimental.pallas import tpu as pltpu
from jax.sharding import PartitionSpec as P

PANEL = 256
SECTIONS = 2
HEAD = PANEL * SECTIONS
PB = 128
LANES = 128
BLOCK = 128
HALF = 256
SUB = 8
NOTE = 16
EXACT = lax.Precision.HIGHEST
F32 = jnp.float32
BF16 = jnp.bfloat16


def iota(shape, axis):
    return lax.broadcasted_iota(jnp.int32, shape, axis)


def dot(left, right, contract=((1,), (0,)), precision=None):
    return lax.dot_general(
        left, right, (contract, ((), ())), preferred_element_type=F32, precision=precision
    )


NT = ((1,), (1,))
TN = ((0,), (0,))
VMEM = pl.BlockSpec(memory_space=pltpu.VMEM)
SMEM = pl.BlockSpec(memory_space=pltpu.SMEM)
ANY = pl.BlockSpec(memory_space=pl.ANY)
FREE = pl.CostEstimate(flops=0, bytes_accessed=0, transcendentals=0)
LIMIT = pltpu.CompilerParams(vmem_limit_bytes=48 << 20)


def permute_kernel(place_ref, *refs):
    sources, refs = refs[:3], refs[3:]
    all_ref, note_ref = refs[:-4]
    order_ref, counts_ref, design_ref = targets = refs[-4:-1]
    copies = [
        pltpu.make_async_copy(source, target, refs[-1].at[n])
        for n, (source, target) in enumerate(zip(sources, targets))
    ]
    for copy in copies:
        copy.start()
    for copy in copies:
        copy.wait()
    epochs = design_ref.shape[0]
    parts, per_part = all_ref.shape[:2]
    lane = iota((PB, PB), 1).astype(F32)
    none = jnp.zeros((epochs, PB), BF16)
    groups = 2 * HALF // PB

    def packed(local, columns, block, part):
        first = block * groups + part
        second = first + HALF // PB
        pick = [jnp.where(local[:, g : g + 1] == lane, 1.0, 0.0) for g in (first, second)]
        pick = jnp.concatenate(pick, axis=1).astype(BF16)
        top = jnp.concatenate([columns(first), none], axis=1)
        low = jnp.concatenate([none, columns(second)], axis=1)
        return dot(pick, jnp.concatenate([top, low], axis=0), NT).astype(BF16)

    def order_of(rows):
        return (order_ref[rows, :] & (PB - 1)).astype(F32).T

    local = order_of(slice(0, per_part * groups))
    for part in range(HALF // PB):
        columns = lambda g: design_ref[:, g * PB : (g + 1) * PB]
        note_ref[0, part * PB : (part + 1) * PB, :] = packed(local, columns, 0, part)
    counts = counts_ref[...].astype(F32)
    counts = jnp.concatenate([counts] * (LANES // epochs), axis=1)
    note_ref[0, HALF:, :] = jnp.broadcast_to(counts, (NOTE, LANES)).astype(BF16)
    for j in range(parts):
        at = j * per_part * groups
        local = order_of(slice(at, at + per_part * groups))
        columns = lambda g: design_ref[:, (at + g) * PB : (at + g + 1) * PB]
        for block in range(per_part):
            for part in range(HALF // PB):
                rows = slice(part * PB, (part + 1) * PB)
                all_ref[j, block, rows, :] = packed(local, columns, block, part)


def permute_local(place, design, order, tap_count, cols_dev):
    epochs, rows = design.shape
    parts, per_part = rows // cols_dev, cols_dev // (2 * HALF)
    piece = jax.ShapeDtypeStruct((parts, per_part, HALF, LANES), BF16)
    note = jax.ShapeDtypeStruct((1, HALF + NOTE, LANES), BF16)
    return pl.pallas_call(
        permute_kernel,
        out_shape=(piece, note),
        in_specs=[SMEM] + [ANY] * 3,
        out_specs=(VMEM,) * 2,
        scratch_shapes=[
            pltpu.VMEM((rows // PB, PB), jnp.int32),
            pltpu.VMEM((1, epochs), jnp.int32),
            pltpu.VMEM((epochs, rows), BF16),
            pltpu.SemaphoreType.DMA((3,)),
        ],
        compiler_params=LIMIT,
        name="permute_local",
    )(place, order.reshape(rows // PB, PB), tap_count.reshape(1, epochs), design)


PLACE_ROW, PLACE_GROUP, PLACE_EP, PLACE_COL, PLACE_TAKES = range(5)


def separate_kernel(place_ref, all_ref, after, *refs):
    del after
    *part_refs, wanted_ref, sem = refs
    parts = len(part_refs)
    copies = [
        pltpu.make_async_copy(all_ref.at[n, j], part_refs[j].at[n], sem.at[n, j])
        for j in range(parts)
        for n in range(all_ref.shape[0])
    ]
    for copy in copies:
        copy.start()
    for j in range(parts):

        @pl.when(lax.rem(place_ref[PLACE_COL], parts) == j)
        def _():
            again = [
                pltpu.make_async_copy(all_ref.at[n, j], wanted_ref.at[n], sem.at[n, parts])
                for n in range(all_ref.shape[0])
            ]
            for copy in again:
                copy.start()
            for copy in again:
                copy.wait()

    for copy in copies:
        copy.wait()


def separate(place, gathered, after):
    width, parts = gathered.shape[:2]
    part = jax.ShapeDtypeStruct((width,) + gathered.shape[2:], BF16)
    *column, wanted = pl.pallas_call(
        separate_kernel,
        out_shape=(part,) * (parts + 1),
        in_specs=[SMEM, ANY, ANY],
        out_specs=(ANY,) * (parts + 1),
        scratch_shapes=[pltpu.SemaphoreType.DMA((width, parts + 1))],
        compiler_params=LIMIT,
        cost_estimate=FREE,
        name="separate",
    )(place, gathered, after)
    return column, wanted


def gate(arrays, after):
    count = len(arrays)
    return pl.pallas_call(
        lambda *refs: None,
        out_shape=tuple(jax.ShapeDtypeStruct(x.shape, x.dtype) for x in arrays),
        in_specs=[ANY] * (count + 1),
        out_specs=(ANY,) * count,
        input_output_aliases={n: n for n in range(count)},
        compiler_params=LIMIT,
        cost_estimate=FREE,
        name="gate",
    )(*arrays, after)


def filter_rows(blocks, band_ref, store):
    for b in range(band_ref.shape[0]):
        first = max(2 * b - 1, 0)
        skip = 0 if b else LANES
        packed = jnp.concatenate([blocks(e) for e in range(first, 2 * b + 2)], axis=1)
        got = dot(packed, band_ref[b, skip:, :]).astype(BF16)
        for half in range(2):
            across = slice(half * LANES, (half + 1) * LANES)
            store(slice(half * HALF, (half + 1) * HALF), slice(b * LANES, (b + 1) * LANES), got[:, across])


def spread(tile, lane):
    return jnp.broadcast_to(tile[:, lane : lane + 1], (SUB, tile.shape[1]))


def row_of(tile, k):
    return jnp.broadcast_to(tile[k : k + 1, :], (SUB, tile.shape[1]))


def factor_block(work):
    groups = BLOCK // SUB
    sub, lane = iota((SUB, BLOCK), 0), iota((SUB, BLOCK), 1)
    tiles = [work[g * SUB : (g + 1) * SUB, :] for g in range(groups)]
    for g in range(groups):
        inside = (lane >= g * SUB) & (lane < (g + 1) * SUB)
        cols = [spread(tiles[g], g * SUB + j) for j in range(SUB)]
        a = {(i, j): row_of(cols[j], i) for j in range(SUB) for i in range(j, SUB)}
        own = jnp.where(inside, jnp.where(lane - g * SUB == sub, 1.0, 0.0), tiles[g])
        u = [row_of(own, k) for k in range(SUB)]
        inv = []
        low = {}
        for k in range(SUB):
            r = lax.rsqrt(a[k, k])
            inv.append(r)
            for i in range(k + 1, SUB):
                low[i, k] = a[i, k] * r
            for j in range(k + 1, SUB):
                for i in range(j, SUB):
                    a[i, j] = a[i, j] - low[i, k] * low[j, k]
            u[k] = u[k] * r
            for j in range(k + 1, SUB):
                u[j] = u[j] - low[j, k] * u[k]
        for t in range(g + 1, groups):
            left = [spread(tiles[t], g * SUB + j) for j in range(SUB)]
            tile = jnp.where(inside, 0.0, tiles[t])
            for k in range(SUB):
                left[k] = left[k] * inv[k]
                for j in range(k + 1, SUB):
                    left[j] = left[j] - low[j, k] * left[k]
                tile = tile - left[k] * u[k]
            tiles[t] = tile
        merged = u[0]
        for k in range(1, SUB):
            merged = jnp.where(sub == k, u[k], merged)
        work[g * SUB : (g + 1) * SUB, :] = jnp.where(lane < (g + 1) * SUB, merged, 0.0)


def start_kernel(
    chain, place_ref, taps_ref, own_ref, came_ref, reg_ref, band_ref, taper_ref, aug_ref, notes, a1,
    work,
):
    epochs = aug_ref.shape[1] - HEAD
    half = LANES // 2

    @pl.when(place_ref[0] % 2 == 0)
    def _():
        for rel in range(own_ref.shape[0]):
            notes[place_ref[chain + rel]] = own_ref[rel]

    @pl.when(place_ref[0] % 2 == 1)
    def _():
        for rel in range(own_ref.shape[0]):
            notes[place_ref[chain + rel]] = came_ref[rel]

    shape = (half, LANES)
    lag = iota(shape, 1) - iota(shape, 0)
    base = lax.fori_loop(
        0,
        taps_ref.shape[0],
        lambda k, kept: jnp.where(lag == k, taps_ref[k], kept),
        jnp.zeros(shape, F32),
    )
    lane = iota(shape, 1)
    swapped = jnp.concatenate([base[:, half:], base[:, :half]], axis=1)
    patterns = (jnp.where(lane < half, swapped, 0.0), base, jnp.where(lane >= half, swapped, 0.0))
    row = iota((1, LANES), 1)
    sources = epochs // half
    counts = [notes[e, HALF : HALF + NOTE, :].astype(F32)[:1] for e in range(sources)]
    counts.append(jnp.zeros_like(counts[0]))
    band_ref[...] = jnp.zeros_like(band_ref)
    for e in range(sources):
        limit = jnp.where(row < half, counts[e], counts[e + 1])
        taper_ref[e] = jnp.where(lag.astype(F32) < limit, base, 0.0).astype(BF16)
    for b in range(epochs // LANES):
        limit = jnp.where(row < half, counts[2 * b], counts[2 * b + 1])
        for j, pattern in enumerate(patterns):
            at = (lag + half - half * j).astype(F32)
            kept = jnp.where(at < limit, pattern, 0.0).astype(BF16)
            for h in range(2):
                rows = slice(j * LANES + h * half, j * LANES + (h + 1) * half)
                band_ref[b, rows, h * LANES : (h + 1) * LANES] = kept

    def store(rows, cols, got):
        a1[rows, cols] = got

    filter_rows(lambda e: notes[e, :HALF, :], band_ref, store)
    columns = a1[...]
    square = (HEAD, HEAD)
    on_diagonal = iota(square, 0) == iota(square, 1)
    aug_ref[:, :HEAD] = dot(columns, columns, NT) + jnp.where(on_diagonal, reg_ref[:, :HEAD], 0.0)
    aug_ref[:, HEAD:] = columns.astype(F32)
    eliminate(aug_ref, 0, work)


def eliminate(aug, kb, work):
    here = slice(kb * BLOCK, (kb + 1) * BLOCK)
    work[...] = aug[here, here]
    factor_block(work)
    rest = slice(kb * BLOCK, aug.shape[1])
    aug[here, rest] = dot(work[...], aug[here, rest], precision=EXACT)
    for rb in range(kb + 1, HEAD // BLOCK):
        below = slice(rb * BLOCK, (rb + 1) * BLOCK)
        rest = slice(rb * BLOCK, aug.shape[1])
        aug[below, rest] -= dot(aug[here, below], aug[here, rest], TN, precision=EXACT)


def next_kernel(kb, aug_in, after, aug_ref, work):
    del after
    aug_ref[...] = aug_in[...]
    eliminate(aug_ref, kb, work)


def last_kernel(kb, aug_in, after, taper_ref, factor_ref, w_ref, high_ref, low_ref, aug, work, high, low):
    del after
    aug[...] = aug_in[...]
    eliminate(aug, kb, work)
    square = (HEAD, HEAD)
    epochs = aug.shape[1] - HEAD
    factor_ref[...] = jnp.where(iota(square, 0) >= iota(square, 1), aug[:, :HEAD].T, 0.0)
    wt = aug[:, HEAD:]

    def keep(rows, cols, values):
        top = values.astype(BF16)
        high[rows, cols] = top
        low[rows, cols] = (values - top.astype(F32)).astype(BF16)

    keep(slice(None), slice(epochs, None), wt.T)
    for b in range(epochs // BLOCK):
        here = slice(b * BLOCK, (b + 1) * BLOCK)
        shape = (BLOCK, epochs)
        unit = jnp.where(iota(shape, 0) + b * BLOCK == iota(shape, 1), 1.0, 0.0)
        keep(here, slice(0, epochs), unit - dot(wt[:, here], wt, TN, precision=EXACT))
    count, half = taper_ref.shape[:2]
    for e in range(count):
        reach = min(LANES, epochs - e * half)
        rows = slice(e * half, e * half + reach)
        taper = taper_ref[e, :, :reach]
        got = dot(taper, high[rows, :]) + dot(taper, low[rows, :])
        here = slice(e * half, (e + 1) * half)
        w_ref[here, :] = got[:, epochs:].astype(BF16)
        top = got[:, :epochs].astype(BF16)
        high_ref[here, :] = top
        low_ref[here, :] = (got[:, :epochs] - top.astype(F32)).astype(BF16)


def start_panel(place, chain, taps, own, came, regular):
    epochs = own.shape[0] * (LANES // 2)
    half = LANES // 2
    return pl.pallas_call(
        functools.partial(start_kernel, chain),
        out_shape=(
            jax.ShapeDtypeStruct((epochs // LANES, 3 * LANES, 2 * LANES), BF16),
            jax.ShapeDtypeStruct((epochs // half, half, LANES), BF16),
            jax.ShapeDtypeStruct((HEAD, HEAD + epochs), F32),
        ),
        in_specs=[SMEM, SMEM, VMEM, VMEM, VMEM],
        out_specs=(VMEM,) * 3,
        scratch_shapes=[
            pltpu.VMEM(own.shape, BF16),
            pltpu.VMEM((HEAD, epochs), BF16),
            pltpu.VMEM((BLOCK, BLOCK), F32),
        ],
        compiler_params=LIMIT,
        cost_estimate=FREE,
        name="start_panel",
    )(place, taps, own, came, regular.reshape(1, -1))


def next_panel(kb, aug, after):
    return pl.pallas_call(
        functools.partial(next_kernel, kb),
        out_shape=jax.ShapeDtypeStruct(aug.shape, F32),
        in_specs=[VMEM, ANY],
        out_specs=VMEM,
        scratch_shapes=[pltpu.VMEM((BLOCK, BLOCK), F32)],
        compiler_params=LIMIT,
        cost_estimate=FREE,
        name="next_panel",
    )(aug, after)


def last_panel(kb, aug, after, taper):
    epochs = aug.shape[1] - HEAD
    return pl.pallas_call(
        functools.partial(last_kernel, kb),
        out_shape=(
            jax.ShapeDtypeStruct((HEAD, HEAD), F32),
            jax.ShapeDtypeStruct((epochs, HEAD), BF16),
            jax.ShapeDtypeStruct((epochs, epochs), BF16),
            jax.ShapeDtypeStruct((epochs, epochs), BF16),
        ),
        in_specs=[VMEM, ANY, VMEM],
        out_specs=(VMEM,) * 4,
        scratch_shapes=[
            pltpu.VMEM(aug.shape, F32),
            pltpu.VMEM((BLOCK, BLOCK), F32),
            pltpu.VMEM((epochs, epochs + HEAD), BF16),
            pltpu.VMEM((epochs, epochs + HEAD), BF16),
        ],
        compiler_params=LIMIT,
        cost_estimate=FREE,
        name="last_panel",
    )(aug, after, taper)


def shards_of(ref, block):
    return [ref.at[n, block] for n in range(ref.shape[0])]


def unpack(place_ref, own, other, blocks):
    width = len(own)
    here = place_ref[PLACE_EP] * width
    there = width - here
    for n in range(width):
        blocks[here + n] = own[n][...]
        blocks[there + n] = other[n][...]


def choose(condition, yes, no):
    pl.when(condition)(yes)
    pl.when(jnp.logical_not(condition))(no)


def fixed(array):
    return pl.BlockSpec(
        array.shape, lambda i, place: (0,) * array.ndim, pipeline_mode=pl.Buffered(1)
    )


def tile_kernel(part, parts, place_ref, left_ref, *refs):
    if part == 0:
        own, own_came, other, other_came, w_ref, high_ref, low_ref, band_ref = refs[:8]
        factor_ref, reg_ref, out_ref, right_ref, lhs, columns, blocks = refs[8:]
    else:
        right_ref, _, factor_ref, reg_ref, out_ref, lhs = refs
    i, steps = pl.program_id(0), pl.num_programs(0)
    rows, cols = out_ref.shape
    half = LANES // 2
    block = part * steps + i
    first_row = (place_ref[PLACE_ROW] * parts * steps + block) * rows
    first_col = place_ref[PLACE_GROUP] * cols

    if part == 0:

        @pl.when(i == 0)
        def _():
            def store(rows, cols, got):
                columns[rows, cols] = got

            for n in range(cols // rows):
                choose(
                    place_ref[PLACE_TAKES] != 0,
                    lambda: unpack(place_ref, shards_of(own_came, n), shards_of(other_came, n), blocks),
                    lambda: unpack(place_ref, shards_of(own, n), shards_of(other, n), blocks),
                )
                filter_rows(lambda e: blocks[e], band_ref, store)
                wanted = columns[...]
                projected = dot(high_ref[...], wanted, NT) + dot(low_ref[...], wanted, NT)
                right_ref[:, n * rows : (n + 1) * rows] = projected.astype(BF16)

            @pl.when(first_col == 0)
            def _():
                right_ref[:, :HEAD] = w_ref[...]

    @pl.when(first_row >= HEAD)
    def _():
        eps, width = left_ref.shape[:2]
        sources = [left_ref.at[e, n, 0] for e in range(eps) for n in range(width)]
        for pair in range(lhs.shape[1] // LANES):
            even, odd = sources[2 * pair][...], sources[2 * pair + 1][...]
            across = slice(pair * LANES, (pair + 1) * LANES)
            lhs[:HALF, across] = jnp.concatenate([even[:, :half], odd[:, :half]], axis=1)
            lhs[HALF:, across] = jnp.concatenate([even[:, half:], odd[:, half:]], axis=1)
        out_ref[...] = dot(lhs[...], right_ref[...])

        @pl.when((first_row >= first_col) & (first_row < first_col + cols))
        def _():
            at = pl.multiple_of(first_row - first_col, rows)
            on_diagonal = iota((rows, rows), 0) == iota((rows, rows), 1)
            out_ref[:, pl.ds(at, rows)] += jnp.where(on_diagonal, reg_ref[...], 0.0)

    @pl.when(first_row < HEAD)
    def _():
        out_ref[...] = jnp.zeros_like(out_ref)

        @pl.when(first_col == 0)
        def _():
            out_ref[:, :HEAD] = factor_ref[...]


def multiply_part(part, parts, place, left, factor, regular, extra, out, right):
    eps, width, steps = left.shape[:3]
    rows = 2 * HALF
    cols = steps * rows
    epochs = eps * width * (LANES // 2)

    def reg_block(i, place):
        return 0, (place[PLACE_ROW] * parts + part) * steps + i

    def out_block(i, place):
        return part * steps + i, 0

    out_shape = [jax.ShapeDtypeStruct((parts * steps * rows, cols), F32)]
    out_specs = [pl.BlockSpec((rows, cols), out_block)]
    scratch = [pltpu.VMEM((rows, epochs), BF16)]
    operands = [left]
    in_specs = [
        pl.BlockSpec((eps, width, 1, HALF, LANES), lambda i, place: (0, 0, i, 0, 0)),
    ]
    if part == 0:
        operands += extra
        in_specs += [fixed(array) for array in extra]
        out_shape.append(jax.ShapeDtypeStruct((epochs, cols), BF16))
        out_specs.append(pl.BlockSpec((epochs, cols), lambda i, place: (0, 0)))
        scratch.append(pltpu.VMEM((rows, epochs), BF16))
        scratch.append(pltpu.VMEM((eps * width, HALF, LANES), BF16))
    else:
        operands += [right, out]
        in_specs += [fixed(right), ANY]
    alias = {len(operands): 0} if part else {}
    operands += [factor, regular.reshape(1, -1)]
    in_specs += [fixed(factor), pl.BlockSpec((1, rows), reg_block)]
    return pl.pallas_call(
        functools.partial(tile_kernel, part, parts),
        out_shape=out_shape,
        grid_spec=pltpu.PrefetchScalarGridSpec(
            num_scalar_prefetch=1,
            grid=(steps,),
            in_specs=in_specs,
            out_specs=out_specs,
            scratch_shapes=scratch,
        ),
        input_output_aliases=alias,
        compiler_params=pltpu.CompilerParams(vmem_limit_bytes=48 << 20),
        cost_estimate=FREE,
        name="multiply_part",
    )(place, *operands)


AXES = ("ep", "row", "col")


def sizes():
    return tuple(lax.axis_size(axis) for axis in AXES)


def flat(ep, row, col):
    _, rows, cols = sizes()
    return (ep * rows + row) * cols + col


def doubling(count, least):
    distances = []
    distance = count // 2
    while distance >= least:
        distances.append(distance)
        distance //= 2
    return distances


def spread_step(block, owner_of, distance):
    eps, rows, cols = sizes()
    route = []
    for e in range(eps):
        for c in range(cols):
            for other in range(0, rows, 2 * distance):
                source = owner_of(e, c) ^ other
                route.append((flat(e, source, c), flat(e, source ^ distance, c)))
    return lax.ppermute(block, AXES, route)


def panel_steps():
    eps, _, cols = sizes()
    return [(de, dc) for de in range(eps) for dc in range(cols)]


def gather_panel(note):
    eps, rows, cols = sizes()
    row = lax.axis_index("row")
    for distance in doubling(rows, 2):
        came = spread_step(note, lambda e, c: 0, distance)
        note = jnp.where((row & (2 * distance - 1)) == distance, came, note)
    notes = [note]
    for de, dc in panel_steps()[1:]:
        route = [
            (flat(e, r, c), flat((e + de) % eps, r, (c + dc) % cols))
            for e in range(eps)
            for r in range(0, rows, 2)
            for c in range(cols)
        ]
        notes.append(lax.ppermute(note, AXES, route))
    notes = jnp.concatenate(notes)
    came = lax.ppermute(notes, "row", [(r, r + 1) for r in range(0, rows, 2)])
    return notes, came


def on_device(design, taps, tap_count, order, regular):
    rows_dev = design.shape[1]
    eps, rows, cols = sizes()
    cols_dev = regular.shape[0] // (eps * cols)
    parts = rows_dev // cols_dev
    row, ep, col = (lax.axis_index(axis) for axis in ("row", "ep", "col"))
    group = lax.axis_index(("ep", "col"))
    everywhere = [(e, r, c) for e in range(eps) for r in range(rows) for c in range(cols)]
    owner = lambda e, c: (e * cols + c) * cols_dev // rows_dev
    inside = lambda r, c: c // parts == (r * parts % cols) // parts
    owns = lambda e, r, c: inside(r, c) and r * parts // cols == e
    first_owner = group * cols_dev // rows_dev
    takes = ((row ^ first_owner) & 1) == 1
    place = [row, group, ep, col, takes]
    chain = len(place)
    place += [((ep - de) % eps) * cols + (col - dc) % cols for de, dc in panel_steps()]
    place = jnp.stack([jnp.asarray(p, jnp.int32) for p in place])

    local, note = permute_local(place, design, order, tap_count, cols_dev)

    def across(block, wanted):
        route = [(flat(1 - e, r, c), flat(e, r, c)) for e, r, c in everywhere if wanted(e, r, c)]
        return lax.ppermute(block, AXES, route)

    distances = doubling(rows, 1)

    def spread_rest(block, got):
        for n, distance in enumerate(distances[1:]):
            hit = ((row ^ first_owner) & (4 * distance - 1)) == 2 * distance
            block = jnp.where(hit, got, block)
            got = spread_step(block, owner, distance)
        return block, got

    gathered = lax.all_gather(local, "col", axis=0)
    notes, came = gather_panel(note)
    band, taper, aug = start_panel(place, chain, taps, notes, came, regular)
    column, mine = separate(place, gathered, aug)
    theirs = across(mine, owns)
    own_got = spread_step(mine, owner, distances[0])
    rows_of = [lax.all_gather(part, "ep", axis=0) for part in column]
    aug = next_panel(1, aug, mine)
    aug = next_panel(2, aug, mine)
    theirs, own_got = gate([theirs, own_got], aug)
    other_got = spread_step(theirs, owner, distances[0])
    own_block, own_came = spread_rest(mine, own_got)
    factor, w, high, low = last_panel(3, aug, theirs, taper)
    (other_got,) = gate([other_got], factor)
    other_block, other_came = spread_rest(theirs, other_got)
    extra = [own_block, own_came, other_block, other_came, w, high, low, band]
    out, right = multiply_part(
        0, parts, place, rows_of[0], factor, regular, extra, None, None
    )
    for j in range(1, parts):
        (out,) = multiply_part(
            j, parts, place, rows_of[j], factor, regular, None, out, right
        )
    return out


def solution(mesh):
    in_specs = (P(("ep", "col"), "row"), P(), P(("ep", "col")), P("row"), P())
    out_specs = P("row", ("ep", "col"))
    return jax.shard_map(
        on_device, mesh=mesh, in_specs=in_specs, out_specs=out_specs, check_vma=False
    )
```

time: 145 us -> 179 us (1.23)
  the two profiles are of different devices: /device:TPU:29 before, /device:TPU:0 now
where the time goes in v5:
time: 179 us; the launch traced here: 178 us
  Pallas kernels  53.5 us (30%)
  waiting for transfers between devices  47.7 us (27%)
  starting transfers between devices  42.5 us (24%)
  local copies, waits for them, and re-layouts  19 us (11%)
  between operations  13.5 us (8%)
    ppermute x1, waiting for transfers between devices, across(): return lax.ppermute(block, AXES, route)  24.6 us
    ppermute x7, starting transfers between devices, gather_panel(): notes.append(lax.ppermute(note, AXES, route))  23.7 us
    pallas_call x2, Pallas kernels, multiply_part(): pl.pallas_call(functools.partial(tile_kernel, part, parts), out_shape=out...  23.2 us
    unnamed x58, local copies, waits for them, and re-layouts  18.9 us
    ppermute x7, waiting for transfers between devices, gather_panel(): notes.append(lax.ppermute(note, AXES, route))  16.5 us
    ppermute x5, starting transfers between devices, spread_step(): return lax.ppermute(block, AXES, route)  15.9 us
    pallas_call x2, Pallas kernels, next_panel(): pl.pallas_call(functools.partial(next_kernel, kb), out_shape=jax.ShapeDty...  11.3 us
    pallas_call x1, Pallas kernels, start_panel(): pl.pallas_call(functools.partial(start_kernel, chain), out_shape=(jax.Sha...  8.08 us
  transfers between devices with their start and end apart: 17, of which 7 were waited for; matrix products, arithmetic and copies ran while one was open for 1% of the time, Pallas kernels for 23%

profile of v5, /device:TPU:0, one launch (start us, length us, event | category | flops | bytes accessed | tf_op | source)
XLA Modules:
  0.0 177.6 jit_solution(649112574151322898)
XLA Ops:
  6.6 1.0 copy-done.22
  7.7 0.7 copy-done.23
  8.4 0.7 copy-done.25
  9.1 2.5 %permute_local.1 = (bf16[2,4,256,128]{3,2,1,0:T(8,128)(2,1)}, bf16[1,272,128]{2,1,0:T(8,128)(2,1)S(1)}) custom-call(s32[13]{0:T(128)S(1)} %stack.59.place_ref, s32[32,128]{1,0:T(8,128)S(1)} %bitcast.24, s32[1,64]{1,0:T(1,128)S(1)} %bitcast.25, bf16[64,4096]{1,0:T(8,128)(2,1)S(1)} %copy-done.22), custom_call_target="tpu_custom_call" | custom-call | tf_op jit(solution)/shard_map/permute_local/pallas_call | solution.py:95
  11.6 4.9 %collective-permute-start = (bf16[1,272,128]{2,1,0:T(8,128)(2,1)S(1)}, bf16[1,272,128]{2,1,0:T(8,128)(2,1)S(1)}, u32[]{:S(2)}, u32[]{:S(2)}) collective-permute-start(bf16[1,272,128]{2,1,0:T(8,128)(2,1)S(1)} %get-tuple-element.22), channel_id=1, source_target_pairs={{0,8},{1,9},{2,10},{3,11},{16,24},{17,25},{18,26},{19,27}} | collective-permute-start | bytes 208904 | tf_op jit(solution)/shard_map/ppermute | solution.py:560
  16.5 1.9 %collective-permute-done = bf16[1,272,128]{2,1,0:T(8,128)(2,1)S(1)} collective-permute-done((bf16[1,272,128]{2,1,0:T(8,128)(2,1)S(1)}, bf16[1,272,128]{2,1,0:T(8,128)(2,1)S(1)}, u32[]{:S(2)}, u32[]{:S(2)}) %collective-permute-start) | collective-permute-done | bytes 69664 | tf_op jit(solution)/shard_map/ppermute | solution.py:560
  18.4 3.5 %collective-permute-start.1 = (bf16[1,272,128]{2,1,0:T(8,128)(2,1)S(1)}, bf16[1,272,128]{2,1,0:T(8,128)(2,1)S(1)}, u32[]{:S(2)}, u32[]{:S(2)}) collective-permute-start(bf16[1,272,128]{2,1,0:T(8,128)(2,1)S(1)} %get-tuple-element.38), channel_id=1, source_target_pairs={{0,1},{1,2},{2,3},{3,0},{8,9},{9,10},{10,11},{11,8},{16,17},{17,18... | collective-permute-start | bytes 208904 | tf_op jit(solution)/shard_map/ppermute | solution.py:582
  21.9 5.1 %collective-permute-start.7 = (bf16[1,272,128]{2,1,0:T(8,128)(2,1)S(1)}, bf16[1,272,128]{2,1,0:T(8,128)(2,1)S(1)}, u32[]{:S(2)}, u32[]{:S(2)}) collective-permute-start(bf16[1,272,128]{2,1,0:T(8,128)(2,1)S(1)} %get-tuple-element.38), channel_id=1, source_target_pairs={{0,19},{1,16},{2,17},{3,18},{8,27},{9,24},{10,25},{11,26},{16,3},{... | collective-permute-start | bytes 208904 | tf_op jit(solution)/shard_map/ppermute | solution.py:582
  27.0 2.7 %collective-permute-start.6 = (bf16[1,272,128]{2,1,0:T(8,128)(2,1)S(1)}, bf16[1,272,128]{2,1,0:T(8,128)(2,1)S(1)}, u32[]{:S(2)}, u32[]{:S(2)}) collective-permute-start(bf16[1,272,128]{2,1,0:T(8,128)(2,1)S(1)} %get-tuple-element.38), channel_id=1, source_target_pairs={{0,18},{1,19},{2,16},{3,17},{8,26},{9,27},{10,24},{11,25},{16,2},{... | collective-permute-start | bytes 208904 | tf_op jit(solution)/shard_map/ppermute | solution.py:582
  29.7 4.4 %collective-permute-start.5 = (bf16[1,272,128]{2,1,0:T(8,128)(2,1)S(1)}, bf16[1,272,128]{2,1,0:T(8,128)(2,1)S(1)}, u32[]{:S(2)}, u32[]{:S(2)}) collective-permute-start(bf16[1,272,128]{2,1,0:T(8,128)(2,1)S(1)} %get-tuple-element.38), channel_id=1, source_target_pairs={{0,17},{1,18},{2,19},{3,16},{8,25},{9,26},{10,27},{11,24},{16,1},{... | collective-permute-start | bytes 208904 | tf_op jit(solution)/shard_map/ppermute | solution.py:582
  34.1 2.4 %collective-permute-start.4 = (bf16[1,272,128]{2,1,0:T(8,128)(2,1)S(1)}, bf16[1,272,128]{2,1,0:T(8,128)(2,1)S(1)}, u32[]{:S(2)}, u32[]{:S(2)}) collective-permute-start(bf16[1,272,128]{2,1,0:T(8,128)(2,1)S(1)} %get-tuple-element.38), channel_id=1, source_target_pairs={{0,16},{1,17},{2,18},{3,19},{8,24},{9,25},{10,26},{11,27},{16,0},{... | collective-permute-start | bytes 208904 | tf_op jit(solution)/shard_map/ppermute | solution.py:582
  36.6 2.5 %collective-permute-start.2 = (bf16[1,272,128]{2,1,0:T(8,128)(2,1)S(1)}, bf16[1,272,128]{2,1,0:T(8,128)(2,1)S(1)}, u32[]{:S(2)}, u32[]{:S(2)}) collective-permute-start(bf16[1,272,128]{2,1,0:T(8,128)(2,1)S(1)} %get-tuple-element.38), channel_id=1, source_target_pairs={{0,2},{1,3},{2,0},{3,1},{8,10},{9,11},{10,8},{11,9},{16,18},{17,19... | collective-permute-start | bytes 208904 | tf_op jit(solution)/shard_map/ppermute | solution.py:582
  39.1 9.6 %collective-permute-done.2 = bf16[1,272,128]{2,1,0:T(8,128)(2,1)S(1)} collective-permute-done((bf16[1,272,128]{2,1,0:T(8,128)(2,1)S(1)}, bf16[1,272,128]{2,1,0:T(8,128)(2,1)S(1)}, u32[]{:S(2)}, u32[]{:S(2)}) %collective-permute-start.2) | collective-permute-done | bytes 69664 | tf_op jit(solution)/shard_map/ppermute | solution.py:582
  48.7 3.1 %collective-permute-start.3 = (bf16[1,272,128]{2,1,0:T(8,128)(2,1)S(1)}, bf16[1,272,128]{2,1,0:T(8,128)(2,1)S(1)}, u32[]{:S(2)}, u32[]{:S(2)}) collective-permute-start(bf16[1,272,128]{2,1,0:T(8,128)(2,1)S(1)} %get-tuple-element.38), channel_id=1, source_target_pairs={{0,3},{1,0},{2,1},{3,2},{8,11},{9,8},{10,9},{11,10},{16,19},{17,16... | collective-permute-start | bytes 208904 | tf_op jit(solution)/shard_map/ppermute | solution.py:582
  51.9 6.9 %collective-permute-done.3 = bf16[1,272,128]{2,1,0:T(8,128)(2,1)S(1)} collective-permute-done((bf16[1,272,128]{2,1,0:T(8,128)(2,1)S(1)}, bf16[1,272,128]{2,1,0:T(8,128)(2,1)S(1)}, u32[]{:S(2)}, u32[]{:S(2)}) %collective-permute-start.3) | collective-permute-done | bytes 69664 | tf_op jit(solution)/shard_map/ppermute | solution.py:582
  59.0 1.3 collective-permute-start.8
  60.3 1.5 collective-permute-done.8.came_ref
  61.8 8.1 %start_panel.1 = (bf16[4,384,256]{2,1,0:T(8,128)(2,1)S(1)}, bf16[8,64,128]{2,1,0:T(8,128)(2,1)S(1)}, f32[512,1024]{1,0:T(8,128)S(1)}) custom-call(s32[13]{0:T(128)S(1)} %stack.59.place_ref, f32[64]{0:T(128)S(1)} %copy-done.24, bf16[8,272,128]{2,1,0:T(8,128)(2,1)S(1)} %constant_dynamic-update-slice_fusion.own_ref, ...), custom_call_target="tpu_custom_call" | custom-call | tf_op jit(solution)/shard_map/start_panel/pallas_call | solution.py:340
  69.9 1.3 copy-done.2
  71.2 0.9 copy-done.13
  72.2 1.6 copy-done.8
  73.7 0.9 separate.1
  74.7 1.0 copy-done.11
  75.6 1.0 copy-done.12
  76.7 2.7 %collective-permute-start.10 = (bf16[4,4,256,128]{3,2,1,0:T(8,128)(2,1)S(1)}, bf16[4,4,256,128]{3,2,1,0:T(8,128)(2,1)S(1)}, u32[]{:S(2)}, u32[]{:S(2)}) collective-permute-start(bf16[4,4,256,128]{3,2,1,0:T(8,128)(2,1)S(1)} %get-tuple-element.26.after), channel_id=1, source_target_pairs={{0,8},{1,9},{6,14},{7,15},{24,16},{25,17},{30,22},{31,23}} | collective-permute-start | bytes 3145736 | tf_op jit(solution)/shard_map/ppermute | solution.py:560
  79.4 1.5 collective-permute-start.9
  80.9 5.8 %next_panel.2.aug_in = f32[512,1024]{1,0:T(8,128)S(1)} custom-call(f32[512,1024]{1,0:T(8,128)S(1)} %copy-done.3, bf16[4,4,256,128]{3,2,1,0:T(8,128)(2,1)S(1)} %get-tuple-element.26.after), custom_call_target="tpu_custom_call" | custom-call | tf_op jit(solution)/shard_map/next_panel/pallas_call | solution.py:361
  86.7 5.5 %next_panel.3.refs_2_.aug_in = f32[512,1024]{1,0:T(8,128)S(1)} custom-call(f32[512,1024]{1,0:T(8,128)S(1)} %next_panel.2.aug_in, bf16[4,4,256,128]{3,2,1,0:T(8,128)(2,1)S(1)} %get-tuple-element.26.after), custom_call_target="tpu_custom_call" | custom-call | tf_op jit(solution)/shard_map/next_panel/pallas_call | solution.py:361
  92.2 24.6 %collective-permute-done.9.refs_0_ = bf16[4,4,256,128]{3,2,1,0:T(8,128)(2,1)} collective-permute-done((bf16[4,4,256,128]{3,2,1,0:T(8,128)(2,1)S(1)}, bf16[4,4,256,128]{3,2,1,0:T(8,128)(2,1)}, u32[]{:S(2)}, u32[]{:S(2)}) %collective-permute-start.9) | collective-permute-done | bytes 1048608 | tf_op jit(solution)/shard_map/ppermute | solution.py:610
  116.8 1.0 copy-done.4
  117.8 4.7 %collective-permute-start.12 = (bf16[4,4,256,128]{3,2,1,0:T(8,128)(2,1)}, bf16[4,4,256,128]{3,2,1,0:T(8,128)(2,1)}, u32[]{:S(2)}, u32[]{:S(2)}) collective-permute-start(bf16[4,4,256,128]{3,2,1,0:T(8,128)(2,1)} %get-tuple-element.28.after), channel_id=1, source_target_pairs={{0,8},{1,9},{6,14},{7,15},{24,16},{25,17},{30,22},{31,23}} | collective-permute-start | bytes 3145736 | tf_op jit(solution)/shard_map/ppermute | solution.py:560
  122.5 7.5 %last_panel.1 = (f32[512,512]{1,0:T(8,128)S(1)}, bf16[512,512]{1,0:T(8,128)(2,1)S(1)}, bf16[512,512]{1,0:T(8,128)(2,1)S(1)}, bf16[512,512]{1,0:T(8,128)(2,1)S(1)}) custom-call(f32[512,1024]{1,0:T(8,128)S(1)} %next_panel.3.refs_2_.aug_in, bf16[4,4,256,128]{3,2,1,0:T(8,128)(2,1)} %get-tuple-element.28.after, bf16[8,64,128]{2,1,0:T(8,128)(2,1)S(1)} %get-tuple-element.29.taper_ref), custom_call_target="tpu_custom_call" | custom-call | tf_op jit(solution)/shard_map/last_panel/pallas_call | solution.py:375
  130.1 0.1 broadcast_select_fusion.1.refs_0_
  130.2 1.4 collective-permute-start.11
  131.5 2.6 %collective-permute-done.12.refs_0_ = bf16[4,4,256,128]{3,2,1,0:T(8,128)(2,1)} collective-permute-done((bf16[4,4,256,128]{3,2,1,0:T(8,128)(2,1)}, bf16[4,4,256,128]{3,2,1,0:T(8,128)(2,1)}, u32[]{:S(2)}, u32[]{:S(2)}) %collective-permute-start.12) | collective-permute-done | bytes 1048608 | tf_op jit(solution)/shard_map/ppermute | solution.py:560
  134.1 1.4 broadcast_select_fusion.refs_2_
  135.5 2.3 %collective-permute-start.13 = (bf16[4,4,256,128]{3,2,1,0:T(8,128)(2,1)S(1)}, bf16[4,4,256,128]{3,2,1,0:T(8,128)(2,1)}, u32[]{:S(2)}, u32[]{:S(2)}) collective-permute-start(bf16[4,4,256,128]{3,2,1,0:T(8,128)(2,1)S(1)} %broadcast_select_fusion.refs_2_), channel_id=1, source_target_pairs={{0,4},{8,12},{1,5},{9,13},{6,2},{14,10},{7,3},{15,11},{24,28},{16,... | collective-permute-start | bytes 3145736 | tf_op jit(solution)/shard_map/ppermute | solution.py:560
  137.8 1.0 copy-done.9
  138.7 0.5 collective-permute-done.13.refs_3_
  139.2 1.2 copy-done.10
  140.4 1.1 copy-done.14
  141.6 1.0 copy-done.17
  142.6 1.0 copy-done.19
  143.6 1.0 copy-done.21
  144.7 14.5 %multiply_part.2 = (f32[4096,2048]{1,0:T(8,128)}, bf16[512,2048]{1,0:T(8,128)(2,1)}) custom-call(s32[13]{0:T(128)S(1)} %stack.59.place_ref, bf16[2,4,4,256,128]{4,3,2,1,0:T(8,128)(2,1)} %bitcast.26, bf16[4,4,256,128]{3,2,1,0:T(8,128)(2,1)S(1)} %broadcast_select_fusion.1.refs_0_, bf16[4,4,256,128]{3,2,1,0:T(8,128)(2,1)S(1)} %copy-done.10, ...), custom_call_target="tpu_custom_call" | custom-call | tf_op jit(solution)/shard_map/multiply_part/pallas_call | solution.py:514
  159.2 1.6 copy-done.6
  160.8 1.6 copy-done.7
  162.4 8.7 %multiply_part.3 = f32[4096,2048]{1,0:T(8,128)} custom-call(s32[13]{0:T(128)S(1)} %stack.59.place_ref, bf16[2,4,4,256,128]{4,3,2,1,0:T(8,128)(2,1)S(1)} %bitcast.19, bf16[512,2048]{1,0:T(8,128)(2,1)S(1)} %copy-done.7, f32[4096,2048]{1,0:T(8,128)} %get-tuple-element.36.refs_1_, f32[512,512]{1,0:T(8,128)S(1)} %copy-done.1, ...), custom_call_target="tpu_custom_call", output_to_operand_aliasing={{}: (3, {})} | custom-call | tf_op jit(solution)/shard_map/multiply_part/pallas_call | solution.py:514
  (62 shorter events, 0.4 us)
Async XLA Ops:
  6.5 55.3 %copy-start.15 = (f32[16384]{0:T(1024)S(1)}, f32[16384]{0:T(1024)}, u32[]{:S(2)}) copy-start(f32[16384]{0:T(1024)} %param.9) | copy-start | bytes 196612
  6.5 55.3 %copy-start.24 = (f32[64]{0:T(128)S(1)}, f32[64]{0:T(128)}, u32[]{:S(2)}) copy-start(f32[64]{0:T(128)} %taps_ref.1) | copy-start | bytes 772
  6.5 65.6 %all-gather.7.cloned.1.call-start = ((), (), s32[]{:S(2)}) async-start(), calls=%async_computation | async-start | bytes 2621440 | tf_op jit(solution)/shard_map/all_gather | solution.py:621
  6.6 1.0 copy-start.22
  7.7 0.7 copy-start.23
  8.4 0.7 copy-start.25
  11.6 126.2 %all-gather.11.cloned.1.call-start = ((), (), s32[]{:S(2)}) async-start(), calls=%async_computation.2 | async-start | bytes 3145728 | tf_op jit(solution)/shard_map/all_gather | solution.py:627
  11.6 6.8 %collective-permute-start = (bf16[1,272,128]{2,1,0:T(8,128)(2,1)S(1)}, bf16[1,272,128]{2,1,0:T(8,128)(2,1)S(1)}, u32[]{:S(2)}, u32[]{:S(2)}) collective-permute-start(bf16[1,272,128]{2,1,0:T(8,128)(2,1)S(1)} %get-tuple-element.22), channel_id=1, source_target_pairs={{0,8},{1,9},{2,10},{3,11},{16,24},{17,25},{18,26},{19,27}} | collective-permute-start | bytes 208904 | tf_op jit(solution)/shard_map/ppermute | solution.py:560
  18.4 18.1 %collective-permute-start.1 = (bf16[1,272,128]{2,1,0:T(8,128)(2,1)S(1)}, bf16[1,272,128]{2,1,0:T(8,128)(2,1)S(1)}, u32[]{:S(2)}, u32[]{:S(2)}) collective-permute-start(bf16[1,272,128]{2,1,0:T(8,128)(2,1)S(1)} %get-tuple-element.38), channel_id=1, source_target_pairs={{0,1},{1,2},{2,3},{3,0},{8,9},{9,10},{10,11},{11,8},{16,17},{17,18... | collective-permute-start | bytes 208904 | tf_op jit(solution)/shard_map/ppermute | solution.py:582
  21.9 37.0 %collective-permute-start.7 = (bf16[1,272,128]{2,1,0:T(8,128)(2,1)S(1)}, bf16[1,272,128]{2,1,0:T(8,128)(2,1)S(1)}, u32[]{:S(2)}, u32[]{:S(2)}) collective-permute-start(bf16[1,272,128]{2,1,0:T(8,128)(2,1)S(1)} %get-tuple-element.38), channel_id=1, source_target_pairs={{0,19},{1,16},{2,17},{3,18},{8,27},{9,24},{10,25},{11,26},{16,3},{... | collective-permute-start | bytes 208904 | tf_op jit(solution)/shard_map/ppermute | solution.py:582
  27.0 31.9 %collective-permute-start.6 = (bf16[1,272,128]{2,1,0:T(8,128)(2,1)S(1)}, bf16[1,272,128]{2,1,0:T(8,128)(2,1)S(1)}, u32[]{:S(2)}, u32[]{:S(2)}) collective-permute-start(bf16[1,272,128]{2,1,0:T(8,128)(2,1)S(1)} %get-tuple-element.38), channel_id=1, source_target_pairs={{0,18},{1,19},{2,16},{3,17},{8,26},{9,27},{10,24},{11,25},{16,2},{... | collective-permute-start | bytes 208904 | tf_op jit(solution)/shard_map/ppermute | solution.py:582
  29.7 29.2 %collective-permute-start.5 = (bf16[1,272,128]{2,1,0:T(8,128)(2,1)S(1)}, bf16[1,272,128]{2,1,0:T(8,128)(2,1)S(1)}, u32[]{:S(2)}, u32[]{:S(2)}) collective-permute-start(bf16[1,272,128]{2,1,0:T(8,128)(2,1)S(1)} %get-tuple-element.38), channel_id=1, source_target_pairs={{0,17},{1,18},{2,19},{3,16},{8,25},{9,26},{10,27},{11,24},{16,1},{... | collective-permute-start | bytes 208904 | tf_op jit(solution)/shard_map/ppermute | solution.py:582
  34.1 24.7 %collective-permute-start.4 = (bf16[1,272,128]{2,1,0:T(8,128)(2,1)S(1)}, bf16[1,272,128]{2,1,0:T(8,128)(2,1)S(1)}, u32[]{:S(2)}, u32[]{:S(2)}) collective-permute-start(bf16[1,272,128]{2,1,0:T(8,128)(2,1)S(1)} %get-tuple-element.38), channel_id=1, source_target_pairs={{0,16},{1,17},{2,18},{3,19},{8,24},{9,25},{10,26},{11,27},{16,0},{... | collective-permute-start | bytes 208904 | tf_op jit(solution)/shard_map/ppermute | solution.py:582
  36.6 12.1 %collective-permute-start.2 = (bf16[1,272,128]{2,1,0:T(8,128)(2,1)S(1)}, bf16[1,272,128]{2,1,0:T(8,128)(2,1)S(1)}, u32[]{:S(2)}, u32[]{:S(2)}) collective-permute-start(bf16[1,272,128]{2,1,0:T(8,128)(2,1)S(1)} %get-tuple-element.38), channel_id=1, source_target_pairs={{0,2},{1,3},{2,0},{3,1},{8,10},{9,11},{10,8},{11,9},{16,18},{17,19... | collective-permute-start | bytes 208904 | tf_op jit(solution)/shard_map/ppermute | solution.py:582
  48.7 10.1 %collective-permute-start.3 = (bf16[1,272,128]{2,1,0:T(8,128)(2,1)S(1)}, bf16[1,272,128]{2,1,0:T(8,128)(2,1)S(1)}, u32[]{:S(2)}, u32[]{:S(2)}) collective-permute-start(bf16[1,272,128]{2,1,0:T(8,128)(2,1)S(1)} %get-tuple-element.38), channel_id=1, source_target_pairs={{0,3},{1,0},{2,1},{3,2},{8,11},{9,8},{10,9},{11,10},{16,19},{17,16... | collective-permute-start | bytes 208904 | tf_op jit(solution)/shard_map/ppermute | solution.py:582
  59.0 2.9 %collective-permute-start.8 = (bf16[8,272,128]{2,1,0:T(8,128)(2,1)S(1)}, bf16[8,272,128]{2,1,0:T(8,128)(2,1)S(1)}, u32[]{:S(2)}, u32[]{:S(2)}) collective-permute-start(bf16[8,272,128]{2,1,0:T(8,128)(2,1)S(1)} %constant_dynamic-update-slice_fusion.own_ref), channel_id=1, source_target_pairs={{0,4},{8,12},{1,5},{9,13},{2,6},{10,14},{3,7},{11,15},{16,20},{24,... | collective-permute-start | bytes 1671176 | tf_op jit(solution)/shard_map/ppermute | solution.py:584
  69.9 1.3 copy-start.2
  71.2 0.9 copy-start.13
  72.2 1.6 copy-start.8
  73.7 7.1 %copy-start.3 = (f32[512,1024]{1,0:T(8,128)S(1)}, f32[512,1024]{1,0:T(8,128)}, u32[]{:S(2)}) copy-start(f32[512,1024]{1,0:T(8,128)} %copy-done.2) | copy-start | bytes 6291460
  74.7 1.0 copy-start.11
  75.6 1.0 copy-start.12
  76.6 82.6 %all-gather.9.cloned.1.call-start = ((), (), s32[]{:S(2)}) async-start(), calls=%async_computation.1 | async-start | bytes 3145728 | tf_op jit(solution)/shard_map/all_gather | solution.py:627
  76.7 15.5 %collective-permute-start.10 = (bf16[4,4,256,128]{3,2,1,0:T(8,128)(2,1)S(1)}, bf16[4,4,256,128]{3,2,1,0:T(8,128)(2,1)S(1)}, u32[]{:S(2)}, u32[]{:S(2)}) collective-permute-start(bf16[4,4,256,128]{3,2,1,0:T(8,128)(2,1)S(1)} %get-tuple-element.26.after), channel_id=1, source_target_pairs={{0,8},{1,9},{6,14},{7,15},{24,16},{25,17},{30,22},{31,23}} | collective-permute-start | bytes 3145736 | tf_op jit(solution)/shard_map/ppermute | solution.py:560
  79.4 37.4 %collective-permute-start.9 = (bf16[4,4,256,128]{3,2,1,0:T(8,128)(2,1)S(1)}, bf16[4,4,256,128]{3,2,1,0:T(8,128)(2,1)}, u32[]{:S(2)}, u32[]{:S(2)}) collective-permute-start(bf16[4,4,256,128]{3,2,1,0:T(8,128)(2,1)S(1)} %get-tuple-element.26.after), channel_id=1, source_target_pairs={{16,0},{17,1},{22,6},{23,7},{8,24},{9,25},{14,30},{15,31}} | collective-permute-start | bytes 3145736 | tf_op jit(solution)/shard_map/ppermute | solution.py:610
  116.8 1.0 copy-start.4
  117.8 16.4 %collective-permute-start.12 = (bf16[4,4,256,128]{3,2,1,0:T(8,128)(2,1)}, bf16[4,4,256,128]{3,2,1,0:T(8,128)(2,1)}, u32[]{:S(2)}, u32[]{:S(2)}) collective-permute-start(bf16[4,4,256,128]{3,2,1,0:T(8,128)(2,1)} %get-tuple-element.28.after), channel_id=1, source_target_pairs={{0,8},{1,9},{6,14},{7,15},{24,16},{25,17},{30,22},{31,23}} | collective-permute-start | bytes 3145736 | tf_op jit(solution)/shard_map/ppermute | solution.py:560
  122.5 7.5 %copy-start.5 = (bf16[4,4,256,128]{3,2,1,0:T(8,128)(2,1)S(1)}, bf16[4,4,256,128]{3,2,1,0:T(8,128)(2,1)}, u32[]{:S(2)}) copy-start(bf16[4,4,256,128]{3,2,1,0:T(8,128)(2,1)} %copy-done.4) | copy-start | bytes 3145732
  130.0 4.1 %copy-start = (f32[512,512]{1,0:T(8,128)}, f32[512,512]{1,0:T(8,128)S(1)}, u32[]{:S(2)}) copy-start(f32[512,512]{1,0:T(8,128)S(1)} %get-tuple-element.30.refs_1_.refs_8_.refs_2_) | copy-start | bytes 3145732
  130.0 4.1 %copy-start.16 = (bf16[512,512]{1,0:T(8,128)(2,1)}, bf16[512,512]{1,0:T(8,128)(2,1)S(1)}, u32[]{:S(2)}) copy-start(bf16[512,512]{1,0:T(8,128)(2,1)S(1)} %get-tuple-element.31.refs_4_) | copy-start | bytes 1572868
  130.0 4.1 %copy-start.18 = (bf16[512,512]{1,0:T(8,128)(2,1)}, bf16[512,512]{1,0:T(8,128)(2,1)S(1)}, u32[]{:S(2)}) copy-start(bf16[512,512]{1,0:T(8,128)(2,1)S(1)} %get-tuple-element.32.refs_5_) | copy-start | bytes 1572868
  130.0 4.1 %copy-start.20 = (bf16[512,512]{1,0:T(8,128)(2,1)}, bf16[512,512]{1,0:T(8,128)(2,1)S(1)}, u32[]{:S(2)}) copy-start(bf16[512,512]{1,0:T(8,128)(2,1)S(1)} %get-tuple-element.33.refs_6_) | copy-start | bytes 1572868
  130.2 7.6 %collective-permute-start.11 = (bf16[4,4,256,128]{3,2,1,0:T(8,128)(2,1)S(1)}, bf16[4,4,256,128]{3,2,1,0:T(8,128)(2,1)S(1)}, u32[]{:S(2)}, u32[]{:S(2)}) collective-permute-start(bf16[4,4,256,128]{3,2,1,0:T(8,128)(2,1)S(1)} %broadcast_select_fusion.1.refs_0_), channel_id=1, source_target_pairs={{0,4},{8,12},{1,5},{9,13},{6,2},{14,10},{7,3},{15,11},{24,28},{16,... | collective-permute-start | bytes 3145736 | tf_op jit(solution)/shard_map/ppermute | solution.py:560
  135.5 3.7 %collective-permute-start.13 = (bf16[4,4,256,128]{3,2,1,0:T(8,128)(2,1)S(1)}, bf16[4,4,256,128]{3,2,1,0:T(8,128)(2,1)}, u32[]{:S(2)}, u32[]{:S(2)}) collective-permute-start(bf16[4,4,256,128]{3,2,1,0:T(8,128)(2,1)S(1)} %broadcast_select_fusion.refs_2_), channel_id=1, source_target_pairs={{0,4},{8,12},{1,5},{9,13},{6,2},{14,10},{7,3},{15,11},{24,28},{16,... | collective-permute-start | bytes 3145736 | tf_op jit(solution)/shard_map/ppermute | solution.py:560
  137.8 1.0 copy-start.9
  139.2 1.2 copy-start.10
  140.4 1.1 copy-start.14
  141.5 1.0 copy-start.17
  142.6 1.0 copy-start.19
  143.6 1.0 copy-start.21
  144.7 14.6 %copy-start.1 = (f32[512,512]{1,0:T(8,128)S(1)}, f32[512,512]{1,0:T(8,128)}, u32[]{:S(2)}) copy-start(f32[512,512]{1,0:T(8,128)} %copy-done) | copy-start | bytes 3145732
  159.2 1.6 copy-start.6
  160.8 1.6 copy-start.7
Sparse Core Ops, SparseCore 0:
  11.7 54.0 all-gather.6
  76.8 41.9 all-gather.10
  122.6 30.2 all-gather.8

commit v6 on v5

--- a/solution.py
+++ b/solution.py
@@ -37,12 +37,13 @@
 SMEM = pl.BlockSpec(memory_space=pltpu.SMEM)
 ANY = pl.BlockSpec(memory_space=pl.ANY)
 FREE = pl.CostEstimate(flops=0, bytes_accessed=0, transcendentals=0)
-LIMIT = pltpu.CompilerParams(vmem_limit_bytes=48 << 20)
+LIMIT = pltpu.CompilerParams(vmem_limit_bytes=24 << 20)
+WIDE = pltpu.CompilerParams(vmem_limit_bytes=58 << 20)
 
 
 def permute_kernel(place_ref, *refs):
     sources, refs = refs[:3], refs[3:]
-    all_ref, note_ref = refs[:-4]
+    *part_refs, both_ref, note_ref = refs[:-4]
     order_ref, counts_ref, design_ref = targets = refs[-4:-1]
     copies = [
         pltpu.make_async_copy(source, target, refs[-1].at[n])
@@ -53,7 +54,7 @@
     for copy in copies:
         copy.wait()
     epochs = design_ref.shape[0]
-    parts, per_part = all_ref.shape[:2]
+    parts, per_part = len(part_refs), part_refs[0].shape[0]
     lane = iota((PB, PB), 1).astype(F32)
     none = jnp.zeros((epochs, PB), BF16)
     groups = 2 * HALF // PB
@@ -78,81 +79,100 @@
     counts = jnp.concatenate([counts] * (LANES // epochs), axis=1)
     note_ref[0, HALF:, :] = jnp.broadcast_to(counts, (NOTE, LANES)).astype(BF16)
     for j in range(parts):
-        at = j * per_part * groups
-        local = order_of(slice(at, at + per_part * groups))
-        columns = lambda g: design_ref[:, (at + g) * PB : (at + g + 1) * PB]
+        piece = lax.rem(place_ref[PLACE_COL] + j, parts)
+        at = pl.multiple_of(piece * per_part * groups, per_part * groups)
+        local = order_of(pl.ds(at, per_part * groups))
+        columns = lambda g: design_ref[:, pl.ds(pl.multiple_of((at + g) * PB, PB), PB)]
         for block in range(per_part):
             for part in range(HALF // PB):
                 rows = slice(part * PB, (part + 1) * PB)
-                all_ref[j, block, rows, :] = packed(local, columns, block, part)
+                part_refs[j][block, rows, :] = packed(local, columns, block, part)
+        both_ref[j] = part_refs[j][...]
 
 
 def permute_local(place, design, order, tap_count, cols_dev):
     epochs, rows = design.shape
     parts, per_part = rows // cols_dev, cols_dev // (2 * HALF)
-    piece = jax.ShapeDtypeStruct((parts, per_part, HALF, LANES), BF16)
+    piece = jax.ShapeDtypeStruct((per_part, HALF, LANES), BF16)
+    both = jax.ShapeDtypeStruct((parts,) + piece.shape, BF16)
     note = jax.ShapeDtypeStruct((1, HALF + NOTE, LANES), BF16)
     return pl.pallas_call(
         permute_kernel,
-        out_shape=(piece, note),
+        out_shape=(piece,) * parts + (both, note),
         in_specs=[SMEM] + [ANY] * 3,
-        out_specs=(VMEM,) * 2,
+        out_specs=(VMEM,) * (parts + 2),
         scratch_shapes=[
             pltpu.VMEM((rows // PB, PB), jnp.int32),
             pltpu.VMEM((1, epochs), jnp.int32),
             pltpu.VMEM((epochs, rows), BF16),
             pltpu.SemaphoreType.DMA((3,)),
         ],
-        compiler_params=LIMIT,
+        compiler_params=WIDE,
         name="permute_local",
     )(place, order.reshape(rows // PB, PB), tap_count.reshape(1, epochs), design)
 
 
-PLACE_ROW, PLACE_GROUP, PLACE_EP, PLACE_COL, PLACE_TAKES = range(5)
-
-
-def separate_kernel(place_ref, all_ref, after, *refs):
-    del after
-    *part_refs, wanted_ref, sem = refs
-    parts = len(part_refs)
-    copies = [
-        pltpu.make_async_copy(all_ref.at[n, j], part_refs[j].at[n], sem.at[n, j])
-        for j in range(parts)
-        for n in range(all_ref.shape[0])
-    ]
+PLACE_ROW, PLACE_GROUP, PLACE_EP, PLACE_COL, PLACE_TAKES, PLACE_OWNS, PLACE_FAR, PLACE_BACK = range(8)
+
+
+def assemble_kernel(count, gated, after, whole, place_ref, *refs):
+    shards, kept = refs[:count], refs[count : count + gated]
+    out_refs, sem = refs[count + gated + after : -1], refs[-1]
+    copies = [(shard, out_refs[0].at[n]) for n, shard in enumerate(shards)]
+    if whole:
+        copies += [(shard, out_refs[-1].at[n]) for n, shard in enumerate([kept[0], *shards])]
+    copies = [pltpu.make_async_copy(a, b, sem.at[n]) for n, (a, b) in enumerate(copies)]
     for copy in copies:
         copy.start()
-    for j in range(parts):
-
-        @pl.when(lax.rem(place_ref[PLACE_COL], parts) == j)
-        def _():
-            again = [
-                pltpu.make_async_copy(all_ref.at[n, j], wanted_ref.at[n], sem.at[n, parts])
-                for n in range(all_ref.shape[0])
-            ]
-            for copy in again:
-                copy.start()
-            for copy in again:
-                copy.wait()
-
     for copy in copies:
         copy.wait()
 
 
-def separate(place, gathered, after):
-    width, parts = gathered.shape[:2]
-    part = jax.ShapeDtypeStruct((width,) + gathered.shape[2:], BF16)
-    *column, wanted = pl.pallas_call(
-        separate_kernel,
-        out_shape=(part,) * (parts + 1),
-        in_specs=[SMEM, ANY, ANY],
-        out_specs=(ANY,) * (parts + 1),
-        scratch_shapes=[pltpu.SemaphoreType.DMA((width, parts + 1))],
+def assemble(place, shards, gated, after, whole):
+    count = len(shards)
+    out_shape = [jax.ShapeDtypeStruct((count,) + shards[0].shape, BF16)]
+    out_shape += [jax.ShapeDtypeStruct(g.shape, g.dtype) for g in gated]
+    if whole:
+        out_shape.append(jax.ShapeDtypeStruct((count + 1,) + shards[0].shape, BF16))
+    return pl.pallas_call(
+        functools.partial(assemble_kernel, count, len(gated), len(after), whole),
+        out_shape=out_shape,
+        in_specs=[SMEM] + [ANY] * (count + len(gated) + len(after)),
+        out_specs=[ANY] * len(out_shape),
+        input_output_aliases={1 + count + n: 1 + n for n in range(len(gated))},
+        scratch_shapes=[pltpu.SemaphoreType.DMA((2 * count + 1,))],
         compiler_params=LIMIT,
         cost_estimate=FREE,
-        name="separate",
-    )(place, gathered, after)
-    return column, wanted
+        name="assemble",
+    )(place, *shards, *gated, *after)
+
+
+def collect_kernel(place_ref, *refs):
+    near, far, (out_ref, sem) = refs[:2], refs[2:4], refs[5:]
+
+    def copy(sources):
+        copies = [
+            pltpu.make_async_copy(source, out_ref.at[n], sem.at[n]) for n, source in enumerate(sources)
+        ]
+        for c in copies:
+            c.start()
+        for c in copies:
+            c.wait()
+
+    choose(place_ref[PLACE_FAR] != 0, lambda: copy(far), lambda: copy(near))
+
+
+def collect(place, near, far, after):
+    return pl.pallas_call(
+        collect_kernel,
+        out_shape=jax.ShapeDtypeStruct((2,) + near[0].shape, BF16),
+        in_specs=[SMEM] + [ANY] * 5,
+        out_specs=ANY,
+        scratch_shapes=[pltpu.SemaphoreType.DMA((2,))],
+        compiler_params=LIMIT,
+        cost_estimate=FREE,
+        name="collect",
+    )(place, *near, *far, after)
 
 
 def gate(arrays, after):
@@ -227,9 +247,10 @@
 
 
 def start_kernel(
-    chain, place_ref, taps_ref, own_ref, came_ref, reg_ref, band_ref, taper_ref, aug_ref, notes, a1,
+    chain, place_ref, taps_ref, own_ref, came_ref, reg_ref, after, band_ref, taper_ref, aug_ref, notes, a1,
     work,
 ):
+    del after
     epochs = aug_ref.shape[1] - HEAD
     half = LANES // 2
 
@@ -334,7 +355,7 @@
         low_ref[here, :] = (got[:, :epochs] - top.astype(F32)).astype(BF16)
 
 
-def start_panel(place, chain, taps, own, came, regular):
+def start_panel(place, chain, taps, own, came, regular, after):
     epochs = own.shape[0] * (LANES // 2)
     half = LANES // 2
     return pl.pallas_call(
@@ -344,7 +365,7 @@
             jax.ShapeDtypeStruct((epochs // half, half, LANES), BF16),
             jax.ShapeDtypeStruct((HEAD, HEAD + epochs), F32),
         ),
-        in_specs=[SMEM, SMEM, VMEM, VMEM, VMEM],
+        in_specs=[SMEM, SMEM, VMEM, VMEM, VMEM, ANY],
         out_specs=(VMEM,) * 3,
         scratch_shapes=[
             pltpu.VMEM(own.shape, BF16),
@@ -354,7 +375,7 @@
         compiler_params=LIMIT,
         cost_estimate=FREE,
         name="start_panel",
-    )(place, taps, own, came, regular.reshape(1, -1))
+    )(place, taps, own, came, regular.reshape(1, -1), after)
 
 
 def next_panel(kb, aug, after):
@@ -403,8 +424,13 @@
     here = place_ref[PLACE_EP] * width
     there = width - here
     for n in range(width):
-        blocks[here + n] = own[n][...]
-        blocks[there + n] = other[n][...]
+        back = place_ref[PLACE_BACK + n]
+        blocks[here + back] = own[n][...]
+        blocks[there + back] = other[n][...]
+
+
+def unpack_both(place_ref, both, block, blocks):
+    unpack(place_ref, shards_of(both.at[0], block), shards_of(both.at[1], block), blocks)
 
 
 def choose(condition, yes, no):
@@ -418,16 +444,16 @@
     )
 
 
-def tile_kernel(part, parts, place_ref, left_ref, *refs):
+def tile_kernel(part, parts, place_ref, own_first, own_rest, other_first, other_rest, *refs):
     if part == 0:
-        own, own_came, other, other_came, w_ref, high_ref, low_ref, band_ref = refs[:8]
-        factor_ref, reg_ref, out_ref, right_ref, lhs, columns, blocks = refs[8:]
+        theirs_ref, near_ref, came_ref, w_ref, high_ref, low_ref, band_ref = refs[:7]
+        factor_ref, reg_ref, out_ref, right_ref, blocks, lhs, columns = refs[7:]
     else:
-        right_ref, _, factor_ref, reg_ref, out_ref, lhs = refs
+        right_ref, _, factor_ref, reg_ref, out_ref, blocks, lhs = refs
     i, steps = pl.program_id(0), pl.num_programs(0)
     rows, cols = out_ref.shape
     half = LANES // 2
-    block = part * steps + i
+    block = lax.rem(place_ref[PLACE_COL] + part, parts) * steps + i
     first_row = (place_ref[PLACE_ROW] * parts * steps + block) * rows
     first_col = place_ref[PLACE_GROUP] * cols
 
@@ -441,8 +467,8 @@
             for n in range(cols // rows):
                 choose(
                     place_ref[PLACE_TAKES] != 0,
-                    lambda: unpack(place_ref, shards_of(own_came, n), shards_of(other_came, n), blocks),
-                    lambda: unpack(place_ref, shards_of(own, n), shards_of(other, n), blocks),
+                    lambda: unpack_both(place_ref, came_ref, n, blocks),
+                    lambda: unpack_both(place_ref, near_ref, n, blocks),
                 )
                 filter_rows(lambda e: blocks[e], band_ref, store)
                 wanted = columns[...]
@@ -455,10 +481,18 @@
 
     @pl.when(first_row >= HEAD)
     def _():
-        eps, width = left_ref.shape[:2]
-        sources = [left_ref.at[e, n, 0] for e in range(eps) for n in range(width)]
+        mine = [own_first.at[0], *shards_of(own_rest, 0)]
+        others = [other_first.at[0, 0], *shards_of(other_rest, 0)]
+        if part == 0:
+            choose(
+                place_ref[PLACE_OWNS] != 0,
+                lambda: unpack(place_ref, mine, shards_of(theirs_ref, 0), blocks),
+                lambda: unpack(place_ref, mine, others, blocks),
+            )
+        else:
+            unpack(place_ref, mine, others, blocks)
         for pair in range(lhs.shape[1] // LANES):
-            even, odd = sources[2 * pair][...], sources[2 * pair + 1][...]
+            even, odd = blocks[2 * pair], blocks[2 * pair + 1]
             across = slice(pair * LANES, (pair + 1) * LANES)
             lhs[:HALF, across] = jnp.concatenate([even[:, :half], odd[:, :half]], axis=1)
             lhs[HALF:, across] = jnp.concatenate([even[:, half:], odd[:, half:]], axis=1)
@@ -479,32 +513,39 @@
             out_ref[:, :HEAD] = factor_ref[...]
 
 
-def multiply_part(part, parts, place, left, factor, regular, extra, out, right):
-    eps, width, steps = left.shape[:3]
+def multiply_part(part, parts, place, own, other, factor, regular, extra, out, right):
+    steps = own[0].shape[0]
     rows = 2 * HALF
     cols = steps * rows
-    epochs = eps * width * (LANES // 2)
+    epochs = (own[1].shape[0] + 1) * 2 * (LANES // 2)
 
     def reg_block(i, place):
-        return 0, (place[PLACE_ROW] * parts + part) * steps + i
+        block = lax.rem(place[PLACE_COL] + part, parts) * steps + i
+        return 0, place[PLACE_ROW] * parts * steps + block
 
     def out_block(i, place):
-        return part * steps + i, 0
+        return lax.rem(place[PLACE_COL] + part, parts) * steps + i, 0
+
+    def shards_spec(array):
+        return pl.BlockSpec((array.shape[0], 1, HALF, LANES), lambda i, place: (0, i, 0, 0))
 
     out_shape = [jax.ShapeDtypeStruct((parts * steps * rows, cols), F32)]
     out_specs = [pl.BlockSpec((rows, cols), out_block)]
-    scratch = [pltpu.VMEM((rows, epochs), BF16)]
-    operands = [left]
-    in_specs = [
-        pl.BlockSpec((eps, width, 1, HALF, LANES), lambda i, place: (0, 0, i, 0, 0)),
+    scratch = [
+        pltpu.VMEM((epochs // (LANES // 2), HALF, LANES), BF16),
+        pltpu.VMEM((rows, epochs), BF16),
     ]
+    operands = [*own, *other]
+    in_specs = [pl.BlockSpec((1, HALF, LANES), lambda i, place: (i, 0, 0)), shards_spec(own[1])]
+    in_specs += [pl.BlockSpec((1, 1, HALF, LANES), lambda i, place: (part, i, 0, 0))]
+    in_specs += [shards_spec(other[1])]
     if part == 0:
         operands += extra
-        in_specs += [fixed(array) for array in extra]
+        in_specs += [shards_spec(extra[0])]
+        in_specs += [fixed(array) for array in extra[1:]]
         out_shape.append(jax.ShapeDtypeStruct((epochs, cols), BF16))
         out_specs.append(pl.BlockSpec((epochs, cols), lambda i, place: (0, 0)))
         scratch.append(pltpu.VMEM((rows, epochs), BF16))
-        scratch.append(pltpu.VMEM((eps * width, HALF, LANES), BF16))
     else:
         operands += [right, out]
         in_specs += [fixed(right), ANY]
@@ -522,7 +563,7 @@
             scratch_shapes=scratch,
         ),
         input_output_aliases=alias,
-        compiler_params=pltpu.CompilerParams(vmem_limit_bytes=48 << 20),
+        compiler_params=WIDE,
         cost_estimate=FREE,
         name="multiply_part",
     )(place, *operands)
@@ -594,16 +635,21 @@
     group = lax.axis_index(("ep", "col"))
     everywhere = [(e, r, c) for e in range(eps) for r in range(rows) for c in range(cols)]
     owner = lambda e, c: (e * cols + c) * cols_dev // rows_dev
-    inside = lambda r, c: c // parts == (r * parts % cols) // parts
-    owns = lambda e, r, c: inside(r, c) and r * parts // cols == e
+    owns = lambda e, r, c: (c // parts == (r * parts % cols) // parts) & (r * parts // cols == e)
     first_owner = group * cols_dev // rows_dev
     takes = ((row ^ first_owner) & 1) == 1
-    place = [row, group, ep, col, takes]
+    far = (row ^ first_owner) >= rows // 2
+    back = [(col - n) % cols for n in range(cols)]
+    place = [row, group, ep, col, takes, owns(ep, row, col), far, *back]
     chain = len(place)
     place += [((ep - de) % eps) * cols + (col - dc) % cols for de, dc in panel_steps()]
     place = jnp.stack([jnp.asarray(p, jnp.int32) for p in place])
 
-    local, note = permute_local(place, design, order, tap_count, cols_dev)
+    *local, both, note = permute_local(place, design, order, tap_count, cols_dev)
+
+    def shift(block, n):
+        route = [(flat(e, r, (c - n) % cols), flat(e, r, c)) for e, r, c in everywhere]
+        return lax.ppermute(block, AXES, route)
 
     def across(block, wanted):
         route = [(flat(1 - e, r, c), flat(e, r, c)) for e, r, c in everywhere if wanted(e, r, c)]
@@ -611,35 +657,54 @@
 
     distances = doubling(rows, 1)
 
-    def spread_rest(block, got):
-        for n, distance in enumerate(distances[1:]):
-            hit = ((row ^ first_owner) & (4 * distance - 1)) == 2 * distance
-            block = jnp.where(hit, got, block)
-            got = spread_step(block, owner, distance)
-        return block, got
-
-    gathered = lax.all_gather(local, "col", axis=0)
+    def diagonal(block):
+        route = [
+            (flat(1 - e, owner(e, c), c), flat(e, owner(e, c) ^ distances[0], c))
+            for e in range(eps)
+            for c in range(cols)
+        ]
+        return lax.ppermute(block, AXES, route)
+
+    anyone = lambda e, r, c: True
     notes, came = gather_panel(note)
-    band, taper, aug = start_panel(place, chain, taps, notes, came, regular)
-    column, mine = separate(place, gathered, aug)
-    theirs = across(mine, owns)
-    own_got = spread_step(mine, owner, distances[0])
-    rows_of = [lax.all_gather(part, "ep", axis=0) for part in column]
-    aug = next_panel(1, aug, mine)
-    aug = next_panel(2, aug, mine)
-    theirs, own_got = gate([theirs, own_got], aug)
-    other_got = spread_step(theirs, owner, distances[0])
-    own_block, own_came = spread_rest(mine, own_got)
+    *local, both = gate([*local, both], notes)
+    early = [shift(local[n % parts], n) for n in range(1, cols)]
+    swapped = across(both, anyone)
+    band, taper, aug = start_panel(place, chain, taps, notes, came, regular, notes)
+    aug = next_panel(1, aug, aug)
+    rest, *local, first = assemble(place, early, local, [aug, swapped], True)
+    theirs = across(first, owns)
+    far_own = spread_step(first, owner, distances[0])
+    far_other = diagonal(first)
+    others = [across(rest, lambda e, r, c: not owns(e, r, c))]
+    mine = [rest]
+    order = [(j, n) for j in range(1, parts) for n in range(1, cols)]
+    late = [shift(local[(n + j) % parts], n) for j, n in order[:1]]
+    aug = next_panel(2, aug, first)
+    theirs, far_own, far_other, *passed = gate([theirs, far_own, far_other, *late, *local], aug)
+    late, local = passed[: len(late)], passed[len(late) :]
+    late += [shift(local[(n + j) % parts], n) for j, n in order[1:]]
     factor, w, high, low = last_panel(3, aug, theirs, taper)
-    (other_got,) = gate([other_got], factor)
-    other_block, other_came = spread_rest(theirs, other_got)
-    extra = [own_block, own_came, other_block, other_came, w, high, low, band]
+    others[0], *late[1:] = gate([others[0], *late[1:]], factor)
+    wanted = collect(place, [first, theirs], [far_own, far_other], others[0])
+    for distance in distances[1:]:
+        got = spread_step(wanted, owner, distance)
+        if distance > 1:
+            wanted = jnp.where(((row ^ first_owner) & (2 * distance - 1)) == distance, got, wanted)
+    for j in range(1, parts):
+        shards = late[(j - 1) * (cols - 1) : j * (cols - 1)]
+        (whole,) = assemble(place, shards, [], [factor], False)
+        mine.append(whole)
+        others.append(across(whole, anyone))
+    extra = [theirs, wanted, got, w, high, low, band]
+    mine = [(local[j], mine[j]) for j in range(parts)]
+    others = [(swapped, others[j]) for j in range(parts)]
     out, right = multiply_part(
-        0, parts, place, rows_of[0], factor, regular, extra, None, None
+        0, parts, place, mine[0], others[0], factor, regular, extra, None, None
     )
     for j in range(1, parts):
         (out,) = multiply_part(
-            j, parts, place, rows_of[j], factor, regular, None, out, right
+            j, parts, place, mine[j], others[j], factor, regular, None, out, right
         )
     return out
 

time: 179 us -> 158 us (0.88)
  the two profiles are of different devices: /device:TPU:0 before, /device:TPU:25 now
where the time goes in v6:
time: 158 us; the launch traced here: 157 us
  Pallas kernels  63.4 us (40%)
  waiting for transfers between devices  60.2 us (38%)
  starting transfers between devices  25.9 us (16%)
  local copies, waits for them, and re-layouts  6.12 us (4%)
    pallas_call x2, Pallas kernels, multiply_part(): pl.pallas_call(functools.partial(tile_kernel, part, parts), out_shape=out...  29.3 us
    ppermute x1, waiting for transfers between devices, gather_panel(): came = lax.ppermute(notes, 'row', [(r, r + 1) for r in range(0, rows, 2)])  28.7 us
    ppermute x6, waiting for transfers between devices, shift(): return lax.ppermute(block, AXES, route)  11.7 us
    pallas_call x2, Pallas kernels, next_panel(): pl.pallas_call(functools.partial(next_kernel, kb), out_shape=jax.ShapeDty...  11.3 us
    ppermute x3, waiting for transfers between devices, spread_step(): return lax.ppermute(block, AXES, route)  10.7 us
    ppermute x4, waiting for transfers between devices, across(): return lax.ppermute(block, AXES, route)  9.2 us
    ppermute x3, starting transfers between devices, spread_step(): return lax.ppermute(block, AXES, route)  8.89 us
    pallas_call x1, Pallas kernels, start_panel(): pl.pallas_call(functools.partial(start_kernel, chain), out_shape=(jax.Sha...  8.3 us
  transfers between devices with their start and end apart: 22, of which 6 were waited for; matrix products, arithmetic and copies ran while one was open for 0% of the time, Pallas kernels for 29%

profile of v6, /device:TPU:25, one launch (start us, length us, event | category | flops | bytes accessed | tf_op | source)
XLA Modules:
  0.0 157.1 jit_solution(16101247693589927416)
XLA Ops:
  0.0 0.7 stack.91.place_ref
  0.7 3.9 %permute_local.1 = (bf16[4,256,128]{2,1,0:T(8,128)(2,1)}, bf16[4,256,128]{2,1,0:T(8,128)(2,1)}, bf16[2,4,256,128]{3,2,1,0:T(8,128)(2,1)}, bf16[1,272,128]{2,1,0:T(8,128)(2,1)}) custom-call(s32[19]{0:T(128)} %stack.91.place_ref, s32[32,128]{1,0:T(8,128)} %bitcast.25, s32[1,64]{1,0:T(1,128)} %bitcast.26, bf16[64,4096]{1,0:T(8,128)(2,1)} %refs_2_.1), custom_call_target="tpu_custom_call" | custom-call | tf_op jit(solution)/shard_map/permute_local/pallas_call | solution.py:99
  4.6 0.7 collective-permute-start
  5.3 0.0 collective-permute-done
  5.3 0.9 constant_dynamic-update-slice_fusion.7
  6.2 0.7 collective-permute-start.1
  6.9 0.7 collective-permute-start.7
  7.6 0.7 collective-permute-start.6
  8.3 0.7 collective-permute-start.5
  8.9 0.7 collective-permute-start.4
  9.6 0.7 collective-permute-start.2
  10.3 0.7 collective-permute-start.3
  11.2 1.3 collective-permute-start.11
  12.5 0.9 copy-done.5
  13.4 1.2 collective-permute-start.12
  14.6 0.1 collective-permute-start.9
  14.7 0.2 collective-permute-start.10
  14.8 3.1 %collective-permute-start.8 = (bf16[4,256,128]{2,1,0:T(8,128)(2,1)S(1)}, bf16[4,256,128]{2,1,0:T(8,128)(2,1)S(1)}, u32[]{:S(2)}, u32[]{:S(2)}) collective-permute-start(bf16[4,256,128]{2,1,0:T(8,128)(2,1)S(1)} %get-tuple-element.38.refs_4_), channel_id=1, source_target_pairs={{3,0},{0,1},{1,2},{2,3},{7,4},{4,5},{5,6},{6,7},{11,8},{8,9},{9,10... | collective-permute-start | bytes 786440 | tf_op jit(solution)/shard_map/ppermute | solution.py:652
  17.9 28.7 %collective-permute-done.11.came_ref = bf16[8,272,128]{2,1,0:T(8,128)(2,1)S(1)} collective-permute-done((bf16[8,272,128]{2,1,0:T(8,128)(2,1)S(1)}, bf16[8,272,128]{2,1,0:T(8,128)(2,1)S(1)}, u32[]{:S(2)}, u32[]{:S(2)}) %collective-permute-start.11) | collective-permute-done | bytes 557088 | tf_op jit(solution)/shard_map/ppermute | solution.py:625
  46.6 8.3 %start_panel.1 = (bf16[4,384,256]{2,1,0:T(8,128)(2,1)S(1)}, bf16[8,64,128]{2,1,0:T(8,128)(2,1)S(1)}, f32[512,1024]{1,0:T(8,128)S(1)}) custom-call(s32[19]{0:T(128)S(1)} %copy-done.18, f32[64]{0:T(128)S(1)} %copy-done.19, bf16[8,272,128]{2,1,0:T(8,128)(2,1)S(1)} %constant_dynamic-update-slice_fusion.refs_3_.own_ref.after, ...), custom_call_target="tpu_custom_call" | custom-call | tf_op jit(solution)/shard_map/start_panel/pallas_call | solution.py:361
  55.0 5.8 %next_panel.2.refs_5_.aug_in = f32[512,1024]{1,0:T(8,128)S(1)} custom-call(f32[512,1024]{1,0:T(8,128)S(1)} %get-tuple-element.40.aug_in.after, f32[512,1024]{1,0:T(8,128)S(1)} %get-tuple-element.40.aug_in.after), custom_call_target="tpu_custom_call" | custom-call | tf_op jit(solution)/shard_map/next_panel/pallas_call | solution.py:382
  60.8 0.0 collective-permute-done.10.refs_2_
  60.9 0.9 copy-done.7
  61.8 1.6 %assemble.2 = (bf16[3,4,256,128]{3,2,1,0:T(8,128)(2,1)S(1)}, bf16[4,256,128]{2,1,0:T(8,128)(2,1)}, bf16[4,256,128]{2,1,0:T(8,128)(2,1)S(1)}, bf16[4,4,256,128]{3,2,1,0:T(8,128)(2,1)S(1)}) custom-call(s32[19]{0:T(128)S(1)} %copy-done.18, bf16[4,256,128]{2,1,0:T(8,128)(2,1)S(1)} %collective-permute-done.8.refs_0_, ...), custom_call_target="tpu_custom_call", output_to_operand_aliasing={{1}: (4, {}), {2}: (5, {})} | custom-call | tf_op jit(solution)/shard_map/assemble/pallas_call | solution.py:137
  63.4 0.0 copy-start.8
  63.5 0.7 collective-permute-start.15
  64.2 5.5 %collective-permute-start.14 = (bf16[4,4,256,128]{3,2,1,0:T(8,128)(2,1)S(1)}, bf16[4,4,256,128]{3,2,1,0:T(8,128)(2,1)S(1)}, u32[]{:S(2)}, u32[]{:S(2)}) collective-permute-start(bf16[4,4,256,128]{3,2,1,0:T(8,128)(2,1)S(1)} %get-tuple-element.42.after.refs_0_), channel_id=1, source_target_pairs={{0,8},{1,9},{6,14},{7,15},{24,16},{25,17},{30,22},{31,23}} | collective-permute-start | bytes 3145736 | tf_op jit(solution)/shard_map/ppermute | solution.py:601
  69.8 1.3 collective-permute-start.13
  71.1 4.1 %collective-permute-start.17 = (bf16[3,4,256,128]{3,2,1,0:T(8,128)(2,1)S(1)}, bf16[3,4,256,128]{3,2,1,0:T(8,128)(2,1)S(1)}, u32[]{:S(2)}, u32[]{:S(2)}) collective-permute-start(bf16[3,4,256,128]{3,2,1,0:T(8,128)(2,1)S(1)} %get-tuple-element.47.own_rest), channel_id=1, source_target_pairs={{18,2},{19,3},{20,4},{21,5},{24,8},{25,9},{26,10},{27,11},{28,12},... | collective-permute-start | bytes 2359304 | tf_op jit(solution)/shard_map/ppermute | solution.py:656
  75.2 0.3 collective-permute-start.16
  75.5 5.5 %next_panel.3.refs_6_.aug_in = f32[512,1024]{1,0:T(8,128)S(1)} custom-call(f32[512,1024]{1,0:T(8,128)S(1)} %next_panel.2.refs_5_.aug_in, bf16[4,4,256,128]{3,2,1,0:T(8,128)(2,1)S(1)} %get-tuple-element.42.after.refs_0_), custom_call_target="tpu_custom_call" | custom-call | tf_op jit(solution)/shard_map/next_panel/pallas_call | solution.py:382
  81.0 1.3 collective-permute-done.16.refs_3_
  82.3 8.0 %collective-permute-done.14.refs_1_ = bf16[4,4,256,128]{3,2,1,0:T(8,128)(2,1)S(1)} collective-permute-done((bf16[4,4,256,128]{3,2,1,0:T(8,128)(2,1)S(1)}, bf16[4,4,256,128]{3,2,1,0:T(8,128)(2,1)S(1)}, u32[]{:S(2)}, u32[]{:S(2)}) %collective-permute-start.14) | collective-permute-done | bytes 1048608 | tf_op jit(solution)/shard_map/ppermute | solution.py:601
  90.3 9.2 %collective-permute-done.13.refs_0_ = bf16[4,4,256,128]{3,2,1,0:T(8,128)(2,1)S(1)} collective-permute-done((bf16[4,4,256,128]{3,2,1,0:T(8,128)(2,1)S(1)}, bf16[4,4,256,128]{3,2,1,0:T(8,128)(2,1)S(1)}, u32[]{:S(2)}, u32[]{:S(2)}) %collective-permute-start.13) | collective-permute-done | bytes 1048608 | tf_op jit(solution)/shard_map/ppermute | solution.py:656
  99.5 0.9 copy-done.9
  100.5 0.1 collective-permute-start.19
  100.6 7.5 %last_panel.1 = (f32[512,512]{1,0:T(8,128)S(1)}, bf16[512,512]{1,0:T(8,128)(2,1)S(1)}, bf16[512,512]{1,0:T(8,128)(2,1)S(1)}, bf16[512,512]{1,0:T(8,128)(2,1)S(1)}) custom-call(f32[512,1024]{1,0:T(8,128)S(1)} %next_panel.3.refs_6_.aug_in, bf16[4,4,256,128]{3,2,1,0:T(8,128)(2,1)S(1)} %get-tuple-element.49.after.refs_1_.refs_0_, ...), custom_call_target="tpu_custom_call" | custom-call | tf_op jit(solution)/shard_map/last_panel/pallas_call | solution.py:396
  108.2 10.4 %collective-permute-done.18.refs_1_ = bf16[4,256,128]{2,1,0:T(8,128)(2,1)S(1)} collective-permute-done((bf16[4,256,128]{2,1,0:T(8,128)(2,1)S(1)}, bf16[4,256,128]{2,1,0:T(8,128)(2,1)S(1)}, u32[]{:S(2)}, u32[]{:S(2)}) %collective-permute-start.18) | collective-permute-done | bytes 262176 | tf_op jit(solution)/shard_map/ppermute | solution.py:652
  118.5 0.7 collect.1.refs_1_
  119.3 0.1 copy-done.3
  119.4 2.7 %collective-permute-start.21 = (bf16[2,4,4,256,128]{4,3,2,1,0:T(8,128)(2,1)S(1)}, bf16[2,4,4,256,128]{4,3,2,1,0:T(8,128)(2,1)S(1)}, u32[]{:S(2)}, u32[]{:S(2)}) collective-permute-start(bf16[2,4,4,256,128]{4,3,2,1,0:T(8,128)(2,1)S(1)} %collect.1.refs_1_), channel_id=1, source_target_pairs={{0,4},{8,12},{1,5},{9,13},{6,2},{14,10},{7,3},{15,11},{24,28},{16,... | collective-permute-start | bytes 6291464 | tf_op jit(solution)/shard_map/ppermute | solution.py:601
  122.1 0.7 assemble.3.own_rest
  122.8 0.1 collective-permute-start.20
  122.9 2.6 %collective-permute-done.21.refs_2_ = bf16[2,4,4,256,128]{4,3,2,1,0:T(8,128)(2,1)S(1)} collective-permute-done((bf16[2,4,4,256,128]{4,3,2,1,0:T(8,128)(2,1)S(1)}, bf16[2,4,4,256,128]{4,3,2,1,0:T(8,128)(2,1)S(1)}, u32[]{:S(2)}, u32[]{:S(2)}) %collective-permute-start.21) | collective-permute-done | bytes 2097184 | tf_op jit(solution)/shard_map/ppermute | solution.py:601
  125.5 1.4 copy-done.20
  126.8 18.0 %multiply_part.2 = (f32[4096,2048]{1,0:T(8,128)}, bf16[512,2048]{1,0:T(8,128)(2,1)}) custom-call(s32[19]{0:T(128)} %stack.91.place_ref, bf16[4,256,128]{2,1,0:T(8,128)(2,1)} %get-tuple-element.48.own_first, bf16[3,4,256,128]{3,2,1,0:T(8,128)(2,1)} %copy-done.13, bf16[2,4,256,128]{3,2,1,0:T(8,128)(2,1)} %copy-done.4, bf16[3,4,256,128]{3,2,1,0:T(8,128)(2,1)} %copy-done.3, ...), custom_call_target="tpu_custom_call" | custom-call | tf_op jit(solution)/shard_map/multiply_part/pallas_call | solution.py:555
  144.9 0.9 copy-done.21
  145.9 11.3 %multiply_part.3 = f32[4096,2048]{1,0:T(8,128)} custom-call(s32[19]{0:T(128)} %stack.91.place_ref, bf16[4,256,128]{2,1,0:T(8,128)(2,1)} %copy-done.10, bf16[3,4,256,128]{3,2,1,0:T(8,128)(2,1)} %copy-done.11, bf16[2,4,256,128]{3,2,1,0:T(8,128)(2,1)} %copy-done.4, bf16[3,4,256,128]{3,2,1,0:T(8,128)(2,1)} %copy-done.21, ...), custom_call_target="tpu_custom_call", output_to_operand_aliasing={{}: (6, {})} | custom-call | tf_op jit(solution)/shard_map/multiply_part/pallas_call | solution.py:555
  (62 shorter events, 0.2 us)
Async XLA Ops:
  0.0 46.6 %copy-start.14 = (f32[16384]{0:T(1024)S(1)}, f32[16384]{0:T(1024)}, u32[]{:S(2)}) copy-start(f32[16384]{0:T(1024)} %param.9) | copy-start | bytes 196612
  0.0 46.6 %copy-start.19 = (f32[64]{0:T(128)S(1)}, f32[64]{0:T(128)}, u32[]{:S(2)}) copy-start(f32[64]{0:T(128)} %taps_ref.1) | copy-start | bytes 772
  0.7 45.9 %copy-start.18 = (s32[19]{0:T(128)S(1)}, s32[19]{0:T(128)}, u32[]{:S(2)}) copy-start(s32[19]{0:T(128)} %stack.91.place_ref) | copy-start | bytes 232
  4.6 0.7 collective-permute-start
  6.2 3.4 %collective-permute-start.1 = (bf16[1,272,128]{2,1,0:T(8,128)(2,1)S(1)}, bf16[1,272,128]{2,1,0:T(8,128)(2,1)S(1)}, u32[]{:S(2)}, u32[]{:S(2)}) collective-permute-start(bf16[1,272,128]{2,1,0:T(8,128)(2,1)S(1)} %get-tuple-element.64), channel_id=1, source_target_pairs={{0,1},{1,2},{2,3},{3,0},{8,9},{9,10},{10,11},{11,8},{16,17},{17,18... | collective-permute-start | bytes 208904 | tf_op jit(solution)/shard_map/ppermute | solution.py:623
  6.9 4.2 %collective-permute-start.7 = (bf16[1,272,128]{2,1,0:T(8,128)(2,1)S(1)}, bf16[1,272,128]{2,1,0:T(8,128)(2,1)S(1)}, u32[]{:S(2)}, u32[]{:S(2)}) collective-permute-start(bf16[1,272,128]{2,1,0:T(8,128)(2,1)S(1)} %get-tuple-element.64), channel_id=1, source_target_pairs={{0,19},{1,16},{2,17},{3,18},{8,27},{9,24},{10,25},{11,26},{16,3},{... | collective-permute-start | bytes 208904 | tf_op jit(solution)/shard_map/ppermute | solution.py:623
  7.6 3.5 %collective-permute-start.6 = (bf16[1,272,128]{2,1,0:T(8,128)(2,1)S(1)}, bf16[1,272,128]{2,1,0:T(8,128)(2,1)S(1)}, u32[]{:S(2)}, u32[]{:S(2)}) collective-permute-start(bf16[1,272,128]{2,1,0:T(8,128)(2,1)S(1)} %get-tuple-element.64), channel_id=1, source_target_pairs={{0,18},{1,19},{2,16},{3,17},{8,26},{9,27},{10,24},{11,25},{16,2},{... | collective-permute-start | bytes 208904 | tf_op jit(solution)/shard_map/ppermute | solution.py:623
  8.3 2.8 %collective-permute-start.5 = (bf16[1,272,128]{2,1,0:T(8,128)(2,1)S(1)}, bf16[1,272,128]{2,1,0:T(8,128)(2,1)S(1)}, u32[]{:S(2)}, u32[]{:S(2)}) collective-permute-start(bf16[1,272,128]{2,1,0:T(8,128)(2,1)S(1)} %get-tuple-element.64), channel_id=1, source_target_pairs={{0,17},{1,18},{2,19},{3,16},{8,25},{9,26},{10,27},{11,24},{16,1},{... | collective-permute-start | bytes 208904 | tf_op jit(solution)/shard_map/ppermute | solution.py:623
  8.9 2.1 %collective-permute-start.4 = (bf16[1,272,128]{2,1,0:T(8,128)(2,1)S(1)}, bf16[1,272,128]{2,1,0:T(8,128)(2,1)S(1)}, u32[]{:S(2)}, u32[]{:S(2)}) collective-permute-start(bf16[1,272,128]{2,1,0:T(8,128)(2,1)S(1)} %get-tuple-element.64), channel_id=1, source_target_pairs={{0,16},{1,17},{2,18},{3,19},{8,24},{9,25},{10,26},{11,27},{16,0},{... | collective-permute-start | bytes 208904 | tf_op jit(solution)/shard_map/ppermute | solution.py:623
  9.6 0.7 collective-permute-start.2
  10.3 0.7 collective-permute-start.3
  11.2 35.5 %collective-permute-start.11 = (bf16[8,272,128]{2,1,0:T(8,128)(2,1)S(1)}, bf16[8,272,128]{2,1,0:T(8,128)(2,1)S(1)}, u32[]{:S(2)}, u32[]{:S(2)}) collective-permute-start(bf16[8,272,128]{2,1,0:T(8,128)(2,1)S(1)} %constant_dynamic-update-slice_fusion.refs_3_.own_ref.after), channel_id=1, source_target_pairs={{0,4},{8,12},{1,5},{9,13},{2,6},{10,14},{3,7},{11,15},{16,20},{24,... | collective-permute-start | bytes 1671176 | tf_op jit(solution)/shard_map/ppermute | solution.py:625
  12.5 1.0 copy-start.5
  13.4 47.4 %copy-start.6 = (bf16[4,256,128]{2,1,0:T(8,128)(2,1)}, bf16[4,256,128]{2,1,0:T(8,128)(2,1)S(1)}, u32[]{:S(2)}) copy-start(bf16[4,256,128]{2,1,0:T(8,128)(2,1)S(1)} %get-tuple-element.38.refs_4_) | copy-start | bytes 786436
  13.4 47.5 %collective-permute-start.12 = (bf16[2,4,256,128]{3,2,1,0:T(8,128)(2,1)}, bf16[2,4,256,128]{3,2,1,0:T(8,128)(2,1)S(1)}, u32[]{:S(2)}, u32[]{:S(2)}) collective-permute-start(bf16[2,4,256,128]{3,2,1,0:T(8,128)(2,1)} %get-tuple-element.41), channel_id=1, source_target_pairs={{16,0},{17,1},{18,2},{19,3},{20,4},{21,5},{22,6},{23,7},{24,8},{25... | collective-permute-start | bytes 1572872 | tf_op jit(solution)/shard_map/ppermute | solution.py:656
  14.6 46.2 %collective-permute-start.9 = (bf16[4,256,128]{2,1,0:T(8,128)(2,1)}, bf16[4,256,128]{2,1,0:T(8,128)(2,1)S(1)}, u32[]{:S(2)}, u32[]{:S(2)}) collective-permute-start(bf16[4,256,128]{2,1,0:T(8,128)(2,1)} %get-tuple-element.39.refs_3_), channel_id=1, source_target_pairs={{2,0},{3,1},{0,2},{1,3},{6,4},{7,5},{4,6},{5,7},{10,8},{11,9},{8,1... | collective-permute-start | bytes 786440 | tf_op jit(solution)/shard_map/ppermute | solution.py:652
  14.7 46.2 %collective-permute-start.10 = (bf16[4,256,128]{2,1,0:T(8,128)(2,1)S(1)}, bf16[4,256,128]{2,1,0:T(8,128)(2,1)S(1)}, u32[]{:S(2)}, u32[]{:S(2)}) collective-permute-start(bf16[4,256,128]{2,1,0:T(8,128)(2,1)S(1)} %get-tuple-element.38.refs_4_), channel_id=1, source_target_pairs={{1,0},{2,1},{3,2},{0,3},{5,4},{6,5},{7,6},{4,7},{9,8},{10,9},{11,1... | collective-permute-start | bytes 786440 | tf_op jit(solution)/shard_map/ppermute | solution.py:652
  14.8 46.0 %collective-permute-start.8 = (bf16[4,256,128]{2,1,0:T(8,128)(2,1)S(1)}, bf16[4,256,128]{2,1,0:T(8,128)(2,1)S(1)}, u32[]{:S(2)}, u32[]{:S(2)}) collective-permute-start(bf16[4,256,128]{2,1,0:T(8,128)(2,1)S(1)} %get-tuple-element.38.refs_4_), channel_id=1, source_target_pairs={{3,0},{0,1},{1,2},{2,3},{7,4},{4,5},{5,6},{6,7},{11,8},{8,9},{9,10... | collective-permute-start | bytes 786440 | tf_op jit(solution)/shard_map/ppermute | solution.py:652
  54.9 5.9 %copy-start.12 = (bf16[4,384,256]{2,1,0:T(8,128)(2,1)}, bf16[4,384,256]{2,1,0:T(8,128)(2,1)S(1)}, u32[]{:S(2)}) copy-start(bf16[4,384,256]{2,1,0:T(8,128)(2,1)S(1)} %get-tuple-element.60.refs_6_) | copy-start | bytes 2359300
  60.9 1.0 copy-start.7
  61.8 19.1 %copy-start.4 = (bf16[2,4,256,128]{3,2,1,0:T(8,128)(2,1)}, bf16[2,4,256,128]{3,2,1,0:T(8,128)(2,1)S(1)}, u32[]{:S(2)}) copy-start(bf16[2,4,256,128]{3,2,1,0:T(8,128)(2,1)S(1)} %collective-permute-done.12.refs_6_.other_first) | copy-start | bytes 1572868
  63.4 17.5 %copy-start.8 = (bf16[4,256,128]{2,1,0:T(8,128)(2,1)}, bf16[4,256,128]{2,1,0:T(8,128)(2,1)S(1)}, u32[]{:S(2)}) copy-start(bf16[4,256,128]{2,1,0:T(8,128)(2,1)S(1)} %get-tuple-element.44.refs_5_) | copy-start | bytes 786436
  63.5 17.5 %copy-start.13 = (bf16[3,4,256,128]{3,2,1,0:T(8,128)(2,1)}, bf16[3,4,256,128]{3,2,1,0:T(8,128)(2,1)S(1)}, u32[]{:S(2)}) copy-start(bf16[3,4,256,128]{3,2,1,0:T(8,128)(2,1)S(1)} %get-tuple-element.47.own_rest) | copy-start | bytes 2359300
  63.5 18.8 %collective-permute-start.15 = (bf16[4,4,256,128]{3,2,1,0:T(8,128)(2,1)S(1)}, bf16[4,4,256,128]{3,2,1,0:T(8,128)(2,1)S(1)}, u32[]{:S(2)}, u32[]{:S(2)}) collective-permute-start(bf16[4,4,256,128]{3,2,1,0:T(8,128)(2,1)S(1)} %get-tuple-element.42.after.refs_0_), channel_id=1, source_target_pairs={{16,8},{17,9},{22,14},{23,15},{8,16},{9,17},{14,22},{15,23}} | collective-permute-start | bytes 3145736 | tf_op jit(solution)/shard_map/ppermute | solution.py:666
  64.2 26.1 %collective-permute-start.14 = (bf16[4,4,256,128]{3,2,1,0:T(8,128)(2,1)S(1)}, bf16[4,4,256,128]{3,2,1,0:T(8,128)(2,1)S(1)}, u32[]{:S(2)}, u32[]{:S(2)}) collective-permute-start(bf16[4,4,256,128]{3,2,1,0:T(8,128)(2,1)S(1)} %get-tuple-element.42.after.refs_0_), channel_id=1, source_target_pairs={{0,8},{1,9},{6,14},{7,15},{24,16},{25,17},{30,22},{31,23}} | collective-permute-start | bytes 3145736 | tf_op jit(solution)/shard_map/ppermute | solution.py:601
  69.8 29.8 %collective-permute-start.13 = (bf16[4,4,256,128]{3,2,1,0:T(8,128)(2,1)S(1)}, bf16[4,4,256,128]{3,2,1,0:T(8,128)(2,1)S(1)}, u32[]{:S(2)}, u32[]{:S(2)}) collective-permute-start(bf16[4,4,256,128]{3,2,1,0:T(8,128)(2,1)S(1)} %get-tuple-element.42.after.refs_0_), channel_id=1, source_target_pairs={{16,0},{17,1},{22,6},{23,7},{8,24},{9,25},{14,30},{15,31}} | collective-permute-start | bytes 3145736 | tf_op jit(solution)/shard_map/ppermute | solution.py:656
  71.1 37.1 %collective-permute-start.17 = (bf16[3,4,256,128]{3,2,1,0:T(8,128)(2,1)S(1)}, bf16[3,4,256,128]{3,2,1,0:T(8,128)(2,1)S(1)}, u32[]{:S(2)}, u32[]{:S(2)}) collective-permute-start(bf16[3,4,256,128]{3,2,1,0:T(8,128)(2,1)S(1)} %get-tuple-element.47.own_rest), channel_id=1, source_target_pairs={{18,2},{19,3},{20,4},{21,5},{24,8},{25,9},{26,10},{27,11},{28,12},... | collective-permute-start | bytes 2359304 | tf_op jit(solution)/shard_map/ppermute | solution.py:656
  75.2 7.1 %collective-permute-start.16 = (bf16[4,256,128]{2,1,0:T(8,128)(2,1)}, bf16[4,256,128]{2,1,0:T(8,128)(2,1)S(1)}, u32[]{:S(2)}, u32[]{:S(2)}) collective-permute-start(bf16[4,256,128]{2,1,0:T(8,128)(2,1)} %get-tuple-element.43.refs_4_), channel_id=1, source_target_pairs={{3,0},{0,1},{1,2},{2,3},{7,4},{4,5},{5,6},{6,7},{11,8},{8,9},{9,10... | collective-permute-start | bytes 786440 | tf_op jit(solution)/shard_map/ppermute | solution.py:652
  99.5 1.0 copy-start.9
  100.5 18.0 %copy-start.10 = (bf16[4,256,128]{2,1,0:T(8,128)(2,1)}, bf16[4,256,128]{2,1,0:T(8,128)(2,1)S(1)}, u32[]{:S(2)}) copy-start(bf16[4,256,128]{2,1,0:T(8,128)(2,1)S(1)} %get-tuple-element.45.own_first) | copy-start | bytes 786436
  100.5 18.0 %copy-start.1 = (bf16[4,4,256,128]{3,2,1,0:T(8,128)(2,1)}, bf16[4,4,256,128]{3,2,1,0:T(8,128)(2,1)S(1)}, u32[]{:S(2)}) copy-start(bf16[4,4,256,128]{3,2,1,0:T(8,128)(2,1)S(1)} %get-tuple-element.49.after.refs_1_.refs_0_) | copy-start | bytes 3145732
  100.5 18.0 %collective-permute-start.18 = (bf16[4,256,128]{2,1,0:T(8,128)(2,1)S(1)}, bf16[4,256,128]{2,1,0:T(8,128)(2,1)S(1)}, u32[]{:S(2)}, u32[]{:S(2)}) collective-permute-start(bf16[4,256,128]{2,1,0:T(8,128)(2,1)S(1)} %get-tuple-element.45.own_first), channel_id=1, source_target_pairs={{2,0},{3,1},{0,2},{1,3},{6,4},{7,5},{4,6},{5,7},{10,8},{11,9},{8,1... | collective-permute-start | bytes 786440 | tf_op jit(solution)/shard_map/ppermute | solution.py:652
  100.5 18.0 %collective-permute-start.19 = (bf16[4,256,128]{2,1,0:T(8,128)(2,1)}, bf16[4,256,128]{2,1,0:T(8,128)(2,1)S(1)}, u32[]{:S(2)}, u32[]{:S(2)}) collective-permute-start(bf16[4,256,128]{2,1,0:T(8,128)(2,1)} %get-tuple-element.48.own_first), channel_id=1, source_target_pairs={{1,0},{2,1},{3,2},{0,3},{5,4},{6,5},{7,6},{4,7},{9,8},{10,9},{11,1... | collective-permute-start | bytes 786440 | tf_op jit(solution)/shard_map/ppermute | solution.py:652
  108.1 11.2 %copy-start.15 = (bf16[512,512]{1,0:T(8,128)(2,1)}, bf16[512,512]{1,0:T(8,128)(2,1)S(1)}, u32[]{:S(2)}) copy-start(bf16[512,512]{1,0:T(8,128)(2,1)S(1)} %get-tuple-element.57.refs_3_) | copy-start | bytes 1572868
  108.1 11.2 %copy-start.16 = (bf16[512,512]{1,0:T(8,128)(2,1)}, bf16[512,512]{1,0:T(8,128)(2,1)S(1)}, u32[]{:S(2)}) copy-start(bf16[512,512]{1,0:T(8,128)(2,1)S(1)} %get-tuple-element.58.refs_4_) | copy-start | bytes 1572868
  108.1 11.2 %copy-start.17 = (bf16[512,512]{1,0:T(8,128)(2,1)}, bf16[512,512]{1,0:T(8,128)(2,1)S(1)}, u32[]{:S(2)}) copy-start(bf16[512,512]{1,0:T(8,128)(2,1)S(1)} %get-tuple-element.59.refs_5_) | copy-start | bytes 1572868
  108.1 14.0 %copy-start = (f32[512,512]{1,0:T(8,128)}, f32[512,512]{1,0:T(8,128)S(1)}, u32[]{:S(2)}) copy-start(f32[512,512]{1,0:T(8,128)S(1)} %get-tuple-element.51.refs_3_.refs_7_.refs_2_) | copy-start | bytes 3145732
  118.5 0.9 copy-start.3
  119.4 7.4 %copy-start.2 = (bf16[2,4,4,256,128]{4,3,2,1,0:T(8,128)(2,1)}, bf16[2,4,4,256,128]{4,3,2,1,0:T(8,128)(2,1)S(1)}, u32[]{:S(2)}) copy-start(bf16[2,4,4,256,128]{4,3,2,1,0:T(8,128)(2,1)S(1)} %collect.1.refs_1_) | copy-start | bytes 6291460
  119.4 6.1 %collective-permute-start.21 = (bf16[2,4,4,256,128]{4,3,2,1,0:T(8,128)(2,1)S(1)}, bf16[2,4,4,256,128]{4,3,2,1,0:T(8,128)(2,1)S(1)}, u32[]{:S(2)}, u32[]{:S(2)}) collective-permute-start(bf16[2,4,4,256,128]{4,3,2,1,0:T(8,128)(2,1)S(1)} %collect.1.refs_1_), channel_id=1, source_target_pairs={{0,4},{8,12},{1,5},{9,13},{6,2},{14,10},{7,3},{15,11},{24,28},{16,... | collective-permute-start | bytes 6291464 | tf_op jit(solution)/shard_map/ppermute | solution.py:601
  122.8 22.1 %copy-start.11 = (bf16[3,4,256,128]{3,2,1,0:T(8,128)(2,1)}, bf16[3,4,256,128]{3,2,1,0:T(8,128)(2,1)S(1)}, u32[]{:S(2)}) copy-start(bf16[3,4,256,128]{3,2,1,0:T(8,128)(2,1)S(1)} %assemble.3.own_rest) | copy-start | bytes 2359300
  122.8 22.1 %collective-permute-start.20 = (bf16[3,4,256,128]{3,2,1,0:T(8,128)(2,1)S(1)}, bf16[3,4,256,128]{3,2,1,0:T(8,128)(2,1)S(1)}, u32[]{:S(2)}, u32[]{:S(2)}) collective-permute-start(bf16[3,4,256,128]{3,2,1,0:T(8,128)(2,1)S(1)} %assemble.3.own_rest), channel_id=1, source_target_pairs={{16,0},{17,1},{18,2},{19,3},{20,4},{21,5},{22,6},{23,7},{24,8},{25... | collective-permute-start | bytes 2359304 | tf_op jit(solution)/shard_map/ppermute | solution.py:656
  125.5 1.4 copy-start.20
  144.9 1.0 copy-start.21

commit v7 on v6

--- a/solution.py
+++ b/solution.py
@@ -38,6 +38,7 @@
 ANY = pl.BlockSpec(memory_space=pl.ANY)
 FREE = pl.CostEstimate(flops=0, bytes_accessed=0, transcendentals=0)
 LIMIT = pltpu.CompilerParams(vmem_limit_bytes=24 << 20)
+MIDDLE = pltpu.CompilerParams(vmem_limit_bytes=32 << 20)
 WIDE = pltpu.CompilerParams(vmem_limit_bytes=58 << 20)
 
 
@@ -112,7 +113,7 @@
     )(place, order.reshape(rows // PB, PB), tap_count.reshape(1, epochs), design)
 
 
-PLACE_ROW, PLACE_GROUP, PLACE_EP, PLACE_COL, PLACE_TAKES, PLACE_OWNS, PLACE_FAR, PLACE_BACK = range(8)
+PLACE_ROW, PLACE_GROUP, PLACE_EP, PLACE_COL, PLACE_TAKES, PLACE_OWNS, PLACE_HOME, PLACE_BACK = range(8)
 
 
 def assemble_kernel(count, gated, after, whole, place_ref, *refs):
@@ -147,32 +148,36 @@
     )(place, *shards, *gated, *after)
 
 
-def collect_kernel(place_ref, *refs):
-    near, far, (out_ref, sem) = refs[:2], refs[2:4], refs[5:]
-
-    def copy(sources):
+def sort_kernel(place_ref, native_ref, foreign_ref, keep_ref, send_ref, sem):
+    def copy(kept, sent):
         copies = [
-            pltpu.make_async_copy(source, out_ref.at[n], sem.at[n]) for n, source in enumerate(sources)
+            pltpu.make_async_copy(kept, keep_ref, sem.at[0]),
+            pltpu.make_async_copy(sent, send_ref, sem.at[1]),
         ]
         for c in copies:
             c.start()
         for c in copies:
             c.wait()
 
-    choose(place_ref[PLACE_FAR] != 0, lambda: copy(far), lambda: copy(near))
-
-
-def collect(place, near, far, after):
-    return pl.pallas_call(
-        collect_kernel,
-        out_shape=jax.ShapeDtypeStruct((2,) + near[0].shape, BF16),
-        in_specs=[SMEM] + [ANY] * 5,
-        out_specs=ANY,
+    choose(
+        place_ref[PLACE_HOME] != 0,
+        lambda: copy(native_ref, foreign_ref),
+        lambda: copy(foreign_ref, native_ref),
+    )
+
+
+def sort(place, native, foreign):
+    shape = jax.ShapeDtypeStruct(native.shape, BF16)
+    return pl.pallas_call(
+        sort_kernel,
+        out_shape=(shape, shape),
+        in_specs=[SMEM, ANY, ANY],
+        out_specs=(ANY, ANY),
         scratch_shapes=[pltpu.SemaphoreType.DMA((2,))],
         compiler_params=LIMIT,
         cost_estimate=FREE,
-        name="collect",
-    )(place, *near, *far, after)
+        name="sort",
+    )(place, native, foreign)
 
 
 def gate(arrays, after):
@@ -341,7 +346,7 @@
         here = slice(b * BLOCK, (b + 1) * BLOCK)
         shape = (BLOCK, epochs)
         unit = jnp.where(iota(shape, 0) + b * BLOCK == iota(shape, 1), 1.0, 0.0)
-        keep(here, slice(0, epochs), unit - dot(wt[:, here], wt, TN, precision=EXACT))
+        keep(here, slice(0, epochs), unit - dot(wt[:, here], wt, TN, precision=lax.Precision.HIGH))
     count, half = taper_ref.shape[:2]
     for e in range(count):
         reach = min(LANES, epochs - e * half)
@@ -429,10 +434,6 @@
         blocks[there + back] = other[n][...]
 
 
-def unpack_both(place_ref, both, block, blocks):
-    unpack(place_ref, shards_of(both.at[0], block), shards_of(both.at[1], block), blocks)
-
-
 def choose(condition, yes, no):
     pl.when(condition)(yes)
     pl.when(jnp.logical_not(condition))(no)
@@ -444,40 +445,71 @@
     )
 
 
+def project_kernel(
+    place_ref, own, own_came, other, other_came, w_ref, high_ref, low_ref, band_ref, right_ref,
+    both, blocks, columns, sem,
+):
+    def bring(sources):
+        copies = [
+            pltpu.make_async_copy(source, both.at[n], sem.at[n]) for n, source in enumerate(sources)
+        ]
+        for copy in copies:
+            copy.start()
+        for copy in copies:
+            copy.wait()
+
+    choose(
+        place_ref[PLACE_TAKES] != 0,
+        lambda: bring((own_came, other_came)),
+        lambda: bring((own, other)),
+    )
+
+    def store(rows, cols, got):
+        columns[rows, cols] = got
+
+    rows = 2 * HALF
+    for n in range(right_ref.shape[1] // rows):
+        unpack(place_ref, shards_of(both.at[0], n), shards_of(both.at[1], n), blocks)
+        filter_rows(lambda e: blocks[e], band_ref, store)
+        wanted = columns[...]
+        projected = dot(high_ref[...], wanted, NT) + dot(low_ref[...], wanted, NT)
+        right_ref[:, n * rows : (n + 1) * rows] = projected.astype(BF16)
+
+    @pl.when(place_ref[PLACE_GROUP] == 0)
+    def _():
+        right_ref[:, :HEAD] = w_ref[...]
+
+
+def project(place, own, own_came, other, other_came, w, high, low, band):
+    width, count = own.shape[:2]
+    epochs = high.shape[0]
+    return pl.pallas_call(
+        project_kernel,
+        out_shape=jax.ShapeDtypeStruct((epochs, count * 2 * HALF), BF16),
+        in_specs=[SMEM] + [ANY] * 4 + [VMEM] * 4,
+        out_specs=VMEM,
+        scratch_shapes=[
+            pltpu.VMEM((2,) + own.shape, BF16),
+            pltpu.VMEM((2 * width, HALF, LANES), BF16),
+            pltpu.VMEM((2 * HALF, epochs), BF16),
+            pltpu.SemaphoreType.DMA((2,)),
+        ],
+        compiler_params=LIMIT,
+        cost_estimate=FREE,
+        name="project",
+    )(place, own, own_came, other, other_came, w, high, low, band)
+
+
 def tile_kernel(part, parts, place_ref, own_first, own_rest, other_first, other_rest, *refs):
-    if part == 0:
-        theirs_ref, near_ref, came_ref, w_ref, high_ref, low_ref, band_ref = refs[:7]
-        factor_ref, reg_ref, out_ref, right_ref, blocks, lhs, columns = refs[7:]
-    else:
-        right_ref, _, factor_ref, reg_ref, out_ref, blocks, lhs = refs
+    theirs_ref = refs[0]
+    right_ref, factor_ref, reg_ref = refs[:3] if part else refs[1:4]
+    out_ref, blocks, lhs = refs[-3:]
     i, steps = pl.program_id(0), pl.num_programs(0)
     rows, cols = out_ref.shape
     half = LANES // 2
     block = lax.rem(place_ref[PLACE_COL] + part, parts) * steps + i
     first_row = (place_ref[PLACE_ROW] * parts * steps + block) * rows
     first_col = place_ref[PLACE_GROUP] * cols
-
-    if part == 0:
-
-        @pl.when(i == 0)
-        def _():
-            def store(rows, cols, got):
-                columns[rows, cols] = got
-
-            for n in range(cols // rows):
-                choose(
-                    place_ref[PLACE_TAKES] != 0,
-                    lambda: unpack_both(place_ref, came_ref, n, blocks),
-                    lambda: unpack_both(place_ref, near_ref, n, blocks),
-                )
-                filter_rows(lambda e: blocks[e], band_ref, store)
-                wanted = columns[...]
-                projected = dot(high_ref[...], wanted, NT) + dot(low_ref[...], wanted, NT)
-                right_ref[:, n * rows : (n + 1) * rows] = projected.astype(BF16)
-
-            @pl.when(first_col == 0)
-            def _():
-                right_ref[:, :HEAD] = w_ref[...]
 
     @pl.when(first_row >= HEAD)
     def _():
@@ -513,11 +545,10 @@
             out_ref[:, :HEAD] = factor_ref[...]
 
 
-def multiply_part(part, parts, place, own, other, factor, regular, extra, out, right):
+def multiply_part(part, parts, place, own, other, theirs, right, factor, regular, out):
     steps = own[0].shape[0]
     rows = 2 * HALF
-    cols = steps * rows
-    epochs = (own[1].shape[0] + 1) * 2 * (LANES // 2)
+    epochs, cols = right.shape
 
     def reg_block(i, place):
         block = lax.rem(place[PLACE_COL] + part, parts) * steps + i
@@ -529,41 +560,33 @@
     def shards_spec(array):
         return pl.BlockSpec((array.shape[0], 1, HALF, LANES), lambda i, place: (0, i, 0, 0))
 
-    out_shape = [jax.ShapeDtypeStruct((parts * steps * rows, cols), F32)]
-    out_specs = [pl.BlockSpec((rows, cols), out_block)]
-    scratch = [
-        pltpu.VMEM((epochs // (LANES // 2), HALF, LANES), BF16),
-        pltpu.VMEM((rows, epochs), BF16),
-    ]
     operands = [*own, *other]
     in_specs = [pl.BlockSpec((1, HALF, LANES), lambda i, place: (i, 0, 0)), shards_spec(own[1])]
     in_specs += [pl.BlockSpec((1, 1, HALF, LANES), lambda i, place: (part, i, 0, 0))]
     in_specs += [shards_spec(other[1])]
     if part == 0:
-        operands += extra
-        in_specs += [shards_spec(extra[0])]
-        in_specs += [fixed(array) for array in extra[1:]]
-        out_shape.append(jax.ShapeDtypeStruct((epochs, cols), BF16))
-        out_specs.append(pl.BlockSpec((epochs, cols), lambda i, place: (0, 0)))
-        scratch.append(pltpu.VMEM((rows, epochs), BF16))
-    else:
-        operands += [right, out]
-        in_specs += [fixed(right), ANY]
-    alias = {len(operands): 0} if part else {}
-    operands += [factor, regular.reshape(1, -1)]
-    in_specs += [fixed(factor), pl.BlockSpec((1, rows), reg_block)]
+        operands.append(theirs)
+        in_specs.append(shards_spec(theirs))
+    operands += [right, factor, regular.reshape(1, -1)]
+    in_specs += [fixed(right), fixed(factor), pl.BlockSpec((1, rows), reg_block)]
+    if part:
+        operands.append(out)
+        in_specs.append(ANY)
     return pl.pallas_call(
         functools.partial(tile_kernel, part, parts),
-        out_shape=out_shape,
+        out_shape=jax.ShapeDtypeStruct((parts * steps * rows, cols), F32),
         grid_spec=pltpu.PrefetchScalarGridSpec(
             num_scalar_prefetch=1,
             grid=(steps,),
             in_specs=in_specs,
-            out_specs=out_specs,
-            scratch_shapes=scratch,
+            out_specs=pl.BlockSpec((rows, cols), out_block),
+            scratch_shapes=[
+                pltpu.VMEM((epochs // (LANES // 2), HALF, LANES), BF16),
+                pltpu.VMEM((rows, epochs), BF16),
+            ],
         ),
-        input_output_aliases=alias,
-        compiler_params=WIDE,
+        input_output_aliases={len(operands): 0} if part else {},
+        compiler_params=MIDDLE,
         cost_estimate=FREE,
         name="multiply_part",
     )(place, *operands)
@@ -601,9 +624,9 @@
     return lax.ppermute(block, AXES, route)
 
 
-def panel_steps():
+def panel_hops():
     eps, _, cols = sizes()
-    return [(de, dc) for de in range(eps) for dc in range(cols)]
+    return [(d, 0) for d in doubling(eps, 1)] + [(0, d) for d in reversed(doubling(cols, 1))]
 
 
 def gather_panel(note):
@@ -612,18 +635,16 @@
     for distance in doubling(rows, 2):
         came = spread_step(note, lambda e, c: 0, distance)
         note = jnp.where((row & (2 * distance - 1)) == distance, came, note)
-    notes = [note]
-    for de, dc in panel_steps()[1:]:
+    for de, dc in panel_hops():
         route = [
-            (flat(e, r, c), flat((e + de) % eps, r, (c + dc) % cols))
+            (flat(e, r, c), flat(e ^ de, r, c ^ dc))
             for e in range(eps)
             for r in range(0, rows, 2)
             for c in range(cols)
         ]
-        notes.append(lax.ppermute(note, AXES, route))
-    notes = jnp.concatenate(notes)
-    came = lax.ppermute(notes, "row", [(r, r + 1) for r in range(0, rows, 2)])
-    return notes, came
+        note = jnp.concatenate([note, lax.ppermute(note, AXES, route)])
+    came = lax.ppermute(note, "row", [(r, r + 1) for r in range(0, rows, 2)])
+    return note, came
 
 
 def on_device(design, taps, tap_count, order, regular):
@@ -635,14 +656,18 @@
     group = lax.axis_index(("ep", "col"))
     everywhere = [(e, r, c) for e in range(eps) for r in range(rows) for c in range(cols)]
     owner = lambda e, c: (e * cols + c) * cols_dev // rows_dev
-    owns = lambda e, r, c: (c // parts == (r * parts % cols) // parts) & (r * parts // cols == e)
+    inside = lambda r, c: c // parts == (r * parts % cols) // parts
+    owns = lambda e, r, c: inside(r, c) & (r * parts // cols == e)
     first_owner = group * cols_dev // rows_dev
     takes = ((row ^ first_owner) & 1) == 1
-    far = (row ^ first_owner) >= rows // 2
+    home = row * parts // cols == ep
     back = [(col - n) % cols for n in range(cols)]
-    place = [row, group, ep, col, takes, owns(ep, row, col), far, *back]
+    place = [row, group, ep, col, takes, owns(ep, row, col), home, *back]
     chain = len(place)
-    place += [((ep - de) % eps) * cols + (col - dc) % cols for de, dc in panel_steps()]
+    steps = [(0, 0)]
+    for de, dc in panel_hops():
+        steps += [(e ^ de, c ^ dc) for e, c in steps]
+    place += [(ep ^ de) * cols + (col ^ dc) for de, dc in steps]
     place = jnp.stack([jnp.asarray(p, jnp.int32) for p in place])
 
     *local, both, note = permute_local(place, design, order, tap_count, cols_dev)
@@ -657,54 +682,49 @@
 
     distances = doubling(rows, 1)
 
-    def diagonal(block):
+    def trade(block):
         route = [
-            (flat(1 - e, owner(e, c), c), flat(e, owner(e, c) ^ distances[0], c))
-            for e in range(eps)
-            for c in range(cols)
+            (flat(e, r, c), flat(e, r ^ distances[0], c)) for e, r, c in everywhere if inside(r, c)
         ]
         return lax.ppermute(block, AXES, route)
 
-    anyone = lambda e, r, c: True
+    def spread_rest(block):
+        for distance in distances[1:-1]:
+            got = spread_step(block, owner, distance)
+            hit = ((row ^ first_owner) & (2 * distance - 1)) == distance
+            block = jnp.where(hit, got, block)
+        return block, spread_step(block, owner, distances[-1])
+
     notes, came = gather_panel(note)
-    *local, both = gate([*local, both], notes)
     early = [shift(local[n % parts], n) for n in range(1, cols)]
-    swapped = across(both, anyone)
+    swapped = across(both, lambda e, r, c: True)
     band, taper, aug = start_panel(place, chain, taps, notes, came, regular, notes)
     aug = next_panel(1, aug, aug)
     rest, *local, first = assemble(place, early, local, [aug, swapped], True)
-    theirs = across(first, owns)
-    far_own = spread_step(first, owner, distances[0])
-    far_other = diagonal(first)
+    foreign = trade(first)
     others = [across(rest, lambda e, r, c: not owns(e, r, c))]
     mine = [rest]
     order = [(j, n) for j in range(1, parts) for n in range(1, cols)]
-    late = [shift(local[(n + j) % parts], n) for j, n in order[:1]]
+    late = [shift(local[(n + j) % parts], n) for j, n in order]
     aug = next_panel(2, aug, first)
-    theirs, far_own, far_other, *passed = gate([theirs, far_own, far_other, *late, *local], aug)
-    late, local = passed[: len(late)], passed[len(late) :]
-    late += [shift(local[(n + j) % parts], n) for j, n in order[1:]]
-    factor, w, high, low = last_panel(3, aug, theirs, taper)
-    others[0], *late[1:] = gate([others[0], *late[1:]], factor)
-    wanted = collect(place, [first, theirs], [far_own, far_other], others[0])
-    for distance in distances[1:]:
-        got = spread_step(wanted, owner, distance)
-        if distance > 1:
-            wanted = jnp.where(((row ^ first_owner) & (2 * distance - 1)) == distance, got, wanted)
+    foreign, *late[:1] = gate([foreign, *late[:1]], aug)
+    own, sent = sort(place, first, foreign)
+    theirs = across(sent, lambda e, r, c: inside(r, c))
+    factor, w, high, low = last_panel(3, aug, own, taper)
+    theirs, others[0], *late[1:] = gate([theirs, others[0], *late[1:]], factor)
+    own, own_came = spread_rest(own)
+    other, other_came = spread_rest(theirs)
     for j in range(1, parts):
         shards = late[(j - 1) * (cols - 1) : j * (cols - 1)]
         (whole,) = assemble(place, shards, [], [factor], False)
         mine.append(whole)
-        others.append(across(whole, anyone))
-    extra = [theirs, wanted, got, w, high, low, band]
-    mine = [(local[j], mine[j]) for j in range(parts)]
-    others = [(swapped, others[j]) for j in range(parts)]
-    out, right = multiply_part(
-        0, parts, place, mine[0], others[0], factor, regular, extra, None, None
-    )
-    for j in range(1, parts):
-        (out,) = multiply_part(
-            j, parts, place, mine[j], others[j], factor, regular, None, out, right
+        others.append(across(whole, lambda e, r, c: True))
+    right = project(place, own, own_came, other, other_came, w, high, low, band)
+    out = None
+    for j in range(parts):
+        out = multiply_part(
+            j, parts, place, (local[j], mine[j]), (swapped, others[j]), theirs, right, factor,
+            regular, out,
         )
     return out
 

time: 158 us -> 138 us (0.87)
  the two profiles are of different devices: /device:TPU:25 before, /device:TPU:0 now
where the time goes in v7:
time: 138 us; the launch traced here: 136 us
  Pallas kernels  54 us (39%)
  starting transfers between devices  44 us (32%)
  waiting for transfers between devices  36.5 us (26%)
    pallas_call x2, Pallas kernels, multiply_part(): pl.pallas_call(functools.partial(tile_kernel, part, parts), out_shape=jax...  17 us
    ppermute x3, waiting for transfers between devices, gather_panel(): note = jnp.concatenate([note, lax.ppermute(note, AXES, route)])  15.3 us
    ppermute x4, waiting for transfers between devices, across(): return lax.ppermute(block, AXES, route)  13.3 us
    pallas_call x2, Pallas kernels, next_panel(): pl.pallas_call(functools.partial(next_kernel, kb), out_shape=jax.ShapeDty...  11.3 us
    ppermute x3, starting transfers between devices, gather_panel(): note = jnp.concatenate([note, lax.ppermute(note, AXES, route)])  11.1 us
    ppermute x6, starting transfers between devices, shift(): return lax.ppermute(block, AXES, route)  10.7 us
    ppermute x4, starting transfers between devices, across(): return lax.ppermute(block, AXES, route)  9.76 us
    pallas_call x1, Pallas kernels, start_panel(): pl.pallas_call(functools.partial(start_kernel, chain), out_shape=(jax.Sha...  8.11 us
  transfers between devices with their start and end apart: 18, of which 7 were waited for; matrix products, arithmetic and copies ran while one was open for 0% of the time, Pallas kernels for 29%

profile of v7, /device:TPU:0, one launch (start us, length us, event | category | flops | bytes accessed | tf_op | source)
XLA Modules:
  0.0 136.4 jit_solution(7222118077452802066)
XLA Ops:
  0.0 0.7 stack.88.place_ref
  0.7 3.9 %permute_local.1 = (bf16[4,256,128]{2,1,0:T(8,128)(2,1)}, bf16[4,256,128]{2,1,0:T(8,128)(2,1)}, bf16[2,4,256,128]{3,2,1,0:T(8,128)(2,1)}, bf16[1,272,128]{2,1,0:T(8,128)(2,1)}) custom-call(s32[19]{0:T(128)} %stack.88.place_ref, s32[32,128]{1,0:T(8,128)} %bitcast.24, s32[1,64]{1,0:T(1,128)} %bitcast.25, bf16[64,4096]{1,0:T(8,128)(2,1)} %refs_2_.1), custom_call_target="tpu_custom_call" | custom-call | tf_op jit(solution)/shard_map/permute_local/pallas_call | solution.py:100
  4.6 0.0 copy-start.5
  4.6 5.0 %collective-permute-start.3 = (bf16[1,272,128]{2,1,0:T(8,128)(2,1)}, bf16[1,272,128]{2,1,0:T(8,128)(2,1)S(1)}, u32[]{:S(2)}, u32[]{:S(2)}) collective-permute-start(bf16[1,272,128]{2,1,0:T(8,128)(2,1)} %get-tuple-element.30), channel_id=1, source_target_pairs={{0,8},{1,9},{2,10},{3,11},{16,24},{17,25},{18,26},{19,27}} | collective-permute-start | bytes 208904 | tf_op jit(solution)/shard_map/ppermute | solution.py:624
  9.7 2.2 %collective-permute-done.3 = bf16[1,272,128]{2,1,0:T(8,128)(2,1)S(1)} collective-permute-done((bf16[1,272,128]{2,1,0:T(8,128)(2,1)}, bf16[1,272,128]{2,1,0:T(8,128)(2,1)S(1)}, u32[]{:S(2)}, u32[]{:S(2)}) %collective-permute-start.3) | collective-permute-done | bytes 69664 | tf_op jit(solution)/shard_map/ppermute | solution.py:624
  11.9 0.9 broadcast_select_fusion
  12.8 3.4 %collective-permute-start.4 = (bf16[1,272,128]{2,1,0:T(8,128)(2,1)S(1)}, bf16[1,272,128]{2,1,0:T(8,128)(2,1)S(1)}, u32[]{:S(2)}, u32[]{:S(2)}) collective-permute-start(bf16[1,272,128]{2,1,0:T(8,128)(2,1)S(1)} %broadcast_select_fusion), channel_id=1, source_target_pairs={{0,16},{1,17},{2,18},{3,19},{8,24},{9,25},{10,26},{11,27},{16,0},{... | collective-permute-start | bytes 208904 | tf_op jit(solution)/shard_map/ppermute | solution.py:645
  16.2 3.6 %collective-permute-done.4 = bf16[1,272,128]{2,1,0:T(8,128)(2,1)S(1)} collective-permute-done((bf16[1,272,128]{2,1,0:T(8,128)(2,1)S(1)}, bf16[1,272,128]{2,1,0:T(8,128)(2,1)S(1)}, u32[]{:S(2)}, u32[]{:S(2)}) %collective-permute-start.4) | collective-permute-done | bytes 69664 | tf_op jit(solution)/shard_map/ppermute | solution.py:645
  19.8 3.5 %collective-permute-start.5 = (bf16[2,272,128]{2,1,0:T(8,128)(2,1)S(1)}, bf16[2,272,128]{2,1,0:T(8,128)(2,1)S(1)}, u32[]{:S(2)}, u32[]{:S(2)}) collective-permute-start(bf16[2,272,128]{2,1,0:T(8,128)(2,1)S(1)} %pad_maximum_fusion.2), channel_id=1, source_target_pairs={{0,1},{1,0},{2,3},{3,2},{8,9},{9,8},{10,11},{11,10},{16,17},{17,16... | collective-permute-start | bytes 417800 | tf_op jit(solution)/shard_map/ppermute | solution.py:645
  23.3 3.7 %collective-permute-done.5 = bf16[2,272,128]{2,1,0:T(8,128)(2,1)S(1)} collective-permute-done((bf16[2,272,128]{2,1,0:T(8,128)(2,1)S(1)}, bf16[2,272,128]{2,1,0:T(8,128)(2,1)S(1)}, u32[]{:S(2)}, u32[]{:S(2)}) %collective-permute-start.5) | collective-permute-done | bytes 139296 | tf_op jit(solution)/shard_map/ppermute | solution.py:645
  27.0 4.3 %collective-permute-start.6 = (bf16[4,272,128]{2,1,0:T(8,128)(2,1)S(1)}, bf16[4,272,128]{2,1,0:T(8,128)(2,1)S(1)}, u32[]{:S(2)}, u32[]{:S(2)}) collective-permute-start(bf16[4,272,128]{2,1,0:T(8,128)(2,1)S(1)} %pad_maximum_fusion.1), channel_id=1, source_target_pairs={{0,2},{1,3},{2,0},{3,1},{8,10},{9,11},{10,8},{11,9},{16,18},{17,19... | collective-permute-start | bytes 835592 | tf_op jit(solution)/shard_map/ppermute | solution.py:645
  31.3 8.1 %collective-permute-done.6 = bf16[4,272,128]{2,1,0:T(8,128)(2,1)S(1)} collective-permute-done((bf16[4,272,128]{2,1,0:T(8,128)(2,1)S(1)}, bf16[4,272,128]{2,1,0:T(8,128)(2,1)S(1)}, u32[]{:S(2)}, u32[]{:S(2)}) %collective-permute-start.6) | collective-permute-done | bytes 278560 | tf_op jit(solution)/shard_map/ppermute | solution.py:645
  39.4 0.1 pad_maximum_fusion.own_ref.after
  39.4 1.3 collective-permute-start.7
  40.8 1.3 collective-permute-start.8
  42.1 0.0 collective-permute-start.1
  42.1 3.5 %collective-permute-start.2 = (bf16[4,256,128]{2,1,0:T(8,128)(2,1)S(1)}, bf16[4,256,128]{2,1,0:T(8,128)(2,1)S(1)}, u32[]{:S(2)}, u32[]{:S(2)}) collective-permute-start(bf16[4,256,128]{2,1,0:T(8,128)(2,1)S(1)} %copy-done.1), channel_id=1, source_target_pairs={{1,0},{2,1},{3,2},{0,3},{5,4},{6,5},{7,6},{4,7},{9,8},{10,9},{11,1... | collective-permute-start | bytes 786440 | tf_op jit(solution)/shard_map/ppermute | solution.py:677
  45.6 0.5 collective-permute-start
  46.1 0.0 collective-permute-done.7.came_ref
  46.2 8.1 %start_panel.1 = (bf16[4,384,256]{2,1,0:T(8,128)(2,1)S(1)}, bf16[8,64,128]{2,1,0:T(8,128)(2,1)S(1)}, f32[512,1024]{1,0:T(8,128)S(1)}) custom-call(s32[19]{0:T(128)S(1)} %copy-done.3, f32[64]{0:T(128)S(1)} %copy-done.4, bf16[8,272,128]{2,1,0:T(8,128)(2,1)S(1)} %pad_maximum_fusion.own_ref.after, bf16[8,272,128]{2,1,0:T(8,128)(2,1)S(1)} %collective-permute-done.7.came_ref, ...), custom_call_target="tpu_custom_call" | custom-call | tf_op jit(solution)/shard_map/start_panel/pallas_call | solution.py:366
  54.3 5.9 %next_panel.2.refs_5_.aug_in = f32[512,1024]{1,0:T(8,128)S(1)} custom-call(f32[512,1024]{1,0:T(8,128)S(1)} %get-tuple-element.31.aug_in.after, f32[512,1024]{1,0:T(8,128)S(1)} %get-tuple-element.31.aug_in.after), custom_call_target="tpu_custom_call" | custom-call | tf_op jit(solution)/shard_map/next_panel/pallas_call | solution.py:387
  60.1 0.0 collective-permute-done.1.refs_1_
  60.2 0.0 collective-permute-done.refs_0_
  60.2 0.0 collective-permute-done.8.refs_6_.other_first
  60.2 0.7 assemble.2
  60.9 3.3 %collective-permute-start.9 = (bf16[4,4,256,128]{3,2,1,0:T(8,128)(2,1)S(1)}, bf16[4,4,256,128]{3,2,1,0:T(8,128)(2,1)S(1)}, u32[]{:S(2)}, u32[]{:S(2)}) collective-permute-start(bf16[4,4,256,128]{3,2,1,0:T(8,128)(2,1)S(1)} %get-tuple-element.34.after.native_ref), channel_id=1, source_target_pairs={{0,8},{1,9},{6,14},{7,15},{8,0},{9,1},{14,6},{15,7},{16,24},{17,25... | collective-permute-start | bytes 3145736 | tf_op jit(solution)/shard_map/ppermute | solution.py:689
  64.2 2.3 %collective-permute-start.10 = (bf16[4,256,128]{2,1,0:T(8,128)(2,1)S(1)}, bf16[4,256,128]{2,1,0:T(8,128)(2,1)S(1)}, u32[]{:S(2)}, u32[]{:S(2)}) collective-permute-start(bf16[4,256,128]{2,1,0:T(8,128)(2,1)S(1)} %get-tuple-element.35.own_first), channel_id=1, source_target_pairs={{3,0},{0,1},{1,2},{2,3},{7,4},{4,5},{5,6},{6,7},{11,8},{8,9},{9,10... | collective-permute-start | bytes 786440 | tf_op jit(solution)/shard_map/ppermute | solution.py:677
  66.5 5.5 %next_panel.3.refs_2_.aug_in = f32[512,1024]{1,0:T(8,128)S(1)} custom-call(f32[512,1024]{1,0:T(8,128)S(1)} %next_panel.2.refs_5_.aug_in, bf16[4,4,256,128]{3,2,1,0:T(8,128)(2,1)S(1)} %get-tuple-element.34.after.native_ref), custom_call_target="tpu_custom_call" | custom-call | tf_op jit(solution)/shard_map/next_panel/pallas_call | solution.py:387
  72.0 0.6 collective-permute-done.10.refs_1_
  72.7 5.0 %collective-permute-done.9.refs_0_ = bf16[4,4,256,128]{3,2,1,0:T(8,128)(2,1)S(1)} collective-permute-done((bf16[4,4,256,128]{3,2,1,0:T(8,128)(2,1)S(1)}, bf16[4,4,256,128]{3,2,1,0:T(8,128)(2,1)S(1)}, u32[]{:S(2)}, u32[]{:S(2)}) %collective-permute-start.9) | collective-permute-done | bytes 1048608 | tf_op jit(solution)/shard_map/ppermute | solution.py:689
  77.6 0.7 sort.1
  78.4 2.4 %collective-permute-start.11 = (bf16[4,4,256,128]{3,2,1,0:T(8,128)(2,1)S(1)}, bf16[4,4,256,128]{3,2,1,0:T(8,128)(2,1)S(1)}, u32[]{:S(2)}, u32[]{:S(2)}) collective-permute-start(bf16[4,4,256,128]{3,2,1,0:T(8,128)(2,1)S(1)} %get-tuple-element.38), channel_id=1, source_target_pairs={{16,0},{17,1},{22,6},{23,7},{24,8},{25,9},{30,14},{31,15},{0,16},{... | collective-permute-start | bytes 3145736 | tf_op jit(solution)/shard_map/ppermute | solution.py:681
  80.8 3.4 %collective-permute-start.12 = (bf16[3,4,256,128]{3,2,1,0:T(8,128)(2,1)S(1)}, bf16[3,4,256,128]{3,2,1,0:T(8,128)(2,1)S(1)}, u32[]{:S(2)}, u32[]{:S(2)}) collective-permute-start(bf16[3,4,256,128]{3,2,1,0:T(8,128)(2,1)S(1)} %get-tuple-element.39.own_rest), channel_id=1, source_target_pairs={{18,2},{19,3},{20,4},{21,5},{24,8},{25,9},{26,10},{27,11},{28,12},... | collective-permute-start | bytes 2359304 | tf_op jit(solution)/shard_map/ppermute | solution.py:681
  84.3 0.1 collective-permute-start.13
  84.3 4.4 %collective-permute-start.14 = (bf16[4,256,128]{2,1,0:T(8,128)(2,1)S(1)}, bf16[4,256,128]{2,1,0:T(8,128)(2,1)S(1)}, u32[]{:S(2)}, u32[]{:S(2)}) collective-permute-start(bf16[4,256,128]{2,1,0:T(8,128)(2,1)S(1)} %get-tuple-element.35.own_first), channel_id=1, source_target_pairs={{1,0},{2,1},{3,2},{0,3},{5,4},{6,5},{7,6},{4,7},{9,8},{10,9},{11,1... | collective-permute-start | bytes 786440 | tf_op jit(solution)/shard_map/ppermute | solution.py:677
  88.7 1.3 collective-permute-start.16
  90.1 6.6 %last_panel.1 = (f32[512,512]{1,0:T(8,128)S(1)}, bf16[512,512]{1,0:T(8,128)(2,1)S(1)}, bf16[512,512]{1,0:T(8,128)(2,1)S(1)}, bf16[512,512]{1,0:T(8,128)(2,1)S(1)}) custom-call(f32[512,1024]{1,0:T(8,128)S(1)} %next_panel.3.refs_2_.aug_in, bf16[4,4,256,128]{3,2,1,0:T(8,128)(2,1)S(1)} %get-tuple-element.40.after.own, ...), custom_call_target="tpu_custom_call" | custom-call | tf_op jit(solution)/shard_map/last_panel/pallas_call | solution.py:401
  96.7 0.0 collective-permute-done.14.refs_3_
  96.7 13.2 %collective-permute-done.12.refs_1_ = bf16[3,4,256,128]{3,2,1,0:T(8,128)(2,1)S(1)} collective-permute-done((bf16[3,4,256,128]{3,2,1,0:T(8,128)(2,1)S(1)}, bf16[3,4,256,128]{3,2,1,0:T(8,128)(2,1)S(1)}, u32[]{:S(2)}, u32[]{:S(2)}) %collective-permute-start.12) | collective-permute-done | bytes 786464 | tf_op jit(solution)/shard_map/ppermute | solution.py:681
  110.0 0.0 collective-permute-done.11.refs_0_
  110.0 1.3 collective-permute-start.17
  111.3 0.7 assemble.3.own_rest
  112.0 2.5 %collective-permute-start.15 = (bf16[3,4,256,128]{3,2,1,0:T(8,128)(2,1)S(1)}, bf16[3,4,256,128]{3,2,1,0:T(8,128)(2,1)S(1)}, u32[]{:S(2)}, u32[]{:S(2)}) collective-permute-start(bf16[3,4,256,128]{3,2,1,0:T(8,128)(2,1)S(1)} %assemble.3.own_rest), channel_id=1, source_target_pairs={{16,0},{17,1},{18,2},{19,3},{20,4},{21,5},{22,6},{23,7},{24,8},{25... | collective-permute-start | bytes 2359304 | tf_op jit(solution)/shard_map/ppermute | solution.py:681
  114.5 0.0 collective-permute-done.16.own_came
  114.5 4.8 %project.1.refs_1_.refs_0_ = bf16[512,2048]{1,0:T(8,128)(2,1)S(1)} custom-call(s32[19]{0:T(128)S(1)} %copy-done.3, bf16[4,4,256,128]{3,2,1,0:T(8,128)(2,1)S(1)} %get-tuple-element.40.after.own, bf16[4,4,256,128]{3,2,1,0:T(8,128)(2,1)S(1)} %collective-permute-done.16.own_came, bf16[4,4,256,128]{3,2,1,0:T(8,128)(2,1)S(1)} %get-tuple-element.45.other.refs_0_, ...), custom_call_target="tpu_custom_call" | custom-call | tf_op jit(solution)/shard_map/project/pallas_call | solution.py:486
  119.4 8.1 %multiply_part.2.refs_3_ = f32[4096,2048]{1,0:T(8,128)} custom-call(s32[19]{0:T(128)S(1)} %copy-done.3, bf16[4,256,128]{2,1,0:T(8,128)(2,1)S(1)} %get-tuple-element.35.own_first, bf16[3,4,256,128]{3,2,1,0:T(8,128)(2,1)S(1)} %get-tuple-element.39.own_rest, bf16[2,4,256,128]{3,2,1,0:T(8,128)(2,1)S(1)} %collective-permute-done.8.refs_6_.other_first, ...), custom_call_target="tpu_custom_call" | custom-call | tf_op jit(solution)/shard_map/multiply_part/pallas_call | solution.py:575
  127.5 0.0 collective-permute-done.15.other_rest
  127.5 8.9 %multiply_part.3 = f32[4096,2048]{1,0:T(8,128)} custom-call(s32[19]{0:T(128)S(1)} %copy-done.3, bf16[4,256,128]{2,1,0:T(8,128)(2,1)S(1)} %get-tuple-element.33.own_first, bf16[3,4,256,128]{3,2,1,0:T(8,128)(2,1)S(1)} %assemble.3.own_rest, bf16[2,4,256,128]{3,2,1,0:T(8,128)(2,1)S(1)} %collective-permute-done.8.refs_6_.other_first, ...), custom_call_target="tpu_custom_call", output_to_operand_aliasing={{}: (8, {})} | custom-call | tf_op jit(solution)/shard_map/multiply_part/pallas_call | solution.py:575
  (18 shorter events, 0.1 us)
Async XLA Ops:
  0.0 46.2 %copy-start.2 = (f32[16384]{0:T(1024)S(1)}, f32[16384]{0:T(1024)}, u32[]{:S(2)}) copy-start(f32[16384]{0:T(1024)} %param.9) | copy-start | bytes 196612
  0.0 46.2 %copy-start.4 = (f32[64]{0:T(128)S(1)}, f32[64]{0:T(128)}, u32[]{:S(2)}) copy-start(f32[64]{0:T(128)} %taps_ref.1) | copy-start | bytes 772
  0.7 45.5 %copy-start.3 = (s32[19]{0:T(128)S(1)}, s32[19]{0:T(128)}, u32[]{:S(2)}) copy-start(s32[19]{0:T(128)} %stack.88.place_ref) | copy-start | bytes 232
  4.6 36.1 %copy-start.5 = (bf16[2,4,256,128]{3,2,1,0:T(8,128)(2,1)S(1)}, bf16[2,4,256,128]{3,2,1,0:T(8,128)(2,1)}, u32[]{:S(2)}) copy-start(bf16[2,4,256,128]{3,2,1,0:T(8,128)(2,1)} %get-tuple-element.32) | copy-start | bytes 1572868
  4.6 37.5 %copy-start = (bf16[4,256,128]{2,1,0:T(8,128)(2,1)S(1)}, bf16[4,256,128]{2,1,0:T(8,128)(2,1)}, u32[]{:S(2)}) copy-start(bf16[4,256,128]{2,1,0:T(8,128)(2,1)} %get-tuple-element.29.refs_3_) | copy-start | bytes 786436
  4.6 37.5 %copy-start.1 = (bf16[4,256,128]{2,1,0:T(8,128)(2,1)S(1)}, bf16[4,256,128]{2,1,0:T(8,128)(2,1)}, u32[]{:S(2)}) copy-start(bf16[4,256,128]{2,1,0:T(8,128)(2,1)} %get-tuple-element.28.refs_4_) | copy-start | bytes 786436
  4.6 7.3 %collective-permute-start.3 = (bf16[1,272,128]{2,1,0:T(8,128)(2,1)}, bf16[1,272,128]{2,1,0:T(8,128)(2,1)S(1)}, u32[]{:S(2)}, u32[]{:S(2)}) collective-permute-start(bf16[1,272,128]{2,1,0:T(8,128)(2,1)} %get-tuple-element.30), channel_id=1, source_target_pairs={{0,8},{1,9},{2,10},{3,11},{16,24},{17,25},{18,26},{19,27}} | collective-permute-start | bytes 208904 | tf_op jit(solution)/shard_map/ppermute | solution.py:624
  12.8 7.0 %collective-permute-start.4 = (bf16[1,272,128]{2,1,0:T(8,128)(2,1)S(1)}, bf16[1,272,128]{2,1,0:T(8,128)(2,1)S(1)}, u32[]{:S(2)}, u32[]{:S(2)}) collective-permute-start(bf16[1,272,128]{2,1,0:T(8,128)(2,1)S(1)} %broadcast_select_fusion), channel_id=1, source_target_pairs={{0,16},{1,17},{2,18},{3,19},{8,24},{9,25},{10,26},{11,27},{16,0},{... | collective-permute-start | bytes 208904 | tf_op jit(solution)/shard_map/ppermute | solution.py:645
  19.8 7.2 %collective-permute-start.5 = (bf16[2,272,128]{2,1,0:T(8,128)(2,1)S(1)}, bf16[2,272,128]{2,1,0:T(8,128)(2,1)S(1)}, u32[]{:S(2)}, u32[]{:S(2)}) collective-permute-start(bf16[2,272,128]{2,1,0:T(8,128)(2,1)S(1)} %pad_maximum_fusion.2), channel_id=1, source_target_pairs={{0,1},{1,0},{2,3},{3,2},{8,9},{9,8},{10,11},{11,10},{16,17},{17,16... | collective-permute-start | bytes 417800 | tf_op jit(solution)/shard_map/ppermute | solution.py:645
  27.0 12.3 %collective-permute-start.6 = (bf16[4,272,128]{2,1,0:T(8,128)(2,1)S(1)}, bf16[4,272,128]{2,1,0:T(8,128)(2,1)S(1)}, u32[]{:S(2)}, u32[]{:S(2)}) collective-permute-start(bf16[4,272,128]{2,1,0:T(8,128)(2,1)S(1)} %pad_maximum_fusion.1), channel_id=1, source_target_pairs={{0,2},{1,3},{2,0},{3,1},{8,10},{9,11},{10,8},{11,9},{16,18},{17,19... | collective-permute-start | bytes 835592 | tf_op jit(solution)/shard_map/ppermute | solution.py:645
  39.4 6.7 %collective-permute-start.7 = (bf16[8,272,128]{2,1,0:T(8,128)(2,1)S(1)}, bf16[8,272,128]{2,1,0:T(8,128)(2,1)S(1)}, u32[]{:S(2)}, u32[]{:S(2)}) collective-permute-start(bf16[8,272,128]{2,1,0:T(8,128)(2,1)S(1)} %pad_maximum_fusion.own_ref.after), channel_id=1, source_target_pairs={{0,4},{8,12},{1,5},{9,13},{2,6},{10,14},{3,7},{11,15},{16,20},{24,... | collective-permute-start | bytes 1671176 | tf_op jit(solution)/shard_map/ppermute | solution.py:646
  40.8 19.4 %collective-permute-start.8 = (bf16[2,4,256,128]{3,2,1,0:T(8,128)(2,1)S(1)}, bf16[2,4,256,128]{3,2,1,0:T(8,128)(2,1)S(1)}, u32[]{:S(2)}, u32[]{:S(2)}) collective-permute-start(bf16[2,4,256,128]{3,2,1,0:T(8,128)(2,1)S(1)} %copy-done.5), channel_id=1, source_target_pairs={{16,0},{17,1},{18,2},{19,3},{20,4},{21,5},{22,6},{23,7},{24,8},{25... | collective-permute-start | bytes 1572872 | tf_op jit(solution)/shard_map/ppermute | solution.py:681
  42.1 18.1 %collective-permute-start.1 = (bf16[4,256,128]{2,1,0:T(8,128)(2,1)S(1)}, bf16[4,256,128]{2,1,0:T(8,128)(2,1)S(1)}, u32[]{:S(2)}, u32[]{:S(2)}) collective-permute-start(bf16[4,256,128]{2,1,0:T(8,128)(2,1)S(1)} %copy-done), channel_id=1, source_target_pairs={{2,0},{3,1},{0,2},{1,3},{6,4},{7,5},{4,6},{5,7},{10,8},{11,9},{8,1... | collective-permute-start | bytes 786440 | tf_op jit(solution)/shard_map/ppermute | solution.py:677
  42.1 18.1 %collective-permute-start.2 = (bf16[4,256,128]{2,1,0:T(8,128)(2,1)S(1)}, bf16[4,256,128]{2,1,0:T(8,128)(2,1)S(1)}, u32[]{:S(2)}, u32[]{:S(2)}) collective-permute-start(bf16[4,256,128]{2,1,0:T(8,128)(2,1)S(1)} %copy-done.1), channel_id=1, source_target_pairs={{1,0},{2,1},{3,2},{0,3},{5,4},{6,5},{7,6},{4,7},{9,8},{10,9},{11,1... | collective-permute-start | bytes 786440 | tf_op jit(solution)/shard_map/ppermute | solution.py:677
  45.6 14.5 %collective-permute-start = (bf16[4,256,128]{2,1,0:T(8,128)(2,1)S(1)}, bf16[4,256,128]{2,1,0:T(8,128)(2,1)S(1)}, u32[]{:S(2)}, u32[]{:S(2)}) collective-permute-start(bf16[4,256,128]{2,1,0:T(8,128)(2,1)S(1)} %copy-done.1), channel_id=1, source_target_pairs={{3,0},{0,1},{1,2},{2,3},{7,4},{4,5},{5,6},{6,7},{11,8},{8,9},{9,10... | collective-permute-start | bytes 786440 | tf_op jit(solution)/shard_map/ppermute | solution.py:677
  60.9 16.7 %collective-permute-start.9 = (bf16[4,4,256,128]{3,2,1,0:T(8,128)(2,1)S(1)}, bf16[4,4,256,128]{3,2,1,0:T(8,128)(2,1)S(1)}, u32[]{:S(2)}, u32[]{:S(2)}) collective-permute-start(bf16[4,4,256,128]{3,2,1,0:T(8,128)(2,1)S(1)} %get-tuple-element.34.after.native_ref), channel_id=1, source_target_pairs={{0,8},{1,9},{6,14},{7,15},{8,0},{9,1},{14,6},{15,7},{16,24},{17,25... | collective-permute-start | bytes 3145736 | tf_op jit(solution)/shard_map/ppermute | solution.py:689
  64.2 8.4 %collective-permute-start.10 = (bf16[4,256,128]{2,1,0:T(8,128)(2,1)S(1)}, bf16[4,256,128]{2,1,0:T(8,128)(2,1)S(1)}, u32[]{:S(2)}, u32[]{:S(2)}) collective-permute-start(bf16[4,256,128]{2,1,0:T(8,128)(2,1)S(1)} %get-tuple-element.35.own_first), channel_id=1, source_target_pairs={{3,0},{0,1},{1,2},{2,3},{7,4},{4,5},{5,6},{6,7},{11,8},{8,9},{9,10... | collective-permute-start | bytes 786440 | tf_op jit(solution)/shard_map/ppermute | solution.py:677
  78.4 31.6 %collective-permute-start.11 = (bf16[4,4,256,128]{3,2,1,0:T(8,128)(2,1)S(1)}, bf16[4,4,256,128]{3,2,1,0:T(8,128)(2,1)S(1)}, u32[]{:S(2)}, u32[]{:S(2)}) collective-permute-start(bf16[4,4,256,128]{3,2,1,0:T(8,128)(2,1)S(1)} %get-tuple-element.38), channel_id=1, source_target_pairs={{16,0},{17,1},{22,6},{23,7},{24,8},{25,9},{30,14},{31,15},{0,16},{... | collective-permute-start | bytes 3145736 | tf_op jit(solution)/shard_map/ppermute | solution.py:681
  80.8 29.1 %collective-permute-start.12 = (bf16[3,4,256,128]{3,2,1,0:T(8,128)(2,1)S(1)}, bf16[3,4,256,128]{3,2,1,0:T(8,128)(2,1)S(1)}, u32[]{:S(2)}, u32[]{:S(2)}) collective-permute-start(bf16[3,4,256,128]{3,2,1,0:T(8,128)(2,1)S(1)} %get-tuple-element.39.own_rest), channel_id=1, source_target_pairs={{18,2},{19,3},{20,4},{21,5},{24,8},{25,9},{26,10},{27,11},{28,12},... | collective-permute-start | bytes 2359304 | tf_op jit(solution)/shard_map/ppermute | solution.py:681
  84.3 12.4 %collective-permute-start.13 = (bf16[4,256,128]{2,1,0:T(8,128)(2,1)S(1)}, bf16[4,256,128]{2,1,0:T(8,128)(2,1)S(1)}, u32[]{:S(2)}, u32[]{:S(2)}) collective-permute-start(bf16[4,256,128]{2,1,0:T(8,128)(2,1)S(1)} %get-tuple-element.33.own_first), channel_id=1, source_target_pairs={{2,0},{3,1},{0,2},{1,3},{6,4},{7,5},{4,6},{5,7},{10,8},{11,9},{8,1... | collective-permute-start | bytes 786440 | tf_op jit(solution)/shard_map/ppermute | solution.py:677
  84.3 12.4 %collective-permute-start.14 = (bf16[4,256,128]{2,1,0:T(8,128)(2,1)S(1)}, bf16[4,256,128]{2,1,0:T(8,128)(2,1)S(1)}, u32[]{:S(2)}, u32[]{:S(2)}) collective-permute-start(bf16[4,256,128]{2,1,0:T(8,128)(2,1)S(1)} %get-tuple-element.35.own_first), channel_id=1, source_target_pairs={{1,0},{2,1},{3,2},{0,3},{5,4},{6,5},{7,6},{4,7},{9,8},{10,9},{11,1... | collective-permute-start | bytes 786440 | tf_op jit(solution)/shard_map/ppermute | solution.py:677
  88.7 25.8 %collective-permute-start.16 = (bf16[4,4,256,128]{3,2,1,0:T(8,128)(2,1)S(1)}, bf16[4,4,256,128]{3,2,1,0:T(8,128)(2,1)S(1)}, u32[]{:S(2)}, u32[]{:S(2)}) collective-permute-start(bf16[4,4,256,128]{3,2,1,0:T(8,128)(2,1)S(1)} %get-tuple-element.40.after.own), channel_id=1, source_target_pairs={{0,4},{8,12},{1,5},{9,13},{6,2},{14,10},{7,3},{15,11},{24,28},{16,... | collective-permute-start | bytes 3145736 | tf_op jit(solution)/shard_map/ppermute | solution.py:624
  110.0 4.6 %collective-permute-start.17 = (bf16[4,4,256,128]{3,2,1,0:T(8,128)(2,1)S(1)}, bf16[4,4,256,128]{3,2,1,0:T(8,128)(2,1)S(1)}, u32[]{:S(2)}, u32[]{:S(2)}) collective-permute-start(bf16[4,4,256,128]{3,2,1,0:T(8,128)(2,1)S(1)} %get-tuple-element.45.other.refs_0_), channel_id=1, source_target_pairs={{0,4},{8,12},{1,5},{9,13},{6,2},{14,10},{7,3},{15,11},{24,28},{16,... | collective-permute-start | bytes 3145736 | tf_op jit(solution)/shard_map/ppermute | solution.py:624
  112.0 15.5 %collective-permute-start.15 = (bf16[3,4,256,128]{3,2,1,0:T(8,128)(2,1)S(1)}, bf16[3,4,256,128]{3,2,1,0:T(8,128)(2,1)S(1)}, u32[]{:S(2)}, u32[]{:S(2)}) collective-permute-start(bf16[3,4,256,128]{3,2,1,0:T(8,128)(2,1)S(1)} %assemble.3.own_rest), channel_id=1, source_target_pairs={{16,0},{17,1},{18,2},{19,3},{20,4},{21,5},{22,6},{23,7},{24,8},{25... | collective-permute-start | bytes 2359304 | tf_op jit(solution)/shard_map/ppermute | solution.py:681

commit v8 on v7

--- a/solution.py
+++ b/solution.py
@@ -699,19 +699,19 @@
     early = [shift(local[n % parts], n) for n in range(1, cols)]
     swapped = across(both, lambda e, r, c: True)
     band, taper, aug = start_panel(place, chain, taps, notes, came, regular, notes)
-    aug = next_panel(1, aug, aug)
     rest, *local, first = assemble(place, early, local, [aug, swapped], True)
+    aug = next_panel(1, aug, first)
     foreign = trade(first)
     others = [across(rest, lambda e, r, c: not owns(e, r, c))]
     mine = [rest]
     order = [(j, n) for j in range(1, parts) for n in range(1, cols)]
     late = [shift(local[(n + j) % parts], n) for j, n in order]
     aug = next_panel(2, aug, first)
-    foreign, *late[:1] = gate([foreign, *late[:1]], aug)
+    foreign, others[0], *late[:2] = gate([foreign, others[0], *late[:2]], aug)
     own, sent = sort(place, first, foreign)
     theirs = across(sent, lambda e, r, c: inside(r, c))
     factor, w, high, low = last_panel(3, aug, own, taper)
-    theirs, others[0], *late[1:] = gate([theirs, others[0], *late[1:]], factor)
+    theirs, *late[2:] = gate([theirs, *late[2:]], factor)
     own, own_came = spread_rest(own)
     other, other_came = spread_rest(theirs)
     for j in range(1, parts):

time: 138 us -> 125 us (0.906)
  the two profiles are of different devices: /device:TPU:0 before, /device:TPU:9 now
where the time goes in v8:
time: 125 us
  Pallas kernels  54.6 us (44%)
  waiting for transfers between devices  44.3 us (35%)
  starting transfers between devices  23.6 us (19%)
    ppermute x1, waiting for transfers between devices, gather_panel(): came = lax.ppermute(note, 'row', [(r, r + 1) for r in range(0, rows, 2)])  25.3 us
    ppermute x3, waiting for transfers between devices, spread_step(): return lax.ppermute(block, AXES, route)  19 us
    pallas_call x2, Pallas kernels, multiply_part(): pl.pallas_call(functools.partial(tile_kernel, part, parts), out_shape=jax...  18 us
    pallas_call x2, Pallas kernels, next_panel(): pl.pallas_call(functools.partial(next_kernel, kb), out_shape=jax.ShapeDty...  11.3 us
    ppermute x6, starting transfers between devices, shift(): return lax.ppermute(block, AXES, route)  10.8 us
    pallas_call x1, Pallas kernels, start_panel(): pl.pallas_call(functools.partial(start_kernel, chain), out_shape=(jax.Sha...  8.08 us
    pallas_call x1, Pallas kernels, last_panel(): pl.pallas_call(functools.partial(last_kernel, kb), out_shape=(jax.ShapeDt...  6.57 us
    ppermute x4, starting transfers between devices, across(): return lax.ppermute(block, AXES, route)  5.19 us
  transfers between devices with their start and end apart: 18, of which 2 were waited for; matrix products, arithmetic and copies ran while one was open for 0% of the time, Pallas kernels for 32%

profile of v8, /device:TPU:9, one launch (start us, length us, event | category | flops | bytes accessed | tf_op | source)
XLA Modules:
  0.0 124.6 jit_solution(16009658441783572574)
XLA Ops:
  0.0 0.7 stack.88.place_ref
  0.7 3.9 %permute_local.1 = (bf16[4,256,128]{2,1,0:T(8,128)(2,1)}, bf16[4,256,128]{2,1,0:T(8,128)(2,1)}, bf16[2,4,256,128]{3,2,1,0:T(8,128)(2,1)}, bf16[1,272,128]{2,1,0:T(8,128)(2,1)}) custom-call(s32[19]{0:T(128)} %stack.88.place_ref, s32[32,128]{1,0:T(8,128)} %bitcast.24, s32[1,64]{1,0:T(1,128)} %bitcast.25, bf16[64,4096]{1,0:T(8,128)(2,1)} %refs_2_.1), custom_call_target="tpu_custom_call" | custom-call | tf_op jit(solution)/shard_map/permute_local/pallas_call | solution.py:100
  4.6 0.0 copy-start.5
  4.6 0.8 collective-permute-start.3
  5.5 0.0 collective-permute-done.3
  5.5 0.9 broadcast_select_fusion
  6.4 0.7 collective-permute-start.4
  7.0 0.0 collective-permute-done.4
  7.1 0.7 collective-permute-start.5
  7.7 0.0 collective-permute-done.5
  7.8 0.7 collective-permute-start.6
  8.5 0.0 collective-permute-done.6
  8.5 0.1 pad_maximum_fusion.own_ref.after
  8.6 1.3 %collective-permute-start.7 = (bf16[8,272,128]{2,1,0:T(8,128)(2,1)S(1)}, bf16[8,272,128]{2,1,0:T(8,128)(2,1)S(1)}, u32[]{:S(2)}, u32[]{:S(2)}) collective-permute-start(bf16[8,272,128]{2,1,0:T(8,128)(2,1)S(1)} %pad_maximum_fusion.own_ref.after), channel_id=1, source_target_pairs={{0,4},{8,12},{1,5},{9,13},{2,6},{10,14},{3,7},{11,15},{16,20},{24,... | collective-permute-start | bytes 1671176 | tf_op jit(solution)/shard_map/ppermute | solution.py:646
  9.9 1.3 %collective-permute-start.8 = (bf16[2,4,256,128]{3,2,1,0:T(8,128)(2,1)S(1)}, bf16[2,4,256,128]{3,2,1,0:T(8,128)(2,1)S(1)}, u32[]{:S(2)}, u32[]{:S(2)}) collective-permute-start(bf16[2,4,256,128]{3,2,1,0:T(8,128)(2,1)S(1)} %copy-done.5), channel_id=1, source_target_pairs={{16,0},{17,1},{18,2},{19,3},{20,4},{21,5},{22,6},{23,7},{24,8},{25... | collective-permute-start | bytes 1572872 | tf_op jit(solution)/shard_map/ppermute | solution.py:681
  11.1 2.3 %collective-permute-start.1 = (bf16[4,256,128]{2,1,0:T(8,128)(2,1)S(1)}, bf16[4,256,128]{2,1,0:T(8,128)(2,1)S(1)}, u32[]{:S(2)}, u32[]{:S(2)}) collective-permute-start(bf16[4,256,128]{2,1,0:T(8,128)(2,1)S(1)} %copy-done), channel_id=1, source_target_pairs={{2,0},{3,1},{0,2},{1,3},{6,4},{7,5},{4,6},{5,7},{10,8},{11,9},{8,1... | collective-permute-start | bytes 786440 | tf_op jit(solution)/shard_map/ppermute | solution.py:677
  13.5 0.2 collective-permute-start.2
  13.6 1.3 %collective-permute-start = (bf16[4,256,128]{2,1,0:T(8,128)(2,1)S(1)}, bf16[4,256,128]{2,1,0:T(8,128)(2,1)S(1)}, u32[]{:S(2)}, u32[]{:S(2)}) collective-permute-start(bf16[4,256,128]{2,1,0:T(8,128)(2,1)S(1)} %copy-done.1), channel_id=1, source_target_pairs={{3,0},{0,1},{1,2},{2,3},{7,4},{4,5},{5,6},{6,7},{11,8},{8,9},{9,10... | collective-permute-start | bytes 786440 | tf_op jit(solution)/shard_map/ppermute | solution.py:677
  14.9 25.3 %collective-permute-done.7.came_ref = bf16[8,272,128]{2,1,0:T(8,128)(2,1)S(1)} collective-permute-done((bf16[8,272,128]{2,1,0:T(8,128)(2,1)S(1)}, bf16[8,272,128]{2,1,0:T(8,128)(2,1)S(1)}, u32[]{:S(2)}, u32[]{:S(2)}) %collective-permute-start.7) | collective-permute-done | bytes 557088 | tf_op jit(solution)/shard_map/ppermute | solution.py:646
  40.2 8.1 %start_panel.1 = (bf16[4,384,256]{2,1,0:T(8,128)(2,1)S(1)}, bf16[8,64,128]{2,1,0:T(8,128)(2,1)S(1)}, f32[512,1024]{1,0:T(8,128)S(1)}) custom-call(s32[19]{0:T(128)S(1)} %copy-done.3, f32[64]{0:T(128)S(1)} %copy-done.4, bf16[8,272,128]{2,1,0:T(8,128)(2,1)S(1)} %pad_maximum_fusion.own_ref.after, bf16[8,272,128]{2,1,0:T(8,128)(2,1)S(1)} %collective-permute-done.7.came_ref, ...), custom_call_target="tpu_custom_call" | custom-call | tf_op jit(solution)/shard_map/start_panel/pallas_call | solution.py:366
  48.3 0.0 collective-permute-done.1.refs_1_
  48.3 0.0 collective-permute-done.2.refs_2_
  48.4 0.0 collective-permute-done.refs_0_
  48.4 0.0 collective-permute-done.8.refs_6_.other_first
  48.4 0.7 assemble.2
  49.1 0.7 collective-permute-start.9
  49.9 3.1 %collective-permute-start.10 = (bf16[3,4,256,128]{3,2,1,0:T(8,128)(2,1)S(1)}, bf16[3,4,256,128]{3,2,1,0:T(8,128)(2,1)S(1)}, u32[]{:S(2)}, u32[]{:S(2)}) collective-permute-start(bf16[3,4,256,128]{3,2,1,0:T(8,128)(2,1)S(1)} %get-tuple-element.35.own_rest), channel_id=1, source_target_pairs={{18,2},{19,3},{20,4},{21,5},{24,8},{25,9},{26,10},{27,11},{28,12},... | collective-permute-start | bytes 2359304 | tf_op jit(solution)/shard_map/ppermute | solution.py:681
  53.0 5.5 %collective-permute-start.12 = (bf16[4,256,128]{2,1,0:T(8,128)(2,1)S(1)}, bf16[4,256,128]{2,1,0:T(8,128)(2,1)S(1)}, u32[]{:S(2)}, u32[]{:S(2)}) collective-permute-start(bf16[4,256,128]{2,1,0:T(8,128)(2,1)S(1)} %get-tuple-element.33.own_first), channel_id=1, source_target_pairs={{2,0},{3,1},{0,2},{1,3},{6,4},{7,5},{4,6},{5,7},{10,8},{11,9},{8,1... | collective-permute-start | bytes 786440 | tf_op jit(solution)/shard_map/ppermute | solution.py:677
  58.5 0.0 collective-permute-start.11
  58.5 5.8 %next_panel.2.aug_in = f32[512,1024]{1,0:T(8,128)S(1)} custom-call(f32[512,1024]{1,0:T(8,128)S(1)} %get-tuple-element.31.refs_5_.aug_in, bf16[4,4,256,128]{3,2,1,0:T(8,128)(2,1)S(1)} %get-tuple-element.34.after.native_ref), custom_call_target="tpu_custom_call" | custom-call | tf_op jit(solution)/shard_map/next_panel/pallas_call | solution.py:387
  64.3 5.5 %next_panel.3.refs_4_.aug_in = f32[512,1024]{1,0:T(8,128)S(1)} custom-call(f32[512,1024]{1,0:T(8,128)S(1)} %next_panel.2.aug_in, bf16[4,4,256,128]{3,2,1,0:T(8,128)(2,1)S(1)} %get-tuple-element.34.after.native_ref), custom_call_target="tpu_custom_call" | custom-call | tf_op jit(solution)/shard_map/next_panel/pallas_call | solution.py:387
  69.8 0.0 collective-permute-done.12.refs_3_
  69.9 0.0 collective-permute-done.10.refs_1_
  69.9 0.0 collective-permute-done.9.refs_0_
  69.9 0.7 sort.1
  70.6 0.7 collective-permute-start.13
  71.4 1.5 %collective-permute-start.14 = (bf16[4,256,128]{2,1,0:T(8,128)(2,1)S(1)}, bf16[4,256,128]{2,1,0:T(8,128)(2,1)S(1)}, u32[]{:S(2)}, u32[]{:S(2)}) collective-permute-start(bf16[4,256,128]{2,1,0:T(8,128)(2,1)S(1)} %get-tuple-element.36.own_first), channel_id=1, source_target_pairs={{1,0},{2,1},{3,2},{0,3},{5,4},{6,5},{7,6},{4,7},{9,8},{10,9},{11,1... | collective-permute-start | bytes 786440 | tf_op jit(solution)/shard_map/ppermute | solution.py:677
  72.9 1.5 %collective-permute-start.16 = (bf16[4,4,256,128]{3,2,1,0:T(8,128)(2,1)S(1)}, bf16[4,4,256,128]{3,2,1,0:T(8,128)(2,1)S(1)}, u32[]{:S(2)}, u32[]{:S(2)}) collective-permute-start(bf16[4,4,256,128]{3,2,1,0:T(8,128)(2,1)S(1)} %get-tuple-element.41.after.own), channel_id=1, source_target_pairs={{0,4},{8,12},{1,5},{9,13},{6,2},{14,10},{7,3},{15,11},{24,28},{16,... | collective-permute-start | bytes 3145736 | tf_op jit(solution)/shard_map/ppermute | solution.py:624
  74.4 6.6 %last_panel.1 = (f32[512,512]{1,0:T(8,128)S(1)}, bf16[512,512]{1,0:T(8,128)(2,1)S(1)}, bf16[512,512]{1,0:T(8,128)(2,1)S(1)}, bf16[512,512]{1,0:T(8,128)(2,1)S(1)}) custom-call(f32[512,1024]{1,0:T(8,128)S(1)} %next_panel.3.refs_4_.aug_in, bf16[4,4,256,128]{3,2,1,0:T(8,128)(2,1)S(1)} %get-tuple-element.41.after.own, ...), custom_call_target="tpu_custom_call" | custom-call | tf_op jit(solution)/shard_map/last_panel/pallas_call | solution.py:401
  81.0 0.0 collective-permute-done.13.refs_0_
  81.0 1.3 %collective-permute-start.17 = (bf16[4,4,256,128]{3,2,1,0:T(8,128)(2,1)S(1)}, bf16[4,4,256,128]{3,2,1,0:T(8,128)(2,1)S(1)}, u32[]{:S(2)}, u32[]{:S(2)}) collective-permute-start(bf16[4,4,256,128]{3,2,1,0:T(8,128)(2,1)S(1)} %get-tuple-element.45.other.refs_0_), channel_id=1, source_target_pairs={{0,4},{8,12},{1,5},{9,13},{6,2},{14,10},{7,3},{15,11},{24,28},{16,... | collective-permute-start | bytes 3145736 | tf_op jit(solution)/shard_map/ppermute | solution.py:624
  82.3 0.7 assemble.3.own_rest
  83.0 0.1 collective-permute-start.15
  83.0 0.0 collective-permute-done.16.own_came
  83.1 19.0 %collective-permute-done.17.other_came = bf16[4,4,256,128]{3,2,1,0:T(8,128)(2,1)S(1)} collective-permute-done((bf16[4,4,256,128]{3,2,1,0:T(8,128)(2,1)S(1)}, bf16[4,4,256,128]{3,2,1,0:T(8,128)(2,1)S(1)}, u32[]{:S(2)}, u32[]{:S(2)}) %collective-permute-start.17) | collective-permute-done | bytes 1048608 | tf_op jit(solution)/shard_map/ppermute | solution.py:624
  102.0 4.6 %project.1.refs_1_.refs_0_ = bf16[512,2048]{1,0:T(8,128)(2,1)S(1)} custom-call(s32[19]{0:T(128)S(1)} %copy-done.3, bf16[4,4,256,128]{3,2,1,0:T(8,128)(2,1)S(1)} %get-tuple-element.41.after.own, bf16[4,4,256,128]{3,2,1,0:T(8,128)(2,1)S(1)} %collective-permute-done.16.own_came, bf16[4,4,256,128]{3,2,1,0:T(8,128)(2,1)S(1)} %get-tuple-element.45.other.refs_0_, ...), custom_call_target="tpu_custom_call" | custom-call | tf_op jit(solution)/shard_map/project/pallas_call | solution.py:486
  106.6 9.0 %multiply_part.2.refs_3_ = f32[4096,2048]{1,0:T(8,128)} custom-call(s32[19]{0:T(128)S(1)} %copy-done.3, bf16[4,256,128]{2,1,0:T(8,128)(2,1)S(1)} %get-tuple-element.36.own_first, bf16[3,4,256,128]{3,2,1,0:T(8,128)(2,1)S(1)} %get-tuple-element.35.own_rest, bf16[2,4,256,128]{3,2,1,0:T(8,128)(2,1)S(1)} %collective-permute-done.8.refs_6_.other_first, ...), custom_call_target="tpu_custom_call" | custom-call | tf_op jit(solution)/shard_map/multiply_part/pallas_call | solution.py:575
  115.7 8.9 %multiply_part.3 = f32[4096,2048]{1,0:T(8,128)} custom-call(s32[19]{0:T(128)S(1)} %copy-done.3, bf16[4,256,128]{2,1,0:T(8,128)(2,1)S(1)} %get-tuple-element.33.own_first, bf16[3,4,256,128]{3,2,1,0:T(8,128)(2,1)S(1)} %assemble.3.own_rest, bf16[2,4,256,128]{3,2,1,0:T(8,128)(2,1)S(1)} %collective-permute-done.8.refs_6_.other_first, ...), custom_call_target="tpu_custom_call", output_to_operand_aliasing={{}: (8, {})} | custom-call | tf_op jit(solution)/shard_map/multiply_part/pallas_call | solution.py:575
  (18 shorter events, 0.1 us)
Async XLA Ops:
  0.0 40.2 %copy-start.2 = (f32[16384]{0:T(1024)S(1)}, f32[16384]{0:T(1024)}, u32[]{:S(2)}) copy-start(f32[16384]{0:T(1024)} %param.9) | copy-start | bytes 196612
  0.0 40.2 %copy-start.4 = (f32[64]{0:T(128)S(1)}, f32[64]{0:T(128)}, u32[]{:S(2)}) copy-start(f32[64]{0:T(128)} %taps_ref.1) | copy-start | bytes 772
  0.7 39.6 %copy-start.3 = (s32[19]{0:T(128)S(1)}, s32[19]{0:T(128)}, u32[]{:S(2)}) copy-start(s32[19]{0:T(128)} %stack.88.place_ref) | copy-start | bytes 232
  4.6 5.2 %copy-start.5 = (bf16[2,4,256,128]{3,2,1,0:T(8,128)(2,1)S(1)}, bf16[2,4,256,128]{3,2,1,0:T(8,128)(2,1)}, u32[]{:S(2)}) copy-start(bf16[2,4,256,128]{3,2,1,0:T(8,128)(2,1)} %get-tuple-element.32) | copy-start | bytes 1572868
  4.6 6.5 %copy-start = (bf16[4,256,128]{2,1,0:T(8,128)(2,1)S(1)}, bf16[4,256,128]{2,1,0:T(8,128)(2,1)}, u32[]{:S(2)}) copy-start(bf16[4,256,128]{2,1,0:T(8,128)(2,1)} %get-tuple-element.29.refs_3_) | copy-start | bytes 786436
  4.6 8.8 %copy-start.1 = (bf16[4,256,128]{2,1,0:T(8,128)(2,1)S(1)}, bf16[4,256,128]{2,1,0:T(8,128)(2,1)}, u32[]{:S(2)}) copy-start(bf16[4,256,128]{2,1,0:T(8,128)(2,1)} %get-tuple-element.28.refs_4_) | copy-start | bytes 786436
  4.6 0.8 collective-permute-start.3
  6.4 0.7 collective-permute-start.4
  7.1 0.7 collective-permute-start.5
  7.8 0.7 collective-permute-start.6
  8.6 31.7 %collective-permute-start.7 = (bf16[8,272,128]{2,1,0:T(8,128)(2,1)S(1)}, bf16[8,272,128]{2,1,0:T(8,128)(2,1)S(1)}, u32[]{:S(2)}, u32[]{:S(2)}) collective-permute-start(bf16[8,272,128]{2,1,0:T(8,128)(2,1)S(1)} %pad_maximum_fusion.own_ref.after), channel_id=1, source_target_pairs={{0,4},{8,12},{1,5},{9,13},{2,6},{10,14},{3,7},{11,15},{16,20},{24,... | collective-permute-start | bytes 1671176 | tf_op jit(solution)/shard_map/ppermute | solution.py:646
  9.9 38.5 %collective-permute-start.8 = (bf16[2,4,256,128]{3,2,1,0:T(8,128)(2,1)S(1)}, bf16[2,4,256,128]{3,2,1,0:T(8,128)(2,1)S(1)}, u32[]{:S(2)}, u32[]{:S(2)}) collective-permute-start(bf16[2,4,256,128]{3,2,1,0:T(8,128)(2,1)S(1)} %copy-done.5), channel_id=1, source_target_pairs={{16,0},{17,1},{18,2},{19,3},{20,4},{21,5},{22,6},{23,7},{24,8},{25... | collective-permute-start | bytes 1572872 | tf_op jit(solution)/shard_map/ppermute | solution.py:681
  11.1 37.2 %collective-permute-start.1 = (bf16[4,256,128]{2,1,0:T(8,128)(2,1)S(1)}, bf16[4,256,128]{2,1,0:T(8,128)(2,1)S(1)}, u32[]{:S(2)}, u32[]{:S(2)}) collective-permute-start(bf16[4,256,128]{2,1,0:T(8,128)(2,1)S(1)} %copy-done), channel_id=1, source_target_pairs={{2,0},{3,1},{0,2},{1,3},{6,4},{7,5},{4,6},{5,7},{10,8},{11,9},{8,1... | collective-permute-start | bytes 786440 | tf_op jit(solution)/shard_map/ppermute | solution.py:677
  13.5 34.9 %collective-permute-start.2 = (bf16[4,256,128]{2,1,0:T(8,128)(2,1)S(1)}, bf16[4,256,128]{2,1,0:T(8,128)(2,1)S(1)}, u32[]{:S(2)}, u32[]{:S(2)}) collective-permute-start(bf16[4,256,128]{2,1,0:T(8,128)(2,1)S(1)} %copy-done.1), channel_id=1, source_target_pairs={{1,0},{2,1},{3,2},{0,3},{5,4},{6,5},{7,6},{4,7},{9,8},{10,9},{11,1... | collective-permute-start | bytes 786440 | tf_op jit(solution)/shard_map/ppermute | solution.py:677
  13.6 34.7 %collective-permute-start = (bf16[4,256,128]{2,1,0:T(8,128)(2,1)S(1)}, bf16[4,256,128]{2,1,0:T(8,128)(2,1)S(1)}, u32[]{:S(2)}, u32[]{:S(2)}) collective-permute-start(bf16[4,256,128]{2,1,0:T(8,128)(2,1)S(1)} %copy-done.1), channel_id=1, source_target_pairs={{3,0},{0,1},{1,2},{2,3},{7,4},{4,5},{5,6},{6,7},{11,8},{8,9},{9,10... | collective-permute-start | bytes 786440 | tf_op jit(solution)/shard_map/ppermute | solution.py:677
  49.1 20.7 %collective-permute-start.9 = (bf16[4,4,256,128]{3,2,1,0:T(8,128)(2,1)S(1)}, bf16[4,4,256,128]{3,2,1,0:T(8,128)(2,1)S(1)}, u32[]{:S(2)}, u32[]{:S(2)}) collective-permute-start(bf16[4,4,256,128]{3,2,1,0:T(8,128)(2,1)S(1)} %get-tuple-element.34.after.native_ref), channel_id=1, source_target_pairs={{0,8},{1,9},{6,14},{7,15},{8,0},{9,1},{14,6},{15,7},{16,24},{17,25... | collective-permute-start | bytes 3145736 | tf_op jit(solution)/shard_map/ppermute | solution.py:689
  49.9 20.0 %collective-permute-start.10 = (bf16[3,4,256,128]{3,2,1,0:T(8,128)(2,1)S(1)}, bf16[3,4,256,128]{3,2,1,0:T(8,128)(2,1)S(1)}, u32[]{:S(2)}, u32[]{:S(2)}) collective-permute-start(bf16[3,4,256,128]{3,2,1,0:T(8,128)(2,1)S(1)} %get-tuple-element.35.own_rest), channel_id=1, source_target_pairs={{18,2},{19,3},{20,4},{21,5},{24,8},{25,9},{26,10},{27,11},{28,12},... | collective-permute-start | bytes 2359304 | tf_op jit(solution)/shard_map/ppermute | solution.py:681
  53.0 16.9 %collective-permute-start.12 = (bf16[4,256,128]{2,1,0:T(8,128)(2,1)S(1)}, bf16[4,256,128]{2,1,0:T(8,128)(2,1)S(1)}, u32[]{:S(2)}, u32[]{:S(2)}) collective-permute-start(bf16[4,256,128]{2,1,0:T(8,128)(2,1)S(1)} %get-tuple-element.33.own_first), channel_id=1, source_target_pairs={{2,0},{3,1},{0,2},{1,3},{6,4},{7,5},{4,6},{5,7},{10,8},{11,9},{8,1... | collective-permute-start | bytes 786440 | tf_op jit(solution)/shard_map/ppermute | solution.py:677
  58.5 11.4 %collective-permute-start.11 = (bf16[4,256,128]{2,1,0:T(8,128)(2,1)S(1)}, bf16[4,256,128]{2,1,0:T(8,128)(2,1)S(1)}, u32[]{:S(2)}, u32[]{:S(2)}) collective-permute-start(bf16[4,256,128]{2,1,0:T(8,128)(2,1)S(1)} %get-tuple-element.36.own_first), channel_id=1, source_target_pairs={{3,0},{0,1},{1,2},{2,3},{7,4},{4,5},{5,6},{6,7},{11,8},{8,9},{9,10... | collective-permute-start | bytes 786440 | tf_op jit(solution)/shard_map/ppermute | solution.py:677
  70.6 10.3 %collective-permute-start.13 = (bf16[4,4,256,128]{3,2,1,0:T(8,128)(2,1)S(1)}, bf16[4,4,256,128]{3,2,1,0:T(8,128)(2,1)S(1)}, u32[]{:S(2)}, u32[]{:S(2)}) collective-permute-start(bf16[4,4,256,128]{3,2,1,0:T(8,128)(2,1)S(1)} %get-tuple-element.40), channel_id=1, source_target_pairs={{16,0},{17,1},{22,6},{23,7},{24,8},{25,9},{30,14},{31,15},{0,16},{... | collective-permute-start | bytes 3145736 | tf_op jit(solution)/shard_map/ppermute | solution.py:681
  71.4 9.6 %collective-permute-start.14 = (bf16[4,256,128]{2,1,0:T(8,128)(2,1)S(1)}, bf16[4,256,128]{2,1,0:T(8,128)(2,1)S(1)}, u32[]{:S(2)}, u32[]{:S(2)}) collective-permute-start(bf16[4,256,128]{2,1,0:T(8,128)(2,1)S(1)} %get-tuple-element.36.own_first), channel_id=1, source_target_pairs={{1,0},{2,1},{3,2},{0,3},{5,4},{6,5},{7,6},{4,7},{9,8},{10,9},{11,1... | collective-permute-start | bytes 786440 | tf_op jit(solution)/shard_map/ppermute | solution.py:677
  72.9 10.2 %collective-permute-start.16 = (bf16[4,4,256,128]{3,2,1,0:T(8,128)(2,1)S(1)}, bf16[4,4,256,128]{3,2,1,0:T(8,128)(2,1)S(1)}, u32[]{:S(2)}, u32[]{:S(2)}) collective-permute-start(bf16[4,4,256,128]{3,2,1,0:T(8,128)(2,1)S(1)} %get-tuple-element.41.after.own), channel_id=1, source_target_pairs={{0,4},{8,12},{1,5},{9,13},{6,2},{14,10},{7,3},{15,11},{24,28},{16,... | collective-permute-start | bytes 3145736 | tf_op jit(solution)/shard_map/ppermute | solution.py:624
  81.0 21.0 %collective-permute-start.17 = (bf16[4,4,256,128]{3,2,1,0:T(8,128)(2,1)S(1)}, bf16[4,4,256,128]{3,2,1,0:T(8,128)(2,1)S(1)}, u32[]{:S(2)}, u32[]{:S(2)}) collective-permute-start(bf16[4,4,256,128]{3,2,1,0:T(8,128)(2,1)S(1)} %get-tuple-element.45.other.refs_0_), channel_id=1, source_target_pairs={{0,4},{8,12},{1,5},{9,13},{6,2},{14,10},{7,3},{15,11},{24,28},{16,... | collective-permute-start | bytes 3145736 | tf_op jit(solution)/shard_map/ppermute | solution.py:624
  83.0 32.7 %collective-permute-start.15 = (bf16[3,4,256,128]{3,2,1,0:T(8,128)(2,1)S(1)}, bf16[3,4,256,128]{3,2,1,0:T(8,128)(2,1)S(1)}, u32[]{:S(2)}, u32[]{:S(2)}) collective-permute-start(bf16[3,4,256,128]{3,2,1,0:T(8,128)(2,1)S(1)} %assemble.3.own_rest), channel_id=1, source_target_pairs={{16,0},{17,1},{18,2},{19,3},{20,4},{21,5},{22,6},{23,7},{24,8},{25... | collective-permute-start | bytes 2359304 | tf_op jit(solution)/shard_map/ppermute | solution.py:681

commit v9 on v8

--- a/solution.py
+++ b/solution.py
@@ -42,7 +42,7 @@
 WIDE = pltpu.CompilerParams(vmem_limit_bytes=58 << 20)
 
 
-def permute_kernel(place_ref, *refs):
+def permute_kernel(*refs):
     sources, refs = refs[:3], refs[3:]
     *part_refs, both_ref, note_ref = refs[:-4]
     order_ref, counts_ref, design_ref = targets = refs[-4:-1]
@@ -80,7 +80,7 @@
     counts = jnp.concatenate([counts] * (LANES // epochs), axis=1)
     note_ref[0, HALF:, :] = jnp.broadcast_to(counts, (NOTE, LANES)).astype(BF16)
     for j in range(parts):
-        piece = lax.rem(place_ref[PLACE_COL] + j, parts)
+        piece = lax.rem(lax.axis_index("col") + j, parts)
         at = pl.multiple_of(piece * per_part * groups, per_part * groups)
         local = order_of(pl.ds(at, per_part * groups))
         columns = lambda g: design_ref[:, pl.ds(pl.multiple_of((at + g) * PB, PB), PB)]
@@ -91,7 +91,7 @@
         both_ref[j] = part_refs[j][...]
 
 
-def permute_local(place, design, order, tap_count, cols_dev):
+def permute_local(design, order, tap_count, cols_dev):
     epochs, rows = design.shape
     parts, per_part = rows // cols_dev, cols_dev // (2 * HALF)
     piece = jax.ShapeDtypeStruct((per_part, HALF, LANES), BF16)
@@ -100,7 +100,7 @@
     return pl.pallas_call(
         permute_kernel,
         out_shape=(piece,) * parts + (both, note),
-        in_specs=[SMEM] + [ANY] * 3,
+        in_specs=[ANY] * 3,
         out_specs=(VMEM,) * (parts + 2),
         scratch_shapes=[
             pltpu.VMEM((rows // PB, PB), jnp.int32),
@@ -110,7 +110,7 @@
         ],
         compiler_params=WIDE,
         name="permute_local",
-    )(place, order.reshape(rows // PB, PB), tap_count.reshape(1, epochs), design)
+    )(order.reshape(rows // PB, PB), tap_count.reshape(1, epochs), design)
 
 
 PLACE_ROW, PLACE_GROUP, PLACE_EP, PLACE_COL, PLACE_TAKES, PLACE_OWNS, PLACE_HOME, PLACE_BACK = range(8)
@@ -271,12 +271,9 @@
 
     shape = (half, LANES)
     lag = iota(shape, 1) - iota(shape, 0)
-    base = lax.fori_loop(
-        0,
-        taps_ref.shape[0],
-        lambda k, kept: jnp.where(lag == k, taps_ref[k], kept),
-        jnp.zeros(shape, F32),
-    )
+    base = jnp.zeros(shape, F32)
+    for k in range(taps_ref.shape[0]):
+        base = jnp.where(lag == k, taps_ref[k], base)
     lane = iota(shape, 1)
     swapped = jnp.concatenate([base[:, half:], base[:, :half]], axis=1)
     patterns = (jnp.where(lane < half, swapped, 0.0), base, jnp.where(lane >= half, swapped, 0.0))
@@ -321,10 +318,11 @@
         aug[below, rest] -= dot(aug[here, below], aug[here, rest], TN, precision=EXACT)
 
 
-def next_kernel(kb, aug_in, after, aug_ref, work):
+def next_kernel(blocks, aug_in, after, aug_ref, work):
     del after
     aug_ref[...] = aug_in[...]
-    eliminate(aug_ref, kb, work)
+    for kb in blocks:
+        eliminate(aug_ref, kb, work)
 
 
 def last_kernel(kb, aug_in, after, taper_ref, factor_ref, w_ref, high_ref, low_ref, aug, work, high, low):
@@ -383,9 +381,9 @@
     )(place, taps, own, came, regular.reshape(1, -1), after)
 
 
-def next_panel(kb, aug, after):
-    return pl.pallas_call(
-        functools.partial(next_kernel, kb),
+def next_panel(blocks, aug, after):
+    return pl.pallas_call(
+        functools.partial(next_kernel, blocks),
         out_shape=jax.ShapeDtypeStruct(aug.shape, F32),
         in_specs=[VMEM, ANY],
         out_specs=VMEM,
@@ -626,7 +624,8 @@
 
 def panel_hops():
     eps, _, cols = sizes()
-    return [(d, 0) for d in doubling(eps, 1)] + [(0, d) for d in reversed(doubling(cols, 1))]
+    across = [(0, d) for d in doubling(cols, 1)]
+    return across[:-1] + [(d, 0) for d in doubling(eps, 1)] + across[-1:]
 
 
 def gather_panel(note):
@@ -670,7 +669,7 @@
     place += [(ep ^ de) * cols + (col ^ dc) for de, dc in steps]
     place = jnp.stack([jnp.asarray(p, jnp.int32) for p in place])
 
-    *local, both, note = permute_local(place, design, order, tap_count, cols_dev)
+    *local, both, note = permute_local(design, order, tap_count, cols_dev)
 
     def shift(block, n):
         route = [(flat(e, r, (c - n) % cols), flat(e, r, c)) for e, r, c in everywhere]
@@ -700,17 +699,16 @@
     swapped = across(both, lambda e, r, c: True)
     band, taper, aug = start_panel(place, chain, taps, notes, came, regular, notes)
     rest, *local, first = assemble(place, early, local, [aug, swapped], True)
-    aug = next_panel(1, aug, first)
     foreign = trade(first)
     others = [across(rest, lambda e, r, c: not owns(e, r, c))]
     mine = [rest]
     order = [(j, n) for j in range(1, parts) for n in range(1, cols)]
     late = [shift(local[(n + j) % parts], n) for j, n in order]
-    aug = next_panel(2, aug, first)
+    aug = next_panel(range(1, HEAD // BLOCK - 1), aug, first)
     foreign, others[0], *late[:2] = gate([foreign, others[0], *late[:2]], aug)
     own, sent = sort(place, first, foreign)
     theirs = across(sent, lambda e, r, c: inside(r, c))
-    factor, w, high, low = last_panel(3, aug, own, taper)
+    factor, w, high, low = last_panel(HEAD // BLOCK - 1, aug, own, taper)
     theirs, *late[2:] = gate([theirs, *late[2:]], factor)
     own, own_came = spread_rest(own)
     other, other_came = spread_rest(theirs)

time: 125 us -> 123 us (0.984)
  Pallas kernels: 54.6 us -> 53.2 us
    ppermute x6, waiting for transfers between devices: 0.02 us -> 2.88 us  [shift(): return lax.ppermute(block, AXES, route)]
    ppermute x3, waiting for transfers between devices: 19 us -> 16.7 us  [spread_step(): return lax.ppermute(block, AXES, route)]
    ppermute x6, starting transfers between devices: 10.8 us -> 9.47 us  [shift(): return lax.ppermute(block, AXES, route)]
    pallas_call x2 -> x1, Pallas kernels: 11.3 us -> 11 us  [next_panel(): pl.pallas_call(functools.partial(next_kernel, blocks), out_shape=jax.Shap...]
  transfers between devices with their start and end apart: 18 -> 18, of which waited for: 2 -> 3; matrix products, arithmetic and copies ran while one was open for 0% -> 0% of each run, Pallas kernels for 32% -> 32%
where the time goes in v9:
time: 123 us
  Pallas kernels  53.2 us (43%)
  waiting for transfers between devices  45 us (37%)
  starting transfers between devices  23 us (19%)
    ppermute x1, waiting for transfers between devices, gather_panel(): came = lax.ppermute(note, 'row', [(r, r + 1) for r in range(0, rows, 2)])  25.4 us
    pallas_call x2, Pallas kernels, multiply_part(): pl.pallas_call(functools.partial(tile_kernel, part, parts), out_shape=jax...  18 us
    ppermute x3, waiting for transfers between devices, spread_step(): return lax.ppermute(block, AXES, route)  16.7 us
    pallas_call x1, Pallas kernels, next_panel(): pl.pallas_call(functools.partial(next_kernel, blocks), out_shape=jax.Shap...  11 us
    ppermute x6, starting transfers between devices, shift(): return lax.ppermute(block, AXES, route)  9.47 us
    pallas_call x1, Pallas kernels, start_panel(): pl.pallas_call(functools.partial(start_kernel, chain), out_shape=(jax.Sha...  7.77 us
    pallas_call x1, Pallas kernels, last_panel(): pl.pallas_call(functools.partial(last_kernel, kb), out_shape=(jax.ShapeDt...  6.57 us
    ppermute x4, starting transfers between devices, across(): return lax.ppermute(block, AXES, route)  5.88 us
  transfers between devices with their start and end apart: 18, of which 3 were waited for; matrix products, arithmetic and copies ran while one was open for 0% of the time, Pallas kernels for 32%

profile of v9, /device:TPU:9, one launch (start us, length us, event | category | flops | bytes accessed | tf_op | source)
XLA Modules:
  0.0 122.6 jit_solution(4730931483153942693)
XLA Ops:
  0.0 3.2 %permute_local.1 = (bf16[4,256,128]{2,1,0:T(8,128)(2,1)}, bf16[4,256,128]{2,1,0:T(8,128)(2,1)}, bf16[2,4,256,128]{3,2,1,0:T(8,128)(2,1)}, bf16[1,272,128]{2,1,0:T(8,128)(2,1)}) custom-call(s32[32,128]{1,0:T(8,128)} %bitcast.24, s32[1,64]{1,0:T(1,128)} %bitcast.25, bf16[64,4096]{1,0:T(8,128)(2,1)} %refs_2_.1), custom_call_target="tpu_custom_call" | custom-call | tf_op jit(solution)/shard_map/permute_local/pallas_call | solution.py:100
  3.2 0.0 copy-start.4
  3.3 0.8 collective-permute-start.3
  4.1 0.0 collective-permute-done.3
  4.1 0.9 broadcast_select_fusion
  5.0 0.7 collective-permute-start.4
  5.6 0.0 collective-permute-done.4
  5.7 0.7 collective-permute-start.5
  6.4 0.0 collective-permute-done.5
  6.4 0.7 collective-permute-start.6
  7.1 0.0 collective-permute-done.6
  7.1 0.1 pad_maximum_fusion.own_ref.after
  7.2 1.3 %collective-permute-start.7 = (bf16[8,272,128]{2,1,0:T(8,128)(2,1)S(1)}, bf16[8,272,128]{2,1,0:T(8,128)(2,1)S(1)}, u32[]{:S(2)}, u32[]{:S(2)}) collective-permute-start(bf16[8,272,128]{2,1,0:T(8,128)(2,1)S(1)} %pad_maximum_fusion.own_ref.after), channel_id=1, source_target_pairs={{0,4},{8,12},{1,5},{9,13},{2,6},{10,14},{3,7},{11,15},{16,20},{24,... | collective-permute-start | bytes 1671176 | tf_op jit(solution)/shard_map/ppermute | solution.py:645
  8.5 1.3 %collective-permute-start.8 = (bf16[2,4,256,128]{3,2,1,0:T(8,128)(2,1)S(1)}, bf16[2,4,256,128]{3,2,1,0:T(8,128)(2,1)S(1)}, u32[]{:S(2)}, u32[]{:S(2)}) collective-permute-start(bf16[2,4,256,128]{3,2,1,0:T(8,128)(2,1)S(1)} %copy-done.4), channel_id=1, source_target_pairs={{16,0},{17,1},{18,2},{19,3},{20,4},{21,5},{22,6},{23,7},{24,8},{25... | collective-permute-start | bytes 1572872 | tf_op jit(solution)/shard_map/ppermute | solution.py:680
  9.8 2.3 %collective-permute-start.1 = (bf16[4,256,128]{2,1,0:T(8,128)(2,1)S(1)}, bf16[4,256,128]{2,1,0:T(8,128)(2,1)S(1)}, u32[]{:S(2)}, u32[]{:S(2)}) collective-permute-start(bf16[4,256,128]{2,1,0:T(8,128)(2,1)S(1)} %copy-done), channel_id=1, source_target_pairs={{2,0},{3,1},{0,2},{1,3},{6,4},{7,5},{4,6},{5,7},{10,8},{11,9},{8,1... | collective-permute-start | bytes 786440 | tf_op jit(solution)/shard_map/ppermute | solution.py:676
  12.1 0.2 collective-permute-start.2
  12.2 1.3 %collective-permute-start = (bf16[4,256,128]{2,1,0:T(8,128)(2,1)S(1)}, bf16[4,256,128]{2,1,0:T(8,128)(2,1)S(1)}, u32[]{:S(2)}, u32[]{:S(2)}) collective-permute-start(bf16[4,256,128]{2,1,0:T(8,128)(2,1)S(1)} %copy-done.1), channel_id=1, source_target_pairs={{3,0},{0,1},{1,2},{2,3},{7,4},{4,5},{5,6},{6,7},{11,8},{8,9},{9,10... | collective-permute-start | bytes 786440 | tf_op jit(solution)/shard_map/ppermute | solution.py:676
  13.5 0.1 stack.88.place_ref
  13.6 25.4 %collective-permute-done.7.came_ref = bf16[8,272,128]{2,1,0:T(8,128)(2,1)S(1)} collective-permute-done((bf16[8,272,128]{2,1,0:T(8,128)(2,1)S(1)}, bf16[8,272,128]{2,1,0:T(8,128)(2,1)S(1)}, u32[]{:S(2)}, u32[]{:S(2)}) %collective-permute-start.7) | collective-permute-done | bytes 557088 | tf_op jit(solution)/shard_map/ppermute | solution.py:645
  39.0 7.8 %start_panel.1 = (bf16[4,384,256]{2,1,0:T(8,128)(2,1)S(1)}, bf16[8,64,128]{2,1,0:T(8,128)(2,1)S(1)}, f32[512,1024]{1,0:T(8,128)S(1)}) custom-call(s32[19]{0:T(128)S(1)} %stack.88.place_ref, f32[64]{0:T(128)S(1)} %copy-done.3, bf16[8,272,128]{2,1,0:T(8,128)(2,1)S(1)} %pad_maximum_fusion.own_ref.after, ...), custom_call_target="tpu_custom_call" | custom-call | tf_op jit(solution)/shard_map/start_panel/pallas_call | solution.py:364
  46.8 0.0 collective-permute-done.1.refs_1_
  46.8 0.0 collective-permute-done.2.refs_2_
  46.8 0.0 collective-permute-done.refs_0_
  46.9 0.0 collective-permute-done.8.refs_6_.other_first
  46.9 0.7 assemble.2
  47.6 0.7 collective-permute-start.9
  48.4 2.2 %collective-permute-start.10 = (bf16[3,4,256,128]{3,2,1,0:T(8,128)(2,1)S(1)}, bf16[3,4,256,128]{3,2,1,0:T(8,128)(2,1)S(1)}, u32[]{:S(2)}, u32[]{:S(2)}) collective-permute-start(bf16[3,4,256,128]{3,2,1,0:T(8,128)(2,1)S(1)} %get-tuple-element.35.own_rest), channel_id=1, source_target_pairs={{18,2},{19,3},{20,4},{21,5},{24,8},{25,9},{26,10},{27,11},{28,12},... | collective-permute-start | bytes 2359304 | tf_op jit(solution)/shard_map/ppermute | solution.py:680
  50.6 5.6 %collective-permute-start.12 = (bf16[4,256,128]{2,1,0:T(8,128)(2,1)S(1)}, bf16[4,256,128]{2,1,0:T(8,128)(2,1)S(1)}, u32[]{:S(2)}, u32[]{:S(2)}) collective-permute-start(bf16[4,256,128]{2,1,0:T(8,128)(2,1)S(1)} %get-tuple-element.33.own_first), channel_id=1, source_target_pairs={{2,0},{3,1},{0,2},{1,3},{6,4},{7,5},{4,6},{5,7},{10,8},{11,9},{8,1... | collective-permute-start | bytes 786440 | tf_op jit(solution)/shard_map/ppermute | solution.py:676
  56.2 0.0 collective-permute-start.11
  56.2 11.0 %next_panel.1.refs_4_.aug_in = f32[512,1024]{1,0:T(8,128)S(1)} custom-call(f32[512,1024]{1,0:T(8,128)S(1)} %get-tuple-element.31.refs_5_.aug_in, bf16[4,4,256,128]{3,2,1,0:T(8,128)(2,1)S(1)} %get-tuple-element.34.after.native_ref), custom_call_target="tpu_custom_call" | custom-call | tf_op jit(solution)/shard_map/next_panel/pallas_call | solution.py:385
  67.2 0.0 collective-permute-done.12.refs_3_
  67.2 2.9 %collective-permute-done.11.refs_2_ = bf16[4,256,128]{2,1,0:T(8,128)(2,1)S(1)} collective-permute-done((bf16[4,256,128]{2,1,0:T(8,128)(2,1)S(1)}, bf16[4,256,128]{2,1,0:T(8,128)(2,1)S(1)}, u32[]{:S(2)}, u32[]{:S(2)}) %collective-permute-start.11) | collective-permute-done | bytes 262176 | tf_op jit(solution)/shard_map/ppermute | solution.py:676
  70.0 0.0 collective-permute-done.10.refs_1_
  70.0 0.7 sort.1
  70.8 0.7 collective-permute-start.13
  71.5 0.1 collective-permute-start.14
  71.6 1.5 %collective-permute-start.16 = (bf16[4,4,256,128]{3,2,1,0:T(8,128)(2,1)S(1)}, bf16[4,4,256,128]{3,2,1,0:T(8,128)(2,1)S(1)}, u32[]{:S(2)}, u32[]{:S(2)}) collective-permute-start(bf16[4,4,256,128]{3,2,1,0:T(8,128)(2,1)S(1)} %get-tuple-element.41.after.own), channel_id=1, source_target_pairs={{0,4},{8,12},{1,5},{9,13},{6,2},{14,10},{7,3},{15,11},{24,28},{16,... | collective-permute-start | bytes 3145736 | tf_op jit(solution)/shard_map/ppermute | solution.py:622
  73.1 6.6 %last_panel.1 = (f32[512,512]{1,0:T(8,128)S(1)}, bf16[512,512]{1,0:T(8,128)(2,1)S(1)}, bf16[512,512]{1,0:T(8,128)(2,1)S(1)}, bf16[512,512]{1,0:T(8,128)(2,1)S(1)}) custom-call(f32[512,1024]{1,0:T(8,128)S(1)} %next_panel.1.refs_4_.aug_in, bf16[4,4,256,128]{3,2,1,0:T(8,128)(2,1)S(1)} %get-tuple-element.41.after.own, ...), custom_call_target="tpu_custom_call" | custom-call | tf_op jit(solution)/shard_map/last_panel/pallas_call | solution.py:399
  79.7 0.0 collective-permute-done.13.refs_0_
  79.7 1.3 %collective-permute-start.17 = (bf16[4,4,256,128]{3,2,1,0:T(8,128)(2,1)S(1)}, bf16[4,4,256,128]{3,2,1,0:T(8,128)(2,1)S(1)}, u32[]{:S(2)}, u32[]{:S(2)}) collective-permute-start(bf16[4,4,256,128]{3,2,1,0:T(8,128)(2,1)S(1)} %get-tuple-element.45.other.refs_0_), channel_id=1, source_target_pairs={{0,4},{8,12},{1,5},{9,13},{6,2},{14,10},{7,3},{15,11},{24,28},{16,... | collective-permute-start | bytes 3145736 | tf_op jit(solution)/shard_map/ppermute | solution.py:622
  81.0 0.7 assemble.3.own_rest
  81.7 1.7 %collective-permute-start.15 = (bf16[3,4,256,128]{3,2,1,0:T(8,128)(2,1)S(1)}, bf16[3,4,256,128]{3,2,1,0:T(8,128)(2,1)S(1)}, u32[]{:S(2)}, u32[]{:S(2)}) collective-permute-start(bf16[3,4,256,128]{3,2,1,0:T(8,128)(2,1)S(1)} %assemble.3.own_rest), channel_id=1, source_target_pairs={{16,0},{17,1},{18,2},{19,3},{20,4},{21,5},{22,6},{23,7},{24,8},{25... | collective-permute-start | bytes 2359304 | tf_op jit(solution)/shard_map/ppermute | solution.py:680
  83.3 0.0 collective-permute-done.16.own_came
  83.3 16.7 %collective-permute-done.17.other_came = bf16[4,4,256,128]{3,2,1,0:T(8,128)(2,1)S(1)} collective-permute-done((bf16[4,4,256,128]{3,2,1,0:T(8,128)(2,1)S(1)}, bf16[4,4,256,128]{3,2,1,0:T(8,128)(2,1)S(1)}, u32[]{:S(2)}, u32[]{:S(2)}) %collective-permute-start.17) | collective-permute-done | bytes 1048608 | tf_op jit(solution)/shard_map/ppermute | solution.py:622
  100.0 4.6 %project.1.refs_1_.refs_0_ = bf16[512,2048]{1,0:T(8,128)(2,1)S(1)} custom-call(s32[19]{0:T(128)S(1)} %stack.88.place_ref, bf16[4,4,256,128]{3,2,1,0:T(8,128)(2,1)S(1)} %get-tuple-element.41.after.own, bf16[4,4,256,128]{3,2,1,0:T(8,128)(2,1)S(1)} %collective-permute-done.16.own_came, bf16[4,4,256,128]{3,2,1,0:T(8,128)(2,1)S(1)} %get-tuple-element.45.other.refs_0_, ...), custom_call_target="tpu_custom_call" | custom-call | tf_op jit(solution)/shard_map/project/pallas_call | solution.py:484
  104.6 9.0 %multiply_part.2.refs_3_ = f32[4096,2048]{1,0:T(8,128)} custom-call(s32[19]{0:T(128)S(1)} %stack.88.place_ref, bf16[4,256,128]{2,1,0:T(8,128)(2,1)S(1)} %get-tuple-element.36.own_first, bf16[3,4,256,128]{3,2,1,0:T(8,128)(2,1)S(1)} %get-tuple-element.35.own_rest, bf16[2,4,256,128]{3,2,1,0:T(8,128)(2,1)S(1)} %collective-permute-done.8.refs_6_.other_first, ...), custom_call_target="tpu_custom_call" | custom-call | tf_op jit(solution)/shard_map/multiply_part/pallas_call | solution.py:573
  113.7 0.0 collective-permute-done.15.other_rest
  113.7 8.9 %multiply_part.3 = f32[4096,2048]{1,0:T(8,128)} custom-call(s32[19]{0:T(128)S(1)} %stack.88.place_ref, bf16[4,256,128]{2,1,0:T(8,128)(2,1)S(1)} %get-tuple-element.33.own_first, bf16[3,4,256,128]{3,2,1,0:T(8,128)(2,1)S(1)} %assemble.3.own_rest, ...), custom_call_target="tpu_custom_call", output_to_operand_aliasing={{}: (8, {})} | custom-call | tf_op jit(solution)/shard_map/multiply_part/pallas_call | solution.py:573
  (15 shorter events, 0.1 us)
Async XLA Ops:
  0.0 39.0 %copy-start.2 = (f32[16384]{0:T(1024)S(1)}, f32[16384]{0:T(1024)}, u32[]{:S(2)}) copy-start(f32[16384]{0:T(1024)} %param.9) | copy-start | bytes 196612
  0.0 39.0 %copy-start.3 = (f32[64]{0:T(128)S(1)}, f32[64]{0:T(128)}, u32[]{:S(2)}) copy-start(f32[64]{0:T(128)} %taps_ref.1) | copy-start | bytes 772
  3.2 5.2 %copy-start.4 = (bf16[2,4,256,128]{3,2,1,0:T(8,128)(2,1)S(1)}, bf16[2,4,256,128]{3,2,1,0:T(8,128)(2,1)}, u32[]{:S(2)}) copy-start(bf16[2,4,256,128]{3,2,1,0:T(8,128)(2,1)} %get-tuple-element.32) | copy-start | bytes 1572868
  3.2 6.5 %copy-start = (bf16[4,256,128]{2,1,0:T(8,128)(2,1)S(1)}, bf16[4,256,128]{2,1,0:T(8,128)(2,1)}, u32[]{:S(2)}) copy-start(bf16[4,256,128]{2,1,0:T(8,128)(2,1)} %get-tuple-element.29.refs_3_) | copy-start | bytes 786436
  3.2 8.8 %copy-start.1 = (bf16[4,256,128]{2,1,0:T(8,128)(2,1)S(1)}, bf16[4,256,128]{2,1,0:T(8,128)(2,1)}, u32[]{:S(2)}) copy-start(bf16[4,256,128]{2,1,0:T(8,128)(2,1)} %get-tuple-element.28.refs_4_) | copy-start | bytes 786436
  3.3 0.8 collective-permute-start.3
  5.0 0.7 collective-permute-start.4
  5.7 0.7 collective-permute-start.5
  6.4 0.7 collective-permute-start.6
  7.2 31.9 %collective-permute-start.7 = (bf16[8,272,128]{2,1,0:T(8,128)(2,1)S(1)}, bf16[8,272,128]{2,1,0:T(8,128)(2,1)S(1)}, u32[]{:S(2)}, u32[]{:S(2)}) collective-permute-start(bf16[8,272,128]{2,1,0:T(8,128)(2,1)S(1)} %pad_maximum_fusion.own_ref.after), channel_id=1, source_target_pairs={{0,4},{8,12},{1,5},{9,13},{2,6},{10,14},{3,7},{11,15},{16,20},{24,... | collective-permute-start | bytes 1671176 | tf_op jit(solution)/shard_map/ppermute | solution.py:645
  8.5 38.4 %collective-permute-start.8 = (bf16[2,4,256,128]{3,2,1,0:T(8,128)(2,1)S(1)}, bf16[2,4,256,128]{3,2,1,0:T(8,128)(2,1)S(1)}, u32[]{:S(2)}, u32[]{:S(2)}) collective-permute-start(bf16[2,4,256,128]{3,2,1,0:T(8,128)(2,1)S(1)} %copy-done.4), channel_id=1, source_target_pairs={{16,0},{17,1},{18,2},{19,3},{20,4},{21,5},{22,6},{23,7},{24,8},{25... | collective-permute-start | bytes 1572872 | tf_op jit(solution)/shard_map/ppermute | solution.py:680
  9.8 37.1 %collective-permute-start.1 = (bf16[4,256,128]{2,1,0:T(8,128)(2,1)S(1)}, bf16[4,256,128]{2,1,0:T(8,128)(2,1)S(1)}, u32[]{:S(2)}, u32[]{:S(2)}) collective-permute-start(bf16[4,256,128]{2,1,0:T(8,128)(2,1)S(1)} %copy-done), channel_id=1, source_target_pairs={{2,0},{3,1},{0,2},{1,3},{6,4},{7,5},{4,6},{5,7},{10,8},{11,9},{8,1... | collective-permute-start | bytes 786440 | tf_op jit(solution)/shard_map/ppermute | solution.py:676
  12.1 34.8 %collective-permute-start.2 = (bf16[4,256,128]{2,1,0:T(8,128)(2,1)S(1)}, bf16[4,256,128]{2,1,0:T(8,128)(2,1)S(1)}, u32[]{:S(2)}, u32[]{:S(2)}) collective-permute-start(bf16[4,256,128]{2,1,0:T(8,128)(2,1)S(1)} %copy-done.1), channel_id=1, source_target_pairs={{1,0},{2,1},{3,2},{0,3},{5,4},{6,5},{7,6},{4,7},{9,8},{10,9},{11,1... | collective-permute-start | bytes 786440 | tf_op jit(solution)/shard_map/ppermute | solution.py:676
  12.2 34.6 %collective-permute-start = (bf16[4,256,128]{2,1,0:T(8,128)(2,1)S(1)}, bf16[4,256,128]{2,1,0:T(8,128)(2,1)S(1)}, u32[]{:S(2)}, u32[]{:S(2)}) collective-permute-start(bf16[4,256,128]{2,1,0:T(8,128)(2,1)S(1)} %copy-done.1), channel_id=1, source_target_pairs={{3,0},{0,1},{1,2},{2,3},{7,4},{4,5},{5,6},{6,7},{11,8},{8,9},{9,10... | collective-permute-start | bytes 786440 | tf_op jit(solution)/shard_map/ppermute | solution.py:676
  47.6 22.4 %collective-permute-start.9 = (bf16[4,4,256,128]{3,2,1,0:T(8,128)(2,1)S(1)}, bf16[4,4,256,128]{3,2,1,0:T(8,128)(2,1)S(1)}, u32[]{:S(2)}, u32[]{:S(2)}) collective-permute-start(bf16[4,4,256,128]{3,2,1,0:T(8,128)(2,1)S(1)} %get-tuple-element.34.after.native_ref), channel_id=1, source_target_pairs={{0,8},{1,9},{6,14},{7,15},{8,0},{9,1},{14,6},{15,7},{16,24},{17,25... | collective-permute-start | bytes 3145736 | tf_op jit(solution)/shard_map/ppermute | solution.py:688
  48.4 21.7 %collective-permute-start.10 = (bf16[3,4,256,128]{3,2,1,0:T(8,128)(2,1)S(1)}, bf16[3,4,256,128]{3,2,1,0:T(8,128)(2,1)S(1)}, u32[]{:S(2)}, u32[]{:S(2)}) collective-permute-start(bf16[3,4,256,128]{3,2,1,0:T(8,128)(2,1)S(1)} %get-tuple-element.35.own_rest), channel_id=1, source_target_pairs={{18,2},{19,3},{20,4},{21,5},{24,8},{25,9},{26,10},{27,11},{28,12},... | collective-permute-start | bytes 2359304 | tf_op jit(solution)/shard_map/ppermute | solution.py:680
  50.6 16.6 %collective-permute-start.12 = (bf16[4,256,128]{2,1,0:T(8,128)(2,1)S(1)}, bf16[4,256,128]{2,1,0:T(8,128)(2,1)S(1)}, u32[]{:S(2)}, u32[]{:S(2)}) collective-permute-start(bf16[4,256,128]{2,1,0:T(8,128)(2,1)S(1)} %get-tuple-element.33.own_first), channel_id=1, source_target_pairs={{2,0},{3,1},{0,2},{1,3},{6,4},{7,5},{4,6},{5,7},{10,8},{11,9},{8,1... | collective-permute-start | bytes 786440 | tf_op jit(solution)/shard_map/ppermute | solution.py:676
  56.2 13.8 %collective-permute-start.11 = (bf16[4,256,128]{2,1,0:T(8,128)(2,1)S(1)}, bf16[4,256,128]{2,1,0:T(8,128)(2,1)S(1)}, u32[]{:S(2)}, u32[]{:S(2)}) collective-permute-start(bf16[4,256,128]{2,1,0:T(8,128)(2,1)S(1)} %get-tuple-element.36.own_first), channel_id=1, source_target_pairs={{3,0},{0,1},{1,2},{2,3},{7,4},{4,5},{5,6},{6,7},{11,8},{8,9},{9,10... | collective-permute-start | bytes 786440 | tf_op jit(solution)/shard_map/ppermute | solution.py:676
  70.8 8.9 %collective-permute-start.13 = (bf16[4,4,256,128]{3,2,1,0:T(8,128)(2,1)S(1)}, bf16[4,4,256,128]{3,2,1,0:T(8,128)(2,1)S(1)}, u32[]{:S(2)}, u32[]{:S(2)}) collective-permute-start(bf16[4,4,256,128]{3,2,1,0:T(8,128)(2,1)S(1)} %get-tuple-element.40), channel_id=1, source_target_pairs={{16,0},{17,1},{22,6},{23,7},{24,8},{25,9},{30,14},{31,15},{0,16},{... | collective-permute-start | bytes 3145736 | tf_op jit(solution)/shard_map/ppermute | solution.py:680
  71.5 8.2 %collective-permute-start.14 = (bf16[4,256,128]{2,1,0:T(8,128)(2,1)S(1)}, bf16[4,256,128]{2,1,0:T(8,128)(2,1)S(1)}, u32[]{:S(2)}, u32[]{:S(2)}) collective-permute-start(bf16[4,256,128]{2,1,0:T(8,128)(2,1)S(1)} %get-tuple-element.36.own_first), channel_id=1, source_target_pairs={{1,0},{2,1},{3,2},{0,3},{5,4},{6,5},{7,6},{4,7},{9,8},{10,9},{11,1... | collective-permute-start | bytes 786440 | tf_op jit(solution)/shard_map/ppermute | solution.py:676
  71.6 11.8 %collective-permute-start.16 = (bf16[4,4,256,128]{3,2,1,0:T(8,128)(2,1)S(1)}, bf16[4,4,256,128]{3,2,1,0:T(8,128)(2,1)S(1)}, u32[]{:S(2)}, u32[]{:S(2)}) collective-permute-start(bf16[4,4,256,128]{3,2,1,0:T(8,128)(2,1)S(1)} %get-tuple-element.41.after.own), channel_id=1, source_target_pairs={{0,4},{8,12},{1,5},{9,13},{6,2},{14,10},{7,3},{15,11},{24,28},{16,... | collective-permute-start | bytes 3145736 | tf_op jit(solution)/shard_map/ppermute | solution.py:622
  79.7 20.3 %collective-permute-start.17 = (bf16[4,4,256,128]{3,2,1,0:T(8,128)(2,1)S(1)}, bf16[4,4,256,128]{3,2,1,0:T(8,128)(2,1)S(1)}, u32[]{:S(2)}, u32[]{:S(2)}) collective-permute-start(bf16[4,4,256,128]{3,2,1,0:T(8,128)(2,1)S(1)} %get-tuple-element.45.other.refs_0_), channel_id=1, source_target_pairs={{0,4},{8,12},{1,5},{9,13},{6,2},{14,10},{7,3},{15,11},{24,28},{16,... | collective-permute-start | bytes 3145736 | tf_op jit(solution)/shard_map/ppermute | solution.py:622
  81.7 32.0 %collective-permute-start.15 = (bf16[3,4,256,128]{3,2,1,0:T(8,128)(2,1)S(1)}, bf16[3,4,256,128]{3,2,1,0:T(8,128)(2,1)S(1)}, u32[]{:S(2)}, u32[]{:S(2)}) collective-permute-start(bf16[3,4,256,128]{3,2,1,0:T(8,128)(2,1)S(1)} %assemble.3.own_rest), channel_id=1, source_target_pairs={{16,0},{17,1},{18,2},{19,3},{20,4},{21,5},{22,6},{23,7},{24,8},{25... | collective-permute-start | bytes 2359304 | tf_op jit(solution)/shard_map/ppermute | solution.py:680

commit v10 on v9

--- a/solution.py
+++ b/solution.py
@@ -470,7 +470,7 @@
         unpack(place_ref, shards_of(both.at[0], n), shards_of(both.at[1], n), blocks)
         filter_rows(lambda e: blocks[e], band_ref, store)
         wanted = columns[...]
-        projected = dot(high_ref[...], wanted, NT) + dot(low_ref[...], wanted, NT)
+        projected = dot(high_ref[...], wanted, NT)
         right_ref[:, n * rows : (n + 1) * rows] = projected.astype(BF16)
 
     @pl.when(place_ref[PLACE_GROUP] == 0)
@@ -704,10 +704,11 @@
     mine = [rest]
     order = [(j, n) for j in range(1, parts) for n in range(1, cols)]
     late = [shift(local[(n + j) % parts], n) for j, n in order]
-    aug = next_panel(range(1, HEAD // BLOCK - 1), aug, first)
+    aug = next_panel(range(1, 2), aug, first)
     foreign, others[0], *late[:2] = gate([foreign, others[0], *late[:2]], aug)
     own, sent = sort(place, first, foreign)
     theirs = across(sent, lambda e, r, c: inside(r, c))
+    aug = next_panel(range(2, HEAD // BLOCK - 1), aug, own)
     factor, w, high, low = last_panel(HEAD // BLOCK - 1, aug, own, taper)
     theirs, *late[2:] = gate([theirs, *late[2:]], factor)
     own, own_came = spread_rest(own)

time: 123 us -> 122 us (level)
  the two profiles are of different devices: /device:TPU:9 before, /device:TPU:0 now
where the time goes in v10:
time: 122 us; the launch traced here: 121 us
  Pallas kernels  51.6 us (42%)
  starting transfers between devices  39.2 us (32%)
  waiting for transfers between devices  28.7 us (24%)
    pallas_call x2, Pallas kernels, multiply_part(): pl.pallas_call(functools.partial(tile_kernel, part, parts), out_shape=jax...  17 us
    ppermute x3, waiting for transfers between devices, gather_panel(): note = jnp.concatenate([note, lax.ppermute(note, AXES, route)])  13.8 us
    pallas_call x2, Pallas kernels, next_panel(): pl.pallas_call(functools.partial(next_kernel, blocks), out_shape=jax.Shap...  11.3 us
    ppermute x3, starting transfers between devices, gather_panel(): note = jnp.concatenate([note, lax.ppermute(note, AXES, route)])  11.3 us
    ppermute x6, starting transfers between devices, shift(): return lax.ppermute(block, AXES, route)  8.03 us
    ppermute x3, starting transfers between devices, spread_step(): return lax.ppermute(block, AXES, route)  7.93 us
    pallas_call x1, Pallas kernels, start_panel(): pl.pallas_call(functools.partial(start_kernel, chain), out_shape=(jax.Sha...  7.77 us
    ppermute x4, starting transfers between devices, across(): return lax.ppermute(block, AXES, route)  7.15 us
  transfers between devices with their start and end apart: 18, of which 9 were waited for; matrix products, arithmetic and copies ran while one was open for 0% of the time, Pallas kernels for 31%

profile of v10, /device:TPU:0, one launch (start us, length us, event | category | flops | bytes accessed | tf_op | source)
XLA Modules:
  0.0 120.8 jit_solution(17809070988604688536)
XLA Ops:
  0.0 3.2 %permute_local.1 = (bf16[4,256,128]{2,1,0:T(8,128)(2,1)}, bf16[4,256,128]{2,1,0:T(8,128)(2,1)}, bf16[2,4,256,128]{3,2,1,0:T(8,128)(2,1)}, bf16[1,272,128]{2,1,0:T(8,128)(2,1)}) custom-call(s32[32,128]{1,0:T(8,128)} %bitcast.24, s32[1,64]{1,0:T(1,128)} %bitcast.25, bf16[64,4096]{1,0:T(8,128)(2,1)} %refs_2_.1), custom_call_target="tpu_custom_call" | custom-call | tf_op jit(solution)/shard_map/permute_local/pallas_call | solution.py:100
  3.2 0.0 copy-start.4
  3.3 5.0 %collective-permute-start.3 = (bf16[1,272,128]{2,1,0:T(8,128)(2,1)}, bf16[1,272,128]{2,1,0:T(8,128)(2,1)S(1)}, u32[]{:S(2)}, u32[]{:S(2)}) collective-permute-start(bf16[1,272,128]{2,1,0:T(8,128)(2,1)} %get-tuple-element.30), channel_id=1, source_target_pairs={{0,8},{1,9},{2,10},{3,11},{16,24},{17,25},{18,26},{19,27}} | collective-permute-start | bytes 208904 | tf_op jit(solution)/shard_map/ppermute | solution.py:622
  8.3 2.2 %collective-permute-done.3 = bf16[1,272,128]{2,1,0:T(8,128)(2,1)S(1)} collective-permute-done((bf16[1,272,128]{2,1,0:T(8,128)(2,1)}, bf16[1,272,128]{2,1,0:T(8,128)(2,1)S(1)}, u32[]{:S(2)}, u32[]{:S(2)}) %collective-permute-start.3) | collective-permute-done | bytes 69664 | tf_op jit(solution)/shard_map/ppermute | solution.py:622
  10.5 0.9 broadcast_select_fusion
  11.4 4.5 %collective-permute-start.4 = (bf16[1,272,128]{2,1,0:T(8,128)(2,1)S(1)}, bf16[1,272,128]{2,1,0:T(8,128)(2,1)S(1)}, u32[]{:S(2)}, u32[]{:S(2)}) collective-permute-start(bf16[1,272,128]{2,1,0:T(8,128)(2,1)S(1)} %broadcast_select_fusion), channel_id=1, source_target_pairs={{0,2},{1,3},{2,0},{3,1},{8,10},{9,11},{10,8},{11,9},{16,18},{17,19... | collective-permute-start | bytes 208904 | tf_op jit(solution)/shard_map/ppermute | solution.py:644
  15.9 4.9 %collective-permute-done.4 = bf16[1,272,128]{2,1,0:T(8,128)(2,1)S(1)} collective-permute-done((bf16[1,272,128]{2,1,0:T(8,128)(2,1)S(1)}, bf16[1,272,128]{2,1,0:T(8,128)(2,1)S(1)}, u32[]{:S(2)}, u32[]{:S(2)}) %collective-permute-start.4) | collective-permute-done | bytes 69664 | tf_op jit(solution)/shard_map/ppermute | solution.py:644
  20.8 2.5 %collective-permute-start.5 = (bf16[2,272,128]{2,1,0:T(8,128)(2,1)S(1)}, bf16[2,272,128]{2,1,0:T(8,128)(2,1)S(1)}, u32[]{:S(2)}, u32[]{:S(2)}) collective-permute-start(bf16[2,272,128]{2,1,0:T(8,128)(2,1)S(1)} %pad_maximum_fusion.2), channel_id=1, source_target_pairs={{0,16},{1,17},{2,18},{3,19},{8,24},{9,25},{10,26},{11,27},{16,0},{... | collective-permute-start | bytes 417800 | tf_op jit(solution)/shard_map/ppermute | solution.py:644
  23.3 4.4 %collective-permute-done.5 = bf16[2,272,128]{2,1,0:T(8,128)(2,1)S(1)} collective-permute-done((bf16[2,272,128]{2,1,0:T(8,128)(2,1)S(1)}, bf16[2,272,128]{2,1,0:T(8,128)(2,1)S(1)}, u32[]{:S(2)}, u32[]{:S(2)}) %collective-permute-start.5) | collective-permute-done | bytes 139296 | tf_op jit(solution)/shard_map/ppermute | solution.py:644
  27.8 4.3 %collective-permute-start.6 = (bf16[4,272,128]{2,1,0:T(8,128)(2,1)S(1)}, bf16[4,272,128]{2,1,0:T(8,128)(2,1)S(1)}, u32[]{:S(2)}, u32[]{:S(2)}) collective-permute-start(bf16[4,272,128]{2,1,0:T(8,128)(2,1)S(1)} %pad_maximum_fusion.1), channel_id=1, source_target_pairs={{0,1},{1,0},{2,3},{3,2},{8,9},{9,8},{10,11},{11,10},{16,17},{17,16... | collective-permute-start | bytes 835592 | tf_op jit(solution)/shard_map/ppermute | solution.py:644
  32.1 4.5 %collective-permute-done.6 = bf16[4,272,128]{2,1,0:T(8,128)(2,1)S(1)} collective-permute-done((bf16[4,272,128]{2,1,0:T(8,128)(2,1)S(1)}, bf16[4,272,128]{2,1,0:T(8,128)(2,1)S(1)}, u32[]{:S(2)}, u32[]{:S(2)}) %collective-permute-start.6) | collective-permute-done | bytes 278560 | tf_op jit(solution)/shard_map/ppermute | solution.py:644
  36.6 0.1 pad_maximum_fusion.own_ref.after
  36.6 1.3 %collective-permute-start.7 = (bf16[8,272,128]{2,1,0:T(8,128)(2,1)S(1)}, bf16[8,272,128]{2,1,0:T(8,128)(2,1)S(1)}, u32[]{:S(2)}, u32[]{:S(2)}) collective-permute-start(bf16[8,272,128]{2,1,0:T(8,128)(2,1)S(1)} %pad_maximum_fusion.own_ref.after), channel_id=1, source_target_pairs={{0,4},{8,12},{1,5},{9,13},{2,6},{10,14},{3,7},{11,15},{16,20},{24,... | collective-permute-start | bytes 1671176 | tf_op jit(solution)/shard_map/ppermute | solution.py:645
  38.0 0.6 collective-permute-start.8
  38.6 3.4 %collective-permute-start.1 = (bf16[4,256,128]{2,1,0:T(8,128)(2,1)S(1)}, bf16[4,256,128]{2,1,0:T(8,128)(2,1)S(1)}, u32[]{:S(2)}, u32[]{:S(2)}) collective-permute-start(bf16[4,256,128]{2,1,0:T(8,128)(2,1)S(1)} %copy-done), channel_id=1, source_target_pairs={{2,0},{3,1},{0,2},{1,3},{6,4},{7,5},{4,6},{5,7},{10,8},{11,9},{8,1... | collective-permute-start | bytes 786440 | tf_op jit(solution)/shard_map/ppermute | solution.py:676
  42.0 1.5 %collective-permute-start.2 = (bf16[4,256,128]{2,1,0:T(8,128)(2,1)S(1)}, bf16[4,256,128]{2,1,0:T(8,128)(2,1)S(1)}, u32[]{:S(2)}, u32[]{:S(2)}) collective-permute-start(bf16[4,256,128]{2,1,0:T(8,128)(2,1)S(1)} %copy-done.1), channel_id=1, source_target_pairs={{1,0},{2,1},{3,2},{0,3},{5,4},{6,5},{7,6},{4,7},{9,8},{10,9},{11,1... | collective-permute-start | bytes 786440 | tf_op jit(solution)/shard_map/ppermute | solution.py:676
  43.5 0.5 collective-permute-start
  44.0 0.1 stack.88.place_ref
  44.1 0.0 collective-permute-done.7.came_ref
  44.2 7.8 %start_panel.1 = (bf16[4,384,256]{2,1,0:T(8,128)(2,1)S(1)}, bf16[8,64,128]{2,1,0:T(8,128)(2,1)S(1)}, f32[512,1024]{1,0:T(8,128)S(1)}) custom-call(s32[19]{0:T(128)S(1)} %stack.88.place_ref, f32[64]{0:T(128)S(1)} %copy-done.3, bf16[8,272,128]{2,1,0:T(8,128)(2,1)S(1)} %pad_maximum_fusion.own_ref.after, ...), custom_call_target="tpu_custom_call" | custom-call | tf_op jit(solution)/shard_map/start_panel/pallas_call | solution.py:364
  52.0 0.0 collective-permute-done.1.refs_1_
  52.0 0.0 collective-permute-done.2.refs_2_
  52.0 1.6 %collective-permute-done.refs_0_ = bf16[4,256,128]{2,1,0:T(8,128)(2,1)S(1)} collective-permute-done((bf16[4,256,128]{2,1,0:T(8,128)(2,1)S(1)}, bf16[4,256,128]{2,1,0:T(8,128)(2,1)S(1)}, u32[]{:S(2)}, u32[]{:S(2)}) %collective-permute-start) | collective-permute-done | bytes 262176 | tf_op jit(solution)/shard_map/ppermute | solution.py:676
  53.6 0.0 collective-permute-done.8.refs_6_.other_first
  53.6 0.7 assemble.2
  54.3 3.4 %collective-permute-start.9 = (bf16[4,4,256,128]{3,2,1,0:T(8,128)(2,1)S(1)}, bf16[4,4,256,128]{3,2,1,0:T(8,128)(2,1)S(1)}, u32[]{:S(2)}, u32[]{:S(2)}) collective-permute-start(bf16[4,4,256,128]{3,2,1,0:T(8,128)(2,1)S(1)} %get-tuple-element.34.after.native_ref), channel_id=1, source_target_pairs={{0,8},{1,9},{6,14},{7,15},{8,0},{9,1},{14,6},{15,7},{16,24},{17,25... | collective-permute-start | bytes 3145736 | tf_op jit(solution)/shard_map/ppermute | solution.py:688
  57.8 3.4 %collective-permute-start.10 = (bf16[3,4,256,128]{3,2,1,0:T(8,128)(2,1)S(1)}, bf16[3,4,256,128]{3,2,1,0:T(8,128)(2,1)S(1)}, u32[]{:S(2)}, u32[]{:S(2)}) collective-permute-start(bf16[3,4,256,128]{3,2,1,0:T(8,128)(2,1)S(1)} %get-tuple-element.35.own_rest), channel_id=1, source_target_pairs={{18,2},{19,3},{20,4},{21,5},{24,8},{25,9},{26,10},{27,11},{28,12},... | collective-permute-start | bytes 2359304 | tf_op jit(solution)/shard_map/ppermute | solution.py:680
  61.2 1.5 %collective-permute-start.12 = (bf16[4,256,128]{2,1,0:T(8,128)(2,1)S(1)}, bf16[4,256,128]{2,1,0:T(8,128)(2,1)S(1)}, u32[]{:S(2)}, u32[]{:S(2)}) collective-permute-start(bf16[4,256,128]{2,1,0:T(8,128)(2,1)S(1)} %get-tuple-element.33.own_first), channel_id=1, source_target_pairs={{2,0},{3,1},{0,2},{1,3},{6,4},{7,5},{4,6},{5,7},{10,8},{11,9},{8,1... | collective-permute-start | bytes 786440 | tf_op jit(solution)/shard_map/ppermute | solution.py:676
  62.7 1.1 collective-permute-start.11
  63.8 5.8 %next_panel.2.refs_4_.aug_in = f32[512,1024]{1,0:T(8,128)S(1)} custom-call(f32[512,1024]{1,0:T(8,128)S(1)} %get-tuple-element.31.refs_5_.aug_in, bf16[4,4,256,128]{3,2,1,0:T(8,128)(2,1)S(1)} %get-tuple-element.34.after.native_ref), custom_call_target="tpu_custom_call" | custom-call | tf_op jit(solution)/shard_map/next_panel/pallas_call | solution.py:385
  69.6 5.4 %collective-permute-done.12.refs_3_ = bf16[4,256,128]{2,1,0:T(8,128)(2,1)S(1)} collective-permute-done((bf16[4,256,128]{2,1,0:T(8,128)(2,1)S(1)}, bf16[4,256,128]{2,1,0:T(8,128)(2,1)S(1)}, u32[]{:S(2)}, u32[]{:S(2)}) %collective-permute-start.12) | collective-permute-done | bytes 262176 | tf_op jit(solution)/shard_map/ppermute | solution.py:676
  75.0 0.0 collective-permute-done.11.refs_2_
  75.0 0.7 sort.1
  75.8 1.9 %collective-permute-start.13 = (bf16[4,4,256,128]{3,2,1,0:T(8,128)(2,1)S(1)}, bf16[4,4,256,128]{3,2,1,0:T(8,128)(2,1)S(1)}, u32[]{:S(2)}, u32[]{:S(2)}) collective-permute-start(bf16[4,4,256,128]{3,2,1,0:T(8,128)(2,1)S(1)} %get-tuple-element.40), channel_id=1, source_target_pairs={{16,0},{17,1},{22,6},{23,7},{24,8},{25,9},{30,14},{31,15},{0,16},{... | collective-permute-start | bytes 3145736 | tf_op jit(solution)/shard_map/ppermute | solution.py:680
  77.7 0.1 collective-permute-start.14
  77.8 5.5 %next_panel.3.aug_in = f32[512,1024]{1,0:T(8,128)S(1)} custom-call(f32[512,1024]{1,0:T(8,128)S(1)} %next_panel.2.refs_4_.aug_in, bf16[4,4,256,128]{3,2,1,0:T(8,128)(2,1)S(1)} %get-tuple-element.41.after.own), custom_call_target="tpu_custom_call" | custom-call | tf_op jit(solution)/shard_map/next_panel/pallas_call | solution.py:385
  83.3 1.6 %collective-permute-start.16 = (bf16[4,4,256,128]{3,2,1,0:T(8,128)(2,1)S(1)}, bf16[4,4,256,128]{3,2,1,0:T(8,128)(2,1)S(1)}, u32[]{:S(2)}, u32[]{:S(2)}) collective-permute-start(bf16[4,4,256,128]{3,2,1,0:T(8,128)(2,1)S(1)} %get-tuple-element.41.after.own), channel_id=1, source_target_pairs={{0,4},{8,12},{1,5},{9,13},{6,2},{14,10},{7,3},{15,11},{24,28},{16,... | collective-permute-start | bytes 3145736 | tf_op jit(solution)/shard_map/ppermute | solution.py:622
  84.9 6.6 %last_panel.1 = (f32[512,512]{1,0:T(8,128)S(1)}, bf16[512,512]{1,0:T(8,128)(2,1)S(1)}, bf16[512,512]{1,0:T(8,128)(2,1)S(1)}, bf16[512,512]{1,0:T(8,128)(2,1)S(1)}) custom-call(f32[512,1024]{1,0:T(8,128)S(1)} %next_panel.3.aug_in, bf16[4,4,256,128]{3,2,1,0:T(8,128)(2,1)S(1)} %get-tuple-element.41.after.own, bf16[8,64,128]{2,1,0:T(8,128)(2,1)S(1)} %get-tuple-element.42.taper_ref), custom_call_target="tpu_custom_call" | custom-call | tf_op jit(solution)/shard_map/last_panel/pallas_call | solution.py:399
  91.4 0.0 collective-permute-done.14.refs_1_
  91.4 1.0 collective-permute-done.13.refs_0_
  92.5 1.3 %collective-permute-start.17 = (bf16[4,4,256,128]{3,2,1,0:T(8,128)(2,1)S(1)}, bf16[4,4,256,128]{3,2,1,0:T(8,128)(2,1)S(1)}, u32[]{:S(2)}, u32[]{:S(2)}) collective-permute-start(bf16[4,4,256,128]{3,2,1,0:T(8,128)(2,1)S(1)} %get-tuple-element.45.other.refs_0_), channel_id=1, source_target_pairs={{0,4},{8,12},{1,5},{9,13},{6,2},{14,10},{7,3},{15,11},{24,28},{16,... | collective-permute-start | bytes 3145736 | tf_op jit(solution)/shard_map/ppermute | solution.py:622
  93.8 0.7 assemble.3.own_rest
  94.5 1.2 collective-permute-start.15
  95.7 0.3 collective-permute-done.17.other_came
  96.0 3.6 %project.1.refs_1_.refs_0_ = bf16[512,2048]{1,0:T(8,128)(2,1)S(1)} custom-call(s32[19]{0:T(128)S(1)} %stack.88.place_ref, bf16[4,4,256,128]{3,2,1,0:T(8,128)(2,1)S(1)} %get-tuple-element.41.after.own, bf16[4,4,256,128]{3,2,1,0:T(8,128)(2,1)S(1)} %collective-permute-done.16.own_came, bf16[4,4,256,128]{3,2,1,0:T(8,128)(2,1)S(1)} %get-tuple-element.45.other.refs_0_, ...), custom_call_target="tpu_custom_call" | custom-call | tf_op jit(solution)/shard_map/project/pallas_call | solution.py:484
  99.6 8.1 %multiply_part.2.refs_3_ = f32[4096,2048]{1,0:T(8,128)} custom-call(s32[19]{0:T(128)S(1)} %stack.88.place_ref, bf16[4,256,128]{2,1,0:T(8,128)(2,1)S(1)} %get-tuple-element.36.own_first, bf16[3,4,256,128]{3,2,1,0:T(8,128)(2,1)S(1)} %get-tuple-element.35.own_rest, bf16[2,4,256,128]{3,2,1,0:T(8,128)(2,1)S(1)} %collective-permute-done.8.refs_6_.other_first, ...), custom_call_target="tpu_custom_call" | custom-call | tf_op jit(solution)/shard_map/multiply_part/pallas_call | solution.py:573
  107.7 4.2 %collective-permute-done.15.other_rest = bf16[3,4,256,128]{3,2,1,0:T(8,128)(2,1)S(1)} collective-permute-done((bf16[3,4,256,128]{3,2,1,0:T(8,128)(2,1)S(1)}, bf16[3,4,256,128]{3,2,1,0:T(8,128)(2,1)S(1)}, u32[]{:S(2)}, u32[]{:S(2)}) %collective-permute-start.15) | collective-permute-done | bytes 786464 | tf_op jit(solution)/shard_map/ppermute | solution.py:680
  111.9 8.9 %multiply_part.3 = f32[4096,2048]{1,0:T(8,128)} custom-call(s32[19]{0:T(128)S(1)} %stack.88.place_ref, bf16[4,256,128]{2,1,0:T(8,128)(2,1)S(1)} %get-tuple-element.33.own_first, bf16[3,4,256,128]{3,2,1,0:T(8,128)(2,1)S(1)} %assemble.3.own_rest, ...), custom_call_target="tpu_custom_call", output_to_operand_aliasing={{}: (8, {})} | custom-call | tf_op jit(solution)/shard_map/multiply_part/pallas_call | solution.py:573
  (16 shorter events, 0.1 us)
Async XLA Ops:
  0.0 44.2 %copy-start.2 = (f32[16384]{0:T(1024)S(1)}, f32[16384]{0:T(1024)}, u32[]{:S(2)}) copy-start(f32[16384]{0:T(1024)} %param.9) | copy-start | bytes 196612
  0.0 44.2 %copy-start.3 = (f32[64]{0:T(128)S(1)}, f32[64]{0:T(128)}, u32[]{:S(2)}) copy-start(f32[64]{0:T(128)} %taps_ref.1) | copy-start | bytes 772
  3.2 34.8 %copy-start.4 = (bf16[2,4,256,128]{3,2,1,0:T(8,128)(2,1)S(1)}, bf16[2,4,256,128]{3,2,1,0:T(8,128)(2,1)}, u32[]{:S(2)}) copy-start(bf16[2,4,256,128]{3,2,1,0:T(8,128)(2,1)} %get-tuple-element.32) | copy-start | bytes 1572868
  3.2 35.4 %copy-start = (bf16[4,256,128]{2,1,0:T(8,128)(2,1)S(1)}, bf16[4,256,128]{2,1,0:T(8,128)(2,1)}, u32[]{:S(2)}) copy-start(bf16[4,256,128]{2,1,0:T(8,128)(2,1)} %get-tuple-element.29.refs_3_) | copy-start | bytes 786436
  3.2 38.8 %copy-start.1 = (bf16[4,256,128]{2,1,0:T(8,128)(2,1)S(1)}, bf16[4,256,128]{2,1,0:T(8,128)(2,1)}, u32[]{:S(2)}) copy-start(bf16[4,256,128]{2,1,0:T(8,128)(2,1)} %get-tuple-element.28.refs_4_) | copy-start | bytes 786436
  3.3 7.3 %collective-permute-start.3 = (bf16[1,272,128]{2,1,0:T(8,128)(2,1)}, bf16[1,272,128]{2,1,0:T(8,128)(2,1)S(1)}, u32[]{:S(2)}, u32[]{:S(2)}) collective-permute-start(bf16[1,272,128]{2,1,0:T(8,128)(2,1)} %get-tuple-element.30), channel_id=1, source_target_pairs={{0,8},{1,9},{2,10},{3,11},{16,24},{17,25},{18,26},{19,27}} | collective-permute-start | bytes 208904 | tf_op jit(solution)/shard_map/ppermute | solution.py:622
  11.4 9.4 %collective-permute-start.4 = (bf16[1,272,128]{2,1,0:T(8,128)(2,1)S(1)}, bf16[1,272,128]{2,1,0:T(8,128)(2,1)S(1)}, u32[]{:S(2)}, u32[]{:S(2)}) collective-permute-start(bf16[1,272,128]{2,1,0:T(8,128)(2,1)S(1)} %broadcast_select_fusion), channel_id=1, source_target_pairs={{0,2},{1,3},{2,0},{3,1},{8,10},{9,11},{10,8},{11,9},{16,18},{17,19... | collective-permute-start | bytes 208904 | tf_op jit(solution)/shard_map/ppermute | solution.py:644
  20.8 6.9 %collective-permute-start.5 = (bf16[2,272,128]{2,1,0:T(8,128)(2,1)S(1)}, bf16[2,272,128]{2,1,0:T(8,128)(2,1)S(1)}, u32[]{:S(2)}, u32[]{:S(2)}) collective-permute-start(bf16[2,272,128]{2,1,0:T(8,128)(2,1)S(1)} %pad_maximum_fusion.2), channel_id=1, source_target_pairs={{0,16},{1,17},{2,18},{3,19},{8,24},{9,25},{10,26},{11,27},{16,0},{... | collective-permute-start | bytes 417800 | tf_op jit(solution)/shard_map/ppermute | solution.py:644
  27.8 8.8 %collective-permute-start.6 = (bf16[4,272,128]{2,1,0:T(8,128)(2,1)S(1)}, bf16[4,272,128]{2,1,0:T(8,128)(2,1)S(1)}, u32[]{:S(2)}, u32[]{:S(2)}) collective-permute-start(bf16[4,272,128]{2,1,0:T(8,128)(2,1)S(1)} %pad_maximum_fusion.1), channel_id=1, source_target_pairs={{0,1},{1,0},{2,3},{3,2},{8,9},{9,8},{10,11},{11,10},{16,17},{17,16... | collective-permute-start | bytes 835592 | tf_op jit(solution)/shard_map/ppermute | solution.py:644
  36.6 7.5 %collective-permute-start.7 = (bf16[8,272,128]{2,1,0:T(8,128)(2,1)S(1)}, bf16[8,272,128]{2,1,0:T(8,128)(2,1)S(1)}, u32[]{:S(2)}, u32[]{:S(2)}) collective-permute-start(bf16[8,272,128]{2,1,0:T(8,128)(2,1)S(1)} %pad_maximum_fusion.own_ref.after), channel_id=1, source_target_pairs={{0,4},{8,12},{1,5},{9,13},{2,6},{10,14},{3,7},{11,15},{16,20},{24,... | collective-permute-start | bytes 1671176 | tf_op jit(solution)/shard_map/ppermute | solution.py:645
  38.0 15.6 %collective-permute-start.8 = (bf16[2,4,256,128]{3,2,1,0:T(8,128)(2,1)S(1)}, bf16[2,4,256,128]{3,2,1,0:T(8,128)(2,1)S(1)}, u32[]{:S(2)}, u32[]{:S(2)}) collective-permute-start(bf16[2,4,256,128]{3,2,1,0:T(8,128)(2,1)S(1)} %copy-done.4), channel_id=1, source_target_pairs={{16,0},{17,1},{18,2},{19,3},{20,4},{21,5},{22,6},{23,7},{24,8},{25... | collective-permute-start | bytes 1572872 | tf_op jit(solution)/shard_map/ppermute | solution.py:680
  38.6 13.3 %collective-permute-start.1 = (bf16[4,256,128]{2,1,0:T(8,128)(2,1)S(1)}, bf16[4,256,128]{2,1,0:T(8,128)(2,1)S(1)}, u32[]{:S(2)}, u32[]{:S(2)}) collective-permute-start(bf16[4,256,128]{2,1,0:T(8,128)(2,1)S(1)} %copy-done), channel_id=1, source_target_pairs={{2,0},{3,1},{0,2},{1,3},{6,4},{7,5},{4,6},{5,7},{10,8},{11,9},{8,1... | collective-permute-start | bytes 786440 | tf_op jit(solution)/shard_map/ppermute | solution.py:676
  42.0 9.9 %collective-permute-start.2 = (bf16[4,256,128]{2,1,0:T(8,128)(2,1)S(1)}, bf16[4,256,128]{2,1,0:T(8,128)(2,1)S(1)}, u32[]{:S(2)}, u32[]{:S(2)}) collective-permute-start(bf16[4,256,128]{2,1,0:T(8,128)(2,1)S(1)} %copy-done.1), channel_id=1, source_target_pairs={{1,0},{2,1},{3,2},{0,3},{5,4},{6,5},{7,6},{4,7},{9,8},{10,9},{11,1... | collective-permute-start | bytes 786440 | tf_op jit(solution)/shard_map/ppermute | solution.py:676
  43.5 10.1 %collective-permute-start = (bf16[4,256,128]{2,1,0:T(8,128)(2,1)S(1)}, bf16[4,256,128]{2,1,0:T(8,128)(2,1)S(1)}, u32[]{:S(2)}, u32[]{:S(2)}) collective-permute-start(bf16[4,256,128]{2,1,0:T(8,128)(2,1)S(1)} %copy-done.1), channel_id=1, source_target_pairs={{3,0},{0,1},{1,2},{2,3},{7,4},{4,5},{5,6},{6,7},{11,8},{8,9},{9,10... | collective-permute-start | bytes 786440 | tf_op jit(solution)/shard_map/ppermute | solution.py:676
  54.3 20.7 %collective-permute-start.9 = (bf16[4,4,256,128]{3,2,1,0:T(8,128)(2,1)S(1)}, bf16[4,4,256,128]{3,2,1,0:T(8,128)(2,1)S(1)}, u32[]{:S(2)}, u32[]{:S(2)}) collective-permute-start(bf16[4,4,256,128]{3,2,1,0:T(8,128)(2,1)S(1)} %get-tuple-element.34.after.native_ref), channel_id=1, source_target_pairs={{0,8},{1,9},{6,14},{7,15},{8,0},{9,1},{14,6},{15,7},{16,24},{17,25... | collective-permute-start | bytes 3145736 | tf_op jit(solution)/shard_map/ppermute | solution.py:688
  57.8 17.3 %collective-permute-start.10 = (bf16[3,4,256,128]{3,2,1,0:T(8,128)(2,1)S(1)}, bf16[3,4,256,128]{3,2,1,0:T(8,128)(2,1)S(1)}, u32[]{:S(2)}, u32[]{:S(2)}) collective-permute-start(bf16[3,4,256,128]{3,2,1,0:T(8,128)(2,1)S(1)} %get-tuple-element.35.own_rest), channel_id=1, source_target_pairs={{18,2},{19,3},{20,4},{21,5},{24,8},{25,9},{26,10},{27,11},{28,12},... | collective-permute-start | bytes 2359304 | tf_op jit(solution)/shard_map/ppermute | solution.py:680
  61.2 13.8 %collective-permute-start.12 = (bf16[4,256,128]{2,1,0:T(8,128)(2,1)S(1)}, bf16[4,256,128]{2,1,0:T(8,128)(2,1)S(1)}, u32[]{:S(2)}, u32[]{:S(2)}) collective-permute-start(bf16[4,256,128]{2,1,0:T(8,128)(2,1)S(1)} %get-tuple-element.33.own_first), channel_id=1, source_target_pairs={{2,0},{3,1},{0,2},{1,3},{6,4},{7,5},{4,6},{5,7},{10,8},{11,9},{8,1... | collective-permute-start | bytes 786440 | tf_op jit(solution)/shard_map/ppermute | solution.py:676
  62.7 12.3 %collective-permute-start.11 = (bf16[4,256,128]{2,1,0:T(8,128)(2,1)S(1)}, bf16[4,256,128]{2,1,0:T(8,128)(2,1)S(1)}, u32[]{:S(2)}, u32[]{:S(2)}) collective-permute-start(bf16[4,256,128]{2,1,0:T(8,128)(2,1)S(1)} %get-tuple-element.36.own_first), channel_id=1, source_target_pairs={{3,0},{0,1},{1,2},{2,3},{7,4},{4,5},{5,6},{6,7},{11,8},{8,9},{9,10... | collective-permute-start | bytes 786440 | tf_op jit(solution)/shard_map/ppermute | solution.py:676
  75.8 16.7 %collective-permute-start.13 = (bf16[4,4,256,128]{3,2,1,0:T(8,128)(2,1)S(1)}, bf16[4,4,256,128]{3,2,1,0:T(8,128)(2,1)S(1)}, u32[]{:S(2)}, u32[]{:S(2)}) collective-permute-start(bf16[4,4,256,128]{3,2,1,0:T(8,128)(2,1)S(1)} %get-tuple-element.40), channel_id=1, source_target_pairs={{16,0},{17,1},{22,6},{23,7},{24,8},{25,9},{30,14},{31,15},{0,16},{... | collective-permute-start | bytes 3145736 | tf_op jit(solution)/shard_map/ppermute | solution.py:680
  77.7 13.7 %collective-permute-start.14 = (bf16[4,256,128]{2,1,0:T(8,128)(2,1)S(1)}, bf16[4,256,128]{2,1,0:T(8,128)(2,1)S(1)}, u32[]{:S(2)}, u32[]{:S(2)}) collective-permute-start(bf16[4,256,128]{2,1,0:T(8,128)(2,1)S(1)} %get-tuple-element.36.own_first), channel_id=1, source_target_pairs={{1,0},{2,1},{3,2},{0,3},{5,4},{6,5},{7,6},{4,7},{9,8},{10,9},{11,1... | collective-permute-start | bytes 786440 | tf_op jit(solution)/shard_map/ppermute | solution.py:676
  83.3 12.4 %collective-permute-start.16 = (bf16[4,4,256,128]{3,2,1,0:T(8,128)(2,1)S(1)}, bf16[4,4,256,128]{3,2,1,0:T(8,128)(2,1)S(1)}, u32[]{:S(2)}, u32[]{:S(2)}) collective-permute-start(bf16[4,4,256,128]{3,2,1,0:T(8,128)(2,1)S(1)} %get-tuple-element.41.after.own), channel_id=1, source_target_pairs={{0,4},{8,12},{1,5},{9,13},{6,2},{14,10},{7,3},{15,11},{24,28},{16,... | collective-permute-start | bytes 3145736 | tf_op jit(solution)/shard_map/ppermute | solution.py:622
  92.5 3.6 %collective-permute-start.17 = (bf16[4,4,256,128]{3,2,1,0:T(8,128)(2,1)S(1)}, bf16[4,4,256,128]{3,2,1,0:T(8,128)(2,1)S(1)}, u32[]{:S(2)}, u32[]{:S(2)}) collective-permute-start(bf16[4,4,256,128]{3,2,1,0:T(8,128)(2,1)S(1)} %get-tuple-element.45.other.refs_0_), channel_id=1, source_target_pairs={{0,4},{8,12},{1,5},{9,13},{6,2},{14,10},{7,3},{15,11},{24,28},{16,... | collective-permute-start | bytes 3145736 | tf_op jit(solution)/shard_map/ppermute | solution.py:622
  94.5 17.4 %collective-permute-start.15 = (bf16[3,4,256,128]{3,2,1,0:T(8,128)(2,1)S(1)}, bf16[3,4,256,128]{3,2,1,0:T(8,128)(2,1)S(1)}, u32[]{:S(2)}, u32[]{:S(2)}) collective-permute-start(bf16[3,4,256,128]{3,2,1,0:T(8,128)(2,1)S(1)} %assemble.3.own_rest), channel_id=1, source_target_pairs={{16,0},{17,1},{18,2},{19,3},{20,4},{21,5},{22,6},{23,7},{24,8},{25... | collective-permute-start | bytes 2359304 | tf_op jit(solution)/shard_map/ppermute | solution.py:680
